TPU v7x, 256 devices: a whole 4x4x8 slice. The times are simulated.
256 devices in a mesh: ctx: 16 (over y_lo, x, core), exp: 16 (over y_hi, z).
Axes of the slice: x: 4, y: 4 (y_hi: 2, y_lo: 2; y = y_hi * 2 + y_lo), z: 8, core: 2. Of those that a mesh axis runs over, the one named last changes fastest.
Arguments:
- query: bfloat16 [4096, 2048], P('ctx', 'exp'), may hold values from -8 to 8
- keys: bfloat16 [4096, 256], P('ctx'), may hold values from -8 to 8
- values: bfloat16 [4096, 256], P('ctx'), may hold values from -6 to 6
- out_proj: bfloat16 [2048, 2048], P('exp'), may hold values from -1.5 to 1.5
- residual: bfloat16 [4096, 2048], P(('ctx', 'exp')), may hold values from -4 to 4
- norm_gain: bfloat16 [2048], replicated, may hold values from 0.5 to 1.5
- expert_ids: int32 [4096, 8], P(('ctx', 'exp')), may hold values from 0 to 15, all different within a row; in each aligned block of 16 rows (0 to 15, 16 to 31, ...) at most 12 rows name the same one
- gate_values: bfloat16 [4096, 8], P(('ctx', 'exp')), may hold values from 0.049804688 to 0.44921875
- w_gate: bfloat16 [16, 2048, 768], P('exp'), may hold values from -0.125 to 0.125
- w_up: bfloat16 [16, 2048, 768], P('exp'), may hold values from -0.125 to 0.125
- w_down: bfloat16 [16, 768, 2048], P('exp'), may hold values from -0.21875 to 0.21875
Outputs:
- layer_out: bfloat16 [4096, 2048], P(('ctx', 'exp'))
Inputs may be any that keep to these rules, and one draw needn't show every extreme that they name: `expert_ids`: each row names 8 different experts. Within each aligned block of 16 rows no expert is named by more than 12 rows, and in some blocks an expert is named by exactly 12 rows.
All inputs are finite; a program needn't handle non-finite values.
Results may differ from a plain program's by a relative error of at most 0.024.
Values may be sent and summed in bfloat16 or wider, within the bound.
No kernel may reach another device: no remote copies, remote signals or barrier semaphores. Data moves between devices by JAX's collectives and lax.ppermute only.
A program may use at most 64 MiB of HBM per device.

v0:
```python
import math

import jax
import jax.numpy as jnp
from jax import lax
from jax.sharding import PartitionSpec as P

D = 2048
HEAD_DIM = 128
TOP = 8
HEADS = 16
KV_HEADS = 2
EXPERTS = 16


NEGATIVE = -1e30


def from_behind(block, axis, distance):
    devices = range(lax.axis_size(axis))
    route = [(i - distance, i) for i in devices if i - distance in devices]
    return lax.ppermute(block, axis, route)


def slot_table(route_ids, route_gates, expert_list, capacity):
    row_count = route_ids.shape[0]
    expert_count = expert_list.shape[0]
    matches = route_ids[:, :, None] == expert_list[None, None, :]
    routed = jnp.any(matches, axis=1)
    weight = jnp.sum(
        jnp.where(matches, route_gates[:, :, None].astype(jnp.float32), jnp.float32(0.0)), axis=1
    )
    position = jnp.cumsum(routed.astype(jnp.int32), axis=0) - 1
    offsets = jnp.arange(expert_count, dtype=jnp.int32)[None, :] * capacity
    target = jnp.where(routed, offsets + position, expert_count * capacity)
    row_numbers = jnp.arange(row_count, dtype=jnp.int32)[:, None]
    slot_rows = (
        jnp.zeros((expert_count * capacity,), jnp.int32)
        .at[target.reshape(-1)]
        .set(row_numbers.reshape(-1), mode="drop")
    )
    slot_gates = (
        jnp.zeros((expert_count * capacity,), jnp.float32)
        .at[target.reshape(-1)]
        .set(weight.reshape(-1), mode="drop")
    )
    return (slot_rows.reshape(expert_count, capacity), slot_gates.reshape(expert_count, capacity))


def expert_apply(rows, gate_w, up_w, down_w):
    gate_part = jnp.einsum("esd,edf->esf", rows, gate_w, preferred_element_type=jnp.float32)
    up_part = jnp.einsum("esd,edf->esf", rows, up_w, preferred_element_type=jnp.float32)
    inner = (jax.nn.silu(gate_part) * up_part).astype(jnp.bfloat16)
    return jnp.einsum("esf,efd->esd", inner, down_w, preferred_element_type=jnp.float32).astype(
        jnp.bfloat16
    )


def start_state(head_count, row_count, width):
    return (
        jnp.full((head_count, row_count), NEGATIVE, jnp.float32),
        jnp.zeros((head_count, row_count), jnp.float32),
        jnp.zeros((head_count, row_count, width), jnp.float32),
    )


def attend(state, queries, query_pos, paired, key_start):
    scale = 1.0 / math.sqrt(queries.shape[-1])

    def update(carry):
        run_max, run_total, run_acc = carry
        scores = (
            jnp.einsum("rhd,kd->hrk", queries, paired[0], preferred_element_type=jnp.float32)
            * scale
        )
        key_pos = key_start + jnp.arange(paired.shape[1], dtype=jnp.int32)
        allowed = key_pos[None, None, :] <= query_pos[None, :, None]
        scores = jnp.where(allowed, scores, jnp.float32(NEGATIVE))
        new_max = jnp.maximum(run_max, jnp.max(scores, axis=2))
        weights = jnp.where(allowed, jnp.exp(scores - new_max[:, :, None]), jnp.float32(0.0))
        factor = jnp.exp(run_max - new_max)
        new_total = run_total * factor + jnp.sum(weights, axis=2)
        mixed = jnp.einsum(
            "hrk,kd->hrd",
            weights.astype(jnp.bfloat16),
            paired[1],
            preferred_element_type=jnp.float32,
        )
        return (new_max, new_total, run_acc * factor[:, :, None] + mixed)

    skipped = (key_start > jnp.max(query_pos)) | (key_start < 0)
    return lax.cond(skipped, lambda carry: carry, update, state)


def finish(state):
    run_max, run_total, run_acc = state
    result = (run_acc / run_total[:, :, None]).astype(jnp.bfloat16)
    return result.transpose(1, 0, 2).reshape(result.shape[1], result.shape[0] * result.shape[2])


def shards(
    query,
    keys,
    values,
    out_proj,
    residual,
    norm_gain,
    expert_ids,
    gate_values,
    w_gate,
    w_up,
    w_down,
):
    tok_c = query.shape[0]
    heads_dev = query.shape[1] // HEAD_DIM
    tok_dev = residual.shape[0]
    exp_dev = w_gate.shape[0]
    n_ctx = lax.axis_size("ctx")
    n_exp = lax.axis_size("exp")
    ctx_index = lax.axis_index("ctx")
    group = HEADS // KV_HEADS
    kv_index = lax.axis_index("exp") * heads_dev // group
    queries = query.reshape(tok_c, heads_dev, HEAD_DIM)
    paired = jnp.stack(
        [
            lax.dynamic_slice_in_dim(keys, kv_index * HEAD_DIM, HEAD_DIM, 1),
            lax.dynamic_slice_in_dim(values, kv_index * HEAD_DIM, HEAD_DIM, 1),
        ]
    )
    query_pos = ctx_index * tok_c + jnp.arange(tok_c, dtype=jnp.int32)
    state = attend(
        start_state(heads_dev, tok_c, HEAD_DIM), queries, query_pos, paired, ctx_index * tok_c
    )

    def forward(turn, carry):
        moving, running = carry
        moving = from_behind(moving, "ctx", 1)
        source = ctx_index - turn
        return (moving, attend(running, queries, query_pos, moving, source * tok_c))

    paired, state = lax.fori_loop(1, n_ctx, forward, (paired, state))
    attn_out = finish(state)
    projected = lax.psum_scatter(
        jnp.dot(attn_out, out_proj, preferred_element_type=jnp.float32).astype(jnp.bfloat16),
        "exp",
        scatter_dimension=0,
        tiled=True,
    ).astype(jnp.float32)
    hidden_state = (residual.astype(jnp.float32) + projected).astype(jnp.bfloat16)
    hidden_wide = hidden_state.astype(jnp.float32)
    inverse = lax.rsqrt(jnp.mean(hidden_wide * hidden_wide, axis=-1, keepdims=True) + 1e-06)
    normed = (hidden_wide * inverse * norm_gain.astype(jnp.float32)).astype(jnp.bfloat16)
    most_dev = 3 * tok_dev * TOP // (2 * EXPERTS)
    rows_all, gates_all = (
        lax.all_gather(normed, "exp", axis=0, tiled=True),
        lax.all_gather(gate_values, "exp", axis=0, tiled=True),
    )
    ids_all = lax.all_gather(expert_ids, "exp", axis=0, tiled=True)
    own_experts = lax.axis_index("exp") * exp_dev + jnp.arange(exp_dev, dtype=jnp.int32)
    slot_rows, slot_gates = slot_table(ids_all, gates_all, own_experts, n_exp * most_dev)
    outputs = expert_apply(rows_all[slot_rows], w_gate, w_up, w_down)
    weighted = slot_gates[:, :, None] * outputs.astype(jnp.float32)
    partial_sums = (
        jnp.zeros((tok_c, D), jnp.float32).at[slot_rows.reshape(-1)].add(weighted.reshape(-1, D))
    )
    moe = lax.psum_scatter(
        partial_sums.astype(jnp.bfloat16), "exp", scatter_dimension=0, tiled=True
    ).astype(jnp.float32)
    return (hidden_wide + moe).astype(jnp.bfloat16)


def solution(mesh):
    return jax.shard_map(
        shards,
        mesh=mesh,
        in_specs=(
            P("ctx", "exp"),
            P("ctx", None),
            P("ctx", None),
            P("exp", None),
            P(("ctx", "exp"), None),
            P(),
            P(("ctx", "exp"), None),
            P(("ctx", "exp"), None),
            P("exp", None, None),
            P("exp", None, None),
            P("exp", None, None),
        ),
        out_specs=P(("ctx", "exp"), None),
        check_vma=False,
    )
```

profile of v0, /device:TPU:32, one launch (start us, length us, event | category | flops | bytes accessed | tf_op | source)
XLA Modules:
  0.0 660.3 jit_solution(7852507614099384812)
XLA Ops:
  9.0 1.6 conditional.2
  9.1 1.1 fusion.74
  10.6 103.4 %while.21 = (s32[]{:T(128)}, bf16[2,256,128]{2,1,0:T(8,128)(2,1)S(1)}, f32[1,256]{1,0:T(1,128)S(1)}, f32[1,256]{1,0:T(1,128)S(1)}, f32[1,256,128]{2,1,0:T(8,128)...) while((s32[]{:T(128)}, ...), condition=%wide.region_10.11_spmd.clone, body=%wide.region_5.10_spmd.clone.sunk | while | flops 34407432 | bytes 2058567 | solution.py:141
  10.6 1.7 collective-permute-start
  13.4 6.2 collective-permute-start
  20.6 5.3 collective-permute-start
  26.9 6.9 %collective-permute-start = (bf16[2,256,128]{2,1,0:T(8,128)(2,1)S(1)}, bf16[2,256,128]{2,1,0:T(8,128)(2,1)S(1)}, u32[]{:S(2)}, u32[]{:S(2)}) collective-permute-start(bf16[2,256,128]{2,1,0:T(8,128)(2,1)S(1)} %get-tuple-element.391), channel_id=1, source_target_pairs={{0,16},{16,32},{32,48},{48,64},{64,80},{80,96},{96,112},{112,128},... | collective-permute-start | bytes 393224 | tf_op jit(solution)/shard_map/while/body/eval_jaxpr/ppermute | solution.py:22
  34.8 5.3 collective-permute-start
  41.1 5.3 collective-permute-start
  47.5 5.3 collective-permute-start
  53.8 5.3 collective-permute-start
  60.1 5.3 collective-permute-start
  66.5 5.3 collective-permute-start
  72.8 5.3 collective-permute-start
  79.1 7.0 %collective-permute-start = (bf16[2,256,128]{2,1,0:T(8,128)(2,1)S(1)}, bf16[2,256,128]{2,1,0:T(8,128)(2,1)S(1)}, u32[]{:S(2)}, u32[]{:S(2)}) collective-permute-start(bf16[2,256,128]{2,1,0:T(8,128)(2,1)S(1)} %get-tuple-element.391), channel_id=1, source_target_pairs={{0,16},{16,32},{32,48},{48,64},{64,80},{80,96},{96,112},{112,128},... | collective-permute-start | bytes 393224 | tf_op jit(solution)/shard_map/while/body/eval_jaxpr/ppermute | solution.py:22
  87.1 7.4 %collective-permute-start = (bf16[2,256,128]{2,1,0:T(8,128)(2,1)S(1)}, bf16[2,256,128]{2,1,0:T(8,128)(2,1)S(1)}, u32[]{:S(2)}, u32[]{:S(2)}) collective-permute-start(bf16[2,256,128]{2,1,0:T(8,128)(2,1)S(1)} %get-tuple-element.391), channel_id=1, source_target_pairs={{0,16},{16,32},{32,48},{48,64},{64,80},{80,96},{96,112},{112,128},... | collective-permute-start | bytes 393224 | tf_op jit(solution)/shard_map/while/body/eval_jaxpr/ppermute | solution.py:22
  95.5 9.0 %collective-permute-start = (bf16[2,256,128]{2,1,0:T(8,128)(2,1)S(1)}, bf16[2,256,128]{2,1,0:T(8,128)(2,1)S(1)}, u32[]{:S(2)}, u32[]{:S(2)}) collective-permute-start(bf16[2,256,128]{2,1,0:T(8,128)(2,1)S(1)} %get-tuple-element.391), channel_id=1, source_target_pairs={{0,16},{16,32},{32,48},{48,64},{64,80},{80,96},{96,112},{112,128},... | collective-permute-start | bytes 393224 | tf_op jit(solution)/shard_map/while/body/eval_jaxpr/ppermute | solution.py:22
  105.5 7.4 %collective-permute-start = (bf16[2,256,128]{2,1,0:T(8,128)(2,1)S(1)}, bf16[2,256,128]{2,1,0:T(8,128)(2,1)S(1)}, u32[]{:S(2)}, u32[]{:S(2)}) collective-permute-start(bf16[2,256,128]{2,1,0:T(8,128)(2,1)S(1)} %get-tuple-element.391), channel_id=1, source_target_pairs={{0,16},{16,32},{32,48},{48,64},{64,80},{80,96},{96,112},{112,128},... | collective-permute-start | bytes 393224 | tf_op jit(solution)/shard_map/while/body/eval_jaxpr/ppermute | solution.py:22
  114.0 2.5 convolution_convert_fusion
  116.7 237.8 %reduce-scatter.3.cloned.1.call-done = bf16[16,2048]{1,0:T(8,128)(2,1)} async-done(((bf16[256,2048]{1,0:T(8,128)(2,1)}), bf16[16,2048]{1,0:T(8,128)(2,1)}) %reduce-scatter.3.cloned.1.call-update) | async-done | bytes 65552 | tf_op jit(solution)/shard_map/reduce_scatter | solution.py:143
  355.4 1.6 fusion.65
  357.1 37.0 %all-gather.1 = bf16[16,16,8]{1,2,0:T(8,128)(2,1)S(1)} all-gather(bf16[1,16,8]{1,2,0:T(8,128)(2,1)S(1)} %bitcast.104), channel_id=1, replica_groups=mesh['ctx'=16,'exp'=16] {'exp'}, dimensions={0}, use_global_device_ids=true | all-gather | bytes 4352 | tf_op jit(solution)/shard_map/all_gather | solution.py:156
  394.1 38.4 %all-gather = s32[16,16,8]{1,2,0:T(8,128)S(1)} all-gather(s32[1,16,8]{1,2,0:T(8,128)S(1)} %bitcast.102), channel_id=1, replica_groups=mesh['ctx'=16,'exp'=16] {'exp'}, dimensions={0}, use_global_device_ids=true | all-gather | bytes 8704 | tf_op jit(solution)/shard_map/all_gather | solution.py:158
  433.6 1.4 scatter_custom_fusion
  435.0 1.4 scatter_custom_fusion.1
  436.5 4.2 gather_fusion
  440.7 3.7 fusion.36
  444.4 5.1 fusion.44
  449.5 5.2 scatter_custom_fusion.2
  454.7 2.8 convert_element_type.96
  457.5 194.8 %reduce-scatter.5.cloned.1.call-done = bf16[16,2048]{1,0:T(8,128)(2,1)} async-done(((bf16[256,2048]{1,0:T(8,128)(2,1)}), bf16[16,2048]{1,0:T(8,128)(2,1)}) %reduce-scatter.5.cloned.1.call-update) | async-done | bytes 65552 | tf_op jit(solution)/shard_map/reduce_scatter | solution.py:166
  652.3 1.5 fusion.66
  (135 shorter events, 9.3 us)
Async XLA Ops:
  6.5 437.9 %copy-start = (bf16[1,768,2048]{2,1,0:T(8,128)(2,1)S(1)}, bf16[1,768,2048]{2,1,0:T(8,128)(2,1)}, u32[]{:S(2)}) copy-start(bf16[1,768,2048]{2,1,0:T(8,128)(2,1)} %param.27) | copy-start | bytes 9437188
  6.5 347.9 %reduce-scatter.3.cloned.1.call-start = ((), (), s32[]{:S(2)}) async-start(), calls=%async_computation.2 | async-start | bytes 1114112 | tf_op jit(solution)/shard_map/reduce_scatter | solution.py:143
  10.6 2.7 collective-permute-start
  13.4 7.2 %collective-permute-start = (bf16[2,256,128]{2,1,0:T(8,128)(2,1)S(1)}, bf16[2,256,128]{2,1,0:T(8,128)(2,1)S(1)}, u32[]{:S(2)}, u32[]{:S(2)}) collective-permute-start(bf16[2,256,128]{2,1,0:T(8,128)(2,1)S(1)} %get-tuple-element.391), channel_id=1, source_target_pairs={{0,16},{16,32},{32,48},{48,64},{64,80},{80,96},{96,112},{112,128},... | collective-permute-start | bytes 393224 | tf_op jit(solution)/shard_map/while/body/eval_jaxpr/ppermute | solution.py:22
  20.6 6.3 collective-permute-start
  26.9 7.9 %collective-permute-start = (bf16[2,256,128]{2,1,0:T(8,128)(2,1)S(1)}, bf16[2,256,128]{2,1,0:T(8,128)(2,1)S(1)}, u32[]{:S(2)}, u32[]{:S(2)}) collective-permute-start(bf16[2,256,128]{2,1,0:T(8,128)(2,1)S(1)} %get-tuple-element.391), channel_id=1, source_target_pairs={{0,16},{16,32},{32,48},{48,64},{64,80},{80,96},{96,112},{112,128},... | collective-permute-start | bytes 393224 | tf_op jit(solution)/shard_map/while/body/eval_jaxpr/ppermute | solution.py:22
  34.8 6.3 collective-permute-start
  41.1 6.3 collective-permute-start
  47.5 6.3 collective-permute-start
  53.8 6.3 collective-permute-start
  60.1 6.3 collective-permute-start
  66.5 6.3 collective-permute-start
  72.8 6.3 collective-permute-start
  79.1 8.0 %collective-permute-start = (bf16[2,256,128]{2,1,0:T(8,128)(2,1)S(1)}, bf16[2,256,128]{2,1,0:T(8,128)(2,1)S(1)}, u32[]{:S(2)}, u32[]{:S(2)}) collective-permute-start(bf16[2,256,128]{2,1,0:T(8,128)(2,1)S(1)} %get-tuple-element.391), channel_id=1, source_target_pairs={{0,16},{16,32},{32,48},{48,64},{64,80},{80,96},{96,112},{112,128},... | collective-permute-start | bytes 393224 | tf_op jit(solution)/shard_map/while/body/eval_jaxpr/ppermute | solution.py:22
  87.1 8.4 %collective-permute-start = (bf16[2,256,128]{2,1,0:T(8,128)(2,1)S(1)}, bf16[2,256,128]{2,1,0:T(8,128)(2,1)S(1)}, u32[]{:S(2)}, u32[]{:S(2)}) collective-permute-start(bf16[2,256,128]{2,1,0:T(8,128)(2,1)S(1)} %get-tuple-element.391), channel_id=1, source_target_pairs={{0,16},{16,32},{32,48},{48,64},{64,80},{80,96},{96,112},{112,128},... | collective-permute-start | bytes 393224 | tf_op jit(solution)/shard_map/while/body/eval_jaxpr/ppermute | solution.py:22
  95.5 10.0 %collective-permute-start = (bf16[2,256,128]{2,1,0:T(8,128)(2,1)S(1)}, bf16[2,256,128]{2,1,0:T(8,128)(2,1)S(1)}, u32[]{:S(2)}, u32[]{:S(2)}) collective-permute-start(bf16[2,256,128]{2,1,0:T(8,128)(2,1)S(1)} %get-tuple-element.391), channel_id=1, source_target_pairs={{0,16},{16,32},{32,48},{48,64},{64,80},{80,96},{96,112},{112,128},... | collective-permute-start | bytes 393224 | tf_op jit(solution)/shard_map/while/body/eval_jaxpr/ppermute | solution.py:22
  105.5 8.4 %collective-permute-start = (bf16[2,256,128]{2,1,0:T(8,128)(2,1)S(1)}, bf16[2,256,128]{2,1,0:T(8,128)(2,1)S(1)}, u32[]{:S(2)}, u32[]{:S(2)}) collective-permute-start(bf16[2,256,128]{2,1,0:T(8,128)(2,1)S(1)} %get-tuple-element.391), channel_id=1, source_target_pairs={{0,16},{16,32},{32,48},{48,64},{64,80},{80,96},{96,112},{112,128},... | collective-permute-start | bytes 393224 | tf_op jit(solution)/shard_map/while/body/eval_jaxpr/ppermute | solution.py:22
  114.0 2.7 copy-start.3
  114.0 240.4 %copy-start.1 = (bf16[16,2048]{1,0:T(8,128)(2,1)S(1)}, bf16[16,2048]{1,0:T(8,128)(2,1)}, u32[]{:S(2)}) copy-start(bf16[16,2048]{1,0:T(8,128)(2,1)} %param.21) | copy-start | bytes 196612
  114.0 243.0 %copy-start.5 = (bf16[16,8]{0,1:T(8,128)(2,1)S(1)}, bf16[16,8]{0,1:T(8,128)(2,1)}, u32[]{:S(2)}) copy-start(bf16[16,8]{0,1:T(8,128)(2,1)} %param.24) | copy-start | bytes 772
  114.0 280.1 %copy-start.4 = (s32[16,8]{0,1:T(8,128)S(1)}, s32[16,8]{0,1:T(8,128)}, u32[]{:S(2)}) copy-start(s32[16,8]{0,1:T(8,128)} %param.23) | copy-start | bytes 1540
  116.6 319.9 %all-gather.4.cloned.1.call-start = ((), (), s32[]{:S(2)}) async-start(), calls=%async_computation.3 | async-start | bytes 1114112 | tf_op jit(solution)/shard_map/all_gather | solution.py:155
  357.0 295.3 %reduce-scatter.5.cloned.1.call-start = ((), (), s32[]{:S(2)}) async-start(), calls=%async_computation.4 | async-start | bytes 1114112 | tf_op jit(solution)/shard_map/reduce_scatter | solution.py:166
  454.7 197.6 %copy-start.2 = (bf16[16,2048]{1,0:T(8,128)(2,1)S(1)}, bf16[16,2048]{1,0:T(8,128)(2,1)}, u32[]{:S(2)}) copy-start(bf16[16,2048]{1,0:T(8,128)(2,1)} %reduce-scatter.3.cloned.1.call-done) | copy-start | bytes 196612
Sparse Core Ops, SparseCore 0:
  116.7 237.6 reduce-scatter.2
  357.1 77.0 all-gather.3
  457.6 194.6 reduce-scatter.4
where the time goes:
time: 663 us; the launch traced here: 660 us
  waiting for transfers between devices  437 us (66%)
  starting transfers between devices  88.3 us (13%)
  blocking collectives  75.5 us (11%)
  between operations  14.2 us (2%)
  other arithmetic  13.4 us (2%)
  matrix products  12.7 us (2%)
  loops' own time  10.2 us (2%)
  local copies, waits for them, and re-layouts  8.69 us (1%)
    reduce_scatter x1, waiting for transfers between devices, shards(): lax.psum_scatter(jnp.dot(attn_out, out_proj, preferred_element_type=jnp.f...  238 us
    reduce_scatter x1, waiting for transfers between devices, shards(): lax.psum_scatter(partial_sums.astype(jnp.bfloat16), 'exp', scatter_dimens...  195 us
    ppermute x15, starting transfers between devices, from_behind(): return lax.ppermute(block, axis, route)  88.2 us
    all_gather x1, blocking collectives, shards(): ids_all = lax.all_gather(expert_ids, 'exp', axis=0, tiled=True)  38.4 us
    all_gather x1, blocking collectives, shards(): lax.all_gather(gate_values, 'exp', axis=0, tiled=True)  37 us
  transfers between devices with their start and end apart: 18, of which 17 were waited for; matrix products, arithmetic and copies ran while one was open for 1% of the time, Pallas kernels for 0%

commit v1 on v0

v1 whole, which is shorter than its diff:
```python
import math

import jax
import jax.numpy as jnp
from jax import lax
from jax.experimental import pallas as pl
from jax.experimental.pallas import tpu as pltpu
from jax.sharding import PartitionSpec as P

D = 2048
HEAD_DIM = 128
FF = 768
TOP = 8
HEADS = 16
KV_HEADS = 2
EXPERTS = 16
TOK_C = 256
TOK_DEV = 16
MOST_DEV = 12
N_CTX = 16
SLOTS = EXPERTS * MOST_DEV
NEGATIVE = -1e30

ROW_SWAP = [(i, i ^ 8) for i in range(16)]
CORE_SWAP = [(i, i ^ 1) for i in range(16)]


def x_shift(step):
    return [
        (y * 8 + x * 2 + c, y * 8 + (x + step) % 4 * 2 + c)
        for y in range(2)
        for x in range(4)
        for c in range(2)
    ]


def gather_blocks(block):
    me = lax.axis_index("ctx")
    row, x, core = me // 8, me // 2 % 4, me % 2
    other = lax.ppermute(block, "ctx", ROW_SWAP)
    pair = jnp.concatenate([block, other], axis=0)
    left = lax.ppermute(pair, "ctx", x_shift(1))
    right = lax.ppermute(pair, "ctx", x_shift(-1))
    half = block.shape[0]
    far_a = lax.ppermute(left[:half], "ctx", x_shift(1))
    far_b = lax.ppermute(right[half:], "ctx", x_shift(-1))
    mine = jnp.concatenate([pair, left, right, far_a, far_b], axis=0)
    theirs = lax.ppermute(mine, "ctx", CORE_SWAP)
    sources = []
    for c in (core, 1 - core):
        for dx in (0, -1, 1, 2):
            for r in (row, 1 - row):
                sources.append(r * 8 + (x + dx) % 4 * 2 + c)
    return jnp.concatenate([mine, theirs], axis=0), jnp.stack(sources)


def attention_kernel(query_ref, kv_ref, qpos_ref, kpos_ref, out_ref):
    scale = math.log2(math.e) / math.sqrt(HEAD_DIM)
    tile = 64

    def rows(i, _):
        at = pl.ds(pl.multiple_of(i * tile, tile), tile)
        scores = lax.dot_general(
            query_ref[at, :],
            kv_ref[:, :HEAD_DIM],
            (((1,), (1,)), ((), ())),
            preferred_element_type=jnp.float32,
        )
        allowed = kpos_ref[...] <= qpos_ref[at, :]
        scores = jnp.where(allowed, scores, jnp.float32(NEGATIVE))
        top = jnp.max(scores, axis=1, keepdims=True)
        weights = jnp.exp2((scores - top) * scale)
        total = jnp.sum(weights, axis=1, keepdims=True)
        mixed = jnp.dot(
            weights.astype(jnp.bfloat16), kv_ref[:, HEAD_DIM:], preferred_element_type=jnp.float32
        )
        out_ref[at, :] = (mixed / total).astype(jnp.bfloat16)
        return 0

    lax.fori_loop(0, query_ref.shape[0] // tile, rows, 0)


def attention(query, kv, query_pos, key_pos):
    rows, keys = query.shape[0], kv.shape[0]
    return pl.pallas_call(
        attention_kernel,
        out_shape=jax.ShapeDtypeStruct(query.shape, jnp.bfloat16),
        in_specs=[pl.BlockSpec(memory_space=pltpu.VMEM)] * 4,
        out_specs=pl.BlockSpec(memory_space=pltpu.VMEM),
        compiler_params=pltpu.CompilerParams(vmem_limit_bytes=32 * 1024 * 1024),
        cost_estimate=pl.CostEstimate(
            flops=4 * rows * keys * HEAD_DIM,
            bytes_accessed=keys * 2 * HEAD_DIM * 2,
            transcendentals=rows * keys,
        ),
    )(query, kv, query_pos.reshape(rows, 1), key_pos.reshape(1, keys))


def routing(ids, gates):
    named = ids[:, :, None] == jnp.arange(EXPERTS, dtype=jnp.int32)
    routed = jnp.any(named, axis=1)
    weight = jnp.sum(jnp.where(named, gates[:, :, None].astype(jnp.float32), 0.0), axis=1)
    position = jnp.cumsum(routed.astype(jnp.int32), axis=0) - 1
    place = position[:, :, None] == jnp.arange(MOST_DEV, dtype=jnp.int32)
    place = place & routed[:, :, None]
    pick = place.astype(jnp.bfloat16).reshape(ids.shape[0], SLOTS)
    mix = jnp.where(place, weight[:, :, None], 0.0).astype(jnp.bfloat16)
    return pick.T, mix.reshape(ids.shape[0], SLOTS)


def shards(
    query,
    keys,
    values,
    out_proj,
    residual,
    norm_gain,
    expert_ids,
    gate_values,
    w_gate,
    w_up,
    w_down,
):
    ctx_index = lax.axis_index("ctx")
    kv_index = lax.axis_index("exp") // (HEADS // KV_HEADS)
    block = jnp.concatenate(
        [
            lax.dynamic_slice_in_dim(keys, kv_index * HEAD_DIM, HEAD_DIM, 1),
            lax.dynamic_slice_in_dim(values, kv_index * HEAD_DIM, HEAD_DIM, 1),
        ],
        axis=1,
    )
    pick, mix = routing(expert_ids, gate_values)
    kv, sources = gather_blocks(block)
    offsets = jnp.arange(TOK_C, dtype=jnp.int32)
    key_pos = (sources[:, None] * TOK_C + offsets[None, :]).reshape(-1)
    attn = attention(query, kv, ctx_index * TOK_C + offsets, key_pos)
    partial = jnp.dot(attn, out_proj, preferred_element_type=jnp.float32).astype(jnp.bfloat16)
    parts = lax.all_to_all(partial, "exp", 0, 0, tiled=True)
    projected = jnp.sum(parts.reshape(16, TOK_DEV, D).astype(jnp.float32), axis=0)
    hidden_state = (residual.astype(jnp.float32) + projected).astype(jnp.bfloat16)
    hidden_wide = hidden_state.astype(jnp.float32)
    inverse = lax.rsqrt(jnp.mean(hidden_wide * hidden_wide, axis=-1, keepdims=True) + 1e-06)
    normed = (hidden_wide * inverse * norm_gain.astype(jnp.float32)).astype(jnp.bfloat16)
    sent = jnp.dot(pick, normed, preferred_element_type=jnp.float32).astype(jnp.bfloat16)
    rows = lax.all_to_all(sent, "exp", 0, 0, tiled=True)
    gate_part = jnp.dot(rows, w_gate[0], preferred_element_type=jnp.float32)
    up_part = jnp.dot(rows, w_up[0], preferred_element_type=jnp.float32)
    inner = (jax.nn.silu(gate_part) * up_part).astype(jnp.bfloat16)
    outputs = jnp.dot(inner, w_down[0], preferred_element_type=jnp.float32).astype(jnp.bfloat16)
    back = lax.all_to_all(outputs, "exp", 0, 0, tiled=True)
    moe = jnp.dot(mix, back, preferred_element_type=jnp.float32)
    return (hidden_wide + moe).astype(jnp.bfloat16)


def solution(mesh):
    return jax.shard_map(
        shards,
        mesh=mesh,
        in_specs=(
            P("ctx", "exp"),
            P("ctx", None),
            P("ctx", None),
            P("exp", None),
            P(("ctx", "exp"), None),
            P(),
            P(("ctx", "exp"), None),
            P(("ctx", "exp"), None),
            P("exp", None, None),
            P("exp", None, None),
            P("exp", None, None),
        ),
        out_specs=P(("ctx", "exp"), None),
        check_vma=False,
    )
```

time: 663 us -> 162 us (0.24)
  waiting for transfers between devices: 437 us -> 66.8 us
  starting transfers between devices: 88.3 us -> 25.1 us
  blocking collectives: 75.5 us -> 33.2 us
  between operations: 14.2 us -> 0.16 us
  other arithmetic: 13.4 us -> 2.65 us
  loops' own time: 10.2 us -> 0 us
    reduce_scatter x2 -> x0, waiting for transfers between devices: 433 us -> none  [the longest x1 238 us: shards(): lax.psum_scatter(jnp.dot(attn_out, out_proj, preferred_element_type=jnp.f...]
    ppermute x15 -> x6, starting transfers between devices: 88.2 us -> 8.28 us  [the longest x1 3.03 us: gather_blocks(): far_b = lax.ppermute(right[half:], 'ctx', x_shift(-1))]
    all_gather x2 -> x0, blocking collectives: 75.5 us -> none  [the longest x1 38.4 us: shards(): ids_all = lax.all_gather(expert_ids, 'exp', axis=0, tiled=True)]
    all_to_all x0 -> x2, waiting for transfers between devices: none -> 54.7 us  [the longest x1 27.5 us: shards(): back = lax.all_to_all(outputs, 'exp', 0, 0, tiled=True)]
    all_to_all x0 -> x1, blocking collectives: none -> 33.2 us  [shards(): rows = lax.all_to_all(sent, 'exp', 0, 0, tiled=True)]
    all_to_all x0 -> x2, starting transfers between devices: none -> 16.8 us  [the longest x1 11.3 us: shards(): parts = lax.all_to_all(partial, 'exp', 0, 0, tiled=True)]
    another operation x17 -> x0, loops' own time: 10.2 us -> none  [the longest x1 10.1 us: shards(): paired, state = lax.fori_loop(1, n_ctx, forward, (paired, state))]
    ppermute x15 -> x6, waiting for transfers between devices: 4.72 us -> 12 us  [the longest x1 4.4 us: gather_blocks(): left = lax.ppermute(pair, 'ctx', x_shift(1))]
  transfers between devices with their start and end apart: 18 -> 8, of which waited for: 17 -> 6; matrix products, arithmetic and copies ran while one was open for 1% -> 3% of each run, Pallas kernels for 0% -> 0%
where the time goes in v1:
time: 162 us; the launch traced here: 161 us
  waiting for transfers between devices  66.8 us (41%)
  blocking collectives  33.2 us (20%)
  starting transfers between devices  25.1 us (15%)
  local copies, waits for them, and re-layouts  14.4 us (9%)
  matrix products  13.8 us (9%)
  Pallas kernels  5.39 us (3%)
  other arithmetic  2.65 us (2%)
    all_to_all x1, blocking collectives, shards(): rows = lax.all_to_all(sent, 'exp', 0, 0, tiled=True)  33.2 us
    all_to_all x1, waiting for transfers between devices, shards(): back = lax.all_to_all(outputs, 'exp', 0, 0, tiled=True)  27.5 us
    all_to_all x1, waiting for transfers between devices, shards(): parts = lax.all_to_all(partial, 'exp', 0, 0, tiled=True)  27.2 us
    all_to_all x1, starting transfers between devices, shards(): parts = lax.all_to_all(partial, 'exp', 0, 0, tiled=True)  11.3 us
    all_to_all x1, starting transfers between devices, shards(): back = lax.all_to_all(outputs, 'exp', 0, 0, tiled=True)  5.49 us
    pallas_call x1, Pallas kernels, attention(): pl.pallas_call(attention_kernel, out_shape=jax.ShapeDtypeStruct(query.sha...  5.39 us
    dot_general x1, matrix products, shards(): jnp.dot(inner, w_down[0], preferred_element_type=jnp.float32)  4.87 us
    ppermute x1, waiting for transfers between devices, gather_blocks(): left = lax.ppermute(pair, 'ctx', x_shift(1))  4.4 us
  transfers between devices with their start and end apart: 8, of which 6 were waited for; matrix products, arithmetic and copies ran while one was open for 3% of the time, Pallas kernels for 0%

profile of v1, /device:TPU:32, one launch (start us, length us, event | category | flops | bytes accessed | tf_op | source)
XLA Modules:
  0.0 161.5 jit_solution(575494904451979672)
XLA Ops:
  0.0 1.0 constant_dynamic-slice_fusion
  1.0 0.7 constant_dynamic-update-slice_fusion.5
  1.8 1.6 collective-permute-start
  3.3 3.7 %collective-permute-done = bf16[256,256]{1,0:T(8,128)(2,1)S(1)} collective-permute-done((bf16[256,256]{1,0:T(8,128)(2,1)S(1)}, bf16[256,256]{1,0:T(8,128)(2,1)S(1)}, u32[]{:S(2)}, u32[]{:S(2)}) %collective-permute-start) | collective-permute-done | bytes 131104 | tf_op jit(solution)/shard_map/ppermute | solution.py:40
  7.0 1.6 collective-permute-start.1
  8.6 1.7 %collective-permute-start.2 = (bf16[512,256]{1,0:T(8,128)(2,1)S(1)}, bf16[512,256]{1,0:T(8,128)(2,1)S(1)}, u32[]{:S(2)}, u32[]{:S(2)}) collective-permute-start(bf16[512,256]{1,0:T(8,128)(2,1)S(1)} %pad_maximum_fusion), channel_id=1, source_target_pairs={{0,96},{16,112},{32,0},{48,16},{64,32},{80,48},{96,64},{112,80},{1... | collective-permute-start | bytes 786440 | tf_op jit(solution)/shard_map/ppermute | solution.py:43
  10.3 0.7 constant_dynamic-update-slice_fusion.4
  11.1 4.4 %collective-permute-done.1 = bf16[512,256]{1,0:T(8,128)(2,1)S(1)} collective-permute-done((bf16[512,256]{1,0:T(8,128)(2,1)S(1)}, bf16[512,256]{1,0:T(8,128)(2,1)S(1)}, u32[]{:S(2)}, u32[]{:S(2)}) %collective-permute-start.1) | collective-permute-done | bytes 262176 | tf_op jit(solution)/shard_map/ppermute | solution.py:42
  15.5 0.4 collective-permute-start.3
  15.9 3.0 %collective-permute-start.4 = (bf16[256,256]{1,0:T(8,128)(2,1)S(1)}, bf16[256,256]{1,0:T(8,128)(2,1)S(1)}, u32[]{:S(2)}, u32[]{:S(2)}) collective-permute-start(bf16[256,256]{1,0:T(8,128)(2,1)S(1)} %slice.9), channel_id=1, source_target_pairs={{0,96},{16,112},{32,0},{48,16},{64,32},{80,48},{96,64},{112,80},{1... | collective-permute-start | bytes 393224 | tf_op jit(solution)/shard_map/ppermute | solution.py:46
  18.9 0.8 constant_dynamic-update-slice_fusion.3
  19.7 0.8 constant_dynamic-update-slice_fusion.2
  20.6 1.2 collective-permute-done.3
  21.8 0.7 constant_dynamic-update-slice_fusion.1
  22.5 0.7 constant_dynamic-update-slice_fusion
  23.4 2.8 %collective-permute-done.5 = bf16[2048,256]{1,0:T(8,128)(2,1)} collective-permute-done((bf16[2048,256]{1,0:T(8,128)(2,1)}, bf16[2048,256]{1,0:T(8,128)(2,1)}, u32[]{:S(2)}, u32[]{:S(2)}) %collective-permute-start.5) | collective-permute-done | bytes 1048608 | tf_op jit(solution)/shard_map/ppermute | solution.py:48
  26.2 2.4 %constant_dynamic-update-slice_fusion.6.kv_ref = bf16[4096,256]{1,0:T(8,128)(2,1)} fusion(bf16[4096,256]{1,0:T(8,128)(2,1)} %get-tuple-element.12, bf16[2048,256]{1,0:T(8,128)(2,1)} %collective-permute-done.5), kind=kLoop, calls=%fused_computation.49 | loop fusion | bytes 2097152 | tf_op jit(solution)/shard_map/concatenate | solution.py:54
  28.6 5.4 %shard_map.109 = bf16[256,128]{1,0:T(8,128)(2,1)S(1)} custom-call(bf16[256,128]{1,0:T(8,128)(2,1)S(1)} %copy-done.1, bf16[4096,256]{1,0:T(8,128)(2,1)} %constant_dynamic-update-slice_fusion.6.kv_ref, s32[256,1]{1,0:T(8,128)S(1)} %iota_add_fusion.qpos_ref, s32[1,4096]{1,0:T(1,128)S(1)} %bitcast.48), custom_call_target="tpu_custom_call" | custom-call | flops 536870912 | bytes 2097152 | tf_op jit(solution)/shard_map/pallas_call | solution.py:85
  34.0 1.4 convolution_convert_fusion
  35.5 11.3 %all-to-all-start = ((bf16[16,16,2048]{2,1,0:T(8,128)(2,1)}), bf16[16,16,2048]{2,1,0:T(8,128)(2,1)}, u32[]{:S(2)}, u32[]{:S(2)}) async-start(bf16[16,16,2048]{2,1,0:T(8,128)(2,1)} %bitcast.49), calls=%async_computation | async-start | bytes 2097152 | tf_op jit(solution)/shard_map/all_to_all | solution.py:139
  47.6 27.2 %all-to-all-done = bf16[16,16,2048]{2,1,0:T(8,128)(2,1)} async-done(((bf16[16,16,2048]{2,1,0:T(8,128)(2,1)}), bf16[16,16,2048]{2,1,0:T(8,128)(2,1)}, u32[]{:S(2)}, u32[]{:S(2)}) %all-to-all-start) | async-done | bytes 1048608 | tf_op jit(solution)/shard_map/all_to_all | solution.py:139
  74.8 1.4 convert_reduce_fusion
  76.4 1.4 convolution_convert_fusion.1
  77.7 2.1 %all_to_all.22 = bf16[16,12,2048]{2,1,0:T(8,128)(2,1)} reshape(bf16[192,2048]{1,0:T(8,128)(2,1)} %convolution_convert_fusion.1) | data formatting | bytes 1572864 | tf_op jit(solution)/shard_map/all_to_all | solution.py:146
  79.9 33.2 %all_to_all.30 = bf16[16,12,2048]{2,1,0:T(8,128)(2,1)} all-to-all(bf16[16,12,2048]{2,1,0:T(8,128)(2,1)} %all_to_all.22), channel_id=1, replica_groups=mesh['ctx'=16,'exp'=16] {'exp'}, dimensions={0} | all-to-all | bytes 1572864 | tf_op jit(solution)/shard_map/all_to_all | solution.py:146
  113.0 2.1 %all_to_all.24 = bf16[192,2048]{1,0:T(8,128)(2,1)} reshape(bf16[16,12,2048]{2,1,0:T(8,128)(2,1)} %all_to_all.30) | data formatting | bytes 1572864 | tf_op jit(solution)/shard_map/all_to_all | solution.py:146
  115.1 3.7 %fusion.4 = f32[192,768]{1,0:T(8,128)} fusion(bf16[192,2048]{1,0:T(8,128)(2,1)} %all_to_all.24, bf16[1,2048,768]{2,1,0:T(8,128)(2,1)} %param.19), kind=kOutput, calls=%fused_computation.4 | convolution fusion | flops 603979776 | bytes 4521984 | tf_op jit(solution)/shard_map/dot_general | solution.py:147
  118.9 4.9 %fusion.6 = bf16[192,2048]{1,0:T(8,128)(2,1)} fusion(bf16[1,768,2048]{2,1,0:T(8,128)(2,1)S(1)} %copy-done, bf16[192,2048]{1,0:T(8,128)(2,1)} %all_to_all.24, bf16[1,2048,768]{2,1,0:T(8,128)(2,1)} %param.20, f32[192,768]{1,0:T(8,128)} %fusion.4), kind=kOutput, calls=%fused_computation.7 | convolution fusion | flops 1209237504 | bytes 8454144 | tf_op jit(solution)/shard_map/dot_general | solution.py:150
  123.7 2.1 %all_to_all.25 = bf16[16,12,2048]{2,1,0:T(8,128)(2,1)} reshape(bf16[192,2048]{1,0:T(8,128)(2,1)} %fusion.6) | data formatting | bytes 1572864 | tf_op jit(solution)/shard_map/all_to_all | solution.py:151
  125.9 5.5 %all-to-all-start.2 = ((bf16[16,12,2048]{2,1,0:T(8,128)(2,1)}), bf16[16,12,2048]{2,1,0:T(8,128)(2,1)}, u32[]{:S(2)}, u32[]{:S(2)}) async-start(bf16[16,12,2048]{2,1,0:T(8,128)(2,1)} %all_to_all.25), calls=%async_computation.2 | async-start | bytes 2097152 | tf_op jit(solution)/shard_map/all_to_all | solution.py:151
  131.5 27.5 %all-to-all-done.2 = bf16[16,12,2048]{2,1,0:T(8,128)(2,1)} async-done(((bf16[16,12,2048]{2,1,0:T(8,128)(2,1)}), bf16[16,12,2048]{2,1,0:T(8,128)(2,1)}, u32[]{:S(2)}, u32[]{:S(2)}) %all-to-all-start.2) | async-done | bytes 786464 | tf_op jit(solution)/shard_map/all_to_all | solution.py:151
  159.1 2.4 %fusion.10 = bf16[16,2048]{1,0:T(8,128)(2,1)} fusion(bf16[16,12,2048]{2,1,0:T(8,128)(2,1)} %all-to-all-done.2, bf16[16,2048]{1,0:T(8,128)(2,1)S(1)} %get-tuple-element.6, bf16[16,16]{1,0:T(8,128)(2,1)S(1)} %select_reduce_fusion, s32[16,16]{1,0:T(8,128)S(1)} %broadcast_add_fusion, pred[16,16]{1,0:T(8,128)(4,1)S(1)} %fusion.33), kind=kOutput, calls=%fused_computation.11 | convolution fusion | flops 12690432 | bytes 919296 | tf_op jit(solution)/shard_map/dot_general | solution.py:152
  (41 shorter events, 1.4 us)
Async XLA Ops:
  0.0 118.9 %copy-start = (bf16[1,768,2048]{2,1,0:T(8,128)(2,1)S(1)}, bf16[1,768,2048]{2,1,0:T(8,128)(2,1)}, u32[]{:S(2)}) copy-start(bf16[1,768,2048]{2,1,0:T(8,128)(2,1)} %param.21) | copy-start | bytes 9437188
  1.8 5.2 %collective-permute-start = (bf16[256,256]{1,0:T(8,128)(2,1)S(1)}, bf16[256,256]{1,0:T(8,128)(2,1)S(1)}, u32[]{:S(2)}, u32[]{:S(2)}) collective-permute-start(bf16[256,256]{1,0:T(8,128)(2,1)S(1)} %get-tuple-element.19), channel_id=1, source_target_pairs={{0,128},{16,144},{32,160},{48,176},{64,192},{80,208},{96,224},{112... | collective-permute-start | bytes 393224 | tf_op jit(solution)/shard_map/ppermute | solution.py:40
  7.0 8.5 %collective-permute-start.1 = (bf16[512,256]{1,0:T(8,128)(2,1)S(1)}, bf16[512,256]{1,0:T(8,128)(2,1)S(1)}, u32[]{:S(2)}, u32[]{:S(2)}) collective-permute-start(bf16[512,256]{1,0:T(8,128)(2,1)S(1)} %pad_maximum_fusion), channel_id=1, source_target_pairs={{0,32},{16,48},{32,64},{48,80},{64,96},{80,112},{96,0},{112,16},{1... | collective-permute-start | bytes 786440 | tf_op jit(solution)/shard_map/ppermute | solution.py:42
  8.6 7.3 %collective-permute-start.2 = (bf16[512,256]{1,0:T(8,128)(2,1)S(1)}, bf16[512,256]{1,0:T(8,128)(2,1)S(1)}, u32[]{:S(2)}, u32[]{:S(2)}) collective-permute-start(bf16[512,256]{1,0:T(8,128)(2,1)S(1)} %pad_maximum_fusion), channel_id=1, source_target_pairs={{0,96},{16,112},{32,0},{48,16},{64,32},{80,48},{96,64},{112,80},{1... | collective-permute-start | bytes 786440 | tf_op jit(solution)/shard_map/ppermute | solution.py:43
  15.5 6.3 %collective-permute-start.3 = (bf16[256,256]{1,0:T(8,128)(2,1)S(1)}, bf16[256,256]{1,0:T(8,128)(2,1)S(1)}, u32[]{:S(2)}, u32[]{:S(2)}) collective-permute-start(bf16[256,256]{1,0:T(8,128)(2,1)S(1)} %slice.8), channel_id=1, source_target_pairs={{0,32},{16,48},{32,64},{48,80},{64,96},{80,112},{96,0},{112,16},{1... | collective-permute-start | bytes 393224 | tf_op jit(solution)/shard_map/ppermute | solution.py:45
  15.9 6.6 %collective-permute-start.4 = (bf16[256,256]{1,0:T(8,128)(2,1)S(1)}, bf16[256,256]{1,0:T(8,128)(2,1)S(1)}, u32[]{:S(2)}, u32[]{:S(2)}) collective-permute-start(bf16[256,256]{1,0:T(8,128)(2,1)S(1)} %slice.9), channel_id=1, source_target_pairs={{0,96},{16,112},{32,0},{48,16},{64,32},{80,48},{96,64},{112,80},{1... | collective-permute-start | bytes 393224 | tf_op jit(solution)/shard_map/ppermute | solution.py:46
  19.7 8.8 %copy-start.1 = (bf16[256,128]{1,0:T(8,128)(2,1)S(1)}, bf16[256,128]{1,0:T(8,128)(2,1)}, u32[]{:S(2)}) copy-start(bf16[256,128]{1,0:T(8,128)(2,1)} %query_ref.1) | copy-start | bytes 196612
  23.2 3.0 %collective-permute-start.5 = (bf16[2048,256]{1,0:T(8,128)(2,1)}, bf16[2048,256]{1,0:T(8,128)(2,1)}, u32[]{:S(2)}, u32[]{:S(2)}) collective-permute-start(bf16[2048,256]{1,0:T(8,128)(2,1)} %get-tuple-element.11), channel_id=1, source_target_pairs={{0,16},{16,0},{32,48},{48,32},{64,80},{80,64},{96,112},{112,96},{1... | collective-permute-start | bytes 3145736 | tf_op jit(solution)/shard_map/ppermute | solution.py:48
  26.2 7.8 %copy-start.2 = (bf16[128,2048]{1,0:T(8,128)(2,1)S(1)}, bf16[128,2048]{1,0:T(8,128)(2,1)}, u32[]{:S(2)}) copy-start(bf16[128,2048]{1,0:T(8,128)(2,1)} %param.14) | copy-start | bytes 1572868
  34.0 12.8 %copy-start.4 = (bf16[2048]{0:T(1024)(128)(2,1)S(1)}, bf16[2048]{0:T(1024)(128)(2,1)}, u32[]{:S(2)}) copy-start(bf16[2048]{0:T(1024)(128)(2,1)} %param.16) | copy-start | bytes 12292
  34.0 12.8 %copy-start.5 = (s32[16,8]{0,1:T(8,128)S(1)}, s32[16,8]{0,1:T(8,128)}, u32[]{:S(2)}) copy-start(s32[16,8]{0,1:T(8,128)} %param.17) | copy-start | bytes 1540
  35.5 40.7 %copy-start.3 = (bf16[16,2048]{1,0:T(8,128)(2,1)S(1)}, bf16[16,2048]{1,0:T(8,128)(2,1)}, u32[]{:S(2)}) copy-start(bf16[16,2048]{1,0:T(8,128)(2,1)} %param.15) | copy-start | bytes 196612
  35.5 39.4 %all-to-all-start = ((bf16[16,16,2048]{2,1,0:T(8,128)(2,1)}), bf16[16,16,2048]{2,1,0:T(8,128)(2,1)}, u32[]{:S(2)}, u32[]{:S(2)}) async-start(bf16[16,16,2048]{2,1,0:T(8,128)(2,1)} %bitcast.49), calls=%async_computation | async-start | bytes 2097152 | tf_op jit(solution)/shard_map/all_to_all | solution.py:139
  123.7 7.6 %copy-start.6 = (bf16[16,8]{0,1:T(8,128)(2,1)S(1)}, bf16[16,8]{0,1:T(8,128)(2,1)}, u32[]{:S(2)}) copy-start(bf16[16,8]{0,1:T(8,128)(2,1)} %param.18) | copy-start | bytes 772
  125.9 33.2 %all-to-all-start.2 = ((bf16[16,12,2048]{2,1,0:T(8,128)(2,1)}), bf16[16,12,2048]{2,1,0:T(8,128)(2,1)}, u32[]{:S(2)}, u32[]{:S(2)}) async-start(bf16[16,12,2048]{2,1,0:T(8,128)(2,1)} %all_to_all.25), calls=%async_computation.2 | async-start | bytes 2097152 | tf_op jit(solution)/shard_map/all_to_all | solution.py:151

commit v2 on v1

v2 whole, which is shorter than its diff:
```python
import math

import jax
import jax.numpy as jnp
from jax import lax
from jax.experimental import pallas as pl
from jax.experimental.pallas import tpu as pltpu
from jax.sharding import PartitionSpec as P

D = 2048
HEAD_DIM = 128
FF = 768
TOP = 8
HEADS = 16
KV_HEADS = 2
EXPERTS = 16
TOK_C = 256
TOK_DEV = 16
NEGATIVE = -1e30
SCALE = math.log2(math.e) / math.sqrt(HEAD_DIM)
F32 = jnp.float32
BF16 = jnp.bfloat16

ROW_SWAP = [(i, i ^ 8) for i in range(16)]
CORE_SWAP = [(i, i ^ 1) for i in range(16)]
Y_SWAP = [(i, i ^ 8) for i in range(16)]
Z_SWAP = [(i, i ^ 1) for i in range(16)]


def x_shift(step):
    return [
        (y * 8 + x * 2 + c, y * 8 + (x + step) % 4 * 2 + c)
        for y in range(2)
        for x in range(4)
        for c in range(2)
    ]


def z_shift(step):
    return [(y * 8 + z, y * 8 + (z + step) % 8) for y in range(2) for z in range(8)]


def on_ctx(block, route):
    return lax.ppermute(block, "ctx", route)


def on_exp(block, route):
    return lax.ppermute(block, "exp", route)


def kernel_call(body, ins, out_shapes, flops, transcendentals=0, scratch=(), scalars=0):
    size = sum(a.size * a.dtype.itemsize for a in ins)
    specs = [pl.BlockSpec(memory_space=pltpu.SMEM)] * scalars
    specs += [pl.BlockSpec(memory_space=pltpu.VMEM)] * (len(ins) - scalars)
    return pl.pallas_call(
        body,
        out_shape=out_shapes,
        in_specs=specs,
        out_specs=jax.tree.map(lambda _: pl.BlockSpec(memory_space=pltpu.VMEM), out_shapes),
        scratch_shapes=list(scratch),
        compiler_params=pltpu.CompilerParams(vmem_limit_bytes=32 * 1024 * 1024),
        cost_estimate=pl.CostEstimate(
            flops=flops, bytes_accessed=size, transcendentals=transcendentals
        ),
    )(*ins)


def struct(shape, dtype):
    return jax.ShapeDtypeStruct(shape, dtype)


def block_scores(queries, qpos, kv_refs, kpos_ref):
    parts = []
    for n, ref in enumerate(kv_refs):
        scores = lax.dot_general(
            queries, ref[:, :HEAD_DIM], (((1,), (1,)), ((), ())), preferred_element_type=F32
        )
        allowed = kpos_ref[:, n * TOK_C : (n + 1) * TOK_C] <= qpos
        parts.append(jnp.where(allowed, scores, F32(NEGATIVE)))
    return parts


def attend(queries, qpos, kv_refs, kpos_ref, state):
    parts = block_scores(queries, qpos, kv_refs, kpos_ref)
    top = jnp.max(parts[0], axis=1, keepdims=True)
    for part in parts[1:]:
        top = jnp.maximum(top, jnp.max(part, axis=1, keepdims=True))
    if state is not None:
        old_top = state[:, HEAD_DIM : HEAD_DIM + 1]
        old_total = state[:, HEAD_DIM + 64 : HEAD_DIM + 65]
        top = jnp.maximum(top, old_top)
        factor = jnp.exp2((old_top - top) * SCALE)
        total, mixed = old_total * factor, state[:, :HEAD_DIM] * factor
    else:
        total, mixed = 0.0, 0.0
    for part, ref in zip(parts, kv_refs):
        weights = jnp.exp2((part - top) * SCALE)
        total = total + jnp.sum(weights, axis=1, keepdims=True)
        mixed = mixed + jnp.dot(
            weights.astype(BF16), ref[:, HEAD_DIM:], preferred_element_type=F32
        )
    lane = lax.broadcasted_iota(jnp.int32, (queries.shape[0], HEAD_DIM), 1)
    return mixed, jnp.where(lane < 64, top, total)


ROWS_TILE = 64


def attend_first(mine_ref, theirs_ref, qpos_ref, kpos_ref, *refs):
    kv_refs, out_ref = refs[:4], refs[4]
    half = mine_ref.shape[0]
    for n, q_ref in enumerate((mine_ref, theirs_ref)):

        def rows(i, _, n=n, q_ref=q_ref):
            at = pl.ds(pl.multiple_of(i * ROWS_TILE, ROWS_TILE), ROWS_TILE)
            to = pl.ds(pl.multiple_of(n * half + i * ROWS_TILE, ROWS_TILE), ROWS_TILE)
            mixed, stats = attend(q_ref[at, :], qpos_ref[to, :], kv_refs, kpos_ref, None)
            out_ref[to, :HEAD_DIM] = mixed
            out_ref[to, HEAD_DIM:] = stats
            return 0

        lax.fori_loop(0, half // ROWS_TILE, rows, 0)


def attend_second(mine_ref, theirs_ref, qpos_ref, kpos_ref, state_ref, *refs):
    kv_refs, outs = refs[:4], refs[4:]
    half = mine_ref.shape[0]
    for n, q_ref in enumerate((mine_ref, theirs_ref)):

        def rows(i, _, n=n, q_ref=q_ref):
            at = pl.ds(pl.multiple_of(i * ROWS_TILE, ROWS_TILE), ROWS_TILE)
            to = pl.ds(pl.multiple_of(n * half + i * ROWS_TILE, ROWS_TILE), ROWS_TILE)
            mixed, stats = attend(
                q_ref[at, :], qpos_ref[to, :], kv_refs, kpos_ref, state_ref[to, :]
            )
            outs[n][at, :HEAD_DIM] = mixed
            outs[n][at, HEAD_DIM:] = stats
            return 0

        lax.fori_loop(0, half // ROWS_TILE, rows, 0)


def project(place_ref, own_ref, other_ref, w_own_ref, *refs):
    near, far = refs[:3], refs[3:6]
    keep_ref, send_ref = refs[6:8]
    core, parity = place_ref[0], place_ref[1]
    own_top = own_ref[:, HEAD_DIM : HEAD_DIM + 1]
    other_top = other_ref[:, HEAD_DIM : HEAD_DIM + 1]
    top = jnp.maximum(own_top, other_top)
    own_factor = jnp.exp2((own_top - top) * SCALE)
    other_factor = jnp.exp2((other_top - top) * SCALE)
    total = own_ref[:, HEAD_DIM + 64 : HEAD_DIM + 65] * own_factor
    total = total + other_ref[:, HEAD_DIM + 64 : HEAD_DIM + 65] * other_factor
    mixed = own_ref[:, :HEAD_DIM] * own_factor + other_ref[:, :HEAD_DIM] * other_factor
    attn = (mixed / total).astype(BF16)
    heads = [attn[n * 64 : (n + 1) * 64] for n in range(4)]
    width = D // 2
    for side, ws in ((core, near), (1 - core, far)):
        at = pl.ds(pl.multiple_of(side * width, width), width)
        sums = jnp.dot(heads[0], w_own_ref[:, at], preferred_element_type=F32)
        for n in range(3):
            sums = sums + jnp.dot(heads[n + 1], ws[n][...], preferred_element_type=F32)
        for y in range(2):
            low, high = sums[y * 32 : y * 32 + 16], sums[y * 32 + 16 : y * 32 + 32]
            rows = pl.ds(y * 16, 16)
            keep_ref[rows, at] = jnp.where(parity == 0, low, high)
            send_ref[rows, at] = jnp.where(parity == 0, high, low).astype(BF16)


def add_up(keep_ref, recv_ref, out_ref, send_ref):
    sums = keep_ref[...] + recv_ref[...].astype(F32)
    out_ref[...] = sums
    send_ref[...] = sums.astype(BF16)


def normalise(place_ref, sums_ref, recv_ref, own_ref, other_ref, gain_ref, hidden_ref, normed_ref):
    y = place_ref[2]
    for n in range(2):
        at = pl.ds(n * 16, 16)
        residual = jnp.where(y == n, own_ref[...].astype(F32), other_ref[...].astype(F32))
        projected = sums_ref[at, :] + recv_ref[at, :].astype(F32)
        hidden = (residual + projected).astype(BF16)
        wide = hidden.astype(F32)
        inverse = lax.rsqrt(jnp.mean(wide * wide, axis=-1, keepdims=True) + 1e-06)
        hidden_ref[at, :] = hidden
        normed_ref[at, :] = (wide * inverse * gain_ref[...].astype(F32)).astype(BF16)


def expert(*refs):
    count = (len(refs) - 3) // 2
    rows_refs, (gate_ref, up_ref, down_ref), outs = refs[:count], refs[count : count + 3], refs[count + 3 :]
    rows = jnp.concatenate([r[...] for r in rows_refs], axis=0)
    gate_part = jnp.dot(rows, gate_ref[...], preferred_element_type=F32)
    up_part = jnp.dot(rows, up_ref[...], preferred_element_type=F32)
    inner = (gate_part * jax.nn.sigmoid(gate_part) * up_part).astype(BF16)
    result = jnp.dot(inner, down_ref[...], preferred_element_type=F32).astype(BF16)
    start = 0
    for out in outs:
        out[...] = result[start : start + out.shape[0]]
        start += out.shape[0]


def run_expert(rows, w_gate, w_up, w_down):
    total = sum(r.shape[0] for r in rows)
    return kernel_call(
        expert,
        [*rows, w_gate, w_up, w_down],
        [struct(r.shape, BF16) for r in rows],
        6 * total * D * FF,
        total * FF,
    )


def weigh(place_ref, weights_ref, *refs):
    outs, (keep_ref, send_ref) = refs[:8], refs[8:]
    y = place_ref[2]
    sums = []
    for half in range(2):
        at = pl.ds(half * 16, 16)
        total = 0.0
        for n in range(8):
            total = total + weights_ref[at, n : n + 1] * outs[n][at, :].astype(F32)
        sums.append(total)
    keep_ref[...] = jnp.where(y == 0, sums[0], sums[1])
    send_ref[...] = jnp.where(y == 0, sums[1], sums[0]).astype(BF16)


def finish(place_ref, hidden_ref, keep_ref, recv_ref, out_ref):
    y = place_ref[2]
    hidden = jnp.where(y == 0, hidden_ref[:16, :].astype(F32), hidden_ref[16:, :].astype(F32))
    out_ref[...] = (hidden + (keep_ref[...] + recv_ref[...].astype(F32))).astype(BF16)


def router_weights(ids, gates):
    named = ids[:, :, None] == jnp.arange(EXPERTS, dtype=jnp.int32)
    weight = jnp.sum(jnp.where(named, gates[:, :, None].astype(F32), 0.0), axis=1)
    return jnp.pad(weight, ((0, 0), (0, 128 - EXPERTS)))


def shards(
    query,
    keys,
    values,
    out_proj,
    residual,
    norm_gain,
    expert_ids,
    gate_values,
    w_gate,
    w_up,
    w_down,
):
    ctx, exp = lax.axis_index("ctx"), lax.axis_index("exp")
    row, x, core = ctx // 8, ctx // 2 % 4, ctx % 2
    y, z = exp // 8, exp % 8
    place = jnp.stack([core, z % 2, y]).astype(jnp.int32)
    kv_index = exp // (HEADS // KV_HEADS)
    block = jnp.concatenate(
        [
            lax.dynamic_slice_in_dim(keys, kv_index * HEAD_DIM, HEAD_DIM, 1),
            lax.dynamic_slice_in_dim(values, kv_index * HEAD_DIM, HEAD_DIM, 1),
        ],
        axis=1,
    )

    other = on_ctx(block, ROW_SWAP)
    near = [block] + [on_ctx(block, x_shift(s)) for s in (1, -1, 2)]

    pairs = query.reshape(2, 4, 32, HEAD_DIM)

    def rows_for(step):
        to = (z + 2 * step) % 8 // 2
        return lax.dynamic_slice_in_dim(pairs, to, 1, 1).reshape(64, HEAD_DIM)

    mine = jnp.concatenate(
        [rows_for(0)] + [on_exp(rows_for(s), z_shift(2 * s)) for s in (1, 2, 3)], axis=0
    )
    theirs = on_ctx(mine, CORE_SWAP)

    far = [other] + [on_ctx(other, x_shift(s)) for s in (1, -1, 2)]

    w_half = lax.dynamic_slice_in_dim(out_proj, core * (D // 2), D // 2, 1)
    w_near = [on_exp(w_half, z_shift(2 * s)) for s in (1, 2, 3)]
    w_far = [on_ctx(w, CORE_SWAP) for w in w_near]
    res_other = on_exp(residual, Y_SWAP)
    own_weights = router_weights(expert_ids, gate_values)
    other_weights = on_exp(own_weights, Y_SWAP)

    offsets = jnp.arange(TOK_C, dtype=jnp.int32)
    token = jnp.arange(64, dtype=jnp.int32)
    token = token // 32 * 128 + z // 2 * 32 + token % 32
    local = jnp.tile(token, 4)
    query_pos = jnp.concatenate([ctx * TOK_C + local, (ctx ^ 1) * TOK_C + local]).reshape(512, 1)

    def key_pos(r):
        sources = jnp.stack([r * 8 + (x + s) % 4 * 2 + core for s in (0, -1, 1, 2)])
        return (sources[:, None] * TOK_C + offsets[None, :]).reshape(1, 4 * TOK_C)

    flops = 4 * 512 * 1024 * HEAD_DIM
    state = kernel_call(
        attend_first,
        [mine, theirs, query_pos, key_pos(row), *near],
        struct((512, 256), F32),
        flops,
        512 * 1024,
    )
    own, swap = kernel_call(
        attend_second,
        [mine, theirs, query_pos, key_pos(1 - row), state, *far],
        [struct((256, 256), F32)] * 2,
        flops,
        512 * 1024,
    )
    joined = on_ctx(swap, CORE_SWAP)
    keep, send = kernel_call(
        project,
        [place, own, joined, out_proj, *w_near, *w_far],
        [struct((32, D), F32), struct((32, D), BF16)],
        2 * 64 * 512 * D,
        scalars=1,
    )
    sums, send = kernel_call(
        add_up,
        [keep, on_exp(send, Z_SWAP)],
        [struct((32, D), F32), struct((32, D), BF16)],
        32 * D,
    )
    hidden, normed = kernel_call(
        normalise,
        [place, sums, on_exp(send, Y_SWAP), residual, res_other, norm_gain.reshape(1, D)],
        [struct((32, D), BF16)] * 2,
        8 * 32 * D,
        scalars=1,
    )

    w = (w_gate[0], w_up[0], w_down[0])
    up, down = [normed], [normed]
    for s in range(3):
        up.append(on_exp(up[-1], z_shift(1)))
        down.append(on_exp(down[-1], z_shift(-1)))
    last_up = on_exp(up[3][:16], z_shift(1))
    last_down = on_exp(down[3][16:], z_shift(-1))
    back = [None] * 8
    back[0] = run_expert([normed], *w)[0]
    for s in (1, 2, 3):
        from_up, from_down = run_expert([up[s], down[s]], *w)
        back[s] = on_exp(from_up, z_shift(-s))
        back[8 - s] = on_exp(from_down, z_shift(s))
    back[4] = on_exp(
        jnp.concatenate(run_expert([last_up, last_down], *w), axis=0), z_shift(4)
    )
    both = jnp.where(
        y == 0,
        jnp.concatenate([own_weights, other_weights], axis=0),
        jnp.concatenate([other_weights, own_weights], axis=0),
    )
    column = y * 8 + (z + jnp.arange(8)) % 8
    chosen = (jnp.arange(128)[:, None] == column[None, :]).astype(F32)
    weights = jnp.sum(both[:, :, None] * chosen[None], axis=1)
    keep, send = kernel_call(
        weigh,
        [place, weights, *back],
        [struct((16, D), F32), struct((16, D), BF16)],
        16 * 32 * D,
        scalars=1,
    )
    return kernel_call(
        finish,
        [place, hidden, keep, on_exp(send, Y_SWAP)],
        struct((16, D), BF16),
        3 * 16 * D,
        scalars=1,
    )


def solution(mesh):
    return jax.shard_map(
        shards,
        mesh=mesh,
        in_specs=(
            P("ctx", "exp"),
            P("ctx", None),
            P("ctx", None),
            P("exp", None),
            P(("ctx", "exp"), None),
            P(),
            P(("ctx", "exp"), None),
            P(("ctx", "exp"), None),
            P("exp", None, None),
            P("exp", None, None),
            P("exp", None, None),
        ),
        out_specs=P(("ctx", "exp"), None),
        check_vma=False,
    )
```

time: 162 us -> 143 us (0.88); the launches traced: 161 us -> 141 us
  waiting for transfers between devices: 66.8 us -> 22.9 us
  starting transfers between devices: 25.1 us -> 66.8 us
  blocking collectives: 33.2 us -> 0 us
  Pallas kernels: 5.39 us -> 26.2 us
  matrix products: 13.8 us -> 0 us
  local copies, waits for them, and re-layouts: 14.4 us -> 22.3 us
    ppermute x6 -> x38, starting transfers between devices: 8.28 us -> 66.8 us  [the longest x26 53.9 us: on_exp(): return lax.ppermute(block, 'exp', route)]
    all_to_all x2 -> x0, waiting for transfers between devices: 54.7 us -> none  [the longest x1 27.5 us: shards(): back = lax.all_to_all(outputs, 'exp', 0, 0, tiled=True)]
    all_to_all x1 -> x0, blocking collectives: 33.2 us -> none  [shards(): rows = lax.all_to_all(sent, 'exp', 0, 0, tiled=True)]
    pallas_call x1 -> x12, Pallas kernels: 5.39 us -> 26.2 us  [kernel_call(): pl.pallas_call(body, out_shape=out_shapes, in_specs=specs, out_specs=jax....]
    all_to_all x2 -> x0, starting transfers between devices: 16.8 us -> none  [the longest x1 11.3 us: shards(): parts = lax.all_to_all(partial, 'exp', 0, 0, tiled=True)]
    dot_general x5 -> x0, matrix products: 13.8 us -> none  [the longest x1 4.87 us: shards(): jnp.dot(inner, w_down[0], preferred_element_type=jnp.float32)]
    unnamed x20 -> x51, local copies, waits for them, and re-layouts: 3.25 us -> 16.7 us
    ppermute x6 -> x38, waiting for transfers between devices: 12 us -> 22.9 us  [the longest x26 21 us: on_exp(): return lax.ppermute(block, 'exp', route)]
  transfers between devices with their start and end apart: 8 -> 38, of which waited for: 6 -> 10; matrix products, arithmetic and copies ran while one was open for 3% -> 6% of each run, Pallas kernels for 0% -> 15%
where the time goes in v2:
time: 143 us; the launch traced here: 141 us
  starting transfers between devices  66.8 us (47%)
  Pallas kernels  26.2 us (18%)
  waiting for transfers between devices  22.9 us (16%)
  local copies, waits for them, and re-layouts  22.3 us (16%)
  other arithmetic  2.15 us (2%)
    ppermute x26, starting transfers between devices, on_exp(): return lax.ppermute(block, 'exp', route)  53.9 us
    pallas_call x12, Pallas kernels, kernel_call(): pl.pallas_call(body, out_shape=out_shapes, in_specs=specs, out_specs=jax....  26.2 us
    ppermute x26, waiting for transfers between devices, on_exp(): return lax.ppermute(block, 'exp', route)  21 us
    unnamed x51, local copies, waits for them, and re-layouts  16.7 us
    ppermute x12, starting transfers between devices, on_ctx(): return lax.ppermute(block, 'ctx', route)  12.9 us
  transfers between devices with their start and end apart: 38, of which 10 were waited for; matrix products, arithmetic and copies ran while one was open for 6% of the time, Pallas kernels for 15%

profile of v2, /device:TPU:32, one launch (start us, length us, event | category | flops | bytes accessed | tf_op | source)
XLA Modules:
  0.0 140.7 jit_solution(5568174511545448115)
XLA Ops:
  4.8 3.3 %collective-permute-start = (bf16[64,128]{1,0:T(8,128)(2,1)S(1)}, bf16[64,128]{1,0:T(8,128)(2,1)S(1)}, u32[]{:S(2)}, u32[]{:S(2)}) collective-permute-start(bf16[64,128]{1,0:T(8,128)(2,1)S(1)} %bitcast.57), channel_id=1, source_target_pairs={{0,2},{1,3},{2,4},{3,5},{4,6},{5,7},{6,0},{7,1},{8,10},{9,11},{10,... | collective-permute-start | bytes 49160 | tf_op jit(solution)/shard_map/ppermute | solution.py:48
  8.1 4.5 %collective-permute-start.1 = (bf16[64,128]{1,0:T(8,128)(2,1)S(1)}, bf16[64,128]{1,0:T(8,128)(2,1)S(1)}, u32[]{:S(2)}, u32[]{:S(2)}) collective-permute-start(bf16[64,128]{1,0:T(8,128)(2,1)S(1)} %bitcast.56), channel_id=1, source_target_pairs={{0,4},{1,5},{2,6},{3,7},{4,0},{5,1},{6,2},{7,3},{8,12},{9,13},{10,... | collective-permute-start | bytes 49160 | tf_op jit(solution)/shard_map/ppermute | solution.py:48
  12.6 2.7 %collective-permute-start.2 = (bf16[64,128]{1,0:T(8,128)(2,1)S(1)}, bf16[64,128]{1,0:T(8,128)(2,1)S(1)}, u32[]{:S(2)}, u32[]{:S(2)}) collective-permute-start(bf16[64,128]{1,0:T(8,128)(2,1)S(1)} %bitcast.55), channel_id=1, source_target_pairs={{0,6},{1,7},{2,0},{3,1},{4,2},{5,3},{6,4},{7,5},{8,14},{9,15},{10,... | collective-permute-start | bytes 49160 | tf_op jit(solution)/shard_map/ppermute | solution.py:48
  17.3 1.8 %collective-permute-start.6 = (bf16[256,256]{1,0:T(8,128)(2,1)S(1)}, bf16[256,256]{1,0:T(8,128)(2,1)S(1)}, u32[]{:S(2)}, u32[]{:S(2)}) collective-permute-start(bf16[256,256]{1,0:T(8,128)(2,1)S(1)} %pad_maximum_fusion.refs_0_), channel_id=1, source_target_pairs={{0,64},{16,80},{32,96},{48,112},{64,0},{80,16},{96,32},{112,48},{1... | collective-permute-start | bytes 393224 | tf_op jit(solution)/shard_map/ppermute | solution.py:44
  22.7 2.2 %collective-permute-start.12 = (bf16[128,1024]{1,0:T(8,128)(2,1)}, bf16[128,1024]{1,0:T(8,128)(2,1)}, u32[]{:S(2)}, u32[]{:S(2)}) collective-permute-start(bf16[128,1024]{1,0:T(8,128)(2,1)} %constant_dynamic-slice_fusion), channel_id=1, source_target_pairs={{0,2},{1,3},{2,4},{3,5},{4,6},{5,7},{6,0},{7,1},{8,10},{9,11},{10,... | collective-permute-start | bytes 786440 | tf_op jit(solution)/shard_map/ppermute | solution.py:48
  24.9 3.2 %collective-permute-start.13 = (bf16[128,1024]{1,0:T(8,128)(2,1)}, bf16[128,1024]{1,0:T(8,128)(2,1)}, u32[]{:S(2)}, u32[]{:S(2)}) collective-permute-start(bf16[128,1024]{1,0:T(8,128)(2,1)} %constant_dynamic-slice_fusion), channel_id=1, source_target_pairs={{0,4},{1,5},{2,6},{3,7},{4,0},{5,1},{6,2},{7,3},{8,12},{9,13},{10,... | collective-permute-start | bytes 786440 | tf_op jit(solution)/shard_map/ppermute | solution.py:48
  28.1 1.9 %collective-permute-start.14 = (bf16[128,1024]{1,0:T(8,128)(2,1)}, bf16[128,1024]{1,0:T(8,128)(2,1)}, u32[]{:S(2)}, u32[]{:S(2)}) collective-permute-start(bf16[128,1024]{1,0:T(8,128)(2,1)} %constant_dynamic-slice_fusion), channel_id=1, source_target_pairs={{0,6},{1,7},{2,0},{3,1},{4,2},{5,3},{6,4},{7,5},{8,14},{9,15},{10,... | collective-permute-start | bytes 786440 | tf_op jit(solution)/shard_map/ppermute | solution.py:48
  38.6 3.6 %shard_map.109.state_ref = f32[512,256]{1,0:T(8,128)S(1)} custom-call(bf16[256,128]{1,0:T(8,128)(2,1)S(1)} %pad_maximum_fusion.2.mine_ref, bf16[256,128]{1,0:T(8,128)(2,1)S(1)} %collective-permute-done.3.theirs_ref, s32[512,1]{1,0:T(8,128)S(1)} %copy.31.qpos_ref, s32[1,1024]{1,0:T(1,128)S(1)} %bitcast.51, bf16[256,256]{1,0:T(8,128)(2,1)S(1)} %copy-done.7, ...), custom_call_target="tpu_custom_call" | custom-call | flops 268435456 | bytes 661504 | tf_op jit(solution)/shard_map/pallas_call | solution.py:55
  43.2 6.2 %shard_map.110 = (f32[256,256]{1,0:T(8,128)S(1)}, f32[256,256]{1,0:T(8,128)}) custom-call(bf16[256,128]{1,0:T(8,128)(2,1)S(1)} %pad_maximum_fusion.2.mine_ref, bf16[256,128]{1,0:T(8,128)(2,1)S(1)} %collective-permute-done.3.theirs_ref, s32[512,1]{1,0:T(8,128)S(1)} %copy.31.qpos_ref, s32[1,1024]{1,0:T(1,128)S(1)} %bitcast.52, ...), custom_call_target="tpu_custom_call" | custom-call | flops 268435456 | bytes 1185792 | tf_op jit(solution)/shard_map/pallas_call | solution.py:55
  55.0 2.0 %shard_map.111 = (f32[32,2048]{1,0:T(8,128)S(1)}, bf16[32,2048]{1,0:T(8,128)(2,1)S(1)}) custom-call(s32[3]{0:T(128)S(1)} %pad_add_fusion.1.place_ref, f32[256,256]{1,0:T(8,128)S(1)} %copy-done.9, f32[256,256]{1,0:T(8,128)S(1)} %collective-permute-done.11.other_ref, bf16[128,2048]{1,0:T(8,128)(2,1)S(1)} %copy-done.5, ...), custom_call_target="tpu_custom_call" | custom-call | flops 134217728 | bytes 2621452 | tf_op jit(solution)/shard_map/pallas_call | solution.py:55
  57.1 3.0 %collective-permute-start.18 = (bf16[32,2048]{1,0:T(8,128)(2,1)S(1)}, bf16[32,2048]{1,0:T(8,128)(2,1)S(1)}, u32[]{:S(2)}, u32[]{:S(2)}) collective-permute-start(bf16[32,2048]{1,0:T(8,128)(2,1)S(1)} %get-tuple-element.26), channel_id=1, source_target_pairs={{0,1},{1,0},{2,3},{3,2},{4,5},{5,4},{6,7},{7,6},{8,9},{9,8},{10,11... | collective-permute-start | bytes 393224 | tf_op jit(solution)/shard_map/ppermute | solution.py:48
  60.1 3.8 %collective-permute-done.18.recv_ref = bf16[32,2048]{1,0:T(8,128)(2,1)S(1)} collective-permute-done((bf16[32,2048]{1,0:T(8,128)(2,1)S(1)}, bf16[32,2048]{1,0:T(8,128)(2,1)S(1)}, u32[]{:S(2)}, u32[]{:S(2)}) %collective-permute-start.18) | collective-permute-done | bytes 131104 | tf_op jit(solution)/shard_map/ppermute | solution.py:48
  64.6 2.9 %collective-permute-start.19 = (bf16[32,2048]{1,0:T(8,128)(2,1)}, bf16[32,2048]{1,0:T(8,128)(2,1)S(1)}, u32[]{:S(2)}, u32[]{:S(2)}) collective-permute-start(bf16[32,2048]{1,0:T(8,128)(2,1)} %get-tuple-element.28), channel_id=1, source_target_pairs={{0,8},{1,9},{2,10},{3,11},{4,12},{5,13},{6,14},{7,15},{8,0},{9,1},... | collective-permute-start | bytes 393224 | tf_op jit(solution)/shard_map/ppermute | solution.py:48
  70.8 2.7 %collective-permute-done.20.other_ref = bf16[16,2048]{1,0:T(8,128)(2,1)} collective-permute-done((bf16[16,2048]{1,0:T(8,128)(2,1)}, bf16[16,2048]{1,0:T(8,128)(2,1)}, u32[]{:S(2)}, u32[]{:S(2)}) %collective-permute-start.20) | collective-permute-done | bytes 65568 | tf_op jit(solution)/shard_map/ppermute | solution.py:48
  77.6 2.3 %collective-permute-start.22 = (bf16[32,2048]{1,0:T(8,128)(2,1)S(1)}, bf16[32,2048]{1,0:T(8,128)(2,1)S(1)}, u32[]{:S(2)}, u32[]{:S(2)}) collective-permute-start(bf16[32,2048]{1,0:T(8,128)(2,1)S(1)} %get-tuple-element.30.refs_0_), channel_id=1, source_target_pairs={{0,1},{1,2},{2,3},{3,4},{4,5},{5,6},{6,7},{7,0},{8,9},{9,10},{10,1... | collective-permute-start | bytes 393224 | tf_op jit(solution)/shard_map/ppermute | solution.py:48
  81.3 1.9 %collective-permute-start.21 = (f32[16,128]{1,0:T(8,128)}, f32[16,128]{1,0:T(8,128)}, u32[]{:S(2)}, u32[]{:S(2)}) collective-permute-start(f32[16,128]{1,0:T(8,128)} %pad.4), channel_id=1, source_target_pairs={{0,8},{1,9},{2,10},{3,11},{4,12},{5,13},{6,14},{7,15},{8,0},{9,1},... | collective-permute-start | bytes 24584 | tf_op jit(solution)/shard_map/ppermute | solution.py:48
  83.2 2.0 %collective-permute-start.25 = (bf16[32,2048]{1,0:T(8,128)(2,1)S(1)}, bf16[32,2048]{1,0:T(8,128)(2,1)S(1)}, u32[]{:S(2)}, u32[]{:S(2)}) collective-permute-start(bf16[32,2048]{1,0:T(8,128)(2,1)S(1)} %collective-permute-done.22.refs_0_), channel_id=1, source_target_pairs={{0,1},{1,2},{2,3},{3,4},{4,5},{5,6},{6,7},{7,0},{8,9},{9,10},{10,1... | collective-permute-start | bytes 393224 | tf_op jit(solution)/shard_map/ppermute | solution.py:48
  86.1 2.8 %collective-permute-done.25.refs_0_ = bf16[32,2048]{1,0:T(8,128)(2,1)S(1)} collective-permute-done((bf16[32,2048]{1,0:T(8,128)(2,1)S(1)}, bf16[32,2048]{1,0:T(8,128)(2,1)S(1)}, u32[]{:S(2)}, u32[]{:S(2)}) %collective-permute-start.25) | collective-permute-done | bytes 131104 | tf_op jit(solution)/shard_map/ppermute | solution.py:48
  88.9 2.5 %collective-permute-start.28 = (bf16[32,2048]{1,0:T(8,128)(2,1)S(1)}, bf16[32,2048]{1,0:T(8,128)(2,1)S(1)}, u32[]{:S(2)}, u32[]{:S(2)}) collective-permute-start(bf16[32,2048]{1,0:T(8,128)(2,1)S(1)} %collective-permute-done.25.refs_0_), channel_id=1, source_target_pairs={{0,1},{1,2},{2,3},{3,4},{4,5},{5,6},{6,7},{7,0},{8,9},{9,10},{10,1... | collective-permute-start | bytes 393224 | tf_op jit(solution)/shard_map/ppermute | solution.py:48
  92.9 1.9 %copy-done.1 = bf16[1,2048,768]{2,1,0:T(8,128)(2,1)S(1)} copy-done((bf16[1,2048,768]{2,1,0:T(8,128)(2,1)S(1)}, bf16[1,2048,768]{2,1,0:T(8,128)(2,1)}, u32[]{:S(2)}) %copy-start.1) | copy-done | bytes 3145752
  94.8 1.9 %copy-done.3 = bf16[1,768,2048]{2,1,0:T(8,128)(2,1)S(1)} copy-done((bf16[1,768,2048]{2,1,0:T(8,128)(2,1)S(1)}, bf16[1,768,2048]{2,1,0:T(8,128)(2,1)}, u32[]{:S(2)}) %copy-start.3) | copy-done | bytes 3145752
  96.7 2.7 %shard_map.115 = (bf16[32,2048]{1,0:T(8,128)(2,1)S(1)}, bf16[32,2048]{1,0:T(8,128)(2,1)S(1)}) custom-call(bf16[32,2048]{1,0:T(8,128)(2,1)S(1)} %collective-permute-done.22.refs_0_, bf16[32,2048]{1,0:T(8,128)(2,1)} %collective-permute-done.23.refs_1_, bf16[2048,768]{1,0:T(8,128)(2,1)S(1)} %bitcast.36, bf16[2048,768]{1,0:T(8,128)(2,1)S(1)} %bitcast.41, ...), custom_call_target="tpu_custom_call" | custom-call | flops 603979776 | bytes 9699328 | tf_op jit(solution)/shard_map/pallas_call | solution.py:55
  99.4 3.6 %collective-permute-start.24 = (bf16[32,2048]{1,0:T(8,128)(2,1)S(1)}, bf16[32,2048]{1,0:T(8,128)(2,1)S(1)}, u32[]{:S(2)}, u32[]{:S(2)}) collective-permute-start(bf16[32,2048]{1,0:T(8,128)(2,1)S(1)} %get-tuple-element.31), channel_id=1, source_target_pairs={{0,7},{1,0},{2,1},{3,2},{4,3},{5,4},{6,5},{7,6},{8,15},{9,8},{10,9... | collective-permute-start | bytes 393224 | tf_op jit(solution)/shard_map/ppermute | solution.py:48
  103.4 2.1 %collective-permute-start.32 = (bf16[16,2048]{1,0:T(8,128)(2,1)S(1)}, bf16[16,2048]{1,0:T(8,128)(2,1)S(1)}, u32[]{:S(2)}, u32[]{:S(2)}) collective-permute-start(bf16[16,2048]{1,0:T(8,128)(2,1)S(1)} %slice.9), channel_id=1, source_target_pairs={{0,7},{1,0},{2,1},{3,2},{4,3},{5,4},{6,5},{7,6},{8,15},{9,8},{10,9... | collective-permute-start | bytes 196616 | tf_op jit(solution)/shard_map/ppermute | solution.py:48
  105.5 2.7 %shard_map.116 = (bf16[32,2048]{1,0:T(8,128)(2,1)S(1)}, bf16[32,2048]{1,0:T(8,128)(2,1)S(1)}) custom-call(bf16[32,2048]{1,0:T(8,128)(2,1)S(1)} %collective-permute-done.25.refs_0_, bf16[32,2048]{1,0:T(8,128)(2,1)} %collective-permute-done.26.refs_1_, bf16[2048,768]{1,0:T(8,128)(2,1)S(1)} %bitcast.37, bf16[2048,768]{1,0:T(8,128)(2,1)S(1)} %bitcast.42, ...), custom_call_target="tpu_custom_call" | custom-call | flops 603979776 | bytes 9699328 | tf_op jit(solution)/shard_map/pallas_call | solution.py:55
  108.2 2.8 %collective-permute-start.27 = (bf16[32,2048]{1,0:T(8,128)(2,1)S(1)}, bf16[32,2048]{1,0:T(8,128)(2,1)S(1)}, u32[]{:S(2)}, u32[]{:S(2)}) collective-permute-start(bf16[32,2048]{1,0:T(8,128)(2,1)S(1)} %get-tuple-element.32), channel_id=1, source_target_pairs={{0,6},{1,7},{2,0},{3,1},{4,2},{5,3},{6,4},{7,5},{8,14},{9,15},{10,... | collective-permute-start | bytes 393224 | tf_op jit(solution)/shard_map/ppermute | solution.py:48
  113.0 3.9 %collective-permute-start.30 = (bf16[32,2048]{1,0:T(8,128)(2,1)S(1)}, bf16[32,2048]{1,0:T(8,128)(2,1)S(1)}, u32[]{:S(2)}, u32[]{:S(2)}) collective-permute-start(bf16[32,2048]{1,0:T(8,128)(2,1)S(1)} %get-tuple-element.33), channel_id=1, source_target_pairs={{0,5},{1,6},{2,7},{3,0},{4,1},{5,2},{6,3},{7,4},{8,13},{9,14},{10,... | collective-permute-start | bytes 393224 | tf_op jit(solution)/shard_map/ppermute | solution.py:48
  119.9 3.1 %collective-permute-start.33 = (bf16[32,2048]{1,0:T(8,128)(2,1)S(1)}, bf16[32,2048]{1,0:T(8,128)(2,1)S(1)}, u32[]{:S(2)}, u32[]{:S(2)}) collective-permute-start(bf16[32,2048]{1,0:T(8,128)(2,1)S(1)} %pad_maximum_fusion.1), channel_id=1, source_target_pairs={{0,4},{1,5},{2,6},{3,7},{4,0},{5,1},{6,2},{7,3},{8,12},{9,13},{10,... | collective-permute-start | bytes 393224 | tf_op jit(solution)/shard_map/ppermute | solution.py:48
  124.9 2.1 %collective-permute-done.35.refs_6_ = bf16[32,2048]{1,0:T(8,128)(2,1)S(1)} collective-permute-done((bf16[32,2048]{1,0:T(8,128)(2,1)S(1)}, bf16[32,2048]{1,0:T(8,128)(2,1)S(1)}, u32[]{:S(2)}, u32[]{:S(2)}) %collective-permute-start.35) | collective-permute-done | bytes 131104 | tf_op jit(solution)/shard_map/ppermute | solution.py:48
  127.0 5.8 %collective-permute-done.34.refs_5_ = bf16[32,2048]{1,0:T(8,128)(2,1)S(1)} collective-permute-done((bf16[32,2048]{1,0:T(8,128)(2,1)S(1)}, bf16[32,2048]{1,0:T(8,128)(2,1)S(1)}, u32[]{:S(2)}, u32[]{:S(2)}) %collective-permute-start.34) | collective-permute-done | bytes 131104 | tf_op jit(solution)/shard_map/ppermute | solution.py:48
  133.6 2.1 %collective-permute-start.37 = (bf16[16,2048]{1,0:T(8,128)(2,1)S(1)}, bf16[16,2048]{1,0:T(8,128)(2,1)S(1)}, u32[]{:S(2)}, u32[]{:S(2)}) collective-permute-start(bf16[16,2048]{1,0:T(8,128)(2,1)S(1)} %get-tuple-element.40), channel_id=1, source_target_pairs={{0,8},{1,9},{2,10},{3,11},{4,12},{5,13},{6,14},{7,15},{8,0},{9,1},... | collective-permute-start | bytes 196616 | tf_op jit(solution)/shard_map/ppermute | solution.py:48
  135.7 3.8 %collective-permute-done.37.recv_ref = bf16[16,2048]{1,0:T(8,128)(2,1)S(1)} collective-permute-done((bf16[16,2048]{1,0:T(8,128)(2,1)S(1)}, bf16[16,2048]{1,0:T(8,128)(2,1)S(1)}, u32[]{:S(2)}, u32[]{:S(2)}) %collective-permute-start.37) | collective-permute-done | bytes 65568 | tf_op jit(solution)/shard_map/ppermute | solution.py:48
  (134 shorter events, 46.7 us)
Async XLA Ops:
  0.9 24.0 %collective-permute-start.4 = (bf16[256,256]{1,0:T(8,128)(2,1)S(1)}, bf16[256,256]{1,0:T(8,128)(2,1)S(1)}, u32[]{:S(2)}, u32[]{:S(2)}) collective-permute-start(bf16[256,256]{1,0:T(8,128)(2,1)S(1)} %pad_maximum_fusion.refs_0_), channel_id=1, source_target_pairs={{0,32},{16,48},{32,64},{48,80},{64,96},{80,112},{96,0},{112,16},{1... | collective-permute-start | bytes 393224 | tf_op jit(solution)/shard_map/ppermute | solution.py:44
  2.5 16.7 %collective-permute-start.7 = (bf16[256,256]{1,0:T(8,128)(2,1)S(1)}, bf16[256,256]{1,0:T(8,128)(2,1)}, u32[]{:S(2)}, u32[]{:S(2)}) collective-permute-start(bf16[256,256]{1,0:T(8,128)(2,1)S(1)} %pad_maximum_fusion.refs_0_), channel_id=1, source_target_pairs={{0,128},{16,144},{32,160},{48,176},{64,192},{80,208},{96,224},{112... | collective-permute-start | bytes 393224 | tf_op jit(solution)/shard_map/ppermute | solution.py:44
  4.8 10.7 %collective-permute-start = (bf16[64,128]{1,0:T(8,128)(2,1)S(1)}, bf16[64,128]{1,0:T(8,128)(2,1)S(1)}, u32[]{:S(2)}, u32[]{:S(2)}) collective-permute-start(bf16[64,128]{1,0:T(8,128)(2,1)S(1)} %bitcast.57), channel_id=1, source_target_pairs={{0,2},{1,3},{2,4},{3,5},{4,6},{5,7},{6,0},{7,1},{8,10},{9,11},{10,... | collective-permute-start | bytes 49160 | tf_op jit(solution)/shard_map/ppermute | solution.py:48
  8.1 9.1 %collective-permute-start.1 = (bf16[64,128]{1,0:T(8,128)(2,1)S(1)}, bf16[64,128]{1,0:T(8,128)(2,1)S(1)}, u32[]{:S(2)}, u32[]{:S(2)}) collective-permute-start(bf16[64,128]{1,0:T(8,128)(2,1)S(1)} %bitcast.56), channel_id=1, source_target_pairs={{0,4},{1,5},{2,6},{3,7},{4,0},{5,1},{6,2},{7,3},{8,12},{9,13},{10,... | collective-permute-start | bytes 49160 | tf_op jit(solution)/shard_map/ppermute | solution.py:48
  12.6 6.5 %collective-permute-start.2 = (bf16[64,128]{1,0:T(8,128)(2,1)S(1)}, bf16[64,128]{1,0:T(8,128)(2,1)S(1)}, u32[]{:S(2)}, u32[]{:S(2)}) collective-permute-start(bf16[64,128]{1,0:T(8,128)(2,1)S(1)} %bitcast.55), channel_id=1, source_target_pairs={{0,6},{1,7},{2,0},{3,1},{4,2},{5,3},{6,4},{7,5},{8,14},{9,15},{10,... | collective-permute-start | bytes 49160 | tf_op jit(solution)/shard_map/ppermute | solution.py:48
  15.5 12.6 %collective-permute-start.5 = (bf16[256,256]{1,0:T(8,128)(2,1)S(1)}, bf16[256,256]{1,0:T(8,128)(2,1)S(1)}, u32[]{:S(2)}, u32[]{:S(2)}) collective-permute-start(bf16[256,256]{1,0:T(8,128)(2,1)S(1)} %pad_maximum_fusion.refs_0_), channel_id=1, source_target_pairs={{0,96},{16,112},{32,0},{48,16},{64,32},{80,48},{96,64},{112,80},{1... | collective-permute-start | bytes 393224 | tf_op jit(solution)/shard_map/ppermute | solution.py:44
  17.3 12.9 %collective-permute-start.6 = (bf16[256,256]{1,0:T(8,128)(2,1)S(1)}, bf16[256,256]{1,0:T(8,128)(2,1)S(1)}, u32[]{:S(2)}, u32[]{:S(2)}) collective-permute-start(bf16[256,256]{1,0:T(8,128)(2,1)S(1)} %pad_maximum_fusion.refs_0_), channel_id=1, source_target_pairs={{0,64},{16,80},{32,96},{48,112},{64,0},{80,16},{96,32},{112,48},{1... | collective-permute-start | bytes 393224 | tf_op jit(solution)/shard_map/ppermute | solution.py:44
  19.2 13.1 %collective-permute-start.10 = (bf16[256,256]{1,0:T(8,128)(2,1)}, bf16[256,256]{1,0:T(8,128)(2,1)S(1)}, u32[]{:S(2)}, u32[]{:S(2)}) collective-permute-start(bf16[256,256]{1,0:T(8,128)(2,1)} %collective-permute-done.7.refs_0_), channel_id=1, source_target_pairs={{0,64},{16,80},{32,96},{48,112},{64,0},{80,16},{96,32},{112,48},{1... | collective-permute-start | bytes 393224 | tf_op jit(solution)/shard_map/ppermute | solution.py:44
  22.7 27.4 %collective-permute-start.12 = (bf16[128,1024]{1,0:T(8,128)(2,1)}, bf16[128,1024]{1,0:T(8,128)(2,1)}, u32[]{:S(2)}, u32[]{:S(2)}) collective-permute-start(bf16[128,1024]{1,0:T(8,128)(2,1)} %constant_dynamic-slice_fusion), channel_id=1, source_target_pairs={{0,2},{1,3},{2,4},{3,5},{4,6},{5,7},{6,0},{7,1},{8,10},{9,11},{10,... | collective-permute-start | bytes 786440 | tf_op jit(solution)/shard_map/ppermute | solution.py:48
  24.9 25.7 %collective-permute-start.13 = (bf16[128,1024]{1,0:T(8,128)(2,1)}, bf16[128,1024]{1,0:T(8,128)(2,1)}, u32[]{:S(2)}, u32[]{:S(2)}) collective-permute-start(bf16[128,1024]{1,0:T(8,128)(2,1)} %constant_dynamic-slice_fusion), channel_id=1, source_target_pairs={{0,4},{1,5},{2,6},{3,7},{4,0},{5,1},{6,2},{7,3},{8,12},{9,13},{10,... | collective-permute-start | bytes 786440 | tf_op jit(solution)/shard_map/ppermute | solution.py:48
  28.1 22.5 %collective-permute-start.14 = (bf16[128,1024]{1,0:T(8,128)(2,1)}, bf16[128,1024]{1,0:T(8,128)(2,1)}, u32[]{:S(2)}, u32[]{:S(2)}) collective-permute-start(bf16[128,1024]{1,0:T(8,128)(2,1)} %constant_dynamic-slice_fusion), channel_id=1, source_target_pairs={{0,6},{1,7},{2,0},{3,1},{4,2},{5,3},{6,4},{7,5},{8,14},{9,15},{10,... | collective-permute-start | bytes 786440 | tf_op jit(solution)/shard_map/ppermute | solution.py:48
  30.9 11.4 %collective-permute-start.8 = (bf16[256,256]{1,0:T(8,128)(2,1)}, bf16[256,256]{1,0:T(8,128)(2,1)}, u32[]{:S(2)}, u32[]{:S(2)}) collective-permute-start(bf16[256,256]{1,0:T(8,128)(2,1)} %collective-permute-done.7.refs_0_), channel_id=1, source_target_pairs={{0,32},{16,48},{32,64},{48,80},{64,96},{80,112},{96,0},{112,16},{1... | collective-permute-start | bytes 393224 | tf_op jit(solution)/shard_map/ppermute | solution.py:44
  33.0 9.2 %collective-permute-start.9 = (bf16[256,256]{1,0:T(8,128)(2,1)}, bf16[256,256]{1,0:T(8,128)(2,1)}, u32[]{:S(2)}, u32[]{:S(2)}) collective-permute-start(bf16[256,256]{1,0:T(8,128)(2,1)} %collective-permute-done.7.refs_0_), channel_id=1, source_target_pairs={{0,96},{16,112},{32,0},{48,16},{64,32},{80,48},{96,64},{112,80},{1... | collective-permute-start | bytes 393224 | tf_op jit(solution)/shard_map/ppermute | solution.py:44
  57.1 6.8 %collective-permute-start.18 = (bf16[32,2048]{1,0:T(8,128)(2,1)S(1)}, bf16[32,2048]{1,0:T(8,128)(2,1)S(1)}, u32[]{:S(2)}, u32[]{:S(2)}) collective-permute-start(bf16[32,2048]{1,0:T(8,128)(2,1)S(1)} %get-tuple-element.26), channel_id=1, source_target_pairs={{0,1},{1,0},{2,3},{3,2},{4,5},{5,4},{6,7},{7,6},{8,9},{9,8},{10,11... | collective-permute-start | bytes 393224 | tf_op jit(solution)/shard_map/ppermute | solution.py:48
  64.6 8.9 %collective-permute-start.19 = (bf16[32,2048]{1,0:T(8,128)(2,1)}, bf16[32,2048]{1,0:T(8,128)(2,1)S(1)}, u32[]{:S(2)}, u32[]{:S(2)}) collective-permute-start(bf16[32,2048]{1,0:T(8,128)(2,1)} %get-tuple-element.28), channel_id=1, source_target_pairs={{0,8},{1,9},{2,10},{3,11},{4,12},{5,13},{6,14},{7,15},{8,0},{9,1},... | collective-permute-start | bytes 393224 | tf_op jit(solution)/shard_map/ppermute | solution.py:48
  67.4 6.1 %collective-permute-start.20 = (bf16[16,2048]{1,0:T(8,128)(2,1)}, bf16[16,2048]{1,0:T(8,128)(2,1)}, u32[]{:S(2)}, u32[]{:S(2)}) collective-permute-start(bf16[16,2048]{1,0:T(8,128)(2,1)} %own_ref.1), channel_id=1, source_target_pairs={{0,8},{1,9},{2,10},{3,11},{4,12},{5,13},{6,14},{7,15},{8,0},{9,1},... | collective-permute-start | bytes 196616 | tf_op jit(solution)/shard_map/ppermute | solution.py:48
  77.6 5.6 %collective-permute-start.22 = (bf16[32,2048]{1,0:T(8,128)(2,1)S(1)}, bf16[32,2048]{1,0:T(8,128)(2,1)S(1)}, u32[]{:S(2)}, u32[]{:S(2)}) collective-permute-start(bf16[32,2048]{1,0:T(8,128)(2,1)S(1)} %get-tuple-element.30.refs_0_), channel_id=1, source_target_pairs={{0,1},{1,2},{2,3},{3,4},{4,5},{5,6},{6,7},{7,0},{8,9},{9,10},{10,1... | collective-permute-start | bytes 393224 | tf_op jit(solution)/shard_map/ppermute | solution.py:48
  81.3 10.8 %collective-permute-start.21 = (f32[16,128]{1,0:T(8,128)}, f32[16,128]{1,0:T(8,128)}, u32[]{:S(2)}, u32[]{:S(2)}) collective-permute-start(f32[16,128]{1,0:T(8,128)} %pad.4), channel_id=1, source_target_pairs={{0,8},{1,9},{2,10},{3,11},{4,12},{5,13},{6,14},{7,15},{8,0},{9,1},... | collective-permute-start | bytes 24584 | tf_op jit(solution)/shard_map/ppermute | solution.py:48
  83.2 5.7 %collective-permute-start.25 = (bf16[32,2048]{1,0:T(8,128)(2,1)S(1)}, bf16[32,2048]{1,0:T(8,128)(2,1)S(1)}, u32[]{:S(2)}, u32[]{:S(2)}) collective-permute-start(bf16[32,2048]{1,0:T(8,128)(2,1)S(1)} %collective-permute-done.22.refs_0_), channel_id=1, source_target_pairs={{0,1},{1,2},{2,3},{3,4},{4,5},{5,6},{6,7},{7,0},{8,9},{9,10},{10,1... | collective-permute-start | bytes 393224 | tf_op jit(solution)/shard_map/ppermute | solution.py:48
  85.3 6.1 %collective-permute-start.26 = (bf16[32,2048]{1,0:T(8,128)(2,1)}, bf16[32,2048]{1,0:T(8,128)(2,1)}, u32[]{:S(2)}, u32[]{:S(2)}) collective-permute-start(bf16[32,2048]{1,0:T(8,128)(2,1)} %collective-permute-done.23.refs_1_), channel_id=1, source_target_pairs={{0,7},{1,0},{2,1},{3,2},{4,3},{5,4},{6,5},{7,6},{8,15},{9,8},{10,9... | collective-permute-start | bytes 393224 | tf_op jit(solution)/shard_map/ppermute | solution.py:48
  88.9 14.1 %collective-permute-start.28 = (bf16[32,2048]{1,0:T(8,128)(2,1)S(1)}, bf16[32,2048]{1,0:T(8,128)(2,1)S(1)}, u32[]{:S(2)}, u32[]{:S(2)}) collective-permute-start(bf16[32,2048]{1,0:T(8,128)(2,1)S(1)} %collective-permute-done.25.refs_0_), channel_id=1, source_target_pairs={{0,1},{1,2},{2,3},{3,4},{4,5},{5,6},{6,7},{7,0},{8,9},{9,10},{10,1... | collective-permute-start | bytes 393224 | tf_op jit(solution)/shard_map/ppermute | solution.py:48
  91.4 12.0 %collective-permute-start.29 = (bf16[32,2048]{1,0:T(8,128)(2,1)}, bf16[32,2048]{1,0:T(8,128)(2,1)S(1)}, u32[]{:S(2)}, u32[]{:S(2)}) collective-permute-start(bf16[32,2048]{1,0:T(8,128)(2,1)} %collective-permute-done.26.refs_1_), channel_id=1, source_target_pairs={{0,7},{1,0},{2,1},{3,2},{4,3},{5,4},{6,5},{7,6},{8,15},{9,8},{10,9... | collective-permute-start | bytes 393224 | tf_op jit(solution)/shard_map/ppermute | solution.py:48
  99.4 19.3 %collective-permute-start.24 = (bf16[32,2048]{1,0:T(8,128)(2,1)S(1)}, bf16[32,2048]{1,0:T(8,128)(2,1)S(1)}, u32[]{:S(2)}, u32[]{:S(2)}) collective-permute-start(bf16[32,2048]{1,0:T(8,128)(2,1)S(1)} %get-tuple-element.31), channel_id=1, source_target_pairs={{0,7},{1,0},{2,1},{3,2},{4,3},{5,4},{6,5},{7,6},{8,15},{9,8},{10,9... | collective-permute-start | bytes 393224 | tf_op jit(solution)/shard_map/ppermute | solution.py:48
  103.0 16.9 %collective-permute-start.36 = (bf16[32,2048]{1,0:T(8,128)(2,1)S(1)}, bf16[32,2048]{1,0:T(8,128)(2,1)S(1)}, u32[]{:S(2)}, u32[]{:S(2)}) collective-permute-start(bf16[32,2048]{1,0:T(8,128)(2,1)S(1)} %get-tuple-element.38), channel_id=1, source_target_pairs={{0,1},{1,2},{2,3},{3,4},{4,5},{5,6},{6,7},{7,0},{8,9},{9,10},{10,1... | collective-permute-start | bytes 393224 | tf_op jit(solution)/shard_map/ppermute | solution.py:48
  103.0 9.7 %collective-permute-start.31 = (bf16[16,2048]{1,0:T(8,128)(2,1)S(1)}, bf16[16,2048]{1,0:T(8,128)(2,1)S(1)}, u32[]{:S(2)}, u32[]{:S(2)}) collective-permute-start(bf16[16,2048]{1,0:T(8,128)(2,1)S(1)} %slice.8), channel_id=1, source_target_pairs={{0,1},{1,2},{2,3},{3,4},{4,5},{5,6},{6,7},{7,0},{8,9},{9,10},{10,1... | collective-permute-start | bytes 196616 | tf_op jit(solution)/shard_map/ppermute | solution.py:48
  103.4 9.7 %collective-permute-start.32 = (bf16[16,2048]{1,0:T(8,128)(2,1)S(1)}, bf16[16,2048]{1,0:T(8,128)(2,1)S(1)}, u32[]{:S(2)}, u32[]{:S(2)}) collective-permute-start(bf16[16,2048]{1,0:T(8,128)(2,1)S(1)} %slice.9), channel_id=1, source_target_pairs={{0,7},{1,0},{2,1},{3,2},{4,3},{5,4},{6,5},{7,6},{8,15},{9,8},{10,9... | collective-permute-start | bytes 196616 | tf_op jit(solution)/shard_map/ppermute | solution.py:48
  108.2 16.8 %collective-permute-start.27 = (bf16[32,2048]{1,0:T(8,128)(2,1)S(1)}, bf16[32,2048]{1,0:T(8,128)(2,1)S(1)}, u32[]{:S(2)}, u32[]{:S(2)}) collective-permute-start(bf16[32,2048]{1,0:T(8,128)(2,1)S(1)} %get-tuple-element.32), channel_id=1, source_target_pairs={{0,6},{1,7},{2,0},{3,1},{4,2},{5,3},{6,4},{7,5},{8,14},{9,15},{10,... | collective-permute-start | bytes 393224 | tf_op jit(solution)/shard_map/ppermute | solution.py:48
  112.8 14.2 %collective-permute-start.35 = (bf16[32,2048]{1,0:T(8,128)(2,1)S(1)}, bf16[32,2048]{1,0:T(8,128)(2,1)S(1)}, u32[]{:S(2)}, u32[]{:S(2)}) collective-permute-start(bf16[32,2048]{1,0:T(8,128)(2,1)S(1)} %get-tuple-element.37), channel_id=1, source_target_pairs={{0,2},{1,3},{2,4},{3,5},{4,6},{5,7},{6,0},{7,1},{8,10},{9,11},{10,... | collective-permute-start | bytes 393224 | tf_op jit(solution)/shard_map/ppermute | solution.py:48
  113.0 14.0 %collective-permute-start.30 = (bf16[32,2048]{1,0:T(8,128)(2,1)S(1)}, bf16[32,2048]{1,0:T(8,128)(2,1)S(1)}, u32[]{:S(2)}, u32[]{:S(2)}) collective-permute-start(bf16[32,2048]{1,0:T(8,128)(2,1)S(1)} %get-tuple-element.33), channel_id=1, source_target_pairs={{0,5},{1,6},{2,7},{3,0},{4,1},{5,2},{6,3},{7,4},{8,13},{9,14},{10,... | collective-permute-start | bytes 393224 | tf_op jit(solution)/shard_map/ppermute | solution.py:48
  118.7 14.1 %collective-permute-start.34 = (bf16[32,2048]{1,0:T(8,128)(2,1)S(1)}, bf16[32,2048]{1,0:T(8,128)(2,1)S(1)}, u32[]{:S(2)}, u32[]{:S(2)}) collective-permute-start(bf16[32,2048]{1,0:T(8,128)(2,1)S(1)} %get-tuple-element.36), channel_id=1, source_target_pairs={{0,3},{1,4},{2,5},{3,6},{4,7},{5,0},{6,1},{7,2},{8,11},{9,12},{10,... | collective-permute-start | bytes 393224 | tf_op jit(solution)/shard_map/ppermute | solution.py:48
  119.9 12.9 %collective-permute-start.33 = (bf16[32,2048]{1,0:T(8,128)(2,1)S(1)}, bf16[32,2048]{1,0:T(8,128)(2,1)S(1)}, u32[]{:S(2)}, u32[]{:S(2)}) collective-permute-start(bf16[32,2048]{1,0:T(8,128)(2,1)S(1)} %pad_maximum_fusion.1), channel_id=1, source_target_pairs={{0,4},{1,5},{2,6},{3,7},{4,0},{5,1},{6,2},{7,3},{8,12},{9,13},{10,... | collective-permute-start | bytes 393224 | tf_op jit(solution)/shard_map/ppermute | solution.py:48
  133.6 5.9 %collective-permute-start.37 = (bf16[16,2048]{1,0:T(8,128)(2,1)S(1)}, bf16[16,2048]{1,0:T(8,128)(2,1)S(1)}, u32[]{:S(2)}, u32[]{:S(2)}) collective-permute-start(bf16[16,2048]{1,0:T(8,128)(2,1)S(1)} %get-tuple-element.40), channel_id=1, source_target_pairs={{0,8},{1,9},{2,10},{3,11},{4,12},{5,13},{6,14},{7,15},{8,0},{9,1},... | collective-permute-start | bytes 196616 | tf_op jit(solution)/shard_map/ppermute | solution.py:48
  (30 other events, 219.0 us)

commit v3 on v2

v3 whole, which is shorter than its diff:
```python
import math

import jax
import jax.numpy as jnp
from jax import lax
from jax.experimental import pallas as pl
from jax.experimental.pallas import tpu as pltpu
from jax.sharding import PartitionSpec as P

D = 2048
HEAD_DIM = 128
FF = 768
TOP = 8
HEADS = 16
KV_HEADS = 2
EXPERTS = 16
TOK_C = 256
TOK_DEV = 16
NEGATIVE = -1e30
SCALE = math.log2(math.e) / math.sqrt(HEAD_DIM)
F32 = jnp.float32
BF16 = jnp.bfloat16

ROW_SWAP = [(i, i ^ 8) for i in range(16)]
CORE_SWAP = [(i, i ^ 1) for i in range(16)]
Y_SWAP = [(i, i ^ 8) for i in range(16)]
Z_SWAP = [(i, i ^ 1) for i in range(16)]


def x_shift(step):
    return [
        (y * 8 + x * 2 + c, y * 8 + (x + step) % 4 * 2 + c)
        for y in range(2)
        for x in range(4)
        for c in range(2)
    ]


def z_shift(step):
    return [(y * 8 + z, y * 8 + (z + step) % 8) for y in range(2) for z in range(8)]


def on_ctx(block, route):
    return lax.ppermute(block, "ctx", route)


def on_exp(block, route):
    return lax.ppermute(block, "exp", route)


def kernel_call(
    body, scalars, resident, fetched, out_shapes, flops, transcendentals=0, limit=16, idle=()
):
    ins = [*resident, *fetched, *idle]
    n_res, n_fetch = len(resident), len(fetched)
    n_out = len(jax.tree.leaves(out_shapes))

    def whole(*refs):
        place, refs = refs[0], refs[1:]
        sources = refs[n_res : n_res + n_fetch]
        outs = refs[len(ins) : len(ins) + n_out]
        buffers = refs[len(ins) + n_out : len(ins) + n_out + n_fetch]
        copies = []
        for n in range(n_fetch):
            copies.append(
                pltpu.make_async_copy(sources[n], buffers[n], refs[len(ins) + n_out + n_fetch + n])
            )
        for copy in copies:
            copy.start()
        body(place, refs[:n_res], buffers, outs, lambda n: copies[n].wait())

    size = sum(a.size * a.dtype.itemsize for a in [*resident, *fetched])
    vmem = pl.BlockSpec(memory_space=pltpu.VMEM)
    return pl.pallas_call(
        whole,
        out_shape=out_shapes,
        in_specs=[pl.BlockSpec(memory_space=pltpu.SMEM)]
        + [vmem] * n_res
        + [pl.BlockSpec(memory_space=pl.ANY)] * n_fetch
        + [vmem] * len(idle),
        out_specs=jax.tree.map(lambda _: vmem, out_shapes),
        scratch_shapes=[pltpu.VMEM(a.shape, a.dtype) for a in fetched]
        + [pltpu.SemaphoreType.DMA] * n_fetch,
        compiler_params=pltpu.CompilerParams(vmem_limit_bytes=limit * 1024 * 1024),
        cost_estimate=pl.CostEstimate(
            flops=flops, bytes_accessed=size, transcendentals=transcendentals
        ),
    )(scalars, *ins)


def struct(shape, dtype):
    return jax.ShapeDtypeStruct(shape, dtype)


def block_scores(queries, qpos, kv_refs, kpos_ref):
    parts = []
    for n, ref in enumerate(kv_refs):
        scores = lax.dot_general(
            queries, ref[:, :HEAD_DIM], (((1,), (1,)), ((), ())), preferred_element_type=F32
        )
        allowed = kpos_ref[:, n * TOK_C : (n + 1) * TOK_C] <= qpos
        parts.append(jnp.where(allowed, scores, F32(NEGATIVE)))
    return parts


def attend(queries, qpos, kv_refs, kpos_ref, state):
    parts = block_scores(queries, qpos, kv_refs, kpos_ref)
    top = jnp.max(parts[0], axis=1, keepdims=True)
    for part in parts[1:]:
        top = jnp.maximum(top, jnp.max(part, axis=1, keepdims=True))
    if state is not None:
        old_top = state[:, HEAD_DIM : HEAD_DIM + 1]
        old_total = state[:, HEAD_DIM + 64 : HEAD_DIM + 65]
        top = jnp.maximum(top, old_top)
        factor = jnp.exp2((old_top - top) * SCALE)
        total, mixed = old_total * factor, state[:, :HEAD_DIM] * factor
    else:
        total, mixed = 0.0, 0.0
    for part, ref in zip(parts, kv_refs):
        weights = jnp.exp2((part - top) * SCALE)
        total = total + jnp.sum(weights, axis=1, keepdims=True)
        mixed = mixed + jnp.dot(
            weights.astype(BF16), ref[:, HEAD_DIM:], preferred_element_type=F32
        )
    lane = lax.broadcasted_iota(jnp.int32, (queries.shape[0], HEAD_DIM), 1)
    return mixed, jnp.where(lane < 64, top, total)


ROWS_TILE = 64


def attend_all(place, resident, fetched, outs, wait):
    mine_ref, theirs_ref, qpos_ref, kpos_ref = resident[:4]
    state_ref = resident[4] if len(resident) > 4 else None
    half = mine_ref.shape[0]
    for n in range(4):
        wait(n)
    for n, q_ref in enumerate((mine_ref, theirs_ref)):

        def rows(i, _, n=n, q_ref=q_ref):
            at = pl.ds(pl.multiple_of(i * ROWS_TILE, ROWS_TILE), ROWS_TILE)
            to = pl.ds(pl.multiple_of(n * half + i * ROWS_TILE, ROWS_TILE), ROWS_TILE)
            state = None if state_ref is None else state_ref[to, :]
            mixed, stats = attend(q_ref[at, :], qpos_ref[to, :], fetched, kpos_ref, state)
            out_ref, into = (outs[0], to) if len(outs) == 1 else (outs[n], at)
            out_ref[into, :HEAD_DIM] = mixed
            out_ref[into, HEAD_DIM:] = stats
            return 0

        lax.fori_loop(0, half // ROWS_TILE, rows, 0)


def project(place, resident, fetched, outs, wait):
    own_ref, w_own_ref = resident
    other_ref, got_ref, swapped_ref, near_ref, far_ref = fetched
    keep_ref, keep_half_ref, send_ref = outs
    core, parity = place[0], place[1]
    wait(0)
    own_top = own_ref[:, HEAD_DIM : HEAD_DIM + 1]
    other_top = other_ref[:, HEAD_DIM : HEAD_DIM + 1]
    top = jnp.maximum(own_top, other_top)
    own_factor = jnp.exp2((own_top - top) * SCALE)
    other_factor = jnp.exp2((other_top - top) * SCALE)
    total = own_ref[:, HEAD_DIM + 64 : HEAD_DIM + 65] * own_factor
    total = total + other_ref[:, HEAD_DIM + 64 : HEAD_DIM + 65] * other_factor
    mixed = own_ref[:, :HEAD_DIM] * own_factor + other_ref[:, :HEAD_DIM] * other_factor
    attn = (mixed / total).astype(BF16)
    heads = [attn[n * 64 : (n + 1) * 64] for n in range(4)]
    got_head = jnp.where(core == 0, heads[1], heads[3])
    swapped_head = jnp.where(core == 0, heads[3], heads[1])
    for n in range(1, 5):
        wait(n)
    width = D // 2
    for side, quarter_ref in ((core, near_ref), (1 - core, far_ref)):
        at = pl.ds(pl.multiple_of(side * width, width), width)
        sums = jnp.dot(heads[0], w_own_ref[:, at], preferred_element_type=F32)
        sums = sums + jnp.dot(got_head, got_ref[:, at], preferred_element_type=F32)
        sums = sums + jnp.dot(swapped_head, swapped_ref[:, at], preferred_element_type=F32)
        sums = sums + jnp.dot(heads[2], quarter_ref[...], preferred_element_type=F32)
        for y in range(2):
            low, high = sums[y * 32 : y * 32 + 16], sums[y * 32 + 16 : y * 32 + 32]
            rows = pl.ds(y * 16, 16)
            keep = jnp.where(parity == 0, low, high)
            keep_ref[rows, at] = keep
            keep_half_ref[rows, at] = keep.astype(BF16)
            send_ref[rows, at] = jnp.where(parity == 0, high, low).astype(BF16)


def normalise(place, resident, fetched, outs, wait):
    own_ref, sums_ref, gain_ref = resident
    other_ref, *recv_refs = fetched
    hidden_ref, normed_ref, both_ref = outs
    y = place[2]
    for n in range(4):
        wait(n)
    for n in range(2):
        at = pl.ds(n * 16, 16)
        extended = jnp.where(y == n, own_ref[...].astype(F32), other_ref[...].astype(F32))
        projected = sums_ref[at, :]
        for ref in recv_refs:
            projected = projected + ref[at, :].astype(F32)
        hidden = (extended[:, :D] + projected).astype(BF16)
        wide = hidden.astype(F32)
        inverse = lax.rsqrt(jnp.mean(wide * wide, axis=-1, keepdims=True) + 1e-06)
        normed = (wide * inverse * gain_ref[...].astype(F32)).astype(BF16)
        hidden_ref[at, :] = hidden
        normed_ref[at, :] = normed
        both_ref[at, :D] = normed
        both_ref[at, D:] = extended[:, D:].astype(BF16)


def expert(place, resident, fetched, outs, wait):
    gate_ref, up_ref, down_ref = resident
    for n in range(len(fetched)):
        wait(n)
    rows = [ref[...] for ref in fetched]
    rows = rows[0] if len(rows) == 1 else jnp.concatenate(rows, axis=0)
    gate_part = jnp.dot(rows, gate_ref[...], preferred_element_type=F32)
    up_part = jnp.dot(rows, up_ref[...], preferred_element_type=F32)
    inner = (gate_part * jax.nn.sigmoid(gate_part) * up_part).astype(BF16)
    result = jnp.dot(inner, down_ref[...], preferred_element_type=F32).astype(BF16)
    start = 0
    for out in outs:
        out[...] = result[start : start + out.shape[0]]
        start += out.shape[0]


def run_expert(place, rows, weights):
    total = sum(r.shape[0] for r in rows)
    return kernel_call(
        expert,
        place,
        weights,
        rows,
        [struct(r.shape, BF16) for r in rows],
        6 * total * D * FF,
        total * FF,
    )


def weigh(place, resident, fetched, outs, wait):
    mine_ref, theirs_ref = resident
    far_ref, *near_refs, own_ref = fetched
    keep_ref, y_ref, core_ref, both_ref = outs
    core, y, z = place[0], place[2], place[3]
    lane = lax.broadcasted_iota(jnp.int32, (32, 128), 1)

    def column(ref, step):
        name = y * 8 + lax.rem(z + step, 8)
        return jnp.sum(jnp.where(lane == name, ref[...].astype(F32), 0.0), axis=1, keepdims=True)

    for n in range(5):
        wait(n)
    mine = column(mine_ref, 0) * own_ref[...].astype(F32)
    mine = mine + column(mine_ref, 4) * far_ref[...].astype(F32)
    theirs = 0.0
    for s in range(3):
        step = jnp.where(core == 0, s + 1, 7 - s)
        mine = mine + column(mine_ref, step) * near_refs[s][:32, :].astype(F32)
        theirs = theirs + column(theirs_ref, step) * near_refs[s][32:, :].astype(F32)
    keep_ref[...] = jnp.where(y == 0, mine[:16], mine[16:])
    y_ref[...] = jnp.where(y == 0, mine[16:], mine[:16]).astype(BF16)
    core_ref[...] = jnp.where(y == 0, theirs[:16], theirs[16:]).astype(BF16)
    both_ref[...] = jnp.where(y == 0, theirs[16:], theirs[:16]).astype(BF16)


def finish(place, resident, fetched, outs, wait):
    hidden_ref, keep_ref = resident
    hidden = jnp.where(
        place[2] == 0, hidden_ref[:16, :].astype(F32), hidden_ref[16:, :].astype(F32)
    )
    moe = keep_ref[...]
    for n in range(3):
        wait(n)
        moe = moe + fetched[n][...].astype(F32)
    outs[0][...] = (hidden + moe).astype(BF16)


def extend(place, resident, fetched, outs, wait):
    residual_ref, ids_ref, gates_ref = resident
    lane = lax.broadcasted_iota(jnp.int32, (TOK_DEV, 128), 1)
    weights = jnp.zeros((TOK_DEV, 128), F32)
    for k in range(TOP):
        gate = gates_ref[:, k : k + 1].astype(F32)
        weights = weights + jnp.where(lane == ids_ref[:, k : k + 1], gate, 0.0)
    outs[0][:, :D] = residual_ref[...]
    outs[0][:, D:] = weights.astype(BF16)


def by_core(step):
    route = []
    for c in range(16):
        way = step if c % 2 == 0 else -step
        for e in range(16):
            route.append((c * 16 + e, c * 16 + e // 8 * 8 + (e + way) % 8))
    return route


def on_both(block, route):
    return lax.ppermute(block, ("ctx", "exp"), route)


def two_swaps(ctx_bit, exp_bit):
    return [
        (c * 16 + e, (c ^ ctx_bit) * 16 + (e ^ exp_bit)) for c in range(16) for e in range(16)
    ]


def shards(
    query,
    keys,
    values,
    out_proj,
    residual,
    norm_gain,
    expert_ids,
    gate_values,
    w_gate,
    w_up,
    w_down,
):
    ctx, exp = lax.axis_index("ctx"), lax.axis_index("exp")
    row, x, core = ctx // 8, ctx // 2 % 4, ctx % 2
    y, z = exp // 8, exp % 8
    place = jnp.stack([core, z % 2, y, z]).astype(jnp.int32)
    kv_index = exp // (HEADS // KV_HEADS)
    block = jnp.concatenate(
        [
            lax.dynamic_slice_in_dim(keys, kv_index * HEAD_DIM, HEAD_DIM, 1),
            lax.dynamic_slice_in_dim(values, kv_index * HEAD_DIM, HEAD_DIM, 1),
        ],
        axis=1,
    )

    other = on_ctx(block, ROW_SWAP)
    near = [block] + [on_ctx(block, x_shift(s)) for s in (1, -1, 2)]

    pairs = query.reshape(2, 4, 32, HEAD_DIM)

    def rows_for(step):
        to = (z + 2 * step) % 8 // 2
        return lax.dynamic_slice_in_dim(pairs, to, 1, 1).reshape(64, HEAD_DIM)

    mine = jnp.concatenate(
        [rows_for(0)] + [on_exp(rows_for(s), z_shift(2 * s)) for s in (1, 2, 3)], axis=0
    )
    theirs = on_ctx(mine, CORE_SWAP)

    far = [other] + [on_ctx(other, x_shift(s)) for s in (1, -1, 2)]

    w_got = on_both(out_proj, by_core(2))
    w_swapped = on_ctx(w_got, CORE_SWAP)
    w_half = lax.dynamic_slice_in_dim(out_proj, core * (D // 2), D // 2, 1)
    w_near = on_exp(w_half, z_shift(4))
    w_far = on_ctx(w_near, CORE_SWAP)

    offsets = jnp.arange(TOK_C, dtype=jnp.int32)
    token = jnp.arange(64, dtype=jnp.int32)
    token = token // 32 * 128 + z // 2 * 32 + token % 32
    local = jnp.tile(token, 4)
    query_pos = jnp.concatenate([ctx * TOK_C + local, (ctx ^ 1) * TOK_C + local]).reshape(512, 1)

    def key_pos(r):
        sources = jnp.stack([r * 8 + (x + s) % 4 * 2 + core for s in (0, -1, 1, 2)])
        return (sources[:, None] * TOK_C + offsets[None, :]).reshape(1, 4 * TOK_C)

    flops = 4 * 512 * 1024 * HEAD_DIM
    (state,) = kernel_call(
        attend_all,
        place,
        [mine, theirs, query_pos, key_pos(row)],
        near,
        [struct((512, 256), F32)],
        flops,
        512 * 1024,
    )
    own, swap = kernel_call(
        attend_all,
        place,
        [mine, theirs, query_pos, key_pos(1 - row), state],
        far,
        [struct((256, 256), F32)] * 2,
        flops,
        512 * 1024,
    )
    joined = on_ctx(swap, CORE_SWAP)
    keep, keep_half, send = kernel_call(
        project,
        place,
        [own, out_proj],
        [joined, w_got, w_swapped, w_near, w_far],
        [struct((32, D), F32), struct((32, D), BF16), struct((32, D), BF16)],
        2 * 64 * 512 * D,
    )
    (extended,) = kernel_call(
        extend,
        place,
        [residual, expert_ids, gate_values],
        [],
        [struct((TOK_DEV, D + 128), BF16)],
        TOK_DEV * D,
    )
    extended, send = lax.optimization_barrier((extended, send))
    sums_y = on_exp(keep_half, Y_SWAP)
    sums_z = on_exp(send, Z_SWAP)
    sums_yz = on_exp(send, [(i, i ^ 9) for i in range(16)])
    extended_other = on_exp(extended, Y_SWAP)
    w = [w_gate[0], w_up[0], w_down[0]]
    hidden, normed, both = kernel_call(
        normalise,
        place,
        [extended, keep, norm_gain.reshape(1, D)],
        [extended_other, sums_z, sums_y, sums_yz],
        [struct((32, D), BF16), struct((32, D), BF16), struct((32, D + 128), BF16)],
        8 * 32 * D,
        idle=w,
    )

    opposite = on_exp(normed, z_shift(4))
    theirs_both = on_ctx(both, CORE_SWAP)
    ring = [jnp.concatenate([normed, theirs_both[:, :D]], axis=0)]
    for s in range(3):
        ring.append(on_both(ring[-1], by_core(1)))
    stay, opposite = run_expert(place, [normed, opposite], w)
    opposite = on_exp(opposite, z_shift(4))
    back = [
        on_both(run_expert(place, [ring[s]], w)[0], by_core(-s)) for s in (1, 2, 3)
    ]
    keep, to_y, to_core, to_both = kernel_call(
        weigh,
        place,
        [both[:, D:], theirs_both[:, D:]],
        [opposite, *back, stay],
        [struct((16, D), F32)] + [struct((16, D), BF16)] * 3,
        16 * 32 * D,
    )
    from_core = on_ctx(to_core, CORE_SWAP)
    from_y = on_exp(to_y, Y_SWAP)
    from_both = on_both(to_both, two_swaps(1, 8))
    return kernel_call(
        finish,
        place,
        [hidden, keep],
        [from_core, from_y, from_both],
        [struct((16, D), BF16)],
        3 * 16 * D,
    )[0]


def solution(mesh):
    return jax.shard_map(
        shards,
        mesh=mesh,
        in_specs=(
            P("ctx", "exp"),
            P("ctx", None),
            P("ctx", None),
            P("exp", None),
            P(("ctx", "exp"), None),
            P(),
            P(("ctx", "exp"), None),
            P(("ctx", "exp"), None),
            P("exp", None, None),
            P("exp", None, None),
            P("exp", None, None),
        ),
        out_specs=P(("ctx", "exp"), None),
        check_vma=False,
    )
```

time: 143 us -> 151 us (1.056)
  waiting for transfers between devices: 22.9 us -> 42.4 us
  local copies, waits for them, and re-layouts: 22.3 us -> 13.4 us
  starting transfers between devices: 66.8 us -> 63 us
  Pallas kernels: 26.2 us -> 28.9 us
    ppermute x26 -> x11, starting transfers between devices: 53.9 us -> 24.3 us  [on_exp(): return lax.ppermute(block, 'exp', route)]
    ppermute x0 -> x8, waiting for transfers between devices: none -> 18.7 us  [on_both(): return lax.ppermute(block, ('ctx', 'exp'), route)]
    ppermute x12 -> x13, starting transfers between devices: 12.9 us -> 26.3 us  [on_ctx(): return lax.ppermute(block, 'ctx', route)]
    ppermute x0 -> x8, starting transfers between devices: none -> 12.3 us  [on_both(): return lax.ppermute(block, ('ctx', 'exp'), route)]
    unnamed x51 -> x26, local copies, waits for them, and re-layouts: 16.7 us -> 9.7 us
    pallas_call x12 -> x11, Pallas kernels: 26.2 us -> 28.9 us  [kernel_call(): pl.pallas_call(whole, out_shape=out_shapes, in_specs=[pl.BlockSpec(memory...]
    ppermute x26 -> x11, waiting for transfers between devices: 21 us -> 22.4 us  [on_exp(): return lax.ppermute(block, 'exp', route)]
  transfers between devices with their start and end apart: 38 -> 32, of which waited for: 10 -> 10; matrix products, arithmetic and copies ran while one was open for 6% -> 3% of each run, Pallas kernels for 15% -> 15%
where the time goes in v3:
time: 151 us; the launch traced here: 149 us
  starting transfers between devices  63 us (42%)
  waiting for transfers between devices  42.4 us (28%)
  Pallas kernels  28.9 us (19%)
  local copies, waits for them, and re-layouts  13.4 us (9%)
    pallas_call x11, Pallas kernels, kernel_call(): pl.pallas_call(whole, out_shape=out_shapes, in_specs=[pl.BlockSpec(memory...  28.9 us
    ppermute x13, starting transfers between devices, on_ctx(): return lax.ppermute(block, 'ctx', route)  26.3 us
    ppermute x11, starting transfers between devices, on_exp(): return lax.ppermute(block, 'exp', route)  24.3 us
    ppermute x11, waiting for transfers between devices, on_exp(): return lax.ppermute(block, 'exp', route)  22.4 us
    ppermute x8, waiting for transfers between devices, on_both(): return lax.ppermute(block, ('ctx', 'exp'), route)  18.7 us
    ppermute x8, starting transfers between devices, on_both(): return lax.ppermute(block, ('ctx', 'exp'), route)  12.3 us
    unnamed x26, local copies, waits for them, and re-layouts  9.7 us
  transfers between devices with their start and end apart: 32, of which 10 were waited for; matrix products, arithmetic and copies ran while one was open for 3% of the time, Pallas kernels for 15%

profile of v3, /device:TPU:32, one launch (start us, length us, event | category | flops | bytes accessed | tf_op | source)
XLA Modules:
  0.0 149.2 jit_solution(7041247011692315556)
XLA Ops:
  3.8 3.3 %collective-permute-start = (bf16[64,128]{1,0:T(8,128)(2,1)S(1)}, bf16[64,128]{1,0:T(8,128)(2,1)S(1)}, u32[]{:S(2)}, u32[]{:S(2)}) collective-permute-start(bf16[64,128]{1,0:T(8,128)(2,1)S(1)} %bitcast.58), channel_id=1, source_target_pairs={{0,2},{1,3},{2,4},{3,5},{4,6},{5,7},{6,0},{7,1},{8,10},{9,11},{10,... | collective-permute-start | bytes 49160 | tf_op jit(solution)/shard_map/ppermute | solution.py:48
  7.1 4.5 %collective-permute-start.1 = (bf16[64,128]{1,0:T(8,128)(2,1)S(1)}, bf16[64,128]{1,0:T(8,128)(2,1)S(1)}, u32[]{:S(2)}, u32[]{:S(2)}) collective-permute-start(bf16[64,128]{1,0:T(8,128)(2,1)S(1)} %bitcast.57), channel_id=1, source_target_pairs={{0,4},{1,5},{2,6},{3,7},{4,0},{5,1},{6,2},{7,3},{8,12},{9,13},{10,... | collective-permute-start | bytes 49160 | tf_op jit(solution)/shard_map/ppermute | solution.py:48
  11.6 2.7 %collective-permute-start.2 = (bf16[64,128]{1,0:T(8,128)(2,1)S(1)}, bf16[64,128]{1,0:T(8,128)(2,1)S(1)}, u32[]{:S(2)}, u32[]{:S(2)}) collective-permute-start(bf16[64,128]{1,0:T(8,128)(2,1)S(1)} %bitcast.56), channel_id=1, source_target_pairs={{0,6},{1,7},{2,0},{3,1},{4,2},{5,3},{6,4},{7,5},{8,14},{9,15},{10,... | collective-permute-start | bytes 49160 | tf_op jit(solution)/shard_map/ppermute | solution.py:48
  14.8 1.8 %collective-permute-start.5 = (bf16[256,256]{1,0:T(8,128)(2,1)}, bf16[256,256]{1,0:T(8,128)(2,1)}, u32[]{:S(2)}, u32[]{:S(2)}) collective-permute-start(bf16[256,256]{1,0:T(8,128)(2,1)} %pad_maximum_fusion.1.refs_5_), channel_id=1, source_target_pairs={{0,96},{16,112},{32,0},{48,16},{64,32},{80,48},{96,64},{112,80},{1... | collective-permute-start | bytes 393224 | tf_op jit(solution)/shard_map/ppermute | solution.py:44
  16.5 1.8 %collective-permute-start.6 = (bf16[256,256]{1,0:T(8,128)(2,1)}, bf16[256,256]{1,0:T(8,128)(2,1)}, u32[]{:S(2)}, u32[]{:S(2)}) collective-permute-start(bf16[256,256]{1,0:T(8,128)(2,1)} %pad_maximum_fusion.1.refs_5_), channel_id=1, source_target_pairs={{0,64},{16,80},{32,96},{48,112},{64,0},{80,16},{96,32},{112,48},{1... | collective-permute-start | bytes 393224 | tf_op jit(solution)/shard_map/ppermute | solution.py:44
  18.5 1.7 %constant_dynamic-slice_fusion = bf16[128,1024]{1,0:T(8,128)(2,1)} fusion(bf16[128,2048]{1,0:T(8,128)(2,1)} %refs_2_.2, s32[]{:T(128)S(6)} %select_n.150), kind=kLoop, calls=%fused_computation.8 | loop fusion | bytes 524292 | tf_op jit(solution)/shard_map/dynamic_slice | solution.py:353
  20.2 1.6 %collective-permute-start.7 = (bf16[256,256]{1,0:T(8,128)(2,1)}, bf16[256,256]{1,0:T(8,128)(2,1)}, u32[]{:S(2)}, u32[]{:S(2)}) collective-permute-start(bf16[256,256]{1,0:T(8,128)(2,1)} %pad_maximum_fusion.1.refs_5_), channel_id=1, source_target_pairs={{0,128},{16,144},{32,160},{48,176},{64,192},{80,208},{96,224},{112... | collective-permute-start | bytes 393224 | tf_op jit(solution)/shard_map/ppermute | solution.py:44
  22.6 3.9 %collective-permute-start.14 = (bf16[128,1024]{1,0:T(8,128)(2,1)}, bf16[128,1024]{1,0:T(8,128)(2,1)}, u32[]{:S(2)}, u32[]{:S(2)}) collective-permute-start(bf16[128,1024]{1,0:T(8,128)(2,1)} %constant_dynamic-slice_fusion), channel_id=1, source_target_pairs={{0,4},{1,5},{2,6},{3,7},{4,0},{5,1},{6,2},{7,3},{8,12},{9,13},{10,... | collective-permute-start | bytes 786440 | tf_op jit(solution)/shard_map/ppermute | solution.py:48
  26.5 3.5 %collective-permute-done.12.refs_4_ = bf16[128,2048]{1,0:T(8,128)(2,1)} collective-permute-done((bf16[128,2048]{1,0:T(8,128)(2,1)}, bf16[128,2048]{1,0:T(8,128)(2,1)}, u32[]{:S(2)}, u32[]{:S(2)}) %collective-permute-start.12) | collective-permute-done | bytes 524320 | tf_op jit(solution)/shard_map/ppermute | solution.py:300
  30.2 15.7 %collective-permute-start.10 = (bf16[256,256]{1,0:T(8,128)(2,1)}, bf16[256,256]{1,0:T(8,128)(2,1)S(1)}, u32[]{:S(2)}, u32[]{:S(2)}) collective-permute-start(bf16[256,256]{1,0:T(8,128)(2,1)} %collective-permute-done.7.refs_6_), channel_id=1, source_target_pairs={{0,64},{16,80},{32,96},{48,112},{64,0},{80,16},{96,32},{112,48},{1... | collective-permute-start | bytes 393224 | tf_op jit(solution)/shard_map/ppermute | solution.py:44
  45.8 3.2 %collective-permute-start.9 = (bf16[256,256]{1,0:T(8,128)(2,1)}, bf16[256,256]{1,0:T(8,128)(2,1)S(1)}, u32[]{:S(2)}, u32[]{:S(2)}) collective-permute-start(bf16[256,256]{1,0:T(8,128)(2,1)} %collective-permute-done.7.refs_6_), channel_id=1, source_target_pairs={{0,96},{16,112},{32,0},{48,16},{64,32},{80,48},{96,64},{112,80},{1... | collective-permute-start | bytes 393224 | tf_op jit(solution)/shard_map/ppermute | solution.py:44
  50.0 5.3 %shard_map.110.refs_5_ = f32[512,256]{1,0:T(8,128)S(1)} custom-call(s32[4]{0:T(128)S(1)} %pad_add_fusion.1.refs_0_, bf16[256,128]{1,0:T(8,128)(2,1)S(1)} %pad_maximum_fusion.2.refs_1_, bf16[256,128]{1,0:T(8,128)(2,1)S(1)} %collective-permute-done.3.refs_2_, s32[512,1]{1,0:T(8,128)S(1)} %copy.25.refs_3_, s32[1,1024]{1,0:T(1,128)S(1)} %bitcast.52, ...), custom_call_target="tpu_custom_call" | custom-call | flops 268435456 | bytes 661504 | tf_op jit(solution)/shard_map/pallas_call | solution.py:74
  55.4 6.6 %shard_map.111 = (f32[256,256]{1,0:T(8,128)S(1)}, f32[256,256]{1,0:T(8,128)}) custom-call(s32[4]{0:T(128)S(1)} %pad_add_fusion.1.refs_0_, bf16[256,128]{1,0:T(8,128)(2,1)S(1)} %pad_maximum_fusion.2.refs_1_, bf16[256,128]{1,0:T(8,128)(2,1)S(1)} %collective-permute-done.3.refs_2_, s32[512,1]{1,0:T(8,128)S(1)} %copy.25.refs_3_, s32[1,1024]{1,0:T(1,128)S(1)} %bitcast.53, ...), custom_call_target="tpu_custom_call" | custom-call | flops 268435456 | bytes 1185792 | tf_op jit(solution)/shard_map/pallas_call | solution.py:74
  67.6 2.4 %shard_map.112 = (f32[32,2048]{1,0:T(8,128)S(1)}, bf16[32,2048]{1,0:T(8,128)(2,1)S(1)}, bf16[32,2048]{1,0:T(8,128)(2,1)S(1)}) custom-call(s32[4]{0:T(128)S(1)} %pad_add_fusion.1.refs_0_, f32[256,256]{1,0:T(8,128)S(1)} %copy-done.5, bf16[128,2048]{1,0:T(8,128)(2,1)S(1)} %copy-done.3, f32[256,256]{1,0:T(8,128)S(1)} %collective-permute-done.11.refs_3_, ...), custom_call_target="tpu_custom_call" | custom-call | flops 134217728 | bytes 2621440 | tf_op jit(solution)/shard_map/pallas_call | solution.py:74
  70.1 2.9 %collective-permute-start.19 = (bf16[32,2048]{1,0:T(8,128)(2,1)S(1)}, bf16[32,2048]{1,0:T(8,128)(2,1)S(1)}, u32[]{:S(2)}, u32[]{:S(2)}) collective-permute-start(bf16[32,2048]{1,0:T(8,128)(2,1)S(1)} %get-tuple-element.26), channel_id=1, source_target_pairs={{0,9},{1,8},{2,11},{3,10},{4,13},{5,12},{6,15},{7,14},{8,1},{9,0},... | collective-permute-start | bytes 393224 | tf_op jit(solution)/shard_map/ppermute | solution.py:48
  73.0 2.1 %collective-permute-start.18 = (bf16[32,2048]{1,0:T(8,128)(2,1)S(1)}, bf16[32,2048]{1,0:T(8,128)(2,1)S(1)}, u32[]{:S(2)}, u32[]{:S(2)}) collective-permute-start(bf16[32,2048]{1,0:T(8,128)(2,1)S(1)} %get-tuple-element.27), channel_id=1, source_target_pairs={{0,8},{1,9},{2,10},{3,11},{4,12},{5,13},{6,14},{7,15},{8,0},{9,1},... | collective-permute-start | bytes 393224 | tf_op jit(solution)/shard_map/ppermute | solution.py:48
  76.5 6.6 %collective-permute-done.16.refs_4_ = bf16[16,2176]{1,0:T(8,128)(2,1)S(1)} collective-permute-done((bf16[16,2176]{1,0:T(8,128)(2,1)S(1)}, bf16[16,2176]{1,0:T(8,128)(2,1)S(1)}, u32[]{:S(2)}, u32[]{:S(2)}) %collective-permute-start.16) | collective-permute-done | bytes 69664 | tf_op jit(solution)/shard_map/ppermute | solution.py:48
  83.1 1.9 %copy-done.1 = bf16[1,2048,768]{2,1,0:T(8,128)(2,1)S(1)} copy-done((bf16[1,2048,768]{2,1,0:T(8,128)(2,1)S(1)}, bf16[1,2048,768]{2,1,0:T(8,128)(2,1)}, u32[]{:S(2)}) %copy-start.1) | copy-done | bytes 3145752
  85.0 1.9 %copy-done.2 = bf16[1,768,2048]{2,1,0:T(8,128)(2,1)S(1)} copy-done((bf16[1,768,2048]{2,1,0:T(8,128)(2,1)S(1)}, bf16[1,768,2048]{2,1,0:T(8,128)(2,1)}, u32[]{:S(2)}) %copy-start.2) | copy-done | bytes 3145752
  89.9 6.4 %collective-permute-done.23.refs_4_ = bf16[64,2048]{1,0:T(8,128)(2,1)S(1)} collective-permute-done((bf16[64,2048]{1,0:T(8,128)(2,1)S(1)}, bf16[64,2048]{1,0:T(8,128)(2,1)S(1)}, u32[]{:S(2)}, u32[]{:S(2)}) %collective-permute-start.23) | collective-permute-done | bytes 262176 | tf_op jit(solution)/shard_map/ppermute | solution.py:300
  96.2 6.4 %collective-permute-done.25.refs_4_ = bf16[64,2048]{1,0:T(8,128)(2,1)S(1)} collective-permute-done((bf16[64,2048]{1,0:T(8,128)(2,1)S(1)}, bf16[64,2048]{1,0:T(8,128)(2,1)S(1)}, u32[]{:S(2)}, u32[]{:S(2)}) %collective-permute-start.25) | collective-permute-done | bytes 262176 | tf_op jit(solution)/shard_map/ppermute | solution.py:300
  104.1 2.4 %shard_map.115 = bf16[64,2048]{1,0:T(8,128)(2,1)S(1)} custom-call(s32[4]{0:T(128)S(1)} %pad_add_fusion.1.refs_0_, bf16[2048,768]{1,0:T(8,128)(2,1)S(1)} %bitcast.38, bf16[2048,768]{1,0:T(8,128)(2,1)S(1)} %bitcast.43, bf16[768,2048]{1,0:T(8,128)(2,1)S(1)} %bitcast.48, bf16[64,2048]{1,0:T(8,128)(2,1)S(1)} %collective-permute-done.23.refs_4_), custom_call_target="tpu_custom_call" | custom-call | flops 603979776 | bytes 9699328 | tf_op jit(solution)/shard_map/pallas_call | solution.py:74
  106.4 1.9 %collective-permute-start.24 = (bf16[64,2048]{1,0:T(8,128)(2,1)S(1)}, bf16[64,2048]{1,0:T(8,128)(2,1)S(1)}, u32[]{:S(2)}, u32[]{:S(2)}) collective-permute-start(bf16[64,2048]{1,0:T(8,128)(2,1)S(1)} %shard_map.115), channel_id=1, source_target_pairs={{0,7},{1,0},{2,1},{3,2},{4,3},{5,4},{6,5},{7,6},{8,15},{9,8},{10,9... | collective-permute-start | bytes 786440 | tf_op jit(solution)/shard_map/ppermute | solution.py:300
  108.3 2.4 %shard_map.116 = bf16[64,2048]{1,0:T(8,128)(2,1)S(1)} custom-call(s32[4]{0:T(128)S(1)} %pad_add_fusion.1.refs_0_, bf16[2048,768]{1,0:T(8,128)(2,1)S(1)} %bitcast.39, bf16[2048,768]{1,0:T(8,128)(2,1)S(1)} %bitcast.44, bf16[768,2048]{1,0:T(8,128)(2,1)S(1)} %bitcast.49, bf16[64,2048]{1,0:T(8,128)(2,1)S(1)} %collective-permute-done.25.refs_4_), custom_call_target="tpu_custom_call" | custom-call | flops 603979776 | bytes 9699328 | tf_op jit(solution)/shard_map/pallas_call | solution.py:74
  110.7 2.8 %collective-permute-start.26 = (bf16[64,2048]{1,0:T(8,128)(2,1)S(1)}, bf16[64,2048]{1,0:T(8,128)(2,1)S(1)}, u32[]{:S(2)}, u32[]{:S(2)}) collective-permute-start(bf16[64,2048]{1,0:T(8,128)(2,1)S(1)} %shard_map.116), channel_id=1, source_target_pairs={{0,6},{1,7},{2,0},{3,1},{4,2},{5,3},{6,4},{7,5},{8,14},{9,15},{10,... | collective-permute-start | bytes 786440 | tf_op jit(solution)/shard_map/ppermute | solution.py:300
  114.3 2.4 %shard_map.117 = bf16[64,2048]{1,0:T(8,128)(2,1)S(1)} custom-call(s32[4]{0:T(128)S(1)} %pad_add_fusion.1.refs_0_, bf16[2048,768]{1,0:T(8,128)(2,1)S(1)} %bitcast.40, bf16[2048,768]{1,0:T(8,128)(2,1)S(1)} %bitcast.45, bf16[768,2048]{1,0:T(8,128)(2,1)S(1)} %bitcast.50, bf16[64,2048]{1,0:T(8,128)(2,1)S(1)} %collective-permute-done.27.refs_4_), custom_call_target="tpu_custom_call" | custom-call | flops 603979776 | bytes 9699328 | tf_op jit(solution)/shard_map/pallas_call | solution.py:74
  116.7 5.9 %collective-permute-start.28 = (bf16[64,2048]{1,0:T(8,128)(2,1)S(1)}, bf16[64,2048]{1,0:T(8,128)(2,1)S(1)}, u32[]{:S(2)}, u32[]{:S(2)}) collective-permute-start(bf16[64,2048]{1,0:T(8,128)(2,1)S(1)} %shard_map.117), channel_id=1, source_target_pairs={{0,5},{1,6},{2,7},{3,0},{4,1},{5,2},{6,3},{7,4},{8,13},{9,14},{10,... | collective-permute-start | bytes 786440 | tf_op jit(solution)/shard_map/ppermute | solution.py:300
  122.6 2.7 %shard_map.114 = (bf16[32,2048]{1,0:T(8,128)(2,1)S(1)}, bf16[32,2048]{1,0:T(8,128)(2,1)S(1)}) custom-call(s32[4]{0:T(128)S(1)} %pad_add_fusion.1.refs_0_, bf16[2048,768]{1,0:T(8,128)(2,1)S(1)} %bitcast.41, bf16[2048,768]{1,0:T(8,128)(2,1)S(1)} %bitcast.46, bf16[768,2048]{1,0:T(8,128)(2,1)S(1)} %bitcast.51, bf16[32,2048]{1,0:T(8,128)(2,1)S(1)} %get-tuple-element.30.refs_4_, ...), custom_call_target="tpu_custom_call" | custom-call | flops 603979776 | bytes 9699328 | tf_op jit(solution)/shard_map/pallas_call | solution.py:74
  125.4 13.1 %collective-permute-done.22.refs_3_ = bf16[32,2048]{1,0:T(8,128)(2,1)S(1)} collective-permute-done((bf16[32,2048]{1,0:T(8,128)(2,1)S(1)}, bf16[32,2048]{1,0:T(8,128)(2,1)S(1)}, u32[]{:S(2)}, u32[]{:S(2)}) %collective-permute-start.22) | collective-permute-done | bytes 131104 | tf_op jit(solution)/shard_map/ppermute | solution.py:48
  140.0 1.9 %collective-permute-start.30 = (bf16[16,2048]{1,0:T(8,128)(2,1)S(1)}, bf16[16,2048]{1,0:T(8,128)(2,1)S(1)}, u32[]{:S(2)}, u32[]{:S(2)}) collective-permute-start(bf16[16,2048]{1,0:T(8,128)(2,1)S(1)} %get-tuple-element.35), channel_id=1, source_target_pairs={{0,8},{1,9},{2,10},{3,11},{4,12},{5,13},{6,14},{7,15},{8,0},{9,1},... | collective-permute-start | bytes 196616 | tf_op jit(solution)/shard_map/ppermute | solution.py:48
  143.4 2.6 %collective-permute-done.30.refs_4_ = bf16[16,2048]{1,0:T(8,128)(2,1)S(1)} collective-permute-done((bf16[16,2048]{1,0:T(8,128)(2,1)S(1)}, bf16[16,2048]{1,0:T(8,128)(2,1)S(1)}, u32[]{:S(2)}, u32[]{:S(2)}) %collective-permute-start.30) | collective-permute-done | bytes 65568 | tf_op jit(solution)/shard_map/ppermute | solution.py:48
  147.5 1.5 %shard_map.119 = bf16[16,2048]{1,0:T(8,128)(2,1)} custom-call(s32[4]{0:T(128)S(1)} %pad_add_fusion.1.refs_0_, bf16[32,2048]{1,0:T(8,128)(2,1)S(1)} %get-tuple-element.28.refs_1_, f32[16,2048]{1,0:T(8,128)S(1)} %get-tuple-element.33.refs_2_, bf16[16,2048]{1,0:T(8,128)(2,1)S(1)} %collective-permute-done.29.refs_3_, ...), custom_call_target="tpu_custom_call" | custom-call | flops 98304 | bytes 458752 | tf_op jit(solution)/shard_map/pallas_call | solution.py:74
  (90 shorter events, 23.3 us)
Async XLA Ops:
  1.6 20.4 %collective-permute-start.4 = (bf16[256,256]{1,0:T(8,128)(2,1)}, bf16[256,256]{1,0:T(8,128)(2,1)S(1)}, u32[]{:S(2)}, u32[]{:S(2)}) collective-permute-start(bf16[256,256]{1,0:T(8,128)(2,1)} %pad_maximum_fusion.1.refs_5_), channel_id=1, source_target_pairs={{0,32},{16,48},{32,64},{48,80},{64,96},{80,112},{96,0},{112,16},{1... | collective-permute-start | bytes 393224 | tf_op jit(solution)/shard_map/ppermute | solution.py:44
  3.8 11.0 %collective-permute-start = (bf16[64,128]{1,0:T(8,128)(2,1)S(1)}, bf16[64,128]{1,0:T(8,128)(2,1)S(1)}, u32[]{:S(2)}, u32[]{:S(2)}) collective-permute-start(bf16[64,128]{1,0:T(8,128)(2,1)S(1)} %bitcast.58), channel_id=1, source_target_pairs={{0,2},{1,3},{2,4},{3,5},{4,6},{5,7},{6,0},{7,1},{8,10},{9,11},{10,... | collective-permute-start | bytes 49160 | tf_op jit(solution)/shard_map/ppermute | solution.py:48
  7.1 9.4 %collective-permute-start.1 = (bf16[64,128]{1,0:T(8,128)(2,1)S(1)}, bf16[64,128]{1,0:T(8,128)(2,1)S(1)}, u32[]{:S(2)}, u32[]{:S(2)}) collective-permute-start(bf16[64,128]{1,0:T(8,128)(2,1)S(1)} %bitcast.57), channel_id=1, source_target_pairs={{0,4},{1,5},{2,6},{3,7},{4,0},{5,1},{6,2},{7,3},{8,12},{9,13},{10,... | collective-permute-start | bytes 49160 | tf_op jit(solution)/shard_map/ppermute | solution.py:48
  11.6 6.7 %collective-permute-start.2 = (bf16[64,128]{1,0:T(8,128)(2,1)S(1)}, bf16[64,128]{1,0:T(8,128)(2,1)S(1)}, u32[]{:S(2)}, u32[]{:S(2)}) collective-permute-start(bf16[64,128]{1,0:T(8,128)(2,1)S(1)} %bitcast.56), channel_id=1, source_target_pairs={{0,6},{1,7},{2,0},{3,1},{4,2},{5,3},{6,4},{7,5},{8,14},{9,15},{10,... | collective-permute-start | bytes 49160 | tf_op jit(solution)/shard_map/ppermute | solution.py:48
  14.3 15.7 %collective-permute-start.12 = (bf16[128,2048]{1,0:T(8,128)(2,1)}, bf16[128,2048]{1,0:T(8,128)(2,1)}, u32[]{:S(2)}, u32[]{:S(2)}) collective-permute-start(bf16[128,2048]{1,0:T(8,128)(2,1)} %refs_2_.2), channel_id=1, source_target_pairs={{0,2},{1,3},{2,4},{3,5},{4,6},{5,7},{6,0},{7,1},{8,10},{9,11},{10,... | collective-permute-start | bytes 1572872 | tf_op jit(solution)/shard_map/ppermute | solution.py:300
  14.8 31.0 %collective-permute-start.5 = (bf16[256,256]{1,0:T(8,128)(2,1)}, bf16[256,256]{1,0:T(8,128)(2,1)}, u32[]{:S(2)}, u32[]{:S(2)}) collective-permute-start(bf16[256,256]{1,0:T(8,128)(2,1)} %pad_maximum_fusion.1.refs_5_), channel_id=1, source_target_pairs={{0,96},{16,112},{32,0},{48,16},{64,32},{80,48},{96,64},{112,80},{1... | collective-permute-start | bytes 393224 | tf_op jit(solution)/shard_map/ppermute | solution.py:44
  16.5 29.3 %collective-permute-start.6 = (bf16[256,256]{1,0:T(8,128)(2,1)}, bf16[256,256]{1,0:T(8,128)(2,1)}, u32[]{:S(2)}, u32[]{:S(2)}) collective-permute-start(bf16[256,256]{1,0:T(8,128)(2,1)} %pad_maximum_fusion.1.refs_5_), channel_id=1, source_target_pairs={{0,64},{16,80},{32,96},{48,112},{64,0},{80,16},{96,32},{112,48},{1... | collective-permute-start | bytes 393224 | tf_op jit(solution)/shard_map/ppermute | solution.py:44
  18.4 1.8 %collective-permute-start.3 = (bf16[256,128]{1,0:T(8,128)(2,1)S(1)}, bf16[256,128]{1,0:T(8,128)(2,1)S(1)}, u32[]{:S(2)}, u32[]{:S(2)}) collective-permute-start(bf16[256,128]{1,0:T(8,128)(2,1)S(1)} %pad_maximum_fusion.2.refs_1_), channel_id=1, source_target_pairs={{0,16},{16,0},{32,48},{48,32},{64,80},{80,64},{96,112},{112,96},{1... | collective-permute-start | bytes 196616 | tf_op jit(solution)/shard_map/ppermute | solution.py:44
  20.2 10.0 %collective-permute-start.7 = (bf16[256,256]{1,0:T(8,128)(2,1)}, bf16[256,256]{1,0:T(8,128)(2,1)}, u32[]{:S(2)}, u32[]{:S(2)}) collective-permute-start(bf16[256,256]{1,0:T(8,128)(2,1)} %pad_maximum_fusion.1.refs_5_), channel_id=1, source_target_pairs={{0,128},{16,144},{32,160},{48,176},{64,192},{80,208},{96,224},{112... | collective-permute-start | bytes 393224 | tf_op jit(solution)/shard_map/ppermute | solution.py:44
  22.6 40.1 %collective-permute-start.14 = (bf16[128,1024]{1,0:T(8,128)(2,1)}, bf16[128,1024]{1,0:T(8,128)(2,1)}, u32[]{:S(2)}, u32[]{:S(2)}) collective-permute-start(bf16[128,1024]{1,0:T(8,128)(2,1)} %constant_dynamic-slice_fusion), channel_id=1, source_target_pairs={{0,4},{1,5},{2,6},{3,7},{4,0},{5,1},{6,2},{7,3},{8,12},{9,13},{10,... | collective-permute-start | bytes 786440 | tf_op jit(solution)/shard_map/ppermute | solution.py:48
  30.0 35.6 %collective-permute-start.13 = (bf16[128,2048]{1,0:T(8,128)(2,1)}, bf16[128,2048]{1,0:T(8,128)(2,1)}, u32[]{:S(2)}, u32[]{:S(2)}) collective-permute-start(bf16[128,2048]{1,0:T(8,128)(2,1)} %collective-permute-done.12.refs_4_), channel_id=1, source_target_pairs={{0,16},{16,0},{32,48},{48,32},{64,80},{80,64},{96,112},{112,96},{1... | collective-permute-start | bytes 1572872 | tf_op jit(solution)/shard_map/ppermute | solution.py:44
  30.2 25.2 %collective-permute-start.10 = (bf16[256,256]{1,0:T(8,128)(2,1)}, bf16[256,256]{1,0:T(8,128)(2,1)S(1)}, u32[]{:S(2)}, u32[]{:S(2)}) collective-permute-start(bf16[256,256]{1,0:T(8,128)(2,1)} %collective-permute-done.7.refs_6_), channel_id=1, source_target_pairs={{0,64},{16,80},{32,96},{48,112},{64,0},{80,16},{96,32},{112,48},{1... | collective-permute-start | bytes 393224 | tf_op jit(solution)/shard_map/ppermute | solution.py:44
  45.8 9.6 %collective-permute-start.8 = (bf16[256,256]{1,0:T(8,128)(2,1)}, bf16[256,256]{1,0:T(8,128)(2,1)S(1)}, u32[]{:S(2)}, u32[]{:S(2)}) collective-permute-start(bf16[256,256]{1,0:T(8,128)(2,1)} %collective-permute-done.7.refs_6_), channel_id=1, source_target_pairs={{0,32},{16,48},{32,64},{48,80},{64,96},{80,112},{96,0},{112,16},{1... | collective-permute-start | bytes 393224 | tf_op jit(solution)/shard_map/ppermute | solution.py:44
  45.8 9.6 %collective-permute-start.9 = (bf16[256,256]{1,0:T(8,128)(2,1)}, bf16[256,256]{1,0:T(8,128)(2,1)S(1)}, u32[]{:S(2)}, u32[]{:S(2)}) collective-permute-start(bf16[256,256]{1,0:T(8,128)(2,1)} %collective-permute-done.7.refs_6_), channel_id=1, source_target_pairs={{0,96},{16,112},{32,0},{48,16},{64,32},{80,48},{96,64},{112,80},{1... | collective-permute-start | bytes 393224 | tf_op jit(solution)/shard_map/ppermute | solution.py:44
  62.7 2.8 %collective-permute-start.11 = (f32[256,256]{1,0:T(8,128)}, f32[256,256]{1,0:T(8,128)S(1)}, u32[]{:S(2)}, u32[]{:S(2)}) collective-permute-start(f32[256,256]{1,0:T(8,128)} %get-tuple-element.22), channel_id=1, source_target_pairs={{0,16},{16,0},{32,48},{48,32},{64,80},{80,64},{96,112},{112,96},{1... | collective-permute-start | bytes 786440 | tf_op jit(solution)/shard_map/ppermute | solution.py:44
  62.7 2.8 %collective-permute-start.15 = (bf16[128,1024]{1,0:T(8,128)(2,1)}, bf16[128,1024]{1,0:T(8,128)(2,1)}, u32[]{:S(2)}, u32[]{:S(2)}) collective-permute-start(bf16[128,1024]{1,0:T(8,128)(2,1)} %collective-permute-done.14.refs_6_), channel_id=1, source_target_pairs={{0,16},{16,0},{32,48},{48,32},{64,80},{80,64},{96,112},{112,96},{1... | collective-permute-start | bytes 786440 | tf_op jit(solution)/shard_map/ppermute | solution.py:44
  70.0 13.1 %collective-permute-start.17 = (bf16[32,2048]{1,0:T(8,128)(2,1)S(1)}, bf16[32,2048]{1,0:T(8,128)(2,1)S(1)}, u32[]{:S(2)}, u32[]{:S(2)}) collective-permute-start(bf16[32,2048]{1,0:T(8,128)(2,1)S(1)} %get-tuple-element.26), channel_id=1, source_target_pairs={{0,1},{1,0},{2,3},{3,2},{4,5},{5,4},{6,7},{7,6},{8,9},{9,8},{10,11... | collective-permute-start | bytes 393224 | tf_op jit(solution)/shard_map/ppermute | solution.py:48
  70.1 13.0 %collective-permute-start.19 = (bf16[32,2048]{1,0:T(8,128)(2,1)S(1)}, bf16[32,2048]{1,0:T(8,128)(2,1)S(1)}, u32[]{:S(2)}, u32[]{:S(2)}) collective-permute-start(bf16[32,2048]{1,0:T(8,128)(2,1)S(1)} %get-tuple-element.26), channel_id=1, source_target_pairs={{0,9},{1,8},{2,11},{3,10},{4,13},{5,12},{6,15},{7,14},{8,1},{9,0},... | collective-permute-start | bytes 393224 | tf_op jit(solution)/shard_map/ppermute | solution.py:48
  73.0 10.1 %collective-permute-start.18 = (bf16[32,2048]{1,0:T(8,128)(2,1)S(1)}, bf16[32,2048]{1,0:T(8,128)(2,1)S(1)}, u32[]{:S(2)}, u32[]{:S(2)}) collective-permute-start(bf16[32,2048]{1,0:T(8,128)(2,1)S(1)} %get-tuple-element.27), channel_id=1, source_target_pairs={{0,8},{1,9},{2,10},{3,11},{4,12},{5,13},{6,14},{7,15},{8,0},{9,1},... | collective-permute-start | bytes 393224 | tf_op jit(solution)/shard_map/ppermute | solution.py:48
  75.0 8.0 %collective-permute-start.16 = (bf16[16,2176]{1,0:T(8,128)(2,1)S(1)}, bf16[16,2176]{1,0:T(8,128)(2,1)S(1)}, u32[]{:S(2)}, u32[]{:S(2)}) collective-permute-start(bf16[16,2176]{1,0:T(8,128)(2,1)S(1)} %shard_map.109.refs_1_), channel_id=1, source_target_pairs={{0,8},{1,9},{2,10},{3,11},{4,12},{5,13},{6,14},{7,15},{8,0},{9,1},... | collective-permute-start | bytes 208904 | tf_op jit(solution)/shard_map/ppermute | solution.py:48
  88.3 1.4 collective-permute-start.20
  89.8 6.4 %collective-permute-start.23 = (bf16[64,2048]{1,0:T(8,128)(2,1)S(1)}, bf16[64,2048]{1,0:T(8,128)(2,1)S(1)}, u32[]{:S(2)}, u32[]{:S(2)}) collective-permute-start(bf16[64,2048]{1,0:T(8,128)(2,1)S(1)} %pad_maximum_fusion), channel_id=1, source_target_pairs={{0,1},{1,2},{2,3},{3,4},{4,5},{5,6},{6,7},{7,0},{8,9},{9,10},{10,1... | collective-permute-start | bytes 786440 | tf_op jit(solution)/shard_map/ppermute | solution.py:300
  96.2 6.4 %collective-permute-start.25 = (bf16[64,2048]{1,0:T(8,128)(2,1)S(1)}, bf16[64,2048]{1,0:T(8,128)(2,1)S(1)}, u32[]{:S(2)}, u32[]{:S(2)}) collective-permute-start(bf16[64,2048]{1,0:T(8,128)(2,1)S(1)} %collective-permute-done.23.refs_4_), channel_id=1, source_target_pairs={{0,1},{1,2},{2,3},{3,4},{4,5},{5,6},{6,7},{7,0},{8,9},{9,10},{10,1... | collective-permute-start | bytes 786440 | tf_op jit(solution)/shard_map/ppermute | solution.py:300
  102.6 11.7 %collective-permute-start.27 = (bf16[64,2048]{1,0:T(8,128)(2,1)S(1)}, bf16[64,2048]{1,0:T(8,128)(2,1)S(1)}, u32[]{:S(2)}, u32[]{:S(2)}) collective-permute-start(bf16[64,2048]{1,0:T(8,128)(2,1)S(1)} %collective-permute-done.25.refs_4_), channel_id=1, source_target_pairs={{0,1},{1,2},{2,3},{3,4},{4,5},{5,6},{6,7},{7,0},{8,9},{9,10},{10,1... | collective-permute-start | bytes 786440 | tf_op jit(solution)/shard_map/ppermute | solution.py:300
  102.6 20.0 %collective-permute-start.21 = (bf16[32,2048]{1,0:T(8,128)(2,1)S(1)}, bf16[32,2048]{1,0:T(8,128)(2,1)S(1)}, u32[]{:S(2)}, u32[]{:S(2)}) collective-permute-start(bf16[32,2048]{1,0:T(8,128)(2,1)S(1)} %get-tuple-element.30.refs_4_), channel_id=1, source_target_pairs={{0,4},{1,5},{2,6},{3,7},{4,0},{5,1},{6,2},{7,3},{8,12},{9,13},{10,... | collective-permute-start | bytes 393224 | tf_op jit(solution)/shard_map/ppermute | solution.py:48
  106.4 32.1 %collective-permute-start.24 = (bf16[64,2048]{1,0:T(8,128)(2,1)S(1)}, bf16[64,2048]{1,0:T(8,128)(2,1)S(1)}, u32[]{:S(2)}, u32[]{:S(2)}) collective-permute-start(bf16[64,2048]{1,0:T(8,128)(2,1)S(1)} %shard_map.115), channel_id=1, source_target_pairs={{0,7},{1,0},{2,1},{3,2},{4,3},{5,4},{6,5},{7,6},{8,15},{9,8},{10,9... | collective-permute-start | bytes 786440 | tf_op jit(solution)/shard_map/ppermute | solution.py:300
  110.7 27.9 %collective-permute-start.26 = (bf16[64,2048]{1,0:T(8,128)(2,1)S(1)}, bf16[64,2048]{1,0:T(8,128)(2,1)S(1)}, u32[]{:S(2)}, u32[]{:S(2)}) collective-permute-start(bf16[64,2048]{1,0:T(8,128)(2,1)S(1)} %shard_map.116), channel_id=1, source_target_pairs={{0,6},{1,7},{2,0},{3,1},{4,2},{5,3},{6,4},{7,5},{8,14},{9,15},{10,... | collective-permute-start | bytes 786440 | tf_op jit(solution)/shard_map/ppermute | solution.py:300
  116.7 21.9 %collective-permute-start.28 = (bf16[64,2048]{1,0:T(8,128)(2,1)S(1)}, bf16[64,2048]{1,0:T(8,128)(2,1)S(1)}, u32[]{:S(2)}, u32[]{:S(2)}) collective-permute-start(bf16[64,2048]{1,0:T(8,128)(2,1)S(1)} %shard_map.117), channel_id=1, source_target_pairs={{0,5},{1,6},{2,7},{3,0},{4,1},{5,2},{6,3},{7,4},{8,13},{9,14},{10,... | collective-permute-start | bytes 786440 | tf_op jit(solution)/shard_map/ppermute | solution.py:300
  125.3 13.3 %collective-permute-start.22 = (bf16[32,2048]{1,0:T(8,128)(2,1)S(1)}, bf16[32,2048]{1,0:T(8,128)(2,1)S(1)}, u32[]{:S(2)}, u32[]{:S(2)}) collective-permute-start(bf16[32,2048]{1,0:T(8,128)(2,1)S(1)} %get-tuple-element.31), channel_id=1, source_target_pairs={{0,4},{1,5},{2,6},{3,7},{4,0},{5,1},{6,2},{7,3},{8,12},{9,13},{10,... | collective-permute-start | bytes 393224 | tf_op jit(solution)/shard_map/ppermute | solution.py:48
  139.9 3.5 %collective-permute-start.29 = (bf16[16,2048]{1,0:T(8,128)(2,1)S(1)}, bf16[16,2048]{1,0:T(8,128)(2,1)S(1)}, u32[]{:S(2)}, u32[]{:S(2)}) collective-permute-start(bf16[16,2048]{1,0:T(8,128)(2,1)S(1)} %get-tuple-element.34), channel_id=1, source_target_pairs={{0,16},{16,0},{32,48},{48,32},{64,80},{80,64},{96,112},{112,96},{1... | collective-permute-start | bytes 196616 | tf_op jit(solution)/shard_map/ppermute | solution.py:44
  140.0 6.0 %collective-permute-start.30 = (bf16[16,2048]{1,0:T(8,128)(2,1)S(1)}, bf16[16,2048]{1,0:T(8,128)(2,1)S(1)}, u32[]{:S(2)}, u32[]{:S(2)}) collective-permute-start(bf16[16,2048]{1,0:T(8,128)(2,1)S(1)} %get-tuple-element.35), channel_id=1, source_target_pairs={{0,8},{1,9},{2,10},{3,11},{4,12},{5,13},{6,14},{7,15},{8,0},{9,1},... | collective-permute-start | bytes 196616 | tf_op jit(solution)/shard_map/ppermute | solution.py:48
  141.9 5.6 %collective-permute-start.31 = (bf16[16,2048]{1,0:T(8,128)(2,1)S(1)}, bf16[16,2048]{1,0:T(8,128)(2,1)S(1)}, u32[]{:S(2)}, u32[]{:S(2)}) collective-permute-start(bf16[16,2048]{1,0:T(8,128)(2,1)S(1)} %get-tuple-element.36), channel_id=1, source_target_pairs={{0,24},{1,25},{2,26},{3,27},{4,28},{5,29},{6,30},{7,31},{8,16},{9,... | collective-permute-start | bytes 196616 | tf_op jit(solution)/shard_map/ppermute | solution.py:300
  (11 other events, 156.2 us)

commit v4 on v3

v4 whole, which is shorter than its diff:
```python
import math

import jax
import jax.numpy as jnp
from jax import lax
from jax.experimental import pallas as pl
from jax.experimental.pallas import tpu as pltpu
from jax.sharding import PartitionSpec as P

D = 2048
HEAD_DIM = 128
FF = 768
TOP = 8
HEADS = 16
KV_HEADS = 2
EXPERTS = 16
TOK_C = 256
TOK_DEV = 16
NEGATIVE = -1e30
SCALE = math.log2(math.e) / math.sqrt(HEAD_DIM)
F32 = jnp.float32
BF16 = jnp.bfloat16

CORE_SWAP = [(i, i ^ 1) for i in range(16)]
Y_SWAP = [(i, i ^ 8) for i in range(16)]


OTHER_ROW = [(i, i + 8) for i in range(8)]


def block_route(step):
    route = []
    for here in range(16):
        there = here // 8 * 8 + (here // 2 + step) % 4 * 2 + here % 2
        if here < there:
            route.append((here, there))
    return route


def relay_route(step):
    return [(8 + i, 8 + (i // 2 + step) % 4 * 2 + i % 2) for i in range(8)]


def z_shift(step):
    return [(y * 8 + z, y * 8 + (z + step) % 8) for y in range(2) for z in range(8)]


def on_ctx(block, route):
    return lax.ppermute(block, "ctx", route)


def on_exp(block, route):
    return lax.ppermute(block, "exp", route)


def kernel_call(
    body, scalars, resident, fetched, out_shapes, flops, transcendentals=0, limit=16, idle=(), scratch=()
):
    n_own = len(resident)
    resident, fetched = [*resident, *fetched], []
    ins = [*resident, *fetched, *idle]
    n_res, n_fetch = len(resident), len(fetched)
    n_out = len(jax.tree.leaves(out_shapes))

    def whole(*refs):
        place, refs = refs[0], refs[1:]
        sources = refs[n_res : n_res + n_fetch]
        outs = refs[len(ins) : len(ins) + n_out]
        buffers = refs[len(ins) + n_out : len(ins) + n_out + n_fetch]
        copies = []
        for n in range(n_fetch):
            copies.append(
                pltpu.make_async_copy(sources[n], buffers[n], refs[len(ins) + n_out + n_fetch + n])
            )
        for copy in copies:
            copy.start()
        extra = refs[len(ins) + n_out + 2 * n_fetch :]
        body(place, refs[:n_own], refs[n_own:n_res], (*outs, *extra), lambda n: None)

    size = sum(a.size * a.dtype.itemsize for a in [*resident, *fetched])
    vmem = pl.BlockSpec(memory_space=pltpu.VMEM)
    return pl.pallas_call(
        whole,
        out_shape=out_shapes,
        in_specs=[pl.BlockSpec(memory_space=pltpu.SMEM)]
        + [vmem] * n_res
        + [pl.BlockSpec(memory_space=pl.ANY)] * n_fetch
        + [vmem] * len(idle),
        out_specs=jax.tree.map(lambda _: vmem, out_shapes),
        scratch_shapes=[pltpu.VMEM(a.shape, a.dtype) for a in fetched]
        + [pltpu.SemaphoreType.DMA] * n_fetch
        + list(scratch),
        compiler_params=pltpu.CompilerParams(vmem_limit_bytes=limit * 1024 * 1024),
        cost_estimate=pl.CostEstimate(
            flops=flops, bytes_accessed=size, transcendentals=transcendentals
        ),
    )(scalars, *ins)


def after(value, *earlier):
    return lax.optimization_barrier((value, *earlier))


def struct(shape, dtype):
    return jax.ShapeDtypeStruct(shape, dtype)


ROWS_TILE = 256
PLACES = [(r, d) for r in (0, 1) for d in (0, -1, 1, 2)]


def attend_all(place, resident, fetched, outs, wait):
    core, y, z, ctx = place[0], place[1], place[2], place[3]
    row, x = ctx // 8, lax.rem(ctx // 2, 4)
    sources = [(row ^ r) * 8 + lax.rem(x + d + 4, 4) * 2 + core for r, d in PLACES]
    half = resident[0].shape[0]
    for n in range(8):
        wait(n)
    token = lax.broadcasted_iota(jnp.int32, (ROWS_TILE, 1), 0) & 127
    part = token >> 4
    key = lax.broadcasted_iota(jnp.int32, (1, TOK_C), 1)
    lane = lax.broadcasted_iota(jnp.int32, (ROWS_TILE, HEAD_DIM), 1)
    for n, q_ref in enumerate(resident):
        q_ctx = ctx ^ n
        first = z + 7 - (core ^ n)
        local = (part >> 2) * 128 + (((part & 3) + first) & 7) * 16 + (token & 15)

        def rows(i, _, n=n, q_ref=q_ref, q_ctx=q_ctx, local=local):
            at = pl.ds(pl.multiple_of(i * ROWS_TILE, ROWS_TILE), ROWS_TILE)
            ahead = key - local
            queries = q_ref[at, :]
            parts = []
            for source, ref in zip(sources, fetched):
                scores = lax.dot_general(
                    queries,
                    ref[:, :HEAD_DIM],
                    (((1,), (1,)), ((), ())),
                    preferred_element_type=F32,
                )
                parts.append(
                    jnp.where(ahead <= (q_ctx - source) * TOK_C, scores, F32(NEGATIVE))
                )
            top = parts[0]
            for part in parts[1:]:
                top = jnp.maximum(top, part)
            top = jnp.max(top, axis=1, keepdims=True)
            total, mixed = 0.0, 0.0
            for part, ref in zip(parts, fetched):
                weights = jnp.exp2((part - top) * SCALE)
                total = total + weights
                mixed = mixed + jnp.dot(
                    weights.astype(BF16), ref[:, HEAD_DIM:], preferred_element_type=F32
                )
            total = jnp.sum(total, axis=1, keepdims=True)
            outs[n][at, :HEAD_DIM] = mixed
            outs[n][at, HEAD_DIM:] = jnp.where(lane < 64, top, total)
            return 0

        lax.fori_loop(0, half // ROWS_TILE, rows, 0)


def project(place, resident, fetched, outs, wait):
    (own_ref,) = resident
    other_ref, near_ref, far_ref, w_own_ref = fetched
    keep_ref, *send_refs, attn_ref = outs
    core = place[0]
    wait(0)
    own_top = own_ref[:, HEAD_DIM : HEAD_DIM + 1]
    other_top = other_ref[:, HEAD_DIM : HEAD_DIM + 1]
    top = jnp.maximum(own_top, other_top)
    own_factor = jnp.exp2((own_top - top) * SCALE)
    other_factor = jnp.exp2((other_top - top) * SCALE)
    total = own_ref[:, HEAD_DIM + 64 : HEAD_DIM + 65] * own_factor
    total = total + other_ref[:, HEAD_DIM + 64 : HEAD_DIM + 65] * other_factor
    mixed = own_ref[:, :HEAD_DIM] * own_factor + other_ref[:, :HEAD_DIM] * other_factor
    attn_ref[...] = (mixed / total).astype(BF16)

    def ordered(head):
        pieces = []
        for low, high in ((1, 2), (0, 1), (2, 3), (3, 0)):
            for half in range(2):
                start = head * 128 + half * 64 + jnp.where(core == 0, low, high) * 16
                pieces.append(attn_ref[pl.ds(pl.multiple_of(start, 16), 16), :])
        return jnp.concatenate(pieces, axis=0)

    heads = [ordered(0), ordered(1)]
    width = D // 2
    for n in range(1, 4):
        wait(n)
    for side, w_ref in ((core, near_ref), (1 - core, far_ref)):
        at = pl.ds(pl.multiple_of(side * width, width), width)
        sums = jnp.dot(heads[0], w_own_ref[:, at], preferred_element_type=F32)
        sums = sums + jnp.dot(heads[1], w_ref[...], preferred_element_type=F32)
        keep_ref[:, at] = sums[:32]
        for s in range(3):
            send_refs[s][:, at] = sums[(s + 1) * 32 : (s + 2) * 32].astype(BF16)


def add_up(place, resident, fetched, outs, wait):
    sums = resident[0][...]
    for n in range(3):
        wait(n)
        sums = sums + fetched[n][...].astype(F32)
    outs[0][...] = sums
    outs[1][...] = sums.astype(BF16)


def normalise(place, resident, fetched, outs, wait):
    own_ref, sums_ref, gain_ref = resident
    y_ref, core_ref, both_ref, sums_y_ref, sums_core_ref, sums_both_ref = fetched
    hidden_ref, normed_ref = outs
    y = place[1]
    for n in range(6):
        wait(n)
    for n in range(4):
        at = pl.ds(n % 2 * 16, 16)
        to = pl.ds(n * 16, 16)
        here, there = (own_ref, y_ref) if n < 2 else (core_ref, both_ref)
        extended = jnp.where(y == n % 2, here[...].astype(F32), there[...].astype(F32))
        if n < 2:
            projected = sums_ref[at, :] + sums_y_ref[at, :].astype(F32)
        else:
            projected = sums_core_ref[at, :].astype(F32) + sums_both_ref[at, :].astype(F32)
        hidden = (extended[:, :D] + projected).astype(BF16)
        wide = hidden.astype(F32)
        inverse = lax.rsqrt(jnp.mean(wide * wide, axis=-1, keepdims=True) + 1e-06)
        normed = (wide * inverse * gain_ref[...].astype(F32)).astype(BF16)
        if n < 2:
            hidden_ref[at, :] = hidden
        normed_ref[to, :D] = normed
        normed_ref[to, D:] = extended[:, D:].astype(BF16)


def early(place, resident, fetched, outs, wait):
    outs[0][...] = resident[0][:8, :128]


def expert(place, resident, fetched, outs, wait):
    gate_ref, up_ref, down_ref = resident
    keep_ref, give_ref = outs
    y, z = place[1], place[2]
    for n in range(len(fetched)):
        wait(n)
    rows = [ref[:, :D] for ref in fetched]
    weights = [ref[:, D:] for ref in fetched]
    rows = rows[0] if len(rows) == 1 else jnp.concatenate(rows, axis=0)
    weights = weights[0] if len(weights) == 1 else jnp.concatenate(weights, axis=0)
    lane = lax.broadcasted_iota(jnp.int32, weights.shape, 1)
    weight = jnp.where(lane == y * 8 + z, weights.astype(F32), 0.0)
    weight = jnp.sum(weight, axis=1, keepdims=True)
    gate_part = jnp.dot(rows, gate_ref[...], preferred_element_type=F32)
    up_part = jnp.dot(rows, up_ref[...], preferred_element_type=F32)
    inner = (gate_part * jax.nn.sigmoid(gate_part) * up_part).astype(BF16)
    result = jnp.dot(inner, down_ref[...], preferred_element_type=F32).astype(BF16)
    result = result.astype(F32) * weight
    for n in range(rows.shape[0] // 32):
        at = pl.ds(n * 16, 16)
        low, high = result[n * 32 : n * 32 + 16], result[n * 32 + 16 : n * 32 + 32]
        keep_ref[at, :] = jnp.where(y == 0, low, high)
        give_ref[at, :] = jnp.where(y == 0, high, low).astype(BF16)


def run_expert(place, rows, weights, idle=()):
    total = sum(r.shape[0] for r in rows)
    keep, give = kernel_call(
        expert,
        place,
        weights,
        rows,
        [struct((total // 2, D), F32), struct((total // 2, D), BF16)],
        6 * total * D * FF,
        total * FF,
        idle=idle,
    )
    return keep, on_exp(give, Y_SWAP)


def join(place, resident, fetched, outs, wait):
    sums = resident[0][...] + resident[1][...].astype(F32)
    start = 0
    for out in outs:
        out[...] = sums[start : start + out.shape[0]].astype(out.dtype)
        start += out.shape[0]


def run_join(place, keep, got, outs):
    return kernel_call(join, place, [keep, got], [], outs, keep.size)


def gather_up(place, resident, fetched, outs, wait):
    own_ref, opposite_ref, *near_refs = resident
    mine = own_ref[...] + opposite_ref[...].astype(F32)
    theirs = 0.0
    for ref in near_refs:
        mine = mine + ref[:16, :].astype(F32)
        theirs = theirs + ref[16:, :].astype(F32)
    outs[0][...] = mine
    outs[1][...] = theirs.astype(BF16)


def finish(place, resident, fetched, outs, wait):
    hidden_ref, keep_ref = resident
    hidden = jnp.where(
        place[1] == 0, hidden_ref[:16, :].astype(F32), hidden_ref[16:, :].astype(F32)
    )
    wait(0)
    moe = keep_ref[...] + fetched[0][...].astype(F32)
    outs[0][...] = (hidden + moe).astype(BF16)


def extend(place, resident, fetched, outs, wait):
    residual_ref, ids_ref, gates_ref = resident
    lane = lax.broadcasted_iota(jnp.int32, (TOK_DEV, 128), 1)
    weights = jnp.zeros((TOK_DEV, 128), F32)
    for k in range(TOP):
        gate = gates_ref[:, k : k + 1].astype(F32)
        weights = weights + jnp.where(lane == ids_ref[:, k : k + 1], gate, 0.0)
    outs[0][:, :D] = residual_ref[...]
    outs[0][:, D:] = weights.astype(BF16)


def by_core(step):
    route = []
    for c in range(16):
        way = step if c % 2 == 0 else -step
        for e in range(16):
            route.append((c * 16 + e, c * 16 + e // 8 * 8 + (e + way) % 8))
    return route


def on_both(block, route):
    return lax.ppermute(block, ("ctx", "exp"), route)


def two_swaps(ctx_bit, exp_bit):
    return [
        (c * 16 + e, (c ^ ctx_bit) * 16 + (e ^ exp_bit)) for c in range(16) for e in range(16)
    ]


def to_three(to_y, to_core, to_both):
    return (
        on_exp(to_y, Y_SWAP),
        on_ctx(to_core, CORE_SWAP),
        on_both(to_both, two_swaps(1, 8)),
    )


def shards(
    query,
    keys,
    values,
    out_proj,
    residual,
    norm_gain,
    expert_ids,
    gate_values,
    w_gate,
    w_up,
    w_down,
):
    ctx, exp = lax.axis_index("ctx"), lax.axis_index("exp")
    core, y, z = ctx % 2, exp // 8, exp % 8
    place = jnp.stack([core, y, z, ctx]).astype(jnp.int32)
    kv_index = exp // (HEADS // KV_HEADS)
    block = jnp.concatenate(
        [
            lax.dynamic_slice_in_dim(keys, kv_index * HEAD_DIM, HEAD_DIM, 1),
            lax.dynamic_slice_in_dim(values, kv_index * HEAD_DIM, HEAD_DIM, 1),
        ],
        axis=1,
    )

    other = on_ctx(block, OTHER_ROW)
    blocks = [block] + [on_ctx(block, block_route(-d)) for _, d in PLACES[1:4]]
    blocks += [other] + [on_ctx(other, relay_route(-d)) for _, d in PLACES[5:]]

    by_holder = query.reshape(2, 8, TOK_DEV, HEAD_DIM)
    by_holder = jnp.concatenate([by_holder, by_holder], axis=1)

    def rows_of(first):
        return lax.dynamic_slice_in_dim(by_holder, first % 8, 4, 1).reshape(128, HEAD_DIM)

    first = z + 7 - core
    mine = jnp.concatenate([rows_of(first), on_exp(rows_of(first + 4), z_shift(4))], axis=0)
    theirs = on_ctx(mine, CORE_SWAP)

    w_out, blocks[4] = after(out_proj, blocks[4])
    w_half = lax.dynamic_slice_in_dim(w_out, core * (D // 2), D // 2, 1)
    w_near = on_exp(w_half, z_shift(4))
    w_far = on_ctx(w_near, CORE_SWAP)

    own, swap = kernel_call(
        attend_all,
        place,
        [mine, theirs],
        blocks,
        [struct((256, 256), F32)] * 2,
        4 * 512 * 2048 * HEAD_DIM,
        512 * 2048,
    )
    joined = on_ctx(swap, CORE_SWAP)
    keep, *sends = kernel_call(
        project,
        place,
        [own],
        [joined, w_near, w_far, out_proj],
        [struct((32, D), F32)] + [struct((32, D), BF16)] * 3,
        2 * 128 * 256 * D,
        scratch=[pltpu.VMEM((256, HEAD_DIM), BF16)],
    )
    recvs = [
        on_exp(sends[0], z_shift(-1)),
        on_exp(sends[1], z_shift(1)),
        on_both(sends[2], by_core(2)),
    ]
    rows, recvs[0] = after(residual, recvs[0])
    (extended,) = kernel_call(
        extend,
        place,
        [rows, expert_ids, gate_values],
        [],
        [struct((TOK_DEV, D + 128), BF16)],
        TOK_DEV * D,
    )
    extended_others = to_three(extended, extended, extended)
    sums, send = kernel_call(
        add_up,
        place,
        [keep],
        recvs,
        [struct((32, D), F32), struct((32, D), BF16)],
        3 * 32 * D,
    )
    hidden, round_0 = kernel_call(
        normalise,
        place,
        [extended, sums, norm_gain.reshape(1, D)],
        [*extended_others, *to_three(send, send, send)],
        [struct((32, D), BF16), struct((64, D + 128), BF16)],
        16 * 32 * D,
    )

    half = struct((32, D), BF16)
    w = [w_gate[0], w_up[0], w_down[0]]
    round_1 = on_both(round_0, by_core(1))
    round_2 = on_both(round_0, by_core(2))
    (seen,) = kernel_call(
        early, place, [round_0], [], [struct((8, 128), BF16)], 8 * 128, idle=w
    )
    round_2, seen = after(round_2, seen)
    round_3 = on_both(round_2, by_core(1))
    round_4 = on_both(round_2[:32], by_core(2))
    keep, got = run_expert(place, [round_1, round_2, round_0[:32]], w, [seen])
    keep_far, got_far = run_expert(place, [round_3, round_4], w)
    sum_1, sum_2, own_sum = run_join(place, keep, got, [half, half, struct((16, D), F32)])
    back_1 = on_both(sum_1, by_core(-1))
    back_2 = on_both(sum_2, by_core(-2))
    got_far, back_1, back_2 = after(got_far, back_1, back_2)
    sum_3, sum_4 = run_join(place, keep_far, got_far, [half, struct((16, D), BF16)])
    back_3 = on_both(sum_3, by_core(-3))
    back_4 = on_exp(sum_4, z_shift(4))
    keep, to_core = kernel_call(
        gather_up,
        place,
        [own_sum, back_4, back_1, back_2, back_3],
        [],
        [struct((16, D), F32), struct((16, D), BF16)],
        8 * 16 * D,
    )
    return kernel_call(
        finish,
        place,
        [hidden, keep],
        [on_ctx(to_core, CORE_SWAP)],
        [struct((16, D), BF16)],
        3 * 16 * D,
    )[0]


def solution(mesh):
    return jax.shard_map(
        shards,
        mesh=mesh,
        in_specs=(
            P("ctx", "exp"),
            P("ctx", None),
            P("ctx", None),
            P("exp", None),
            P(("ctx", "exp"), None),
            P(),
            P(("ctx", "exp"), None),
            P(("ctx", "exp"), None),
            P("exp", None, None),
            P("exp", None, None),
            P("exp", None, None),
        ),
        out_specs=P(("ctx", "exp"), None),
        check_vma=False,
    )
```

time: 151 us -> 136 us (0.901)
  the two profiles are of different devices: /device:TPU:32 before, /device:TPU:41 now
where the time goes in v4:
time: 136 us; the launch traced here: 135 us
  starting transfers between devices  79.1 us (58%)
  waiting for transfers between devices  26 us (19%)
  Pallas kernels  15.7 us (12%)
  local copies, waits for them, and re-layouts  11.6 us (9%)
  other arithmetic  2.32 us (2%)
    ppermute x13, starting transfers between devices, on_ctx(): return lax.ppermute(block, 'ctx', route)  35.5 us
    ppermute x10, starting transfers between devices, on_both(): return lax.ppermute(block, ('ctx', 'exp'), route)  24.9 us
    ppermute x9, starting transfers between devices, on_exp(): return lax.ppermute(block, 'exp', route)  18.7 us
    pallas_call x12, Pallas kernels, kernel_call(): pl.pallas_call(whole, out_shape=out_shapes, in_specs=[pl.BlockSpec(memory...  15.7 us
    ppermute x10, waiting for transfers between devices, on_both(): return lax.ppermute(block, ('ctx', 'exp'), route)  15.3 us
    unnamed x22, local copies, waits for them, and re-layouts  8.95 us
    ppermute x13, waiting for transfers between devices, on_ctx(): return lax.ppermute(block, 'ctx', route)  7.9 us
    ppermute x9, waiting for transfers between devices, on_exp(): return lax.ppermute(block, 'exp', route)  2.81 us
  transfers between devices with their start and end apart: 32, of which 13 were waited for; matrix products, arithmetic and copies ran while one was open for 4% of the time, Pallas kernels for 8%

profile of v4, /device:TPU:41, one launch (start us, length us, event | category | flops | bytes accessed | tf_op | source)
XLA Modules:
  0.0 134.9 jit_solution(5075556403245904241)
XLA Ops:
  2.5 3.1 %collective-permute-start.2 = (bf16[256,256]{1,0:T(8,128)(2,1)S(1)}, bf16[256,256]{1,0:T(8,128)(2,1)S(1)}, u32[]{:S(2)}, u32[]{:S(2)}) collective-permute-start(bf16[256,256]{1,0:T(8,128)(2,1)S(1)} %pad_maximum_fusion.refs_3_), channel_id=1, source_target_pairs={{0,32},{16,48},{32,64},{48,80},{64,96},{80,112},{128,160},{144,176... | collective-permute-start | bytes 393224 | tf_op jit(solution)/shard_map/ppermute | solution.py:49
  5.6 3.2 %collective-permute-start.3 = (bf16[256,256]{1,0:T(8,128)(2,1)S(1)}, bf16[256,256]{1,0:T(8,128)(2,1)}, u32[]{:S(2)}, u32[]{:S(2)}) collective-permute-start(bf16[256,256]{1,0:T(8,128)(2,1)S(1)} %pad_maximum_fusion.refs_3_), channel_id=1, source_target_pairs={{0,96},{16,112},{128,224},{144,240},{1,97},{17,113},{129,225},{145... | collective-permute-start | bytes 393224 | tf_op jit(solution)/shard_map/ppermute | solution.py:49
  10.3 6.0 %collective-permute-start = (bf16[128,128]{1,0:T(8,128)(2,1)}, bf16[128,128]{1,0:T(8,128)(2,1)}, u32[]{:S(2)}, u32[]{:S(2)}) collective-permute-start(bf16[128,128]{1,0:T(8,128)(2,1)} %bitcast.6), channel_id=1, source_target_pairs={{0,4},{1,5},{2,6},{3,7},{4,0},{5,1},{6,2},{7,3},{8,12},{9,13},{10,... | collective-permute-start | bytes 98312 | tf_op jit(solution)/shard_map/ppermute | solution.py:53
  18.7 1.9 %collective-permute-start.1 = (bf16[256,128]{1,0:T(8,128)(2,1)S(1)}, bf16[256,128]{1,0:T(8,128)(2,1)S(1)}, u32[]{:S(2)}, u32[]{:S(2)}) collective-permute-start(bf16[256,128]{1,0:T(8,128)(2,1)S(1)} %pad_maximum_fusion.1.refs_1_), channel_id=1, source_target_pairs={{0,16},{16,0},{32,48},{48,32},{64,80},{80,64},{96,112},{112,96},{1... | collective-permute-start | bytes 196616 | tf_op jit(solution)/shard_map/ppermute | solution.py:49
  20.5 2.5 %collective-permute-start.4 = (bf16[256,256]{1,0:T(8,128)(2,1)S(1)}, bf16[256,256]{1,0:T(8,128)(2,1)S(1)}, u32[]{:S(2)}, u32[]{:S(2)}) collective-permute-start(bf16[256,256]{1,0:T(8,128)(2,1)S(1)} %pad_maximum_fusion.refs_3_), channel_id=1, source_target_pairs={{0,64},{16,80},{32,96},{48,112},{128,192},{144,208},{160,224},{176... | collective-permute-start | bytes 393224 | tf_op jit(solution)/shard_map/ppermute | solution.py:49
  23.0 1.9 %collective-permute-start.6 = (bf16[256,256]{1,0:T(8,128)(2,1)S(1)}, bf16[256,256]{1,0:T(8,128)(2,1)S(1)}, u32[]{:S(2)}, u32[]{:S(2)}) collective-permute-start(bf16[256,256]{1,0:T(8,128)(2,1)S(1)} %collective-permute-done.5.refs_7_), channel_id=1, source_target_pairs={{128,160},{144,176},{160,192},{176,208},{192,224},{208,240},{224,1... | collective-permute-start | bytes 393224 | tf_op jit(solution)/shard_map/ppermute | solution.py:49
  25.6 4.6 %collective-permute-start.7 = (bf16[256,256]{1,0:T(8,128)(2,1)S(1)}, bf16[256,256]{1,0:T(8,128)(2,1)S(1)}, u32[]{:S(2)}, u32[]{:S(2)}) collective-permute-start(bf16[256,256]{1,0:T(8,128)(2,1)S(1)} %collective-permute-done.5.refs_7_), channel_id=1, source_target_pairs={{128,224},{144,240},{160,128},{176,144},{192,160},{208,176},{224,1... | collective-permute-start | bytes 393224 | tf_op jit(solution)/shard_map/ppermute | solution.py:49
  30.2 1.9 %collective-permute-start.8 = (bf16[256,256]{1,0:T(8,128)(2,1)S(1)}, bf16[256,256]{1,0:T(8,128)(2,1)S(1)}, u32[]{:S(2)}, u32[]{:S(2)}) collective-permute-start(bf16[256,256]{1,0:T(8,128)(2,1)S(1)} %collective-permute-done.5.refs_7_), channel_id=1, source_target_pairs={{128,192},{144,208},{160,224},{176,240},{192,128},{208,144},{224,1... | collective-permute-start | bytes 393224 | tf_op jit(solution)/shard_map/ppermute | solution.py:49
  32.4 5.3 %collective-permute-done.8.refs_10_ = bf16[256,256]{1,0:T(8,128)(2,1)S(1)} collective-permute-done((bf16[256,256]{1,0:T(8,128)(2,1)S(1)}, bf16[256,256]{1,0:T(8,128)(2,1)S(1)}, u32[]{:S(2)}, u32[]{:S(2)}) %collective-permute-start.8) | collective-permute-done | bytes 131104 | tf_op jit(solution)/shard_map/ppermute | solution.py:49
  39.5 3.0 %shard_map.109 = (f32[256,256]{1,0:T(8,128)S(1)}, f32[256,256]{1,0:T(8,128)S(1)}) custom-call(s32[4]{0:T(128)S(1)} %pad_add_fusion.refs_0_, bf16[256,128]{1,0:T(8,128)(2,1)S(1)} %pad_maximum_fusion.1.refs_1_, bf16[256,128]{1,0:T(8,128)(2,1)S(1)} %collective-permute-done.1.refs_2_, bf16[256,256]{1,0:T(8,128)(2,1)S(1)} %pad_maximum_fusion.refs_3_, ...), custom_call_target="tpu_custom_call" | custom-call | flops 536870912 | bytes 1179648 | tf_op jit(solution)/shard_map/pallas_call | solution.py:82
  47.0 2.0 %shard_map.110 = (f32[32,2048]{1,0:T(8,128)S(1)}, bf16[32,2048]{1,0:T(8,128)(2,1)}, bf16[32,2048]{1,0:T(8,128)(2,1)}, bf16[32,2048]{1,0:T(8,128)(2,1)}) custom-call(s32[4]{0:T(128)S(1)} %pad_add_fusion.refs_0_, f32[256,256]{1,0:T(8,128)S(1)} %get-tuple-element.36.refs_1_, f32[256,256]{1,0:T(8,128)S(1)} %collective-permute-done.9.refs_2_, ...), custom_call_target="tpu_custom_call" | custom-call | flops 134217728 | bytes 1572864 | tf_op jit(solution)/shard_map/pallas_call | solution.py:82
  50.4 8.8 %collective-permute-start.14 = (bf16[32,2048]{1,0:T(8,128)(2,1)}, bf16[32,2048]{1,0:T(8,128)(2,1)}, u32[]{:S(2)}, u32[]{:S(2)}) collective-permute-start(bf16[32,2048]{1,0:T(8,128)(2,1)} %get-tuple-element.44), channel_id=1, source_target_pairs={{0,2},{1,3},{2,4},{3,5},{4,6},{5,7},{6,0},{7,1},{8,10},{9,11},{10,... | collective-permute-start | bytes 393224 | tf_op jit(solution)/shard_map/ppermute | solution.py:332
  61.6 2.1 %collective-permute-start.15 = (bf16[16,2176]{1,0:T(8,128)(2,1)S(1)}, bf16[16,2176]{1,0:T(8,128)(2,1)S(1)}, u32[]{:S(2)}, u32[]{:S(2)}) collective-permute-start(bf16[16,2176]{1,0:T(8,128)(2,1)S(1)} %shard_map.111.refs_1_), channel_id=1, source_target_pairs={{0,8},{1,9},{2,10},{3,11},{4,12},{5,13},{6,14},{7,15},{8,0},{9,1},... | collective-permute-start | bytes 208904 | tf_op jit(solution)/shard_map/ppermute | solution.py:53
  65.8 3.1 %collective-permute-start.19 = (bf16[32,2048]{1,0:T(8,128)(2,1)S(1)}, bf16[32,2048]{1,0:T(8,128)(2,1)S(1)}, u32[]{:S(2)}, u32[]{:S(2)}) collective-permute-start(bf16[32,2048]{1,0:T(8,128)(2,1)S(1)} %get-tuple-element.46), channel_id=1, source_target_pairs={{0,16},{16,0},{32,48},{48,32},{64,80},{80,64},{96,112},{112,96},{1... | collective-permute-start | bytes 393224 | tf_op jit(solution)/shard_map/ppermute | solution.py:49
  70.2 1.9 %collective-permute-start.17 = (bf16[16,2176]{1,0:T(8,128)(2,1)S(1)}, bf16[16,2176]{1,0:T(8,128)(2,1)S(1)}, u32[]{:S(2)}, u32[]{:S(2)}) collective-permute-start(bf16[16,2176]{1,0:T(8,128)(2,1)S(1)} %shard_map.111.refs_1_), channel_id=1, source_target_pairs={{0,24},{1,25},{2,26},{3,27},{4,28},{5,29},{6,30},{7,31},{8,16},{9,... | collective-permute-start | bytes 208904 | tf_op jit(solution)/shard_map/ppermute | solution.py:332
  72.8 4.1 %collective-permute-done.17.refs_6_ = bf16[16,2176]{1,0:T(8,128)(2,1)S(1)} collective-permute-done((bf16[16,2176]{1,0:T(8,128)(2,1)S(1)}, bf16[16,2176]{1,0:T(8,128)(2,1)S(1)}, u32[]{:S(2)}, u32[]{:S(2)}) %collective-permute-start.17) | collective-permute-done | bytes 69664 | tf_op jit(solution)/shard_map/ppermute | solution.py:332
  77.8 2.3 %collective-permute-start.22 = (bf16[64,2176]{1,0:T(8,128)(2,1)S(1)}, bf16[64,2176]{1,0:T(8,128)(2,1)S(1)}, u32[]{:S(2)}, u32[]{:S(2)}) collective-permute-start(bf16[64,2176]{1,0:T(8,128)(2,1)S(1)} %get-tuple-element.48.refs_1_), channel_id=1, source_target_pairs={{0,2},{1,3},{2,4},{3,5},{4,6},{5,7},{6,0},{7,1},{8,10},{9,11},{10,... | collective-permute-start | bytes 835592 | tf_op jit(solution)/shard_map/ppermute | solution.py:332
  80.1 2.1 %collective-permute-start.21 = (bf16[64,2176]{1,0:T(8,128)(2,1)S(1)}, bf16[64,2176]{1,0:T(8,128)(2,1)S(1)}, u32[]{:S(2)}, u32[]{:S(2)}) collective-permute-start(bf16[64,2176]{1,0:T(8,128)(2,1)S(1)} %get-tuple-element.48.refs_1_), channel_id=1, source_target_pairs={{0,1},{1,2},{2,3},{3,4},{4,5},{5,6},{6,7},{7,0},{8,9},{9,10},{10,1... | collective-permute-start | bytes 835592 | tf_op jit(solution)/shard_map/ppermute | solution.py:332
  82.2 1.9 %copy-done.1 = bf16[1,2048,768]{2,1,0:T(8,128)(2,1)S(1)} copy-done((bf16[1,2048,768]{2,1,0:T(8,128)(2,1)S(1)}, bf16[1,2048,768]{2,1,0:T(8,128)(2,1)}, u32[]{:S(2)}) %copy-start.1) | copy-done | bytes 3145752
  84.1 1.9 %copy-done.2 = bf16[1,768,2048]{2,1,0:T(8,128)(2,1)S(1)} copy-done((bf16[1,768,2048]{2,1,0:T(8,128)(2,1)S(1)}, bf16[1,768,2048]{2,1,0:T(8,128)(2,1)}, u32[]{:S(2)}) %copy-start.2) | copy-done | bytes 3145752
  86.6 3.5 %collective-permute-start.24 = (bf16[64,2176]{1,0:T(8,128)(2,1)S(1)}, bf16[64,2176]{1,0:T(8,128)(2,1)S(1)}, u32[]{:S(2)}, u32[]{:S(2)}) collective-permute-start(bf16[64,2176]{1,0:T(8,128)(2,1)S(1)} %collective-permute-done.22.refs_5_), channel_id=1, source_target_pairs={{0,1},{1,2},{2,3},{3,4},{4,5},{5,6},{6,7},{7,0},{8,9},{9,10},{10,1... | collective-permute-start | bytes 835592 | tf_op jit(solution)/shard_map/ppermute | solution.py:332
  91.5 2.4 %shard_map.115 = (f32[80,2048]{1,0:T(8,128)S(1)}, bf16[80,2048]{1,0:T(8,128)(2,1)S(1)}) custom-call(s32[4]{0:T(128)S(1)} %pad_add_fusion.refs_0_, bf16[2048,768]{1,0:T(8,128)(2,1)S(1)} %bitcast.11, bf16[2048,768]{1,0:T(8,128)(2,1)S(1)} %bitcast.14, bf16[768,2048]{1,0:T(8,128)(2,1)S(1)} %bitcast.17, bf16[64,2176]{1,0:T(8,128)(2,1)S(1)} %collective-permute-done.21.refs_4_, ...), custom_call_target="tpu_custom_call" | custom-call | flops 1509949440 | bytes 10133504 | tf_op jit(solution)/shard_map/pallas_call | solution.py:82
  95.2 2.4 %collective-permute-start.25 = (bf16[32,2176]{1,0:T(8,128)(2,1)S(1)}, bf16[32,2176]{1,0:T(8,128)(2,1)S(1)}, u32[]{:S(2)}, u32[]{:S(2)}) collective-permute-start(bf16[32,2176]{1,0:T(8,128)(2,1)S(1)} %slice.7), channel_id=1, source_target_pairs={{0,2},{1,3},{2,4},{3,5},{4,6},{5,7},{6,0},{7,1},{8,10},{9,11},{10,... | collective-permute-start | bytes 417800 | tf_op jit(solution)/shard_map/ppermute | solution.py:332
  97.6 4.2 %collective-permute-done.25.refs_5_ = bf16[32,2176]{1,0:T(8,128)(2,1)S(1)} collective-permute-done((bf16[32,2176]{1,0:T(8,128)(2,1)S(1)}, bf16[32,2176]{1,0:T(8,128)(2,1)S(1)}, u32[]{:S(2)}, u32[]{:S(2)}) %collective-permute-start.25) | collective-permute-done | bytes 139296 | tf_op jit(solution)/shard_map/ppermute | solution.py:332
  101.9 2.3 %shard_map.117 = (f32[48,2048]{1,0:T(8,128)S(1)}, bf16[48,2048]{1,0:T(8,128)(2,1)S(1)}) custom-call(s32[4]{0:T(128)S(1)} %pad_add_fusion.refs_0_, bf16[2048,768]{1,0:T(8,128)(2,1)S(1)} %bitcast.12, bf16[2048,768]{1,0:T(8,128)(2,1)S(1)} %bitcast.15, bf16[768,2048]{1,0:T(8,128)(2,1)S(1)} %bitcast.18, bf16[64,2176]{1,0:T(8,128)(2,1)S(1)} %collective-permute-done.24.refs_4_, ...), custom_call_target="tpu_custom_call" | custom-call | flops 905969664 | bytes 9854976 | tf_op jit(solution)/shard_map/pallas_call | solution.py:82
  104.1 1.9 %collective-permute-start.26 = (bf16[48,2048]{1,0:T(8,128)(2,1)S(1)}, bf16[48,2048]{1,0:T(8,128)(2,1)S(1)}, u32[]{:S(2)}, u32[]{:S(2)}) collective-permute-start(bf16[48,2048]{1,0:T(8,128)(2,1)S(1)} %get-tuple-element.55), channel_id=1, source_target_pairs={{0,8},{1,9},{2,10},{3,11},{4,12},{5,13},{6,14},{7,15},{8,0},{9,1},... | collective-permute-start | bytes 589832 | tf_op jit(solution)/shard_map/ppermute | solution.py:53
  107.5 3.0 %collective-permute-done.27.refs_3_ = bf16[32,2048]{1,0:T(8,128)(2,1)S(1)} collective-permute-done((bf16[32,2048]{1,0:T(8,128)(2,1)S(1)}, bf16[32,2048]{1,0:T(8,128)(2,1)S(1)}, u32[]{:S(2)}, u32[]{:S(2)}) %collective-permute-start.27) | collective-permute-done | bytes 131104 | tf_op jit(solution)/shard_map/ppermute | solution.py:332
  110.5 2.4 %collective-permute-done.28.refs_4_ = bf16[32,2048]{1,0:T(8,128)(2,1)S(1)} collective-permute-done((bf16[32,2048]{1,0:T(8,128)(2,1)S(1)}, bf16[32,2048]{1,0:T(8,128)(2,1)S(1)}, u32[]{:S(2)}, u32[]{:S(2)}) %collective-permute-start.28) | collective-permute-done | bytes 131104 | tf_op jit(solution)/shard_map/ppermute | solution.py:332
  113.5 2.2 %collective-permute-start.30 = (bf16[32,2048]{1,0:T(8,128)(2,1)S(1)}, bf16[32,2048]{1,0:T(8,128)(2,1)S(1)}, u32[]{:S(2)}, u32[]{:S(2)}) collective-permute-start(bf16[32,2048]{1,0:T(8,128)(2,1)S(1)} %get-tuple-element.62), channel_id=1, source_target_pairs={{0,5},{1,6},{2,7},{3,0},{4,1},{5,2},{6,3},{7,4},{8,13},{9,14},{10,... | collective-permute-start | bytes 393224 | tf_op jit(solution)/shard_map/ppermute | solution.py:332
  115.7 4.8 %collective-permute-start.29 = (bf16[16,2048]{1,0:T(8,128)(2,1)S(1)}, bf16[16,2048]{1,0:T(8,128)(2,1)S(1)}, u32[]{:S(2)}, u32[]{:S(2)}) collective-permute-start(bf16[16,2048]{1,0:T(8,128)(2,1)S(1)} %get-tuple-element.59), channel_id=1, source_target_pairs={{0,4},{1,5},{2,6},{3,7},{4,0},{5,1},{6,2},{7,3},{8,12},{9,13},{10,... | collective-permute-start | bytes 196616 | tf_op jit(solution)/shard_map/ppermute | solution.py:53
  120.5 2.3 %collective-permute-done.29.refs_2_ = bf16[16,2048]{1,0:T(8,128)(2,1)S(1)} collective-permute-done((bf16[16,2048]{1,0:T(8,128)(2,1)S(1)}, bf16[16,2048]{1,0:T(8,128)(2,1)S(1)}, u32[]{:S(2)}, u32[]{:S(2)}) %collective-permute-start.29) | collective-permute-done | bytes 65568 | tf_op jit(solution)/shard_map/ppermute | solution.py:53
  123.4 9.4 %collective-permute-start.31 = (bf16[16,2048]{1,0:T(8,128)(2,1)S(1)}, bf16[16,2048]{1,0:T(8,128)(2,1)S(1)}, u32[]{:S(2)}, u32[]{:S(2)}) collective-permute-start(bf16[16,2048]{1,0:T(8,128)(2,1)S(1)} %get-tuple-element.64), channel_id=1, source_target_pairs={{0,16},{16,0},{32,48},{48,32},{64,80},{80,64},{96,112},{112,96},{1... | collective-permute-start | bytes 196616 | tf_op jit(solution)/shard_map/ppermute | solution.py:49
  (75 shorter events, 30.4 us)
Async XLA Ops:
  0.9 15.3 %collective-permute-start.5 = (bf16[256,256]{1,0:T(8,128)(2,1)S(1)}, bf16[256,256]{1,0:T(8,128)(2,1)S(1)}, u32[]{:S(2)}, u32[]{:S(2)}) collective-permute-start(bf16[256,256]{1,0:T(8,128)(2,1)S(1)} %pad_maximum_fusion.refs_3_), channel_id=1, source_target_pairs={{0,128},{16,144},{32,160},{48,176},{64,192},{80,208},{96,224},{112... | collective-permute-start | bytes 393224 | tf_op jit(solution)/shard_map/ppermute | solution.py:49
  2.5 22.4 %collective-permute-start.2 = (bf16[256,256]{1,0:T(8,128)(2,1)S(1)}, bf16[256,256]{1,0:T(8,128)(2,1)S(1)}, u32[]{:S(2)}, u32[]{:S(2)}) collective-permute-start(bf16[256,256]{1,0:T(8,128)(2,1)S(1)} %pad_maximum_fusion.refs_3_), channel_id=1, source_target_pairs={{0,32},{16,48},{32,64},{48,80},{64,96},{80,112},{128,160},{144,176... | collective-permute-start | bytes 393224 | tf_op jit(solution)/shard_map/ppermute | solution.py:49
  5.6 24.5 %collective-permute-start.3 = (bf16[256,256]{1,0:T(8,128)(2,1)S(1)}, bf16[256,256]{1,0:T(8,128)(2,1)}, u32[]{:S(2)}, u32[]{:S(2)}) collective-permute-start(bf16[256,256]{1,0:T(8,128)(2,1)S(1)} %pad_maximum_fusion.refs_3_), channel_id=1, source_target_pairs={{0,96},{16,112},{128,224},{144,240},{1,97},{17,113},{129,225},{145... | collective-permute-start | bytes 393224 | tf_op jit(solution)/shard_map/ppermute | solution.py:49
  10.3 7.6 %collective-permute-start = (bf16[128,128]{1,0:T(8,128)(2,1)}, bf16[128,128]{1,0:T(8,128)(2,1)}, u32[]{:S(2)}, u32[]{:S(2)}) collective-permute-start(bf16[128,128]{1,0:T(8,128)(2,1)} %bitcast.6), channel_id=1, source_target_pairs={{0,4},{1,5},{2,6},{3,7},{4,0},{5,1},{6,2},{7,3},{8,12},{9,13},{10,... | collective-permute-start | bytes 98312 | tf_op jit(solution)/shard_map/ppermute | solution.py:53
  17.3 27.1 %collective-permute-start.10 = (bf16[128,1024]{1,0:T(8,128)(2,1)S(1)}, bf16[128,1024]{1,0:T(8,128)(2,1)S(1)}, u32[]{:S(2)}, u32[]{:S(2)}) collective-permute-start(bf16[128,1024]{1,0:T(8,128)(2,1)S(1)} %constant_dynamic-slice_fusion), channel_id=1, source_target_pairs={{0,4},{1,5},{2,6},{3,7},{4,0},{5,1},{6,2},{7,3},{8,12},{9,13},{10,... | collective-permute-start | bytes 786440 | tf_op jit(solution)/shard_map/ppermute | solution.py:53
  18.7 4.3 %collective-permute-start.1 = (bf16[256,128]{1,0:T(8,128)(2,1)S(1)}, bf16[256,128]{1,0:T(8,128)(2,1)S(1)}, u32[]{:S(2)}, u32[]{:S(2)}) collective-permute-start(bf16[256,128]{1,0:T(8,128)(2,1)S(1)} %pad_maximum_fusion.1.refs_1_), channel_id=1, source_target_pairs={{0,16},{16,0},{32,48},{48,32},{64,80},{80,64},{96,112},{112,96},{1... | collective-permute-start | bytes 196616 | tf_op jit(solution)/shard_map/ppermute | solution.py:49
  20.5 11.7 %collective-permute-start.4 = (bf16[256,256]{1,0:T(8,128)(2,1)S(1)}, bf16[256,256]{1,0:T(8,128)(2,1)S(1)}, u32[]{:S(2)}, u32[]{:S(2)}) collective-permute-start(bf16[256,256]{1,0:T(8,128)(2,1)S(1)} %pad_maximum_fusion.refs_3_), channel_id=1, source_target_pairs={{0,64},{16,80},{32,96},{48,112},{128,192},{144,208},{160,224},{176... | collective-permute-start | bytes 393224 | tf_op jit(solution)/shard_map/ppermute | solution.py:49
  23.0 9.2 %collective-permute-start.6 = (bf16[256,256]{1,0:T(8,128)(2,1)S(1)}, bf16[256,256]{1,0:T(8,128)(2,1)S(1)}, u32[]{:S(2)}, u32[]{:S(2)}) collective-permute-start(bf16[256,256]{1,0:T(8,128)(2,1)S(1)} %collective-permute-done.5.refs_7_), channel_id=1, source_target_pairs={{128,160},{144,176},{160,192},{176,208},{192,224},{208,240},{224,1... | collective-permute-start | bytes 393224 | tf_op jit(solution)/shard_map/ppermute | solution.py:49
  25.6 6.8 %collective-permute-start.7 = (bf16[256,256]{1,0:T(8,128)(2,1)S(1)}, bf16[256,256]{1,0:T(8,128)(2,1)S(1)}, u32[]{:S(2)}, u32[]{:S(2)}) collective-permute-start(bf16[256,256]{1,0:T(8,128)(2,1)S(1)} %collective-permute-done.5.refs_7_), channel_id=1, source_target_pairs={{128,224},{144,240},{160,128},{176,144},{192,160},{208,176},{224,1... | collective-permute-start | bytes 393224 | tf_op jit(solution)/shard_map/ppermute | solution.py:49
  30.2 7.6 %collective-permute-start.8 = (bf16[256,256]{1,0:T(8,128)(2,1)S(1)}, bf16[256,256]{1,0:T(8,128)(2,1)S(1)}, u32[]{:S(2)}, u32[]{:S(2)}) collective-permute-start(bf16[256,256]{1,0:T(8,128)(2,1)S(1)} %collective-permute-done.5.refs_7_), channel_id=1, source_target_pairs={{128,192},{144,208},{160,224},{176,240},{192,128},{208,144},{224,1... | collective-permute-start | bytes 393224 | tf_op jit(solution)/shard_map/ppermute | solution.py:49
  42.6 3.0 %collective-permute-start.9 = (f32[256,256]{1,0:T(8,128)S(1)}, f32[256,256]{1,0:T(8,128)S(1)}, u32[]{:S(2)}, u32[]{:S(2)}) collective-permute-start(f32[256,256]{1,0:T(8,128)S(1)} %get-tuple-element.37), channel_id=1, source_target_pairs={{0,16},{16,0},{32,48},{48,32},{64,80},{80,64},{96,112},{112,96},{1... | collective-permute-start | bytes 786440 | tf_op jit(solution)/shard_map/ppermute | solution.py:49
  44.4 1.5 %collective-permute-start.11 = (bf16[128,1024]{1,0:T(8,128)(2,1)S(1)}, bf16[128,1024]{1,0:T(8,128)(2,1)S(1)}, u32[]{:S(2)}, u32[]{:S(2)}) collective-permute-start(bf16[128,1024]{1,0:T(8,128)(2,1)S(1)} %collective-permute-done.10.refs_3_), channel_id=1, source_target_pairs={{0,16},{16,0},{32,48},{48,32},{64,80},{80,64},{96,112},{112,96},{1... | collective-permute-start | bytes 786440 | tf_op jit(solution)/shard_map/ppermute | solution.py:49
  49.0 11.1 %collective-permute-start.12 = (bf16[32,2048]{1,0:T(8,128)(2,1)}, bf16[32,2048]{1,0:T(8,128)(2,1)S(1)}, u32[]{:S(2)}, u32[]{:S(2)}) collective-permute-start(bf16[32,2048]{1,0:T(8,128)(2,1)} %get-tuple-element.39), channel_id=1, source_target_pairs={{0,7},{1,0},{2,1},{3,2},{4,3},{5,4},{6,5},{7,6},{8,15},{9,8},{10,9... | collective-permute-start | bytes 393224 | tf_op jit(solution)/shard_map/ppermute | solution.py:53
  49.7 14.0 %collective-permute-start.13 = (bf16[32,2048]{1,0:T(8,128)(2,1)}, bf16[32,2048]{1,0:T(8,128)(2,1)}, u32[]{:S(2)}, u32[]{:S(2)}) collective-permute-start(bf16[32,2048]{1,0:T(8,128)(2,1)} %get-tuple-element.43), channel_id=1, source_target_pairs={{0,1},{1,2},{2,3},{3,4},{4,5},{5,6},{6,7},{7,0},{8,9},{9,10},{10,1... | collective-permute-start | bytes 393224 | tf_op jit(solution)/shard_map/ppermute | solution.py:53
  50.4 13.2 %collective-permute-start.14 = (bf16[32,2048]{1,0:T(8,128)(2,1)}, bf16[32,2048]{1,0:T(8,128)(2,1)}, u32[]{:S(2)}, u32[]{:S(2)}) collective-permute-start(bf16[32,2048]{1,0:T(8,128)(2,1)} %get-tuple-element.44), channel_id=1, source_target_pairs={{0,2},{1,3},{2,4},{3,5},{4,6},{5,7},{6,0},{7,1},{8,10},{9,11},{10,... | collective-permute-start | bytes 393224 | tf_op jit(solution)/shard_map/ppermute | solution.py:332
  61.6 8.6 %collective-permute-start.15 = (bf16[16,2176]{1,0:T(8,128)(2,1)S(1)}, bf16[16,2176]{1,0:T(8,128)(2,1)S(1)}, u32[]{:S(2)}, u32[]{:S(2)}) collective-permute-start(bf16[16,2176]{1,0:T(8,128)(2,1)S(1)} %shard_map.111.refs_1_), channel_id=1, source_target_pairs={{0,8},{1,9},{2,10},{3,11},{4,12},{5,13},{6,14},{7,15},{8,0},{9,1},... | collective-permute-start | bytes 208904 | tf_op jit(solution)/shard_map/ppermute | solution.py:53
  64.7 12.2 %collective-permute-start.18 = (bf16[32,2048]{1,0:T(8,128)(2,1)S(1)}, bf16[32,2048]{1,0:T(8,128)(2,1)S(1)}, u32[]{:S(2)}, u32[]{:S(2)}) collective-permute-start(bf16[32,2048]{1,0:T(8,128)(2,1)S(1)} %get-tuple-element.46), channel_id=1, source_target_pairs={{0,8},{1,9},{2,10},{3,11},{4,12},{5,13},{6,14},{7,15},{8,0},{9,1},... | collective-permute-start | bytes 393224 | tf_op jit(solution)/shard_map/ppermute | solution.py:53
  65.8 11.2 %collective-permute-start.19 = (bf16[32,2048]{1,0:T(8,128)(2,1)S(1)}, bf16[32,2048]{1,0:T(8,128)(2,1)S(1)}, u32[]{:S(2)}, u32[]{:S(2)}) collective-permute-start(bf16[32,2048]{1,0:T(8,128)(2,1)S(1)} %get-tuple-element.46), channel_id=1, source_target_pairs={{0,16},{16,0},{32,48},{48,32},{64,80},{80,64},{96,112},{112,96},{1... | collective-permute-start | bytes 393224 | tf_op jit(solution)/shard_map/ppermute | solution.py:49
  68.9 8.1 %collective-permute-start.20 = (bf16[32,2048]{1,0:T(8,128)(2,1)S(1)}, bf16[32,2048]{1,0:T(8,128)(2,1)S(1)}, u32[]{:S(2)}, u32[]{:S(2)}) collective-permute-start(bf16[32,2048]{1,0:T(8,128)(2,1)S(1)} %get-tuple-element.46), channel_id=1, source_target_pairs={{0,24},{1,25},{2,26},{3,27},{4,28},{5,29},{6,30},{7,31},{8,16},{9,... | collective-permute-start | bytes 393224 | tf_op jit(solution)/shard_map/ppermute | solution.py:332
  69.7 3.1 %collective-permute-start.16 = (bf16[16,2176]{1,0:T(8,128)(2,1)S(1)}, bf16[16,2176]{1,0:T(8,128)(2,1)S(1)}, u32[]{:S(2)}, u32[]{:S(2)}) collective-permute-start(bf16[16,2176]{1,0:T(8,128)(2,1)S(1)} %shard_map.111.refs_1_), channel_id=1, source_target_pairs={{0,16},{16,0},{32,48},{48,32},{64,80},{80,64},{96,112},{112,96},{1... | collective-permute-start | bytes 208904 | tf_op jit(solution)/shard_map/ppermute | solution.py:49
  70.2 6.8 %collective-permute-start.17 = (bf16[16,2176]{1,0:T(8,128)(2,1)S(1)}, bf16[16,2176]{1,0:T(8,128)(2,1)S(1)}, u32[]{:S(2)}, u32[]{:S(2)}) collective-permute-start(bf16[16,2176]{1,0:T(8,128)(2,1)S(1)} %shard_map.111.refs_1_), channel_id=1, source_target_pairs={{0,24},{1,25},{2,26},{3,27},{4,28},{5,29},{6,30},{7,31},{8,16},{9,... | collective-permute-start | bytes 208904 | tf_op jit(solution)/shard_map/ppermute | solution.py:332
  77.8 8.8 %collective-permute-start.22 = (bf16[64,2176]{1,0:T(8,128)(2,1)S(1)}, bf16[64,2176]{1,0:T(8,128)(2,1)S(1)}, u32[]{:S(2)}, u32[]{:S(2)}) collective-permute-start(bf16[64,2176]{1,0:T(8,128)(2,1)S(1)} %get-tuple-element.48.refs_1_), channel_id=1, source_target_pairs={{0,2},{1,3},{2,4},{3,5},{4,6},{5,7},{6,0},{7,1},{8,10},{9,11},{10,... | collective-permute-start | bytes 835592 | tf_op jit(solution)/shard_map/ppermute | solution.py:332
  80.1 11.5 %collective-permute-start.21 = (bf16[64,2176]{1,0:T(8,128)(2,1)S(1)}, bf16[64,2176]{1,0:T(8,128)(2,1)S(1)}, u32[]{:S(2)}, u32[]{:S(2)}) collective-permute-start(bf16[64,2176]{1,0:T(8,128)(2,1)S(1)} %get-tuple-element.48.refs_1_), channel_id=1, source_target_pairs={{0,1},{1,2},{2,3},{3,4},{4,5},{5,6},{6,7},{7,0},{8,9},{9,10},{10,1... | collective-permute-start | bytes 835592 | tf_op jit(solution)/shard_map/ppermute | solution.py:332
  86.6 15.3 %collective-permute-start.24 = (bf16[64,2176]{1,0:T(8,128)(2,1)S(1)}, bf16[64,2176]{1,0:T(8,128)(2,1)S(1)}, u32[]{:S(2)}, u32[]{:S(2)}) collective-permute-start(bf16[64,2176]{1,0:T(8,128)(2,1)S(1)} %collective-permute-done.22.refs_5_), channel_id=1, source_target_pairs={{0,1},{1,2},{2,3},{3,4},{4,5},{5,6},{6,7},{7,0},{8,9},{9,10},{10,1... | collective-permute-start | bytes 835592 | tf_op jit(solution)/shard_map/ppermute | solution.py:332
  93.9 12.1 %collective-permute-start.23 = (bf16[80,2048]{1,0:T(8,128)(2,1)S(1)}, bf16[80,2048]{1,0:T(8,128)(2,1)S(1)}, u32[]{:S(2)}, u32[]{:S(2)}) collective-permute-start(bf16[80,2048]{1,0:T(8,128)(2,1)S(1)} %get-tuple-element.52), channel_id=1, source_target_pairs={{0,8},{1,9},{2,10},{3,11},{4,12},{5,13},{6,14},{7,15},{8,0},{9,1},... | collective-permute-start | bytes 983048 | tf_op jit(solution)/shard_map/ppermute | solution.py:53
  95.2 6.7 %collective-permute-start.25 = (bf16[32,2176]{1,0:T(8,128)(2,1)S(1)}, bf16[32,2176]{1,0:T(8,128)(2,1)S(1)}, u32[]{:S(2)}, u32[]{:S(2)}) collective-permute-start(bf16[32,2176]{1,0:T(8,128)(2,1)S(1)} %slice.7), channel_id=1, source_target_pairs={{0,2},{1,3},{2,4},{3,5},{4,6},{5,7},{6,0},{7,1},{8,10},{9,11},{10,... | collective-permute-start | bytes 417800 | tf_op jit(solution)/shard_map/ppermute | solution.py:332
  104.1 8.8 %collective-permute-start.26 = (bf16[48,2048]{1,0:T(8,128)(2,1)S(1)}, bf16[48,2048]{1,0:T(8,128)(2,1)S(1)}, u32[]{:S(2)}, u32[]{:S(2)}) collective-permute-start(bf16[48,2048]{1,0:T(8,128)(2,1)S(1)} %get-tuple-element.55), channel_id=1, source_target_pairs={{0,8},{1,9},{2,10},{3,11},{4,12},{5,13},{6,14},{7,15},{8,0},{9,1},... | collective-permute-start | bytes 589832 | tf_op jit(solution)/shard_map/ppermute | solution.py:53
  106.6 3.9 %collective-permute-start.27 = (bf16[32,2048]{1,0:T(8,128)(2,1)S(1)}, bf16[32,2048]{1,0:T(8,128)(2,1)S(1)}, u32[]{:S(2)}, u32[]{:S(2)}) collective-permute-start(bf16[32,2048]{1,0:T(8,128)(2,1)S(1)} %get-tuple-element.56), channel_id=1, source_target_pairs={{0,7},{1,0},{2,1},{3,2},{4,3},{5,4},{6,5},{7,6},{8,15},{9,8},{10,9... | collective-permute-start | bytes 393224 | tf_op jit(solution)/shard_map/ppermute | solution.py:332
  106.9 6.0 %collective-permute-start.28 = (bf16[32,2048]{1,0:T(8,128)(2,1)S(1)}, bf16[32,2048]{1,0:T(8,128)(2,1)S(1)}, u32[]{:S(2)}, u32[]{:S(2)}) collective-permute-start(bf16[32,2048]{1,0:T(8,128)(2,1)S(1)} %get-tuple-element.57), channel_id=1, source_target_pairs={{0,6},{1,7},{2,0},{3,1},{4,2},{5,3},{6,4},{7,5},{8,14},{9,15},{10,... | collective-permute-start | bytes 393224 | tf_op jit(solution)/shard_map/ppermute | solution.py:332
  113.5 9.3 %collective-permute-start.30 = (bf16[32,2048]{1,0:T(8,128)(2,1)S(1)}, bf16[32,2048]{1,0:T(8,128)(2,1)S(1)}, u32[]{:S(2)}, u32[]{:S(2)}) collective-permute-start(bf16[32,2048]{1,0:T(8,128)(2,1)S(1)} %get-tuple-element.62), channel_id=1, source_target_pairs={{0,5},{1,6},{2,7},{3,0},{4,1},{5,2},{6,3},{7,4},{8,13},{9,14},{10,... | collective-permute-start | bytes 393224 | tf_op jit(solution)/shard_map/ppermute | solution.py:332
  115.7 7.1 %collective-permute-start.29 = (bf16[16,2048]{1,0:T(8,128)(2,1)S(1)}, bf16[16,2048]{1,0:T(8,128)(2,1)S(1)}, u32[]{:S(2)}, u32[]{:S(2)}) collective-permute-start(bf16[16,2048]{1,0:T(8,128)(2,1)S(1)} %get-tuple-element.59), channel_id=1, source_target_pairs={{0,4},{1,5},{2,6},{3,7},{4,0},{5,1},{6,2},{7,3},{8,12},{9,13},{10,... | collective-permute-start | bytes 196616 | tf_op jit(solution)/shard_map/ppermute | solution.py:53
  123.4 10.3 %collective-permute-start.31 = (bf16[16,2048]{1,0:T(8,128)(2,1)S(1)}, bf16[16,2048]{1,0:T(8,128)(2,1)S(1)}, u32[]{:S(2)}, u32[]{:S(2)}) collective-permute-start(bf16[16,2048]{1,0:T(8,128)(2,1)S(1)} %get-tuple-element.64), channel_id=1, source_target_pairs={{0,16},{16,0},{32,48},{48,32},{64,80},{80,64},{96,112},{112,96},{1... | collective-permute-start | bytes 196616 | tf_op jit(solution)/shard_map/ppermute | solution.py:49
  (10 other events, 164.8 us)

commit v5 on v4

--- a/solution.py
+++ b/solution.py
@@ -25,20 +25,11 @@
 Y_SWAP = [(i, i ^ 8) for i in range(16)]
 
 
-OTHER_ROW = [(i, i + 8) for i in range(8)]
-
-
-def block_route(step):
-    route = []
-    for here in range(16):
-        there = here // 8 * 8 + (here // 2 + step) % 4 * 2 + here % 2
-        if here < there:
-            route.append((here, there))
-    return route
-
-
-def relay_route(step):
-    return [(8 + i, 8 + (i // 2 + step) % 4 * 2 + i % 2) for i in range(8)]
+ROW_SWAP = [(i, i ^ 8) for i in range(16)]
+
+
+def x_shift(step):
+    return [(i, i // 8 * 8 + (i // 2 + step) % 4 * 2 + i % 2) for i in range(16)]
 
 
 def z_shift(step):
@@ -54,7 +45,7 @@
 
 
 def kernel_call(
-    body, scalars, resident, fetched, out_shapes, flops, transcendentals=0, limit=16, idle=(), scratch=()
+    body, scalars, resident, fetched, out_shapes, flops, transcendentals=0, limit=10, idle=(), scratch=()
 ):
     n_own = len(resident)
     resident, fetched = [*resident, *fetched], []
@@ -224,7 +215,7 @@
         hidden = (extended[:, :D] + projected).astype(BF16)
         wide = hidden.astype(F32)
         inverse = lax.rsqrt(jnp.mean(wide * wide, axis=-1, keepdims=True) + 1e-06)
-        normed = (wide * inverse * gain_ref[...].astype(F32)).astype(BF16)
+        normed = (wide * inverse * gain_ref[:1, :]).astype(BF16)
         if n < 2:
             hidden_ref[at, :] = hidden
         normed_ref[to, :D] = normed
@@ -309,7 +300,7 @@
 
 
 def extend(place, resident, fetched, outs, wait):
-    residual_ref, ids_ref, gates_ref = resident
+    residual_ref, ids_ref, gates_ref, gain_ref = resident
     lane = lax.broadcasted_iota(jnp.int32, (TOK_DEV, 128), 1)
     weights = jnp.zeros((TOK_DEV, 128), F32)
     for k in range(TOP):
@@ -317,6 +308,7 @@
         weights = weights + jnp.where(lane == ids_ref[:, k : k + 1], gate, 0.0)
     outs[0][:, :D] = residual_ref[...]
     outs[0][:, D:] = weights.astype(BF16)
+    outs[1][...] = jnp.broadcast_to(gain_ref[...].astype(F32), outs[1].shape)
 
 
 def by_core(step):
@@ -371,9 +363,9 @@
         axis=1,
     )
 
-    other = on_ctx(block, OTHER_ROW)
-    blocks = [block] + [on_ctx(block, block_route(-d)) for _, d in PLACES[1:4]]
-    blocks += [other] + [on_ctx(other, relay_route(-d)) for _, d in PLACES[5:]]
+    other = on_ctx(block, ROW_SWAP)
+    blocks = [block] + [on_ctx(block, x_shift(-d)) for _, d in PLACES[1:4]]
+    blocks += [other] + [on_ctx(other, x_shift(-d)) for _, d in PLACES[5:]]
 
     by_holder = query.reshape(2, 8, TOK_DEV, HEAD_DIM)
     by_holder = jnp.concatenate([by_holder, by_holder], axis=1)
@@ -389,6 +381,18 @@
     w_half = lax.dynamic_slice_in_dim(w_out, core * (D // 2), D // 2, 1)
     w_near = on_exp(w_half, z_shift(4))
     w_far = on_ctx(w_near, CORE_SWAP)
+
+    rows, *blocks[1:7] = after(residual, *blocks[1:7])
+    extended, gain = kernel_call(
+        extend,
+        place,
+        [rows, expert_ids, gate_values, norm_gain.reshape(1, D)],
+        [],
+        [struct((TOK_DEV, D + 128), BF16), struct((8, D), F32)],
+        TOK_DEV * D,
+    )
+    extended_others = to_three(extended, extended, extended)
+    mine, *extended_others = after(mine, *extended_others)
 
     own, swap = kernel_call(
         attend_all,
@@ -414,16 +418,6 @@
         on_exp(sends[1], z_shift(1)),
         on_both(sends[2], by_core(2)),
     ]
-    rows, recvs[0] = after(residual, recvs[0])
-    (extended,) = kernel_call(
-        extend,
-        place,
-        [rows, expert_ids, gate_values],
-        [],
-        [struct((TOK_DEV, D + 128), BF16)],
-        TOK_DEV * D,
-    )
-    extended_others = to_three(extended, extended, extended)
     sums, send = kernel_call(
         add_up,
         place,
@@ -435,7 +429,7 @@
     hidden, round_0 = kernel_call(
         normalise,
         place,
-        [extended, sums, norm_gain.reshape(1, D)],
+        [extended, sums, gain],
         [*extended_others, *to_three(send, send, send)],
         [struct((32, D), BF16), struct((64, D + 128), BF16)],
         16 * 32 * D,
@@ -456,7 +450,7 @@
     sum_1, sum_2, own_sum = run_join(place, keep, got, [half, half, struct((16, D), F32)])
     back_1 = on_both(sum_1, by_core(-1))
     back_2 = on_both(sum_2, by_core(-2))
-    got_far, back_1, back_2 = after(got_far, back_1, back_2)
+    got_far, back_1 = after(got_far, back_1)
     sum_3, sum_4 = run_join(place, keep_far, got_far, [half, struct((16, D), BF16)])
     back_3 = on_both(sum_3, by_core(-3))
     back_4 = on_exp(sum_4, z_shift(4))

time: 136 us -> 121 us (0.89)
  the two profiles are of different devices: /device:TPU:41 before, /device:TPU:32 now
where the time goes in v5:
time: 121 us; the launch traced here: 120 us
  starting transfers between devices  48.9 us (40%)
  waiting for transfers between devices  40.2 us (33%)
  Pallas kernels  14.6 us (12%)
  local copies, waits for them, and re-layouts  13.6 us (11%)
  other arithmetic  2.3 us (2%)
    ppermute x10, waiting for transfers between devices, on_both(): return lax.ppermute(block, ('ctx', 'exp'), route)  21.9 us
    ppermute x9, starting transfers between devices, on_exp(): return lax.ppermute(block, 'exp', route)  20 us
    ppermute x10, starting transfers between devices, on_both(): return lax.ppermute(block, ('ctx', 'exp'), route)  17.3 us
    ppermute x9, waiting for transfers between devices, on_exp(): return lax.ppermute(block, 'exp', route)  15.6 us
    pallas_call x12, Pallas kernels, kernel_call(): pl.pallas_call(whole, out_shape=out_shapes, in_specs=[pl.BlockSpec(memory...  14.6 us
    ppermute x13, starting transfers between devices, on_ctx(): return lax.ppermute(block, 'ctx', route)  11.6 us
    unnamed x22, local copies, waits for them, and re-layouts  10.3 us
    ppermute x13, waiting for transfers between devices, on_ctx(): return lax.ppermute(block, 'ctx', route)  2.7 us
  transfers between devices with their start and end apart: 32, of which 13 were waited for; matrix products, arithmetic and copies ran while one was open for 5% of the time, Pallas kernels for 8%

profile of v5, /device:TPU:32, one launch (start us, length us, event | category | flops | bytes accessed | tf_op | source)
XLA Modules:
  0.0 119.7 jit_solution(713062414070702580)
XLA Ops:
  0.9 1.7 %collective-permute-start.3 = (bf16[256,256]{1,0:T(8,128)(2,1)S(1)}, bf16[256,256]{1,0:T(8,128)(2,1)}, u32[]{:S(2)}, u32[]{:S(2)}) collective-permute-start(bf16[256,256]{1,0:T(8,128)(2,1)S(1)} %pad_maximum_fusion.refs_3_), channel_id=1, source_target_pairs={{0,128},{16,144},{32,160},{48,176},{64,192},{80,208},{96,224},{112... | collective-permute-start | bytes 393224 | tf_op jit(solution)/shard_map/ppermute | solution.py:40
  2.6 1.5 %collective-permute-start = (bf16[256,256]{1,0:T(8,128)(2,1)S(1)}, bf16[256,256]{1,0:T(8,128)(2,1)S(1)}, u32[]{:S(2)}, u32[]{:S(2)}) collective-permute-start(bf16[256,256]{1,0:T(8,128)(2,1)S(1)} %pad_maximum_fusion.refs_3_), channel_id=1, source_target_pairs={{0,32},{16,48},{32,64},{48,80},{64,96},{80,112},{96,0},{112,16},{1... | collective-permute-start | bytes 393224 | tf_op jit(solution)/shard_map/ppermute | solution.py:40
  4.1 1.7 %collective-permute-start.1 = (bf16[256,256]{1,0:T(8,128)(2,1)S(1)}, bf16[256,256]{1,0:T(8,128)(2,1)S(1)}, u32[]{:S(2)}, u32[]{:S(2)}) collective-permute-start(bf16[256,256]{1,0:T(8,128)(2,1)S(1)} %pad_maximum_fusion.refs_3_), channel_id=1, source_target_pairs={{0,96},{16,112},{32,0},{48,16},{64,32},{80,48},{96,64},{112,80},{1... | collective-permute-start | bytes 393224 | tf_op jit(solution)/shard_map/ppermute | solution.py:40
  5.8 1.8 %collective-permute-start.2 = (bf16[256,256]{1,0:T(8,128)(2,1)S(1)}, bf16[256,256]{1,0:T(8,128)(2,1)}, u32[]{:S(2)}, u32[]{:S(2)}) collective-permute-start(bf16[256,256]{1,0:T(8,128)(2,1)S(1)} %pad_maximum_fusion.refs_3_), channel_id=1, source_target_pairs={{0,64},{16,80},{32,96},{48,112},{64,0},{80,16},{96,32},{112,48},{1... | collective-permute-start | bytes 393224 | tf_op jit(solution)/shard_map/ppermute | solution.py:40
  9.7 2.6 %collective-permute-start.5 = (bf16[256,256]{1,0:T(8,128)(2,1)}, bf16[256,256]{1,0:T(8,128)(2,1)}, u32[]{:S(2)}, u32[]{:S(2)}) collective-permute-start(bf16[256,256]{1,0:T(8,128)(2,1)} %collective-permute-done.3.refs_7_), channel_id=1, source_target_pairs={{0,96},{16,112},{32,0},{48,16},{64,32},{80,48},{96,64},{112,80},{1... | collective-permute-start | bytes 393224 | tf_op jit(solution)/shard_map/ppermute | solution.py:40
  12.3 1.7 %constant_dynamic-slice_fusion = bf16[128,1024]{1,0:T(8,128)(2,1)} fusion(bf16[128,2048]{1,0:T(8,128)(2,1)} %refs_5_.1, s32[]{:T(128)S(6)} %select_n.45), kind=kLoop, calls=%fused_computation.8 | loop fusion | bytes 524292 | tf_op jit(solution)/shard_map/dynamic_slice | solution.py:381
  14.6 6.3 %collective-permute-start.6 = (bf16[128,128]{1,0:T(8,128)(2,1)}, bf16[128,128]{1,0:T(8,128)(2,1)}, u32[]{:S(2)}, u32[]{:S(2)}) collective-permute-start(bf16[128,128]{1,0:T(8,128)(2,1)} %bitcast.21), channel_id=1, source_target_pairs={{0,4},{1,5},{2,6},{3,7},{4,0},{5,1},{6,2},{7,3},{8,12},{9,13},{10,... | collective-permute-start | bytes 98312 | tf_op jit(solution)/shard_map/ppermute | solution.py:44
  26.0 3.0 %collective-permute-start.7 = (bf16[16,2176]{1,0:T(8,128)(2,1)S(1)}, bf16[16,2176]{1,0:T(8,128)(2,1)S(1)}, u32[]{:S(2)}, u32[]{:S(2)}) collective-permute-start(bf16[16,2176]{1,0:T(8,128)(2,1)S(1)} %get-tuple-element.47.refs_1_), channel_id=1, source_target_pairs={{0,8},{1,9},{2,10},{3,11},{4,12},{5,13},{6,14},{7,15},{8,0},{9,1},... | collective-permute-start | bytes 208904 | tf_op jit(solution)/shard_map/ppermute | solution.py:44
  31.9 2.4 %collective-permute-done.9.refs_6_ = bf16[16,2176]{1,0:T(8,128)(2,1)S(1)} collective-permute-done((bf16[16,2176]{1,0:T(8,128)(2,1)S(1)}, bf16[16,2176]{1,0:T(8,128)(2,1)S(1)}, u32[]{:S(2)}, u32[]{:S(2)}) %collective-permute-start.9) | collective-permute-done | bytes 69664 | tf_op jit(solution)/shard_map/ppermute | solution.py:324
  36.1 3.2 %shard_map.110 = (f32[256,256]{1,0:T(8,128)S(1)}, f32[256,256]{1,0:T(8,128)S(1)}) custom-call(s32[4]{0:T(128)S(1)} %pad_add_fusion.refs_0_, bf16[256,128]{1,0:T(8,128)(2,1)S(1)} %pad_maximum_fusion.1.refs_1_, bf16[256,128]{1,0:T(8,128)(2,1)S(1)} %collective-permute-done.10.refs_2_, bf16[256,256]{1,0:T(8,128)(2,1)S(1)} %pad_maximum_fusion.refs_3_, ...), custom_call_target="tpu_custom_call" | custom-call | flops 536870912 | bytes 1179648 | tf_op jit(solution)/shard_map/pallas_call | solution.py:73
  46.2 3.8 %collective-permute-start.17 = (bf16[32,2048]{1,0:T(8,128)(2,1)S(1)}, bf16[32,2048]{1,0:T(8,128)(2,1)S(1)}, u32[]{:S(2)}, u32[]{:S(2)}) collective-permute-start(bf16[32,2048]{1,0:T(8,128)(2,1)S(1)} %get-tuple-element.61), channel_id=1, source_target_pairs={{0,2},{1,3},{2,4},{3,5},{4,6},{5,7},{6,0},{7,1},{8,10},{9,11},{10,... | collective-permute-start | bytes 393224 | tf_op jit(solution)/shard_map/ppermute | solution.py:324
  50.1 3.2 %collective-permute-done.16.refs_3_ = bf16[32,2048]{1,0:T(8,128)(2,1)S(1)} collective-permute-done((bf16[32,2048]{1,0:T(8,128)(2,1)S(1)}, bf16[32,2048]{1,0:T(8,128)(2,1)S(1)}, u32[]{:S(2)}, u32[]{:S(2)}) %collective-permute-start.16) | collective-permute-done | bytes 131104 | tf_op jit(solution)/shard_map/ppermute | solution.py:44
  53.3 5.2 %collective-permute-done.17.refs_4_ = bf16[32,2048]{1,0:T(8,128)(2,1)S(1)} collective-permute-done((bf16[32,2048]{1,0:T(8,128)(2,1)S(1)}, bf16[32,2048]{1,0:T(8,128)(2,1)S(1)}, u32[]{:S(2)}, u32[]{:S(2)}) %collective-permute-start.17) | collective-permute-done | bytes 131104 | tf_op jit(solution)/shard_map/ppermute | solution.py:324
  59.1 2.2 %collective-permute-start.18 = (bf16[32,2048]{1,0:T(8,128)(2,1)S(1)}, bf16[32,2048]{1,0:T(8,128)(2,1)S(1)}, u32[]{:S(2)}, u32[]{:S(2)}) collective-permute-start(bf16[32,2048]{1,0:T(8,128)(2,1)S(1)} %get-tuple-element.67), channel_id=1, source_target_pairs={{0,8},{1,9},{2,10},{3,11},{4,12},{5,13},{6,14},{7,15},{8,0},{9,1},... | collective-permute-start | bytes 393224 | tf_op jit(solution)/shard_map/ppermute | solution.py:44
  61.3 1.5 %collective-permute-start.20 = (bf16[32,2048]{1,0:T(8,128)(2,1)S(1)}, bf16[32,2048]{1,0:T(8,128)(2,1)S(1)}, u32[]{:S(2)}, u32[]{:S(2)}) collective-permute-start(bf16[32,2048]{1,0:T(8,128)(2,1)S(1)} %get-tuple-element.67), channel_id=1, source_target_pairs={{0,24},{1,25},{2,26},{3,27},{4,28},{5,29},{6,30},{7,31},{8,16},{9,... | collective-permute-start | bytes 393224 | tf_op jit(solution)/shard_map/ppermute | solution.py:324
  62.8 2.8 %collective-permute-done.18.refs_7_ = bf16[32,2048]{1,0:T(8,128)(2,1)S(1)} collective-permute-done((bf16[32,2048]{1,0:T(8,128)(2,1)S(1)}, bf16[32,2048]{1,0:T(8,128)(2,1)S(1)}, u32[]{:S(2)}, u32[]{:S(2)}) %collective-permute-start.18) | collective-permute-done | bytes 131104 | tf_op jit(solution)/shard_map/ppermute | solution.py:44
  65.7 2.3 %collective-permute-done.20.refs_9_ = bf16[32,2048]{1,0:T(8,128)(2,1)S(1)} collective-permute-done((bf16[32,2048]{1,0:T(8,128)(2,1)S(1)}, bf16[32,2048]{1,0:T(8,128)(2,1)S(1)}, u32[]{:S(2)}, u32[]{:S(2)}) %collective-permute-start.20) | collective-permute-done | bytes 131104 | tf_op jit(solution)/shard_map/ppermute | solution.py:324
  68.8 1.4 %collective-permute-start.21 = (bf16[64,2176]{1,0:T(8,128)(2,1)S(1)}, bf16[64,2176]{1,0:T(8,128)(2,1)S(1)}, u32[]{:S(2)}, u32[]{:S(2)}) collective-permute-start(bf16[64,2176]{1,0:T(8,128)(2,1)S(1)} %get-tuple-element.69.refs_1_), channel_id=1, source_target_pairs={{0,1},{1,2},{2,3},{3,4},{4,5},{5,6},{6,7},{7,0},{8,9},{9,10},{10,1... | collective-permute-start | bytes 835592 | tf_op jit(solution)/shard_map/ppermute | solution.py:324
  70.3 1.9 %copy-done.1 = bf16[1,2048,768]{2,1,0:T(8,128)(2,1)S(1)} copy-done((bf16[1,2048,768]{2,1,0:T(8,128)(2,1)S(1)}, bf16[1,2048,768]{2,1,0:T(8,128)(2,1)}, u32[]{:S(2)}) %copy-start.1) | copy-done | bytes 3145752
  72.2 1.9 %copy-done.3 = bf16[1,768,2048]{2,1,0:T(8,128)(2,1)S(1)} copy-done((bf16[1,768,2048]{2,1,0:T(8,128)(2,1)S(1)}, bf16[1,768,2048]{2,1,0:T(8,128)(2,1)}, u32[]{:S(2)}) %copy-start.3) | copy-done | bytes 3145752
  74.6 4.3 %collective-permute-done.22.refs_5_ = bf16[64,2176]{1,0:T(8,128)(2,1)S(1)} collective-permute-done((bf16[64,2176]{1,0:T(8,128)(2,1)S(1)}, bf16[64,2176]{1,0:T(8,128)(2,1)S(1)}, u32[]{:S(2)}, u32[]{:S(2)}) %collective-permute-start.22) | collective-permute-done | bytes 278560 | tf_op jit(solution)/shard_map/ppermute | solution.py:324
  79.0 2.4 %shard_map.115 = (f32[80,2048]{1,0:T(8,128)S(1)}, bf16[80,2048]{1,0:T(8,128)(2,1)S(1)}) custom-call(s32[4]{0:T(128)S(1)} %pad_add_fusion.refs_0_, bf16[2048,768]{1,0:T(8,128)(2,1)S(1)} %bitcast.11, bf16[2048,768]{1,0:T(8,128)(2,1)S(1)} %bitcast.14, bf16[768,2048]{1,0:T(8,128)(2,1)S(1)} %bitcast.17, bf16[64,2176]{1,0:T(8,128)(2,1)S(1)} %collective-permute-done.21.refs_4_, ...), custom_call_target="tpu_custom_call" | custom-call | flops 1509949440 | bytes 10133504 | tf_op jit(solution)/shard_map/pallas_call | solution.py:73
  81.3 2.2 %collective-permute-start.23 = (bf16[80,2048]{1,0:T(8,128)(2,1)S(1)}, bf16[80,2048]{1,0:T(8,128)(2,1)S(1)}, u32[]{:S(2)}, u32[]{:S(2)}) collective-permute-start(bf16[80,2048]{1,0:T(8,128)(2,1)S(1)} %get-tuple-element.73), channel_id=1, source_target_pairs={{0,8},{1,9},{2,10},{3,11},{4,12},{5,13},{6,14},{7,15},{8,0},{9,1},... | collective-permute-start | bytes 983048 | tf_op jit(solution)/shard_map/ppermute | solution.py:44
  83.5 3.4 %collective-permute-start.25 = (bf16[32,2176]{1,0:T(8,128)(2,1)S(1)}, bf16[32,2176]{1,0:T(8,128)(2,1)S(1)}, u32[]{:S(2)}, u32[]{:S(2)}) collective-permute-start(bf16[32,2176]{1,0:T(8,128)(2,1)S(1)} %slice.7), channel_id=1, source_target_pairs={{0,2},{1,3},{2,4},{3,5},{4,6},{5,7},{6,0},{7,1},{8,10},{9,11},{10,... | collective-permute-start | bytes 417800 | tf_op jit(solution)/shard_map/ppermute | solution.py:324
  86.9 4.0 %collective-permute-done.25.refs_5_ = bf16[32,2176]{1,0:T(8,128)(2,1)S(1)} collective-permute-done((bf16[32,2176]{1,0:T(8,128)(2,1)S(1)}, bf16[32,2176]{1,0:T(8,128)(2,1)S(1)}, u32[]{:S(2)}, u32[]{:S(2)}) %collective-permute-start.25) | collective-permute-done | bytes 139296 | tf_op jit(solution)/shard_map/ppermute | solution.py:324
  90.9 2.3 %shard_map.117 = (f32[48,2048]{1,0:T(8,128)S(1)}, bf16[48,2048]{1,0:T(8,128)(2,1)S(1)}) custom-call(s32[4]{0:T(128)S(1)} %pad_add_fusion.refs_0_, bf16[2048,768]{1,0:T(8,128)(2,1)S(1)} %bitcast.12, bf16[2048,768]{1,0:T(8,128)(2,1)S(1)} %bitcast.15, bf16[768,2048]{1,0:T(8,128)(2,1)S(1)} %bitcast.18, bf16[64,2176]{1,0:T(8,128)(2,1)S(1)} %collective-permute-done.24.refs_4_, ...), custom_call_target="tpu_custom_call" | custom-call | flops 905969664 | bytes 9854976 | tf_op jit(solution)/shard_map/pallas_call | solution.py:73
  93.1 1.5 %collective-permute-start.26 = (bf16[48,2048]{1,0:T(8,128)(2,1)S(1)}, bf16[48,2048]{1,0:T(8,128)(2,1)S(1)}, u32[]{:S(2)}, u32[]{:S(2)}) collective-permute-start(bf16[48,2048]{1,0:T(8,128)(2,1)S(1)} %get-tuple-element.76), channel_id=1, source_target_pairs={{0,8},{1,9},{2,10},{3,11},{4,12},{5,13},{6,14},{7,15},{8,0},{9,1},... | collective-permute-start | bytes 589832 | tf_op jit(solution)/shard_map/ppermute | solution.py:44
  95.3 4.6 %collective-permute-start.27 = (bf16[32,2048]{1,0:T(8,128)(2,1)S(1)}, bf16[32,2048]{1,0:T(8,128)(2,1)S(1)}, u32[]{:S(2)}, u32[]{:S(2)}) collective-permute-start(bf16[32,2048]{1,0:T(8,128)(2,1)S(1)} %get-tuple-element.77), channel_id=1, source_target_pairs={{0,7},{1,0},{2,1},{3,2},{4,3},{5,4},{6,5},{7,6},{8,15},{9,8},{10,9... | collective-permute-start | bytes 393224 | tf_op jit(solution)/shard_map/ppermute | solution.py:324
  100.1 3.7 %collective-permute-done.27.refs_3_ = bf16[32,2048]{1,0:T(8,128)(2,1)S(1)} collective-permute-done((bf16[32,2048]{1,0:T(8,128)(2,1)S(1)}, bf16[32,2048]{1,0:T(8,128)(2,1)S(1)}, u32[]{:S(2)}, u32[]{:S(2)}) %collective-permute-start.27) | collective-permute-done | bytes 131104 | tf_op jit(solution)/shard_map/ppermute | solution.py:324
  104.4 1.5 %collective-permute-start.30 = (bf16[32,2048]{1,0:T(8,128)(2,1)S(1)}, bf16[32,2048]{1,0:T(8,128)(2,1)S(1)}, u32[]{:S(2)}, u32[]{:S(2)}) collective-permute-start(bf16[32,2048]{1,0:T(8,128)(2,1)S(1)} %get-tuple-element.82), channel_id=1, source_target_pairs={{0,5},{1,6},{2,7},{3,0},{4,1},{5,2},{6,3},{7,4},{8,13},{9,14},{10,... | collective-permute-start | bytes 393224 | tf_op jit(solution)/shard_map/ppermute | solution.py:324
  105.9 2.6 %collective-permute-start.28 = (bf16[16,2048]{1,0:T(8,128)(2,1)S(1)}, bf16[16,2048]{1,0:T(8,128)(2,1)S(1)}, u32[]{:S(2)}, u32[]{:S(2)}) collective-permute-start(bf16[16,2048]{1,0:T(8,128)(2,1)S(1)} %get-tuple-element.79), channel_id=1, source_target_pairs={{0,4},{1,5},{2,6},{3,7},{4,0},{5,1},{6,2},{7,3},{8,12},{9,13},{10,... | collective-permute-start | bytes 196616 | tf_op jit(solution)/shard_map/ppermute | solution.py:44
  108.4 8.1 %collective-permute-done.28.refs_2_ = bf16[16,2048]{1,0:T(8,128)(2,1)S(1)} collective-permute-done((bf16[16,2048]{1,0:T(8,128)(2,1)S(1)}, bf16[16,2048]{1,0:T(8,128)(2,1)S(1)}, u32[]{:S(2)}, u32[]{:S(2)}) %collective-permute-start.28) | collective-permute-done | bytes 65568 | tf_op jit(solution)/shard_map/ppermute | solution.py:44
  (75 shorter events, 26.9 us)
Async XLA Ops:
  0.9 8.1 %collective-permute-start.3 = (bf16[256,256]{1,0:T(8,128)(2,1)S(1)}, bf16[256,256]{1,0:T(8,128)(2,1)}, u32[]{:S(2)}, u32[]{:S(2)}) collective-permute-start(bf16[256,256]{1,0:T(8,128)(2,1)S(1)} %pad_maximum_fusion.refs_3_), channel_id=1, source_target_pairs={{0,128},{16,144},{32,160},{48,176},{64,192},{80,208},{96,224},{112... | collective-permute-start | bytes 393224 | tf_op jit(solution)/shard_map/ppermute | solution.py:40
  2.6 11.4 %collective-permute-start = (bf16[256,256]{1,0:T(8,128)(2,1)S(1)}, bf16[256,256]{1,0:T(8,128)(2,1)S(1)}, u32[]{:S(2)}, u32[]{:S(2)}) collective-permute-start(bf16[256,256]{1,0:T(8,128)(2,1)S(1)} %pad_maximum_fusion.refs_3_), channel_id=1, source_target_pairs={{0,32},{16,48},{32,64},{48,80},{64,96},{80,112},{96,0},{112,16},{1... | collective-permute-start | bytes 393224 | tf_op jit(solution)/shard_map/ppermute | solution.py:40
  4.1 16.8 %collective-permute-start.1 = (bf16[256,256]{1,0:T(8,128)(2,1)S(1)}, bf16[256,256]{1,0:T(8,128)(2,1)S(1)}, u32[]{:S(2)}, u32[]{:S(2)}) collective-permute-start(bf16[256,256]{1,0:T(8,128)(2,1)S(1)} %pad_maximum_fusion.refs_3_), channel_id=1, source_target_pairs={{0,96},{16,112},{32,0},{48,16},{64,32},{80,48},{96,64},{112,80},{1... | collective-permute-start | bytes 393224 | tf_op jit(solution)/shard_map/ppermute | solution.py:40
  5.8 18.0 %collective-permute-start.2 = (bf16[256,256]{1,0:T(8,128)(2,1)S(1)}, bf16[256,256]{1,0:T(8,128)(2,1)}, u32[]{:S(2)}, u32[]{:S(2)}) collective-permute-start(bf16[256,256]{1,0:T(8,128)(2,1)S(1)} %pad_maximum_fusion.refs_3_), channel_id=1, source_target_pairs={{0,64},{16,80},{32,96},{48,112},{64,0},{80,16},{96,32},{112,48},{1... | collective-permute-start | bytes 393224 | tf_op jit(solution)/shard_map/ppermute | solution.py:40
  9.1 15.4 %collective-permute-start.4 = (bf16[256,256]{1,0:T(8,128)(2,1)}, bf16[256,256]{1,0:T(8,128)(2,1)}, u32[]{:S(2)}, u32[]{:S(2)}) collective-permute-start(bf16[256,256]{1,0:T(8,128)(2,1)} %collective-permute-done.3.refs_7_), channel_id=1, source_target_pairs={{0,32},{16,48},{32,64},{48,80},{64,96},{80,112},{96,0},{112,16},{1... | collective-permute-start | bytes 393224 | tf_op jit(solution)/shard_map/ppermute | solution.py:40
  9.7 14.8 %collective-permute-start.5 = (bf16[256,256]{1,0:T(8,128)(2,1)}, bf16[256,256]{1,0:T(8,128)(2,1)}, u32[]{:S(2)}, u32[]{:S(2)}) collective-permute-start(bf16[256,256]{1,0:T(8,128)(2,1)} %collective-permute-done.3.refs_7_), channel_id=1, source_target_pairs={{0,96},{16,112},{32,0},{48,16},{64,32},{80,48},{96,64},{112,80},{1... | collective-permute-start | bytes 393224 | tf_op jit(solution)/shard_map/ppermute | solution.py:40
  14.6 14.3 %collective-permute-start.6 = (bf16[128,128]{1,0:T(8,128)(2,1)}, bf16[128,128]{1,0:T(8,128)(2,1)}, u32[]{:S(2)}, u32[]{:S(2)}) collective-permute-start(bf16[128,128]{1,0:T(8,128)(2,1)} %bitcast.21), channel_id=1, source_target_pairs={{0,4},{1,5},{2,6},{3,7},{4,0},{5,1},{6,2},{7,3},{8,12},{9,13},{10,... | collective-permute-start | bytes 98312 | tf_op jit(solution)/shard_map/ppermute | solution.py:44
  21.6 18.6 %collective-permute-start.13 = (bf16[128,1024]{1,0:T(8,128)(2,1)}, bf16[128,1024]{1,0:T(8,128)(2,1)S(1)}, u32[]{:S(2)}, u32[]{:S(2)}) collective-permute-start(bf16[128,1024]{1,0:T(8,128)(2,1)} %constant_dynamic-slice_fusion), channel_id=1, source_target_pairs={{0,4},{1,5},{2,6},{3,7},{4,0},{5,1},{6,2},{7,3},{8,12},{9,13},{10,... | collective-permute-start | bytes 786440 | tf_op jit(solution)/shard_map/ppermute | solution.py:44
  23.9 10.4 %collective-permute-start.11 = (bf16[256,256]{1,0:T(8,128)(2,1)}, bf16[256,256]{1,0:T(8,128)(2,1)S(1)}, u32[]{:S(2)}, u32[]{:S(2)}) collective-permute-start(bf16[256,256]{1,0:T(8,128)(2,1)} %collective-permute-done.3.refs_7_), channel_id=1, source_target_pairs={{0,64},{16,80},{32,96},{48,112},{64,0},{80,16},{96,32},{112,48},{1... | collective-permute-start | bytes 393224 | tf_op jit(solution)/shard_map/ppermute | solution.py:40
  26.0 5.9 %collective-permute-start.7 = (bf16[16,2176]{1,0:T(8,128)(2,1)S(1)}, bf16[16,2176]{1,0:T(8,128)(2,1)S(1)}, u32[]{:S(2)}, u32[]{:S(2)}) collective-permute-start(bf16[16,2176]{1,0:T(8,128)(2,1)S(1)} %get-tuple-element.47.refs_1_), channel_id=1, source_target_pairs={{0,8},{1,9},{2,10},{3,11},{4,12},{5,13},{6,14},{7,15},{8,0},{9,1},... | collective-permute-start | bytes 208904 | tf_op jit(solution)/shard_map/ppermute | solution.py:44
  28.9 2.9 %collective-permute-start.8 = (bf16[16,2176]{1,0:T(8,128)(2,1)S(1)}, bf16[16,2176]{1,0:T(8,128)(2,1)S(1)}, u32[]{:S(2)}, u32[]{:S(2)}) collective-permute-start(bf16[16,2176]{1,0:T(8,128)(2,1)S(1)} %get-tuple-element.47.refs_1_), channel_id=1, source_target_pairs={{0,16},{16,0},{32,48},{48,32},{64,80},{80,64},{96,112},{112,96},{1... | collective-permute-start | bytes 208904 | tf_op jit(solution)/shard_map/ppermute | solution.py:40
  28.9 5.3 %collective-permute-start.9 = (bf16[16,2176]{1,0:T(8,128)(2,1)S(1)}, bf16[16,2176]{1,0:T(8,128)(2,1)S(1)}, u32[]{:S(2)}, u32[]{:S(2)}) collective-permute-start(bf16[16,2176]{1,0:T(8,128)(2,1)S(1)} %get-tuple-element.47.refs_1_), channel_id=1, source_target_pairs={{0,24},{1,25},{2,26},{3,27},{4,28},{5,29},{6,30},{7,31},{8,16},{9,... | collective-permute-start | bytes 208904 | tf_op jit(solution)/shard_map/ppermute | solution.py:324
  31.9 2.4 %collective-permute-start.10 = (bf16[256,128]{1,0:T(8,128)(2,1)S(1)}, bf16[256,128]{1,0:T(8,128)(2,1)S(1)}, u32[]{:S(2)}, u32[]{:S(2)}) collective-permute-start(bf16[256,128]{1,0:T(8,128)(2,1)S(1)} %pad_maximum_fusion.1.refs_1_), channel_id=1, source_target_pairs={{0,16},{16,0},{32,48},{48,32},{64,80},{80,64},{96,112},{112,96},{1... | collective-permute-start | bytes 196616 | tf_op jit(solution)/shard_map/ppermute | solution.py:40
  39.3 2.0 %collective-permute-start.12 = (f32[256,256]{1,0:T(8,128)S(1)}, f32[256,256]{1,0:T(8,128)S(1)}, u32[]{:S(2)}, u32[]{:S(2)}) collective-permute-start(f32[256,256]{1,0:T(8,128)S(1)} %get-tuple-element.56), channel_id=1, source_target_pairs={{0,16},{16,0},{32,48},{48,32},{64,80},{80,64},{96,112},{112,96},{1... | collective-permute-start | bytes 786440 | tf_op jit(solution)/shard_map/ppermute | solution.py:40
  40.1 1.5 %collective-permute-start.14 = (bf16[128,1024]{1,0:T(8,128)(2,1)S(1)}, bf16[128,1024]{1,0:T(8,128)(2,1)S(1)}, u32[]{:S(2)}, u32[]{:S(2)}) collective-permute-start(bf16[128,1024]{1,0:T(8,128)(2,1)S(1)} %collective-permute-done.13.refs_3_), channel_id=1, source_target_pairs={{0,16},{16,0},{32,48},{48,32},{64,80},{80,64},{96,112},{112,96},{1... | collective-permute-start | bytes 786440 | tf_op jit(solution)/shard_map/ppermute | solution.py:40
  43.9 6.1 %collective-permute-start.15 = (bf16[32,2048]{1,0:T(8,128)(2,1)S(1)}, bf16[32,2048]{1,0:T(8,128)(2,1)S(1)}, u32[]{:S(2)}, u32[]{:S(2)}) collective-permute-start(bf16[32,2048]{1,0:T(8,128)(2,1)S(1)} %get-tuple-element.59), channel_id=1, source_target_pairs={{0,7},{1,0},{2,1},{3,2},{4,3},{5,4},{6,5},{7,6},{8,15},{9,8},{10,9... | collective-permute-start | bytes 393224 | tf_op jit(solution)/shard_map/ppermute | solution.py:44
  44.9 8.4 %collective-permute-start.16 = (bf16[32,2048]{1,0:T(8,128)(2,1)S(1)}, bf16[32,2048]{1,0:T(8,128)(2,1)S(1)}, u32[]{:S(2)}, u32[]{:S(2)}) collective-permute-start(bf16[32,2048]{1,0:T(8,128)(2,1)S(1)} %get-tuple-element.60), channel_id=1, source_target_pairs={{0,1},{1,2},{2,3},{3,4},{4,5},{5,6},{6,7},{7,0},{8,9},{9,10},{10,1... | collective-permute-start | bytes 393224 | tf_op jit(solution)/shard_map/ppermute | solution.py:44
  46.2 12.2 %collective-permute-start.17 = (bf16[32,2048]{1,0:T(8,128)(2,1)S(1)}, bf16[32,2048]{1,0:T(8,128)(2,1)S(1)}, u32[]{:S(2)}, u32[]{:S(2)}) collective-permute-start(bf16[32,2048]{1,0:T(8,128)(2,1)S(1)} %get-tuple-element.61), channel_id=1, source_target_pairs={{0,2},{1,3},{2,4},{3,5},{4,6},{5,7},{6,0},{7,1},{8,10},{9,11},{10,... | collective-permute-start | bytes 393224 | tf_op jit(solution)/shard_map/ppermute | solution.py:324
  59.1 6.6 %collective-permute-start.18 = (bf16[32,2048]{1,0:T(8,128)(2,1)S(1)}, bf16[32,2048]{1,0:T(8,128)(2,1)S(1)}, u32[]{:S(2)}, u32[]{:S(2)}) collective-permute-start(bf16[32,2048]{1,0:T(8,128)(2,1)S(1)} %get-tuple-element.67), channel_id=1, source_target_pairs={{0,8},{1,9},{2,10},{3,11},{4,12},{5,13},{6,14},{7,15},{8,0},{9,1},... | collective-permute-start | bytes 393224 | tf_op jit(solution)/shard_map/ppermute | solution.py:44
  61.3 4.4 %collective-permute-start.19 = (bf16[32,2048]{1,0:T(8,128)(2,1)S(1)}, bf16[32,2048]{1,0:T(8,128)(2,1)S(1)}, u32[]{:S(2)}, u32[]{:S(2)}) collective-permute-start(bf16[32,2048]{1,0:T(8,128)(2,1)S(1)} %get-tuple-element.67), channel_id=1, source_target_pairs={{0,16},{16,0},{32,48},{48,32},{64,80},{80,64},{96,112},{112,96},{1... | collective-permute-start | bytes 393224 | tf_op jit(solution)/shard_map/ppermute | solution.py:40
  61.3 6.7 %collective-permute-start.20 = (bf16[32,2048]{1,0:T(8,128)(2,1)S(1)}, bf16[32,2048]{1,0:T(8,128)(2,1)S(1)}, u32[]{:S(2)}, u32[]{:S(2)}) collective-permute-start(bf16[32,2048]{1,0:T(8,128)(2,1)S(1)} %get-tuple-element.67), channel_id=1, source_target_pairs={{0,24},{1,25},{2,26},{3,27},{4,28},{5,29},{6,30},{7,31},{8,16},{9,... | collective-permute-start | bytes 393224 | tf_op jit(solution)/shard_map/ppermute | solution.py:324
  68.8 10.2 %collective-permute-start.22 = (bf16[64,2176]{1,0:T(8,128)(2,1)S(1)}, bf16[64,2176]{1,0:T(8,128)(2,1)S(1)}, u32[]{:S(2)}, u32[]{:S(2)}) collective-permute-start(bf16[64,2176]{1,0:T(8,128)(2,1)S(1)} %get-tuple-element.69.refs_1_), channel_id=1, source_target_pairs={{0,2},{1,3},{2,4},{3,5},{4,6},{5,7},{6,0},{7,1},{8,10},{9,11},{10,... | collective-permute-start | bytes 835592 | tf_op jit(solution)/shard_map/ppermute | solution.py:324
  68.8 10.1 %collective-permute-start.21 = (bf16[64,2176]{1,0:T(8,128)(2,1)S(1)}, bf16[64,2176]{1,0:T(8,128)(2,1)S(1)}, u32[]{:S(2)}, u32[]{:S(2)}) collective-permute-start(bf16[64,2176]{1,0:T(8,128)(2,1)S(1)} %get-tuple-element.69.refs_1_), channel_id=1, source_target_pairs={{0,1},{1,2},{2,3},{3,4},{4,5},{5,6},{6,7},{7,0},{8,9},{9,10},{10,1... | collective-permute-start | bytes 835592 | tf_op jit(solution)/shard_map/ppermute | solution.py:324
  78.9 11.9 %collective-permute-start.24 = (bf16[64,2176]{1,0:T(8,128)(2,1)S(1)}, bf16[64,2176]{1,0:T(8,128)(2,1)S(1)}, u32[]{:S(2)}, u32[]{:S(2)}) collective-permute-start(bf16[64,2176]{1,0:T(8,128)(2,1)S(1)} %collective-permute-done.22.refs_5_), channel_id=1, source_target_pairs={{0,1},{1,2},{2,3},{3,4},{4,5},{5,6},{6,7},{7,0},{8,9},{9,10},{10,1... | collective-permute-start | bytes 835592 | tf_op jit(solution)/shard_map/ppermute | solution.py:324
  81.3 13.3 %collective-permute-start.23 = (bf16[80,2048]{1,0:T(8,128)(2,1)S(1)}, bf16[80,2048]{1,0:T(8,128)(2,1)S(1)}, u32[]{:S(2)}, u32[]{:S(2)}) collective-permute-start(bf16[80,2048]{1,0:T(8,128)(2,1)S(1)} %get-tuple-element.73), channel_id=1, source_target_pairs={{0,8},{1,9},{2,10},{3,11},{4,12},{5,13},{6,14},{7,15},{8,0},{9,1},... | collective-permute-start | bytes 983048 | tf_op jit(solution)/shard_map/ppermute | solution.py:44
  83.5 7.3 %collective-permute-start.25 = (bf16[32,2176]{1,0:T(8,128)(2,1)S(1)}, bf16[32,2176]{1,0:T(8,128)(2,1)S(1)}, u32[]{:S(2)}, u32[]{:S(2)}) collective-permute-start(bf16[32,2176]{1,0:T(8,128)(2,1)S(1)} %slice.7), channel_id=1, source_target_pairs={{0,2},{1,3},{2,4},{3,5},{4,6},{5,7},{6,0},{7,1},{8,10},{9,11},{10,... | collective-permute-start | bytes 417800 | tf_op jit(solution)/shard_map/ppermute | solution.py:324
  93.1 10.7 %collective-permute-start.26 = (bf16[48,2048]{1,0:T(8,128)(2,1)S(1)}, bf16[48,2048]{1,0:T(8,128)(2,1)S(1)}, u32[]{:S(2)}, u32[]{:S(2)}) collective-permute-start(bf16[48,2048]{1,0:T(8,128)(2,1)S(1)} %get-tuple-element.76), channel_id=1, source_target_pairs={{0,8},{1,9},{2,10},{3,11},{4,12},{5,13},{6,14},{7,15},{8,0},{9,1},... | collective-permute-start | bytes 589832 | tf_op jit(solution)/shard_map/ppermute | solution.py:44
  95.3 8.5 %collective-permute-start.27 = (bf16[32,2048]{1,0:T(8,128)(2,1)S(1)}, bf16[32,2048]{1,0:T(8,128)(2,1)S(1)}, u32[]{:S(2)}, u32[]{:S(2)}) collective-permute-start(bf16[32,2048]{1,0:T(8,128)(2,1)S(1)} %get-tuple-element.77), channel_id=1, source_target_pairs={{0,7},{1,0},{2,1},{3,2},{4,3},{5,4},{6,5},{7,6},{8,15},{9,8},{10,9... | collective-permute-start | bytes 393224 | tf_op jit(solution)/shard_map/ppermute | solution.py:324
  99.9 8.5 %collective-permute-start.29 = (bf16[32,2048]{1,0:T(8,128)(2,1)S(1)}, bf16[32,2048]{1,0:T(8,128)(2,1)S(1)}, u32[]{:S(2)}, u32[]{:S(2)}) collective-permute-start(bf16[32,2048]{1,0:T(8,128)(2,1)S(1)} %get-tuple-element.81), channel_id=1, source_target_pairs={{0,6},{1,7},{2,0},{3,1},{4,2},{5,3},{6,4},{7,5},{8,14},{9,15},{10,... | collective-permute-start | bytes 393224 | tf_op jit(solution)/shard_map/ppermute | solution.py:324
  104.4 12.2 %collective-permute-start.30 = (bf16[32,2048]{1,0:T(8,128)(2,1)S(1)}, bf16[32,2048]{1,0:T(8,128)(2,1)S(1)}, u32[]{:S(2)}, u32[]{:S(2)}) collective-permute-start(bf16[32,2048]{1,0:T(8,128)(2,1)S(1)} %get-tuple-element.82), channel_id=1, source_target_pairs={{0,5},{1,6},{2,7},{3,0},{4,1},{5,2},{6,3},{7,4},{8,13},{9,14},{10,... | collective-permute-start | bytes 393224 | tf_op jit(solution)/shard_map/ppermute | solution.py:324
  105.9 10.7 %collective-permute-start.28 = (bf16[16,2048]{1,0:T(8,128)(2,1)S(1)}, bf16[16,2048]{1,0:T(8,128)(2,1)S(1)}, u32[]{:S(2)}, u32[]{:S(2)}) collective-permute-start(bf16[16,2048]{1,0:T(8,128)(2,1)S(1)} %get-tuple-element.79), channel_id=1, source_target_pairs={{0,4},{1,5},{2,6},{3,7},{4,0},{5,1},{6,2},{7,3},{8,12},{9,13},{10,... | collective-permute-start | bytes 196616 | tf_op jit(solution)/shard_map/ppermute | solution.py:44
  117.2 1.3 %collective-permute-start.31 = (bf16[16,2048]{1,0:T(8,128)(2,1)S(1)}, bf16[16,2048]{1,0:T(8,128)(2,1)S(1)}, u32[]{:S(2)}, u32[]{:S(2)}) collective-permute-start(bf16[16,2048]{1,0:T(8,128)(2,1)S(1)} %get-tuple-element.84), channel_id=1, source_target_pairs={{0,16},{16,0},{32,48},{48,32},{64,80},{80,64},{96,112},{112,96},{1... | collective-permute-start | bytes 196616 | tf_op jit(solution)/shard_map/ppermute | solution.py:40
  (10 other events, 83.0 us)

commit v6 on v5

--- a/solution.py
+++ b/solution.py
@@ -47,8 +47,6 @@
 def kernel_call(
     body, scalars, resident, fetched, out_shapes, flops, transcendentals=0, limit=10, idle=(), scratch=()
 ):
-    n_own = len(resident)
-    resident, fetched = [*resident, *fetched], []
     ins = [*resident, *fetched, *idle]
     n_res, n_fetch = len(resident), len(fetched)
     n_out = len(jax.tree.leaves(out_shapes))
@@ -66,7 +64,7 @@
         for copy in copies:
             copy.start()
         extra = refs[len(ins) + n_out + 2 * n_fetch :]
-        body(place, refs[:n_own], refs[n_own:n_res], (*outs, *extra), lambda n: None)
+        body(place, refs[:n_res], buffers, (*outs, *extra), lambda n: copies[n].wait())
 
     size = sum(a.size * a.dtype.itemsize for a in [*resident, *fetched])
     vmem = pl.BlockSpec(memory_space=pltpu.VMEM)
@@ -75,7 +73,7 @@
         out_shape=out_shapes,
         in_specs=[pl.BlockSpec(memory_space=pltpu.SMEM)]
         + [vmem] * n_res
-        + [pl.BlockSpec(memory_space=pl.ANY)] * n_fetch
+        + [pl.BlockSpec(memory_space=pltpu.HBM)] * n_fetch
         + [vmem] * len(idle),
         out_specs=jax.tree.map(lambda _: vmem, out_shapes),
         scratch_shapes=[pltpu.VMEM(a.shape, a.dtype) for a in fetched]
@@ -97,21 +95,20 @@
 
 
 ROWS_TILE = 256
-PLACES = [(r, d) for r in (0, 1) for d in (0, -1, 1, 2)]
+DISTANCES = (0, -1, 1, 2)
 
 
 def attend_all(place, resident, fetched, outs, wait):
     core, y, z, ctx = place[0], place[1], place[2], place[3]
     row, x = ctx // 8, lax.rem(ctx // 2, 4)
-    sources = [(row ^ r) * 8 + lax.rem(x + d + 4, 4) * 2 + core for r, d in PLACES]
+    sources = [(row ^ r) * 8 + lax.rem(x + d + 4, 4) * 2 + core for d in DISTANCES for r in (0, 1)]
     half = resident[0].shape[0]
-    for n in range(8):
-        wait(n)
     token = lax.broadcasted_iota(jnp.int32, (ROWS_TILE, 1), 0) & 127
     part = token >> 4
     key = lax.broadcasted_iota(jnp.int32, (1, TOK_C), 1)
     lane = lax.broadcasted_iota(jnp.int32, (ROWS_TILE, HEAD_DIM), 1)
-    for n, q_ref in enumerate(resident):
+    blocks = [ref.at[pl.ds(r * TOK_C, TOK_C)] for ref in resident[2:] for r in (0, 1)]
+    for n, q_ref in enumerate(resident[:2]):
         q_ctx = ctx ^ n
         first = z + 7 - (core ^ n)
         local = (part >> 2) * 128 + (((part & 3) + first) & 7) * 16 + (token & 15)
@@ -121,7 +118,7 @@
             ahead = key - local
             queries = q_ref[at, :]
             parts = []
-            for source, ref in zip(sources, fetched):
+            for source, ref in zip(sources, blocks):
                 scores = lax.dot_general(
                     queries,
                     ref[:, :HEAD_DIM],
@@ -136,7 +133,7 @@
                 top = jnp.maximum(top, part)
             top = jnp.max(top, axis=1, keepdims=True)
             total, mixed = 0.0, 0.0
-            for part, ref in zip(parts, fetched):
+            for part, ref in zip(parts, blocks):
                 weights = jnp.exp2((part - top) * SCALE)
                 total = total + weights
                 mixed = mixed + jnp.dot(
@@ -151,11 +148,10 @@
 
 
 def project(place, resident, fetched, outs, wait):
-    (own_ref,) = resident
-    other_ref, near_ref, far_ref, w_own_ref = fetched
+    own_ref, other_ref, *part_refs = resident
+    (w_own_ref,) = fetched
     keep_ref, *send_refs, attn_ref = outs
-    core = place[0]
-    wait(0)
+    core, row = place[0], place[3] // 8
     own_top = own_ref[:, HEAD_DIM : HEAD_DIM + 1]
     other_top = other_ref[:, HEAD_DIM : HEAD_DIM + 1]
     top = jnp.maximum(own_top, other_top)
@@ -175,13 +171,13 @@
         return jnp.concatenate(pieces, axis=0)
 
     heads = [ordered(0), ordered(1)]
-    width = D // 2
-    for n in range(1, 4):
-        wait(n)
-    for side, w_ref in ((core, near_ref), (1 - core, far_ref)):
-        at = pl.ds(pl.multiple_of(side * width, width), width)
+    width = D // 4
+    wait(0)
+    for n, w_ref in enumerate(part_refs):
+        column = ((core ^ (n // 2)) * 2 + (row ^ (n % 2))) * width
+        at = pl.ds(pl.multiple_of(column, width), width)
         sums = jnp.dot(heads[0], w_own_ref[:, at], preferred_element_type=F32)
-        sums = sums + jnp.dot(heads[1], w_ref[...], preferred_element_type=F32)
+        sums = sums + jnp.dot(heads[1], w_ref[:, HEAD_DIM:], preferred_element_type=F32)
         keep_ref[:, at] = sums[:32]
         for s in range(3):
             send_refs[s][:, at] = sums[(s + 1) * 32 : (s + 2) * 32].astype(BF16)
@@ -189,20 +185,17 @@
 
 def add_up(place, resident, fetched, outs, wait):
     sums = resident[0][...]
-    for n in range(3):
-        wait(n)
-        sums = sums + fetched[n][...].astype(F32)
+    for ref in resident[1:]:
+        sums = sums + ref[...].astype(F32)
     outs[0][...] = sums
     outs[1][...] = sums.astype(BF16)
 
 
 def normalise(place, resident, fetched, outs, wait):
-    own_ref, sums_ref, gain_ref = resident
-    y_ref, core_ref, both_ref, sums_y_ref, sums_core_ref, sums_both_ref = fetched
+    own_ref, sums_ref, gain_ref, y_ref, core_ref, both_ref = resident[:6]
+    sums_y_ref, sums_core_ref, sums_both_ref = resident[6:]
     hidden_ref, normed_ref = outs
     y = place[1]
-    for n in range(6):
-        wait(n)
     for n in range(4):
         at = pl.ds(n % 2 * 16, 16)
         to = pl.ds(n * 16, 16)
@@ -215,7 +208,7 @@
         hidden = (extended[:, :D] + projected).astype(BF16)
         wide = hidden.astype(F32)
         inverse = lax.rsqrt(jnp.mean(wide * wide, axis=-1, keepdims=True) + 1e-06)
-        normed = (wide * inverse * gain_ref[:1, :]).astype(BF16)
+        normed = (wide * inverse * gain_ref[...].astype(F32)).astype(BF16)
         if n < 2:
             hidden_ref[at, :] = hidden
         normed_ref[to, :D] = normed
@@ -227,13 +220,11 @@
 
 
 def expert(place, resident, fetched, outs, wait):
-    gate_ref, up_ref, down_ref = resident
+    gate_ref, up_ref, down_ref, *inputs = resident
     keep_ref, give_ref = outs
     y, z = place[1], place[2]
-    for n in range(len(fetched)):
-        wait(n)
-    rows = [ref[:, :D] for ref in fetched]
-    weights = [ref[:, D:] for ref in fetched]
+    rows = [ref[:, :D] for ref in inputs]
+    weights = [ref[:, D:] for ref in inputs]
     rows = rows[0] if len(rows) == 1 else jnp.concatenate(rows, axis=0)
     weights = weights[0] if len(weights) == 1 else jnp.concatenate(weights, axis=0)
     lane = lax.broadcasted_iota(jnp.int32, weights.shape, 1)
@@ -256,8 +247,8 @@
     keep, give = kernel_call(
         expert,
         place,
-        weights,
-        rows,
+        [*weights, *rows],
+        [],
         [struct((total // 2, D), F32), struct((total // 2, D), BF16)],
         6 * total * D * FF,
         total * FF,
@@ -290,25 +281,20 @@
 
 
 def finish(place, resident, fetched, outs, wait):
-    hidden_ref, keep_ref = resident
+    hidden_ref, keep_ref, got_ref = resident
     hidden = jnp.where(
         place[1] == 0, hidden_ref[:16, :].astype(F32), hidden_ref[16:, :].astype(F32)
     )
-    wait(0)
-    moe = keep_ref[...] + fetched[0][...].astype(F32)
+    moe = keep_ref[...] + got_ref[...].astype(F32)
     outs[0][...] = (hidden + moe).astype(BF16)
 
 
-def extend(place, resident, fetched, outs, wait):
-    residual_ref, ids_ref, gates_ref, gain_ref = resident
-    lane = lax.broadcasted_iota(jnp.int32, (TOK_DEV, 128), 1)
-    weights = jnp.zeros((TOK_DEV, 128), F32)
+def router_weights(ids, gates):
+    name = jnp.arange(128, dtype=jnp.int32)[None, :]
+    weights = jnp.zeros((ids.shape[0], 128), BF16)
     for k in range(TOP):
-        gate = gates_ref[:, k : k + 1].astype(F32)
-        weights = weights + jnp.where(lane == ids_ref[:, k : k + 1], gate, 0.0)
-    outs[0][:, :D] = residual_ref[...]
-    outs[0][:, D:] = weights.astype(BF16)
-    outs[1][...] = jnp.broadcast_to(gain_ref[...].astype(F32), outs[1].shape)
+        weights = jnp.where(ids[:, k : k + 1] == name, gates[:, k : k + 1], weights)
+    return weights
 
 
 def by_core(step):
@@ -352,7 +338,7 @@
     w_down,
 ):
     ctx, exp = lax.axis_index("ctx"), lax.axis_index("exp")
-    core, y, z = ctx % 2, exp // 8, exp % 8
+    core, row, y, z = ctx % 2, ctx // 8, exp // 8, exp % 8
     place = jnp.stack([core, y, z, ctx]).astype(jnp.int32)
     kv_index = exp // (HEADS // KV_HEADS)
     block = jnp.concatenate(
@@ -364,8 +350,9 @@
     )
 
     other = on_ctx(block, ROW_SWAP)
-    blocks = [block] + [on_ctx(block, x_shift(-d)) for _, d in PLACES[1:4]]
-    blocks += [other] + [on_ctx(other, x_shift(-d)) for _, d in PLACES[5:]]
+    rows, other = after(residual, other)
+    pair = jnp.concatenate([block, other], axis=0)
+    blocks = [pair] + [on_ctx(pair, x_shift(-d)) for d in DISTANCES[1:]]
 
     by_holder = query.reshape(2, 8, TOK_DEV, HEAD_DIM)
     by_holder = jnp.concatenate([by_holder, by_holder], axis=1)
@@ -374,41 +361,35 @@
         return lax.dynamic_slice_in_dim(by_holder, first % 8, 4, 1).reshape(128, HEAD_DIM)
 
     first = z + 7 - core
-    mine = jnp.concatenate([rows_of(first), on_exp(rows_of(first + 4), z_shift(4))], axis=0)
+    quarter = D // 4
+    w_part = lax.dynamic_slice_in_dim(out_proj, (core * 2 + row) * quarter, quarter, 1)
+    part = on_exp(jnp.concatenate([rows_of(first + 4), w_part], axis=1), z_shift(4))
+    mine = jnp.concatenate([rows_of(first), part[:, :HEAD_DIM]], axis=0)
     theirs = on_ctx(mine, CORE_SWAP)
-
-    w_out, blocks[4] = after(out_proj, blocks[4])
-    w_half = lax.dynamic_slice_in_dim(w_out, core * (D // 2), D // 2, 1)
-    w_near = on_exp(w_half, z_shift(4))
-    w_far = on_ctx(w_near, CORE_SWAP)
-
-    rows, *blocks[1:7] = after(residual, *blocks[1:7])
-    extended, gain = kernel_call(
-        extend,
-        place,
-        [rows, expert_ids, gate_values, norm_gain.reshape(1, D)],
-        [],
-        [struct((TOK_DEV, D + 128), BF16), struct((8, D), F32)],
-        TOK_DEV * D,
-    )
-    extended_others = to_three(extended, extended, extended)
-    mine, *extended_others = after(mine, *extended_others)
+    part_row = on_ctx(part, ROW_SWAP)
+    w_parts = [part, part_row, on_ctx(part, CORE_SWAP), on_ctx(part_row, CORE_SWAP)]
+
+    extended = jnp.concatenate([rows, router_weights(expert_ids, gate_values)], axis=1)
+    extended_y = on_exp(extended, Y_SWAP)
+    mine, extended_y = after(mine, extended_y)
+    extended_others = [extended_y, on_ctx(extended, CORE_SWAP), on_ctx(extended_y, CORE_SWAP)]
 
     own, swap = kernel_call(
         attend_all,
         place,
-        [mine, theirs],
-        blocks,
+        [mine, theirs, *blocks],
+        [],
         [struct((256, 256), F32)] * 2,
         4 * 512 * 2048 * HEAD_DIM,
         512 * 2048,
     )
     joined = on_ctx(swap, CORE_SWAP)
+    joined, *extended_others = after(joined, *extended_others)
     keep, *sends = kernel_call(
         project,
         place,
-        [own],
-        [joined, w_near, w_far, out_proj],
+        [own, joined, *w_parts],
+        [out_proj],
         [struct((32, D), F32)] + [struct((32, D), BF16)] * 3,
         2 * 128 * 256 * D,
         scratch=[pltpu.VMEM((256, HEAD_DIM), BF16)],
@@ -421,16 +402,16 @@
     sums, send = kernel_call(
         add_up,
         place,
-        [keep],
-        recvs,
+        [keep, *recvs],
+        [],
         [struct((32, D), F32), struct((32, D), BF16)],
         3 * 32 * D,
     )
     hidden, round_0 = kernel_call(
         normalise,
         place,
-        [extended, sums, gain],
-        [*extended_others, *to_three(send, send, send)],
+        [extended, sums, norm_gain.reshape(1, D), *extended_others, *to_three(send, send, send)],
+        [],
         [struct((32, D), BF16), struct((64, D + 128), BF16)],
         16 * 32 * D,
     )
@@ -465,8 +446,8 @@
     return kernel_call(
         finish,
         place,
-        [hidden, keep],
-        [on_ctx(to_core, CORE_SWAP)],
+        [hidden, keep, on_ctx(to_core, CORE_SWAP)],
+        [],
         [struct((16, D), BF16)],
         3 * 16 * D,
     )[0]

time: 121 us -> 109 us (0.901)
  local copies, waits for them, and re-layouts: 13.6 us -> 5.76 us
  starting transfers between devices: 48.9 us -> 43.8 us
  waiting for transfers between devices: 40.2 us -> 42.6 us
    unnamed x22 -> x12, local copies, waits for them, and re-layouts: 10.3 us -> 1.92 us
    ppermute x10 -> x9, starting transfers between devices: 17.3 us -> 13.6 us  [on_both(): return lax.ppermute(block, ('ctx', 'exp'), route)]
    ppermute x13, starting transfers between devices: 11.6 us -> 8.63 us  [on_ctx(): return lax.ppermute(block, 'ctx', route)]
    ppermute x13, waiting for transfers between devices: 2.7 us -> 5.47 us  [on_ctx(): return lax.ppermute(block, 'ctx', route)]
    ppermute x9 -> x8, starting transfers between devices: 20 us -> 21.6 us  [on_exp(): return lax.ppermute(block, 'exp', route)]
    pallas_call x12 -> x11, Pallas kernels: 14.6 us -> 13.5 us  [kernel_call(): pl.pallas_call(whole, out_shape=out_shapes, in_specs=[pl.BlockSpec(memory...]
    ppermute x9 -> x8, waiting for transfers between devices: 15.6 us -> 14.5 us  [on_exp(): return lax.ppermute(block, 'exp', route)]
    ppermute x10 -> x9, waiting for transfers between devices: 21.9 us -> 22.6 us  [on_both(): return lax.ppermute(block, ('ctx', 'exp'), route)]
  transfers between devices with their start and end apart: 32 -> 30, of which waited for: 13 -> 16; matrix products, arithmetic and copies ran while one was open for 5% -> 4% of each run, Pallas kernels for 8% -> 8%
where the time goes in v6:
time: 109 us; the launch traced here: 108 us
  starting transfers between devices  43.8 us (40%)
  waiting for transfers between devices  42.6 us (39%)
  Pallas kernels  13.5 us (12%)
  local copies, waits for them, and re-layouts  5.76 us (5%)
  other arithmetic  1.91 us (2%)
    ppermute x9, waiting for transfers between devices, on_both(): return lax.ppermute(block, ('ctx', 'exp'), route)  22.6 us
    ppermute x8, starting transfers between devices, on_exp(): return lax.ppermute(block, 'exp', route)  21.6 us
    ppermute x8, waiting for transfers between devices, on_exp(): return lax.ppermute(block, 'exp', route)  14.5 us
    ppermute x9, starting transfers between devices, on_both(): return lax.ppermute(block, ('ctx', 'exp'), route)  13.6 us
    pallas_call x11, Pallas kernels, kernel_call(): pl.pallas_call(whole, out_shape=out_shapes, in_specs=[pl.BlockSpec(memory...  13.5 us
    ppermute x13, starting transfers between devices, on_ctx(): return lax.ppermute(block, 'ctx', route)  8.63 us
    ppermute x13, waiting for transfers between devices, on_ctx(): return lax.ppermute(block, 'ctx', route)  5.47 us
  transfers between devices with their start and end apart: 30, of which 16 were waited for; matrix products, arithmetic and copies ran while one was open for 4% of the time, Pallas kernels for 8%

profile of v6, /device:TPU:32, one launch (start us, length us, event | category | flops | bytes accessed | tf_op | source)
XLA Modules:
  0.0 107.8 jit_solution(6822962964200163314)
XLA Ops:
  1.0 1.7 %collective-permute-start = (bf16[256,256]{1,0:T(8,128)(2,1)S(1)}, bf16[256,256]{1,0:T(8,128)(2,1)S(1)}, u32[]{:S(2)}, u32[]{:S(2)}) collective-permute-start(bf16[256,256]{1,0:T(8,128)(2,1)S(1)} %pad_maximum_fusion.2), channel_id=1, source_target_pairs={{0,128},{16,144},{32,160},{48,176},{64,192},{80,208},{96,224},{112... | collective-permute-start | bytes 393224 | tf_op jit(solution)/shard_map/ppermute | solution.py:40
  4.5 6.4 %collective-permute-start.1 = (bf16[128,640]{1,0:T(8,128)(2,1)S(1)}, bf16[128,640]{1,0:T(8,128)(2,1)S(1)}, u32[]{:S(2)}, u32[]{:S(2)}) collective-permute-start(bf16[128,640]{1,0:T(8,128)(2,1)S(1)} %pad_maximum_fusion.1), channel_id=1, source_target_pairs={{0,4},{1,5},{2,6},{3,7},{4,0},{5,1},{6,2},{7,3},{8,12},{9,13},{10,... | collective-permute-start | bytes 491528 | tf_op jit(solution)/shard_map/ppermute | solution.py:44
  12.9 1.6 %collective-permute-start.4 = (bf16[512,256]{1,0:T(8,128)(2,1)S(1)}, bf16[512,256]{1,0:T(8,128)(2,1)S(1)}, u32[]{:S(2)}, u32[]{:S(2)}) collective-permute-start(bf16[512,256]{1,0:T(8,128)(2,1)S(1)} %pad_maximum_fusion.refs_3_), channel_id=1, source_target_pairs={{0,32},{16,48},{32,64},{48,80},{64,96},{80,112},{96,0},{112,16},{1... | collective-permute-start | bytes 786440 | tf_op jit(solution)/shard_map/ppermute | solution.py:40
  14.5 1.7 %collective-permute-start.5 = (bf16[512,256]{1,0:T(8,128)(2,1)S(1)}, bf16[512,256]{1,0:T(8,128)(2,1)S(1)}, u32[]{:S(2)}, u32[]{:S(2)}) collective-permute-start(bf16[512,256]{1,0:T(8,128)(2,1)S(1)} %pad_maximum_fusion.refs_3_), channel_id=1, source_target_pairs={{0,96},{16,112},{32,0},{48,16},{64,32},{80,48},{96,64},{112,80},{1... | collective-permute-start | bytes 786440 | tf_op jit(solution)/shard_map/ppermute | solution.py:40
  16.3 1.8 %collective-permute-start.6 = (bf16[512,256]{1,0:T(8,128)(2,1)S(1)}, bf16[512,256]{1,0:T(8,128)(2,1)S(1)}, u32[]{:S(2)}, u32[]{:S(2)}) collective-permute-start(bf16[512,256]{1,0:T(8,128)(2,1)S(1)} %pad_maximum_fusion.refs_3_), channel_id=1, source_target_pairs={{0,64},{16,80},{32,96},{48,112},{64,0},{80,16},{96,32},{112,48},{1... | collective-permute-start | bytes 786440 | tf_op jit(solution)/shard_map/ppermute | solution.py:40
  18.9 2.9 %collective-permute-start.2 = (bf16[16,2176]{1,0:T(8,128)(2,1)S(1)}, bf16[16,2176]{1,0:T(8,128)(2,1)S(1)}, u32[]{:S(2)}, u32[]{:S(2)}) collective-permute-start(bf16[16,2176]{1,0:T(8,128)(2,1)S(1)} %pad_maximum_fusion.3.refs_1_), channel_id=1, source_target_pairs={{0,8},{1,9},{2,10},{3,11},{4,12},{5,13},{6,14},{7,15},{8,0},{9,1},... | collective-permute-start | bytes 208904 | tf_op jit(solution)/shard_map/ppermute | solution.py:44
  21.9 2.8 %collective-permute-done.2.refs_4_ = bf16[16,2176]{1,0:T(8,128)(2,1)S(1)} collective-permute-done((bf16[16,2176]{1,0:T(8,128)(2,1)S(1)}, bf16[16,2176]{1,0:T(8,128)(2,1)S(1)}, u32[]{:S(2)}, u32[]{:S(2)}) %collective-permute-start.2) | collective-permute-done | bytes 69664 | tf_op jit(solution)/shard_map/ppermute | solution.py:44
  25.3 1.4 %collective-permute-done.5.refs_5_ = bf16[512,256]{1,0:T(8,128)(2,1)S(1)} collective-permute-done((bf16[512,256]{1,0:T(8,128)(2,1)S(1)}, bf16[512,256]{1,0:T(8,128)(2,1)S(1)}, u32[]{:S(2)}, u32[]{:S(2)}) %collective-permute-start.5) | collective-permute-done | bytes 262176 | tf_op jit(solution)/shard_map/ppermute | solution.py:40
  26.6 1.7 %collective-permute-done.6.refs_6_ = bf16[512,256]{1,0:T(8,128)(2,1)S(1)} collective-permute-done((bf16[512,256]{1,0:T(8,128)(2,1)S(1)}, bf16[512,256]{1,0:T(8,128)(2,1)S(1)}, u32[]{:S(2)}, u32[]{:S(2)}) %collective-permute-start.6) | collective-permute-done | bytes 262176 | tf_op jit(solution)/shard_map/ppermute | solution.py:40
  28.3 2.7 %shard_map.109 = (f32[256,256]{1,0:T(8,128)S(1)}, f32[256,256]{1,0:T(8,128)S(1)}) custom-call(s32[4]{0:T(128)S(1)} %pad_add_fusion.refs_0_, bf16[256,128]{1,0:T(8,128)(2,1)S(1)} %pad_maximum_fusion.4.refs_1_, bf16[256,128]{1,0:T(8,128)(2,1)S(1)} %collective-permute-done.3.refs_2_, bf16[512,256]{1,0:T(8,128)(2,1)S(1)} %pad_maximum_fusion.refs_3_, ...), custom_call_target="tpu_custom_call" | custom-call | flops 536870912 | bytes 1179648 | tf_op jit(solution)/shard_map/pallas_call | solution.py:71
  33.4 1.3 %shard_map.110 = (f32[32,2048]{1,0:T(8,128)S(1)}, bf16[32,2048]{1,0:T(8,128)(2,1)S(1)}, bf16[32,2048]{1,0:T(8,128)(2,1)S(1)}, bf16[32,2048]{1,0:T(8,128)(2,1)S(1)}) custom-call(s32[4]{0:T(128)S(1)} %pad_add_fusion.refs_0_, f32[256,256]{1,0:T(8,128)S(1)} %get-tuple-element.41.refs_1_, f32[256,256]{1,0:T(8,128)S(1)} %collective-permute-done.7.refs_2_, ...), custom_call_target="tpu_custom_call" | custom-call | flops 134217728 | bytes 1703936 | tf_op jit(solution)/shard_map/pallas_call | solution.py:71
  36.8 2.7 %collective-permute-start.15 = (bf16[32,2048]{1,0:T(8,128)(2,1)S(1)}, bf16[32,2048]{1,0:T(8,128)(2,1)S(1)}, u32[]{:S(2)}, u32[]{:S(2)}) collective-permute-start(bf16[32,2048]{1,0:T(8,128)(2,1)S(1)} %get-tuple-element.48), channel_id=1, source_target_pairs={{0,2},{1,3},{2,4},{3,5},{4,6},{5,7},{6,0},{7,1},{8,10},{9,11},{10,... | collective-permute-start | bytes 393224 | tf_op jit(solution)/shard_map/ppermute | solution.py:310
  39.5 2.8 %collective-permute-done.13.refs_2_ = bf16[32,2048]{1,0:T(8,128)(2,1)S(1)} collective-permute-done((bf16[32,2048]{1,0:T(8,128)(2,1)S(1)}, bf16[32,2048]{1,0:T(8,128)(2,1)S(1)}, u32[]{:S(2)}, u32[]{:S(2)}) %collective-permute-start.13) | collective-permute-done | bytes 131104 | tf_op jit(solution)/shard_map/ppermute | solution.py:44
  42.3 2.9 %collective-permute-done.15.refs_4_ = bf16[32,2048]{1,0:T(8,128)(2,1)S(1)} collective-permute-done((bf16[32,2048]{1,0:T(8,128)(2,1)S(1)}, bf16[32,2048]{1,0:T(8,128)(2,1)S(1)}, u32[]{:S(2)}, u32[]{:S(2)}) %collective-permute-start.15) | collective-permute-done | bytes 131104 | tf_op jit(solution)/shard_map/ppermute | solution.py:310
  45.9 3.0 %collective-permute-start.16 = (bf16[32,2048]{1,0:T(8,128)(2,1)S(1)}, bf16[32,2048]{1,0:T(8,128)(2,1)S(1)}, u32[]{:S(2)}, u32[]{:S(2)}) collective-permute-start(bf16[32,2048]{1,0:T(8,128)(2,1)S(1)} %get-tuple-element.53), channel_id=1, source_target_pairs={{0,8},{1,9},{2,10},{3,11},{4,12},{5,13},{6,14},{7,15},{8,0},{9,1},... | collective-permute-start | bytes 393224 | tf_op jit(solution)/shard_map/ppermute | solution.py:44
  49.6 3.1 %collective-permute-done.16.refs_7_ = bf16[32,2048]{1,0:T(8,128)(2,1)S(1)} collective-permute-done((bf16[32,2048]{1,0:T(8,128)(2,1)S(1)}, bf16[32,2048]{1,0:T(8,128)(2,1)S(1)}, u32[]{:S(2)}, u32[]{:S(2)}) %collective-permute-start.16) | collective-permute-done | bytes 131104 | tf_op jit(solution)/shard_map/ppermute | solution.py:44
  52.7 2.8 %collective-permute-done.18.refs_9_ = bf16[32,2048]{1,0:T(8,128)(2,1)S(1)} collective-permute-done((bf16[32,2048]{1,0:T(8,128)(2,1)S(1)}, bf16[32,2048]{1,0:T(8,128)(2,1)S(1)}, u32[]{:S(2)}, u32[]{:S(2)}) %collective-permute-start.18) | collective-permute-done | bytes 131104 | tf_op jit(solution)/shard_map/ppermute | solution.py:310
  57.4 1.2 %collective-permute-start.19 = (bf16[64,2176]{1,0:T(8,128)(2,1)S(1)}, bf16[64,2176]{1,0:T(8,128)(2,1)S(1)}, u32[]{:S(2)}, u32[]{:S(2)}) collective-permute-start(bf16[64,2176]{1,0:T(8,128)(2,1)S(1)} %get-tuple-element.55.refs_1_), channel_id=1, source_target_pairs={{0,1},{1,2},{2,3},{3,4},{4,5},{5,6},{6,7},{7,0},{8,9},{9,10},{10,1... | collective-permute-start | bytes 835592 | tf_op jit(solution)/shard_map/ppermute | solution.py:310
  58.5 1.9 %copy-done.2 = bf16[1,768,2048]{2,1,0:T(8,128)(2,1)S(1)} copy-done((bf16[1,768,2048]{2,1,0:T(8,128)(2,1)S(1)}, bf16[1,768,2048]{2,1,0:T(8,128)(2,1)}, u32[]{:S(2)}) %copy-start.2) | copy-done | bytes 3145752
  61.0 5.7 %collective-permute-done.20.refs_5_ = bf16[64,2176]{1,0:T(8,128)(2,1)S(1)} collective-permute-done((bf16[64,2176]{1,0:T(8,128)(2,1)S(1)}, bf16[64,2176]{1,0:T(8,128)(2,1)S(1)}, u32[]{:S(2)}, u32[]{:S(2)}) %collective-permute-start.20) | collective-permute-done | bytes 278560 | tf_op jit(solution)/shard_map/ppermute | solution.py:310
  67.2 2.3 %shard_map.114 = (f32[80,2048]{1,0:T(8,128)S(1)}, bf16[80,2048]{1,0:T(8,128)(2,1)S(1)}) custom-call(s32[4]{0:T(128)S(1)} %pad_add_fusion.refs_0_, bf16[2048,768]{1,0:T(8,128)(2,1)S(1)} %bitcast.43, bf16[2048,768]{1,0:T(8,128)(2,1)S(1)} %bitcast.46, bf16[768,2048]{1,0:T(8,128)(2,1)S(1)} %bitcast.49, bf16[64,2176]{1,0:T(8,128)(2,1)S(1)} %collective-permute-done.19.refs_4_, ...), custom_call_target="tpu_custom_call" | custom-call | flops 1509949440 | bytes 10133504 | tf_op jit(solution)/shard_map/pallas_call | solution.py:71
  69.5 2.8 %collective-permute-start.21 = (bf16[80,2048]{1,0:T(8,128)(2,1)S(1)}, bf16[80,2048]{1,0:T(8,128)(2,1)S(1)}, u32[]{:S(2)}, u32[]{:S(2)}) collective-permute-start(bf16[80,2048]{1,0:T(8,128)(2,1)S(1)} %get-tuple-element.59), channel_id=1, source_target_pairs={{0,8},{1,9},{2,10},{3,11},{4,12},{5,13},{6,14},{7,15},{8,0},{9,1},... | collective-permute-start | bytes 983048 | tf_op jit(solution)/shard_map/ppermute | solution.py:44
  72.3 2.0 %collective-permute-start.23 = (bf16[32,2176]{1,0:T(8,128)(2,1)S(1)}, bf16[32,2176]{1,0:T(8,128)(2,1)S(1)}, u32[]{:S(2)}, u32[]{:S(2)}) collective-permute-start(bf16[32,2176]{1,0:T(8,128)(2,1)S(1)} %slice.75), channel_id=1, source_target_pairs={{0,2},{1,3},{2,4},{3,5},{4,6},{5,7},{6,0},{7,1},{8,10},{9,11},{10,... | collective-permute-start | bytes 417800 | tf_op jit(solution)/shard_map/ppermute | solution.py:310
  74.3 5.4 %collective-permute-done.23.refs_5_ = bf16[32,2176]{1,0:T(8,128)(2,1)S(1)} collective-permute-done((bf16[32,2176]{1,0:T(8,128)(2,1)S(1)}, bf16[32,2176]{1,0:T(8,128)(2,1)S(1)}, u32[]{:S(2)}, u32[]{:S(2)}) %collective-permute-start.23) | collective-permute-done | bytes 139296 | tf_op jit(solution)/shard_map/ppermute | solution.py:310
  79.7 2.3 %shard_map.116 = (f32[48,2048]{1,0:T(8,128)S(1)}, bf16[48,2048]{1,0:T(8,128)(2,1)S(1)}) custom-call(s32[4]{0:T(128)S(1)} %pad_add_fusion.refs_0_, bf16[2048,768]{1,0:T(8,128)(2,1)S(1)} %bitcast.44, bf16[2048,768]{1,0:T(8,128)(2,1)S(1)} %bitcast.47, bf16[768,2048]{1,0:T(8,128)(2,1)S(1)} %bitcast.50, bf16[64,2176]{1,0:T(8,128)(2,1)S(1)} %collective-permute-done.22.refs_4_, ...), custom_call_target="tpu_custom_call" | custom-call | flops 905969664 | bytes 9854976 | tf_op jit(solution)/shard_map/pallas_call | solution.py:71
  83.5 5.0 %collective-permute-start.25 = (bf16[32,2048]{1,0:T(8,128)(2,1)S(1)}, bf16[32,2048]{1,0:T(8,128)(2,1)S(1)}, u32[]{:S(2)}, u32[]{:S(2)}) collective-permute-start(bf16[32,2048]{1,0:T(8,128)(2,1)S(1)} %get-tuple-element.63), channel_id=1, source_target_pairs={{0,7},{1,0},{2,1},{3,2},{4,3},{5,4},{6,5},{7,6},{8,15},{9,8},{10,9... | collective-permute-start | bytes 393224 | tf_op jit(solution)/shard_map/ppermute | solution.py:310
  88.5 3.9 %collective-permute-done.25.refs_3_ = bf16[32,2048]{1,0:T(8,128)(2,1)S(1)} collective-permute-done((bf16[32,2048]{1,0:T(8,128)(2,1)S(1)}, bf16[32,2048]{1,0:T(8,128)(2,1)S(1)}, u32[]{:S(2)}, u32[]{:S(2)}) %collective-permute-start.25) | collective-permute-done | bytes 131104 | tf_op jit(solution)/shard_map/ppermute | solution.py:310
  94.0 3.5 %collective-permute-start.26 = (bf16[16,2048]{1,0:T(8,128)(2,1)S(1)}, bf16[16,2048]{1,0:T(8,128)(2,1)S(1)}, u32[]{:S(2)}, u32[]{:S(2)}) collective-permute-start(bf16[16,2048]{1,0:T(8,128)(2,1)S(1)} %get-tuple-element.65), channel_id=1, source_target_pairs={{0,4},{1,5},{2,6},{3,7},{4,0},{5,1},{6,2},{7,3},{8,12},{9,13},{10,... | collective-permute-start | bytes 196616 | tf_op jit(solution)/shard_map/ppermute | solution.py:44
  97.5 5.8 %collective-permute-done.26.refs_2_ = bf16[16,2048]{1,0:T(8,128)(2,1)S(1)} collective-permute-done((bf16[16,2048]{1,0:T(8,128)(2,1)S(1)}, bf16[16,2048]{1,0:T(8,128)(2,1)S(1)}, u32[]{:S(2)}, u32[]{:S(2)}) %collective-permute-start.26) | collective-permute-done | bytes 65568 | tf_op jit(solution)/shard_map/ppermute | solution.py:44
  103.2 1.4 %collective-permute-done.28.refs_5_ = bf16[32,2048]{1,0:T(8,128)(2,1)S(1)} collective-permute-done((bf16[32,2048]{1,0:T(8,128)(2,1)S(1)}, bf16[32,2048]{1,0:T(8,128)(2,1)S(1)}, u32[]{:S(2)}, u32[]{:S(2)}) %collective-permute-start.28) | collective-permute-done | bytes 131104 | tf_op jit(solution)/shard_map/ppermute | solution.py:310
  105.3 1.2 %collective-permute-done.29.refs_3_ = bf16[16,2048]{1,0:T(8,128)(2,1)S(1)} collective-permute-done((bf16[16,2048]{1,0:T(8,128)(2,1)S(1)}, bf16[16,2048]{1,0:T(8,128)(2,1)S(1)}, u32[]{:S(2)}, u32[]{:S(2)}) %collective-permute-start.29) | collective-permute-done | bytes 65568 | tf_op jit(solution)/shard_map/ppermute | solution.py:40
  106.6 1.2 %shard_map.119 = bf16[16,2048]{1,0:T(8,128)(2,1)} custom-call(s32[4]{0:T(128)S(1)} %pad_add_fusion.refs_0_, bf16[32,2048]{1,0:T(8,128)(2,1)S(1)} %get-tuple-element.54.refs_1_, f32[16,2048]{1,0:T(8,128)S(1)} %get-tuple-element.69.refs_2_, bf16[16,2048]{1,0:T(8,128)(2,1)S(1)} %collective-permute-done.29.refs_3_), custom_call_target="tpu_custom_call" | custom-call | flops 98304 | bytes 327680 | tf_op jit(solution)/shard_map/pallas_call | solution.py:71
  (67 shorter events, 18.9 us)
Async XLA Ops:
  1.0 11.9 %collective-permute-start = (bf16[256,256]{1,0:T(8,128)(2,1)S(1)}, bf16[256,256]{1,0:T(8,128)(2,1)S(1)}, u32[]{:S(2)}, u32[]{:S(2)}) collective-permute-start(bf16[256,256]{1,0:T(8,128)(2,1)S(1)} %pad_maximum_fusion.2), channel_id=1, source_target_pairs={{0,128},{16,144},{32,160},{48,176},{64,192},{80,208},{96,224},{112... | collective-permute-start | bytes 393224 | tf_op jit(solution)/shard_map/ppermute | solution.py:40
  4.4 54.1 %copy-start.1 = (bf16[1,2048,768]{2,1,0:T(8,128)(2,1)S(1)}, bf16[1,2048,768]{2,1,0:T(8,128)(2,1)}, u32[]{:S(2)}) copy-start(bf16[1,2048,768]{2,1,0:T(8,128)(2,1)} %param.20) | copy-start | bytes 9437188
  4.4 54.1 %copy-start = (bf16[1,2048,768]{2,1,0:T(8,128)(2,1)S(1)}, bf16[1,2048,768]{2,1,0:T(8,128)(2,1)}, u32[]{:S(2)}) copy-start(bf16[1,2048,768]{2,1,0:T(8,128)(2,1)} %param.19) | copy-start | bytes 9437188
  4.5 17.4 %collective-permute-start.1 = (bf16[128,640]{1,0:T(8,128)(2,1)S(1)}, bf16[128,640]{1,0:T(8,128)(2,1)S(1)}, u32[]{:S(2)}, u32[]{:S(2)}) collective-permute-start(bf16[128,640]{1,0:T(8,128)(2,1)S(1)} %pad_maximum_fusion.1), channel_id=1, source_target_pairs={{0,4},{1,5},{2,6},{3,7},{4,0},{5,1},{6,2},{7,3},{8,12},{9,13},{10,... | collective-permute-start | bytes 491528 | tf_op jit(solution)/shard_map/ppermute | solution.py:44
  12.9 12.3 %collective-permute-start.4 = (bf16[512,256]{1,0:T(8,128)(2,1)S(1)}, bf16[512,256]{1,0:T(8,128)(2,1)S(1)}, u32[]{:S(2)}, u32[]{:S(2)}) collective-permute-start(bf16[512,256]{1,0:T(8,128)(2,1)S(1)} %pad_maximum_fusion.refs_3_), channel_id=1, source_target_pairs={{0,32},{16,48},{32,64},{48,80},{64,96},{80,112},{96,0},{112,16},{1... | collective-permute-start | bytes 786440 | tf_op jit(solution)/shard_map/ppermute | solution.py:40
  14.5 12.1 %collective-permute-start.5 = (bf16[512,256]{1,0:T(8,128)(2,1)S(1)}, bf16[512,256]{1,0:T(8,128)(2,1)S(1)}, u32[]{:S(2)}, u32[]{:S(2)}) collective-permute-start(bf16[512,256]{1,0:T(8,128)(2,1)S(1)} %pad_maximum_fusion.refs_3_), channel_id=1, source_target_pairs={{0,96},{16,112},{32,0},{48,16},{64,32},{80,48},{96,64},{112,80},{1... | collective-permute-start | bytes 786440 | tf_op jit(solution)/shard_map/ppermute | solution.py:40
  16.3 12.1 %collective-permute-start.6 = (bf16[512,256]{1,0:T(8,128)(2,1)S(1)}, bf16[512,256]{1,0:T(8,128)(2,1)S(1)}, u32[]{:S(2)}, u32[]{:S(2)}) collective-permute-start(bf16[512,256]{1,0:T(8,128)(2,1)S(1)} %pad_maximum_fusion.refs_3_), channel_id=1, source_target_pairs={{0,64},{16,80},{32,96},{48,112},{64,0},{80,16},{96,32},{112,48},{1... | collective-permute-start | bytes 786440 | tf_op jit(solution)/shard_map/ppermute | solution.py:40
  18.9 5.8 %collective-permute-start.2 = (bf16[16,2176]{1,0:T(8,128)(2,1)S(1)}, bf16[16,2176]{1,0:T(8,128)(2,1)S(1)}, u32[]{:S(2)}, u32[]{:S(2)}) collective-permute-start(bf16[16,2176]{1,0:T(8,128)(2,1)S(1)} %pad_maximum_fusion.3.refs_1_), channel_id=1, source_target_pairs={{0,8},{1,9},{2,10},{3,11},{4,12},{5,13},{6,14},{7,15},{8,0},{9,1},... | collective-permute-start | bytes 208904 | tf_op jit(solution)/shard_map/ppermute | solution.py:44
  21.8 3.4 %collective-permute-start.3 = (bf16[256,128]{1,0:T(8,128)(2,1)S(1)}, bf16[256,128]{1,0:T(8,128)(2,1)S(1)}, u32[]{:S(2)}, u32[]{:S(2)}) collective-permute-start(bf16[256,128]{1,0:T(8,128)(2,1)S(1)} %pad_maximum_fusion.4.refs_1_), channel_id=1, source_target_pairs={{0,16},{16,0},{32,48},{48,32},{64,80},{80,64},{96,112},{112,96},{1... | collective-permute-start | bytes 196616 | tf_op jit(solution)/shard_map/ppermute | solution.py:40
  24.7 6.8 %collective-permute-start.10 = (bf16[128,640]{1,0:T(8,128)(2,1)S(1)}, bf16[128,640]{1,0:T(8,128)(2,1)S(1)}, u32[]{:S(2)}, u32[]{:S(2)}) collective-permute-start(bf16[128,640]{1,0:T(8,128)(2,1)S(1)} %collective-permute-done.1.refs_3_), channel_id=1, source_target_pairs={{0,128},{16,144},{32,160},{48,176},{64,192},{80,208},{96,224},{112... | collective-permute-start | bytes 491528 | tf_op jit(solution)/shard_map/ppermute | solution.py:40
  31.0 2.4 %collective-permute-start.7 = (f32[256,256]{1,0:T(8,128)S(1)}, f32[256,256]{1,0:T(8,128)S(1)}, u32[]{:S(2)}, u32[]{:S(2)}) collective-permute-start(f32[256,256]{1,0:T(8,128)S(1)} %get-tuple-element.42), channel_id=1, source_target_pairs={{0,16},{16,0},{32,48},{48,32},{64,80},{80,64},{96,112},{112,96},{1... | collective-permute-start | bytes 786440 | tf_op jit(solution)/shard_map/ppermute | solution.py:40
  31.1 2.3 %collective-permute-start.11 = (bf16[128,640]{1,0:T(8,128)(2,1)S(1)}, bf16[128,640]{1,0:T(8,128)(2,1)S(1)}, u32[]{:S(2)}, u32[]{:S(2)}) collective-permute-start(bf16[128,640]{1,0:T(8,128)(2,1)S(1)} %collective-permute-done.1.refs_3_), channel_id=1, source_target_pairs={{0,16},{16,0},{32,48},{48,32},{64,80},{80,64},{96,112},{112,96},{1... | collective-permute-start | bytes 491528 | tf_op jit(solution)/shard_map/ppermute | solution.py:40
  31.6 1.8 %collective-permute-start.12 = (bf16[128,640]{1,0:T(8,128)(2,1)S(1)}, bf16[128,640]{1,0:T(8,128)(2,1)S(1)}, u32[]{:S(2)}, u32[]{:S(2)}) collective-permute-start(bf16[128,640]{1,0:T(8,128)(2,1)S(1)} %collective-permute-done.10.refs_4_), channel_id=1, source_target_pairs={{0,16},{16,0},{32,48},{48,32},{64,80},{80,64},{96,112},{112,96},{1... | collective-permute-start | bytes 491528 | tf_op jit(solution)/shard_map/ppermute | solution.py:40
  31.7 1.5 %collective-permute-start.8 = (bf16[16,2176]{1,0:T(8,128)(2,1)S(1)}, bf16[16,2176]{1,0:T(8,128)(2,1)S(1)}, u32[]{:S(2)}, u32[]{:S(2)}) collective-permute-start(bf16[16,2176]{1,0:T(8,128)(2,1)S(1)} %pad_maximum_fusion.3.refs_1_), channel_id=1, source_target_pairs={{0,16},{16,0},{32,48},{48,32},{64,80},{80,64},{96,112},{112,96},{1... | collective-permute-start | bytes 208904 | tf_op jit(solution)/shard_map/ppermute | solution.py:40
  32.1 1.3 %collective-permute-start.9 = (bf16[16,2176]{1,0:T(8,128)(2,1)S(1)}, bf16[16,2176]{1,0:T(8,128)(2,1)S(1)}, u32[]{:S(2)}, u32[]{:S(2)}) collective-permute-start(bf16[16,2176]{1,0:T(8,128)(2,1)S(1)} %collective-permute-done.2.refs_4_), channel_id=1, source_target_pairs={{0,16},{16,0},{32,48},{48,32},{64,80},{80,64},{96,112},{112,96},{1... | collective-permute-start | bytes 208904 | tf_op jit(solution)/shard_map/ppermute | solution.py:40
  34.7 7.6 %collective-permute-start.13 = (bf16[32,2048]{1,0:T(8,128)(2,1)S(1)}, bf16[32,2048]{1,0:T(8,128)(2,1)S(1)}, u32[]{:S(2)}, u32[]{:S(2)}) collective-permute-start(bf16[32,2048]{1,0:T(8,128)(2,1)S(1)} %get-tuple-element.46), channel_id=1, source_target_pairs={{0,7},{1,0},{2,1},{3,2},{4,3},{5,4},{6,5},{7,6},{8,15},{9,8},{10,9... | collective-permute-start | bytes 393224 | tf_op jit(solution)/shard_map/ppermute | solution.py:44
  35.7 6.6 %collective-permute-start.14 = (bf16[32,2048]{1,0:T(8,128)(2,1)S(1)}, bf16[32,2048]{1,0:T(8,128)(2,1)S(1)}, u32[]{:S(2)}, u32[]{:S(2)}) collective-permute-start(bf16[32,2048]{1,0:T(8,128)(2,1)S(1)} %get-tuple-element.47), channel_id=1, source_target_pairs={{0,1},{1,2},{2,3},{3,4},{4,5},{5,6},{6,7},{7,0},{8,9},{9,10},{10,1... | collective-permute-start | bytes 393224 | tf_op jit(solution)/shard_map/ppermute | solution.py:44
  36.8 8.5 %collective-permute-start.15 = (bf16[32,2048]{1,0:T(8,128)(2,1)S(1)}, bf16[32,2048]{1,0:T(8,128)(2,1)S(1)}, u32[]{:S(2)}, u32[]{:S(2)}) collective-permute-start(bf16[32,2048]{1,0:T(8,128)(2,1)S(1)} %get-tuple-element.48), channel_id=1, source_target_pairs={{0,2},{1,3},{2,4},{3,5},{4,6},{5,7},{6,0},{7,1},{8,10},{9,11},{10,... | collective-permute-start | bytes 393224 | tf_op jit(solution)/shard_map/ppermute | solution.py:310
  45.9 6.8 %collective-permute-start.16 = (bf16[32,2048]{1,0:T(8,128)(2,1)S(1)}, bf16[32,2048]{1,0:T(8,128)(2,1)S(1)}, u32[]{:S(2)}, u32[]{:S(2)}) collective-permute-start(bf16[32,2048]{1,0:T(8,128)(2,1)S(1)} %get-tuple-element.53), channel_id=1, source_target_pairs={{0,8},{1,9},{2,10},{3,11},{4,12},{5,13},{6,14},{7,15},{8,0},{9,1},... | collective-permute-start | bytes 393224 | tf_op jit(solution)/shard_map/ppermute | solution.py:44
  48.8 3.8 %collective-permute-start.17 = (bf16[32,2048]{1,0:T(8,128)(2,1)S(1)}, bf16[32,2048]{1,0:T(8,128)(2,1)S(1)}, u32[]{:S(2)}, u32[]{:S(2)}) collective-permute-start(bf16[32,2048]{1,0:T(8,128)(2,1)S(1)} %get-tuple-element.53), channel_id=1, source_target_pairs={{0,16},{16,0},{32,48},{48,32},{64,80},{80,64},{96,112},{112,96},{1... | collective-permute-start | bytes 393224 | tf_op jit(solution)/shard_map/ppermute | solution.py:40
  48.9 6.7 %collective-permute-start.18 = (bf16[32,2048]{1,0:T(8,128)(2,1)S(1)}, bf16[32,2048]{1,0:T(8,128)(2,1)S(1)}, u32[]{:S(2)}, u32[]{:S(2)}) collective-permute-start(bf16[32,2048]{1,0:T(8,128)(2,1)S(1)} %get-tuple-element.53), channel_id=1, source_target_pairs={{0,24},{1,25},{2,26},{3,27},{4,28},{5,29},{6,30},{7,31},{8,16},{9,... | collective-permute-start | bytes 393224 | tf_op jit(solution)/shard_map/ppermute | solution.py:310
  56.3 10.4 %collective-permute-start.20 = (bf16[64,2176]{1,0:T(8,128)(2,1)S(1)}, bf16[64,2176]{1,0:T(8,128)(2,1)S(1)}, u32[]{:S(2)}, u32[]{:S(2)}) collective-permute-start(bf16[64,2176]{1,0:T(8,128)(2,1)S(1)} %get-tuple-element.55.refs_1_), channel_id=1, source_target_pairs={{0,2},{1,3},{2,4},{3,5},{4,6},{5,7},{6,0},{7,1},{8,10},{9,11},{10,... | collective-permute-start | bytes 835592 | tf_op jit(solution)/shard_map/ppermute | solution.py:310
  57.4 9.8 %collective-permute-start.19 = (bf16[64,2176]{1,0:T(8,128)(2,1)S(1)}, bf16[64,2176]{1,0:T(8,128)(2,1)S(1)}, u32[]{:S(2)}, u32[]{:S(2)}) collective-permute-start(bf16[64,2176]{1,0:T(8,128)(2,1)S(1)} %get-tuple-element.55.refs_1_), channel_id=1, source_target_pairs={{0,1},{1,2},{2,3},{3,4},{4,5},{5,6},{6,7},{7,0},{8,9},{9,10},{10,1... | collective-permute-start | bytes 835592 | tf_op jit(solution)/shard_map/ppermute | solution.py:310
  66.7 13.0 %collective-permute-start.22 = (bf16[64,2176]{1,0:T(8,128)(2,1)S(1)}, bf16[64,2176]{1,0:T(8,128)(2,1)S(1)}, u32[]{:S(2)}, u32[]{:S(2)}) collective-permute-start(bf16[64,2176]{1,0:T(8,128)(2,1)S(1)} %collective-permute-done.20.refs_5_), channel_id=1, source_target_pairs={{0,1},{1,2},{2,3},{3,4},{4,5},{5,6},{6,7},{7,0},{8,9},{9,10},{10,1... | collective-permute-start | bytes 835592 | tf_op jit(solution)/shard_map/ppermute | solution.py:310
  69.5 13.3 %collective-permute-start.21 = (bf16[80,2048]{1,0:T(8,128)(2,1)S(1)}, bf16[80,2048]{1,0:T(8,128)(2,1)S(1)}, u32[]{:S(2)}, u32[]{:S(2)}) collective-permute-start(bf16[80,2048]{1,0:T(8,128)(2,1)S(1)} %get-tuple-element.59), channel_id=1, source_target_pairs={{0,8},{1,9},{2,10},{3,11},{4,12},{5,13},{6,14},{7,15},{8,0},{9,1},... | collective-permute-start | bytes 983048 | tf_op jit(solution)/shard_map/ppermute | solution.py:44
  72.3 7.3 %collective-permute-start.23 = (bf16[32,2176]{1,0:T(8,128)(2,1)S(1)}, bf16[32,2176]{1,0:T(8,128)(2,1)S(1)}, u32[]{:S(2)}, u32[]{:S(2)}) collective-permute-start(bf16[32,2176]{1,0:T(8,128)(2,1)S(1)} %slice.75), channel_id=1, source_target_pairs={{0,2},{1,3},{2,4},{3,5},{4,6},{5,7},{6,0},{7,1},{8,10},{9,11},{10,... | collective-permute-start | bytes 417800 | tf_op jit(solution)/shard_map/ppermute | solution.py:310
  81.9 10.5 %collective-permute-start.24 = (bf16[48,2048]{1,0:T(8,128)(2,1)S(1)}, bf16[48,2048]{1,0:T(8,128)(2,1)S(1)}, u32[]{:S(2)}, u32[]{:S(2)}) collective-permute-start(bf16[48,2048]{1,0:T(8,128)(2,1)S(1)} %get-tuple-element.62), channel_id=1, source_target_pairs={{0,8},{1,9},{2,10},{3,11},{4,12},{5,13},{6,14},{7,15},{8,0},{9,1},... | collective-permute-start | bytes 589832 | tf_op jit(solution)/shard_map/ppermute | solution.py:44
  83.5 8.9 %collective-permute-start.25 = (bf16[32,2048]{1,0:T(8,128)(2,1)S(1)}, bf16[32,2048]{1,0:T(8,128)(2,1)S(1)}, u32[]{:S(2)}, u32[]{:S(2)}) collective-permute-start(bf16[32,2048]{1,0:T(8,128)(2,1)S(1)} %get-tuple-element.63), channel_id=1, source_target_pairs={{0,7},{1,0},{2,1},{3,2},{4,3},{5,4},{6,5},{7,6},{8,15},{9,8},{10,9... | collective-permute-start | bytes 393224 | tf_op jit(solution)/shard_map/ppermute | solution.py:310
  88.5 8.9 %collective-permute-start.27 = (bf16[32,2048]{1,0:T(8,128)(2,1)S(1)}, bf16[32,2048]{1,0:T(8,128)(2,1)S(1)}, u32[]{:S(2)}, u32[]{:S(2)}) collective-permute-start(bf16[32,2048]{1,0:T(8,128)(2,1)S(1)} %get-tuple-element.67), channel_id=1, source_target_pairs={{0,6},{1,7},{2,0},{3,1},{4,2},{5,3},{6,4},{7,5},{8,14},{9,15},{10,... | collective-permute-start | bytes 393224 | tf_op jit(solution)/shard_map/ppermute | solution.py:310
  93.0 11.6 %collective-permute-start.28 = (bf16[32,2048]{1,0:T(8,128)(2,1)S(1)}, bf16[32,2048]{1,0:T(8,128)(2,1)S(1)}, u32[]{:S(2)}, u32[]{:S(2)}) collective-permute-start(bf16[32,2048]{1,0:T(8,128)(2,1)S(1)} %get-tuple-element.68), channel_id=1, source_target_pairs={{0,5},{1,6},{2,7},{3,0},{4,1},{5,2},{6,3},{7,4},{8,13},{9,14},{10,... | collective-permute-start | bytes 393224 | tf_op jit(solution)/shard_map/ppermute | solution.py:310
  94.0 9.2 %collective-permute-start.26 = (bf16[16,2048]{1,0:T(8,128)(2,1)S(1)}, bf16[16,2048]{1,0:T(8,128)(2,1)S(1)}, u32[]{:S(2)}, u32[]{:S(2)}) collective-permute-start(bf16[16,2048]{1,0:T(8,128)(2,1)S(1)} %get-tuple-element.65), channel_id=1, source_target_pairs={{0,4},{1,5},{2,6},{3,7},{4,0},{5,1},{6,2},{7,3},{8,12},{9,13},{10,... | collective-permute-start | bytes 196616 | tf_op jit(solution)/shard_map/ppermute | solution.py:44
  105.2 1.3 %collective-permute-start.29 = (bf16[16,2048]{1,0:T(8,128)(2,1)S(1)}, bf16[16,2048]{1,0:T(8,128)(2,1)S(1)}, u32[]{:S(2)}, u32[]{:S(2)}) collective-permute-start(bf16[16,2048]{1,0:T(8,128)(2,1)S(1)} %get-tuple-element.70), channel_id=1, source_target_pairs={{0,16},{16,0},{32,48},{48,32},{64,80},{80,64},{96,112},{112,96},{1... | collective-permute-start | bytes 196616 | tf_op jit(solution)/shard_map/ppermute | solution.py:40
  (4 other events, 90.7 us)

commit v7 on v6

--- a/solution.py
+++ b/solution.py
@@ -431,7 +431,6 @@
     sum_1, sum_2, own_sum = run_join(place, keep, got, [half, half, struct((16, D), F32)])
     back_1 = on_both(sum_1, by_core(-1))
     back_2 = on_both(sum_2, by_core(-2))
-    got_far, back_1 = after(got_far, back_1)
     sum_3, sum_4 = run_join(place, keep_far, got_far, [half, struct((16, D), BF16)])
     back_3 = on_both(sum_3, by_core(-3))
     back_4 = on_exp(sum_4, z_shift(4))

time: 109 us -> 106 us (0.972)
  starting transfers between devices: 43.8 us -> 39.7 us
  waiting for transfers between devices: 42.6 us -> 43.8 us
    ppermute x8, waiting for transfers between devices: 14.5 us -> 21.1 us  [on_exp(): return lax.ppermute(block, 'exp', route)]
    ppermute x9, waiting for transfers between devices: 22.6 us -> 17.3 us  [on_both(): return lax.ppermute(block, ('ctx', 'exp'), route)]
    ppermute x8, starting transfers between devices: 21.6 us -> 18.5 us  [on_exp(): return lax.ppermute(block, 'exp', route)]
  transfers between devices with their start and end apart: 30 -> 30, of which waited for: 16 -> 15; matrix products, arithmetic and copies ran while one was open for 4% -> 5% of each run, Pallas kernels for 8% -> 9%
where the time goes in v7:
time: 106 us; the launch traced here: 105 us
  waiting for transfers between devices  43.8 us (41%)
  starting transfers between devices  39.7 us (37%)
  Pallas kernels  13.5 us (13%)
  local copies, waits for them, and re-layouts  5.76 us (5%)
  other arithmetic  1.92 us (2%)
    ppermute x8, waiting for transfers between devices, on_exp(): return lax.ppermute(block, 'exp', route)  21.1 us
    ppermute x8, starting transfers between devices, on_exp(): return lax.ppermute(block, 'exp', route)  18.5 us
    ppermute x9, waiting for transfers between devices, on_both(): return lax.ppermute(block, ('ctx', 'exp'), route)  17.3 us
    pallas_call x11, Pallas kernels, kernel_call(): pl.pallas_call(whole, out_shape=out_shapes, in_specs=[pl.BlockSpec(memory...  13.5 us
    ppermute x9, starting transfers between devices, on_both(): return lax.ppermute(block, ('ctx', 'exp'), route)  12.6 us
    ppermute x13, starting transfers between devices, on_ctx(): return lax.ppermute(block, 'ctx', route)  8.63 us
    ppermute x13, waiting for transfers between devices, on_ctx(): return lax.ppermute(block, 'ctx', route)  5.47 us
  transfers between devices with their start and end apart: 30, of which 15 were waited for; matrix products, arithmetic and copies ran while one was open for 5% of the time, Pallas kernels for 9%

profile of v7, /device:TPU:32, one launch (start us, length us, event | category | flops | bytes accessed | tf_op | source)
XLA Modules:
  0.0 104.9 jit_solution(15353069663336449997)
XLA Ops:
  1.0 1.7 %collective-permute-start = (bf16[256,256]{1,0:T(8,128)(2,1)S(1)}, bf16[256,256]{1,0:T(8,128)(2,1)S(1)}, u32[]{:S(2)}, u32[]{:S(2)}) collective-permute-start(bf16[256,256]{1,0:T(8,128)(2,1)S(1)} %pad_maximum_fusion.2), channel_id=1, source_target_pairs={{0,128},{16,144},{32,160},{48,176},{64,192},{80,208},{96,224},{112... | collective-permute-start | bytes 393224 | tf_op jit(solution)/shard_map/ppermute | solution.py:40
  4.4 6.4 %collective-permute-start.1 = (bf16[128,640]{1,0:T(8,128)(2,1)S(1)}, bf16[128,640]{1,0:T(8,128)(2,1)S(1)}, u32[]{:S(2)}, u32[]{:S(2)}) collective-permute-start(bf16[128,640]{1,0:T(8,128)(2,1)S(1)} %pad_maximum_fusion.1), channel_id=1, source_target_pairs={{0,4},{1,5},{2,6},{3,7},{4,0},{5,1},{6,2},{7,3},{8,12},{9,13},{10,... | collective-permute-start | bytes 491528 | tf_op jit(solution)/shard_map/ppermute | solution.py:44
  12.9 1.6 %collective-permute-start.4 = (bf16[512,256]{1,0:T(8,128)(2,1)S(1)}, bf16[512,256]{1,0:T(8,128)(2,1)S(1)}, u32[]{:S(2)}, u32[]{:S(2)}) collective-permute-start(bf16[512,256]{1,0:T(8,128)(2,1)S(1)} %pad_maximum_fusion.refs_3_), channel_id=1, source_target_pairs={{0,32},{16,48},{32,64},{48,80},{64,96},{80,112},{96,0},{112,16},{1... | collective-permute-start | bytes 786440 | tf_op jit(solution)/shard_map/ppermute | solution.py:40
  14.5 1.7 %collective-permute-start.5 = (bf16[512,256]{1,0:T(8,128)(2,1)S(1)}, bf16[512,256]{1,0:T(8,128)(2,1)S(1)}, u32[]{:S(2)}, u32[]{:S(2)}) collective-permute-start(bf16[512,256]{1,0:T(8,128)(2,1)S(1)} %pad_maximum_fusion.refs_3_), channel_id=1, source_target_pairs={{0,96},{16,112},{32,0},{48,16},{64,32},{80,48},{96,64},{112,80},{1... | collective-permute-start | bytes 786440 | tf_op jit(solution)/shard_map/ppermute | solution.py:40
  16.3 1.8 %collective-permute-start.6 = (bf16[512,256]{1,0:T(8,128)(2,1)S(1)}, bf16[512,256]{1,0:T(8,128)(2,1)S(1)}, u32[]{:S(2)}, u32[]{:S(2)}) collective-permute-start(bf16[512,256]{1,0:T(8,128)(2,1)S(1)} %pad_maximum_fusion.refs_3_), channel_id=1, source_target_pairs={{0,64},{16,80},{32,96},{48,112},{64,0},{80,16},{96,32},{112,48},{1... | collective-permute-start | bytes 786440 | tf_op jit(solution)/shard_map/ppermute | solution.py:40
  18.9 2.9 %collective-permute-start.2 = (bf16[16,2176]{1,0:T(8,128)(2,1)S(1)}, bf16[16,2176]{1,0:T(8,128)(2,1)S(1)}, u32[]{:S(2)}, u32[]{:S(2)}) collective-permute-start(bf16[16,2176]{1,0:T(8,128)(2,1)S(1)} %pad_maximum_fusion.3.refs_1_), channel_id=1, source_target_pairs={{0,8},{1,9},{2,10},{3,11},{4,12},{5,13},{6,14},{7,15},{8,0},{9,1},... | collective-permute-start | bytes 208904 | tf_op jit(solution)/shard_map/ppermute | solution.py:44
  21.9 2.8 %collective-permute-done.2.refs_4_ = bf16[16,2176]{1,0:T(8,128)(2,1)S(1)} collective-permute-done((bf16[16,2176]{1,0:T(8,128)(2,1)S(1)}, bf16[16,2176]{1,0:T(8,128)(2,1)S(1)}, u32[]{:S(2)}, u32[]{:S(2)}) %collective-permute-start.2) | collective-permute-done | bytes 69664 | tf_op jit(solution)/shard_map/ppermute | solution.py:44
  25.3 1.4 %collective-permute-done.5.refs_5_ = bf16[512,256]{1,0:T(8,128)(2,1)S(1)} collective-permute-done((bf16[512,256]{1,0:T(8,128)(2,1)S(1)}, bf16[512,256]{1,0:T(8,128)(2,1)S(1)}, u32[]{:S(2)}, u32[]{:S(2)}) %collective-permute-start.5) | collective-permute-done | bytes 262176 | tf_op jit(solution)/shard_map/ppermute | solution.py:40
  26.6 1.7 %collective-permute-done.6.refs_6_ = bf16[512,256]{1,0:T(8,128)(2,1)S(1)} collective-permute-done((bf16[512,256]{1,0:T(8,128)(2,1)S(1)}, bf16[512,256]{1,0:T(8,128)(2,1)S(1)}, u32[]{:S(2)}, u32[]{:S(2)}) %collective-permute-start.6) | collective-permute-done | bytes 262176 | tf_op jit(solution)/shard_map/ppermute | solution.py:40
  28.3 2.7 %shard_map.109 = (f32[256,256]{1,0:T(8,128)S(1)}, f32[256,256]{1,0:T(8,128)S(1)}) custom-call(s32[4]{0:T(128)S(1)} %pad_add_fusion.refs_0_, bf16[256,128]{1,0:T(8,128)(2,1)S(1)} %pad_maximum_fusion.4.refs_1_, bf16[256,128]{1,0:T(8,128)(2,1)S(1)} %collective-permute-done.3.refs_2_, bf16[512,256]{1,0:T(8,128)(2,1)S(1)} %pad_maximum_fusion.refs_3_, ...), custom_call_target="tpu_custom_call" | custom-call | flops 536870912 | bytes 1179648 | tf_op jit(solution)/shard_map/pallas_call | solution.py:71
  33.4 1.3 %shard_map.110 = (f32[32,2048]{1,0:T(8,128)S(1)}, bf16[32,2048]{1,0:T(8,128)(2,1)S(1)}, bf16[32,2048]{1,0:T(8,128)(2,1)S(1)}, bf16[32,2048]{1,0:T(8,128)(2,1)S(1)}) custom-call(s32[4]{0:T(128)S(1)} %pad_add_fusion.refs_0_, f32[256,256]{1,0:T(8,128)S(1)} %get-tuple-element.39.refs_1_, f32[256,256]{1,0:T(8,128)S(1)} %collective-permute-done.7.refs_2_, ...), custom_call_target="tpu_custom_call" | custom-call | flops 134217728 | bytes 1703936 | tf_op jit(solution)/shard_map/pallas_call | solution.py:71
  36.8 2.7 %collective-permute-start.15 = (bf16[32,2048]{1,0:T(8,128)(2,1)S(1)}, bf16[32,2048]{1,0:T(8,128)(2,1)S(1)}, u32[]{:S(2)}, u32[]{:S(2)}) collective-permute-start(bf16[32,2048]{1,0:T(8,128)(2,1)S(1)} %get-tuple-element.46), channel_id=1, source_target_pairs={{0,2},{1,3},{2,4},{3,5},{4,6},{5,7},{6,0},{7,1},{8,10},{9,11},{10,... | collective-permute-start | bytes 393224 | tf_op jit(solution)/shard_map/ppermute | solution.py:310
  39.5 2.8 %collective-permute-done.13.refs_2_ = bf16[32,2048]{1,0:T(8,128)(2,1)S(1)} collective-permute-done((bf16[32,2048]{1,0:T(8,128)(2,1)S(1)}, bf16[32,2048]{1,0:T(8,128)(2,1)S(1)}, u32[]{:S(2)}, u32[]{:S(2)}) %collective-permute-start.13) | collective-permute-done | bytes 131104 | tf_op jit(solution)/shard_map/ppermute | solution.py:44
  42.3 3.0 %collective-permute-done.15.refs_4_ = bf16[32,2048]{1,0:T(8,128)(2,1)S(1)} collective-permute-done((bf16[32,2048]{1,0:T(8,128)(2,1)S(1)}, bf16[32,2048]{1,0:T(8,128)(2,1)S(1)}, u32[]{:S(2)}, u32[]{:S(2)}) %collective-permute-start.15) | collective-permute-done | bytes 131104 | tf_op jit(solution)/shard_map/ppermute | solution.py:310
  45.8 3.0 %collective-permute-start.16 = (bf16[32,2048]{1,0:T(8,128)(2,1)S(1)}, bf16[32,2048]{1,0:T(8,128)(2,1)S(1)}, u32[]{:S(2)}, u32[]{:S(2)}) collective-permute-start(bf16[32,2048]{1,0:T(8,128)(2,1)S(1)} %get-tuple-element.51), channel_id=1, source_target_pairs={{0,8},{1,9},{2,10},{3,11},{4,12},{5,13},{6,14},{7,15},{8,0},{9,1},... | collective-permute-start | bytes 393224 | tf_op jit(solution)/shard_map/ppermute | solution.py:44
  49.6 3.1 %collective-permute-done.16.refs_7_ = bf16[32,2048]{1,0:T(8,128)(2,1)S(1)} collective-permute-done((bf16[32,2048]{1,0:T(8,128)(2,1)S(1)}, bf16[32,2048]{1,0:T(8,128)(2,1)S(1)}, u32[]{:S(2)}, u32[]{:S(2)}) %collective-permute-start.16) | collective-permute-done | bytes 131104 | tf_op jit(solution)/shard_map/ppermute | solution.py:44
  52.7 2.8 %collective-permute-done.18.refs_9_ = bf16[32,2048]{1,0:T(8,128)(2,1)S(1)} collective-permute-done((bf16[32,2048]{1,0:T(8,128)(2,1)S(1)}, bf16[32,2048]{1,0:T(8,128)(2,1)S(1)}, u32[]{:S(2)}, u32[]{:S(2)}) %collective-permute-start.18) | collective-permute-done | bytes 131104 | tf_op jit(solution)/shard_map/ppermute | solution.py:310
  58.5 1.9 %copy-done.2 = bf16[1,768,2048]{2,1,0:T(8,128)(2,1)S(1)} copy-done((bf16[1,768,2048]{2,1,0:T(8,128)(2,1)S(1)}, bf16[1,768,2048]{2,1,0:T(8,128)(2,1)}, u32[]{:S(2)}) %copy-start.2) | copy-done | bytes 3145752
  61.0 5.7 %collective-permute-done.20.refs_5_ = bf16[64,2176]{1,0:T(8,128)(2,1)S(1)} collective-permute-done((bf16[64,2176]{1,0:T(8,128)(2,1)S(1)}, bf16[64,2176]{1,0:T(8,128)(2,1)S(1)}, u32[]{:S(2)}, u32[]{:S(2)}) %collective-permute-start.20) | collective-permute-done | bytes 278560 | tf_op jit(solution)/shard_map/ppermute | solution.py:310
  66.7 3.7 %collective-permute-start.23 = (bf16[32,2176]{1,0:T(8,128)(2,1)S(1)}, bf16[32,2176]{1,0:T(8,128)(2,1)S(1)}, u32[]{:S(2)}, u32[]{:S(2)}) collective-permute-start(bf16[32,2176]{1,0:T(8,128)(2,1)S(1)} %slice.75), channel_id=1, source_target_pairs={{0,2},{1,3},{2,4},{3,5},{4,6},{5,7},{6,0},{7,1},{8,10},{9,11},{10,... | collective-permute-start | bytes 417800 | tf_op jit(solution)/shard_map/ppermute | solution.py:310
  70.4 2.3 %shard_map.114 = (f32[80,2048]{1,0:T(8,128)S(1)}, bf16[80,2048]{1,0:T(8,128)(2,1)S(1)}) custom-call(s32[4]{0:T(128)S(1)} %pad_add_fusion.refs_0_, bf16[2048,768]{1,0:T(8,128)(2,1)S(1)} %bitcast.43, bf16[2048,768]{1,0:T(8,128)(2,1)S(1)} %bitcast.46, bf16[768,2048]{1,0:T(8,128)(2,1)S(1)} %bitcast.49, bf16[64,2176]{1,0:T(8,128)(2,1)S(1)} %collective-permute-done.19.refs_4_, ...), custom_call_target="tpu_custom_call" | custom-call | flops 1509949440 | bytes 10133504 | tf_op jit(solution)/shard_map/pallas_call | solution.py:71
  72.8 5.8 %collective-permute-done.23.refs_5_ = bf16[32,2176]{1,0:T(8,128)(2,1)S(1)} collective-permute-done((bf16[32,2176]{1,0:T(8,128)(2,1)S(1)}, bf16[32,2176]{1,0:T(8,128)(2,1)S(1)}, u32[]{:S(2)}, u32[]{:S(2)}) %collective-permute-start.23) | collective-permute-done | bytes 139296 | tf_op jit(solution)/shard_map/ppermute | solution.py:310
  78.6 2.3 %shard_map.116 = (f32[48,2048]{1,0:T(8,128)S(1)}, bf16[48,2048]{1,0:T(8,128)(2,1)S(1)}) custom-call(s32[4]{0:T(128)S(1)} %pad_add_fusion.refs_0_, bf16[2048,768]{1,0:T(8,128)(2,1)S(1)} %bitcast.44, bf16[2048,768]{1,0:T(8,128)(2,1)S(1)} %bitcast.47, bf16[768,2048]{1,0:T(8,128)(2,1)S(1)} %bitcast.50, bf16[64,2176]{1,0:T(8,128)(2,1)S(1)} %collective-permute-done.22.refs_4_, ...), custom_call_target="tpu_custom_call" | custom-call | flops 905969664 | bytes 9854976 | tf_op jit(solution)/shard_map/pallas_call | solution.py:71
  80.9 1.4 %collective-permute-start.24 = (bf16[48,2048]{1,0:T(8,128)(2,1)S(1)}, bf16[48,2048]{1,0:T(8,128)(2,1)S(1)}, u32[]{:S(2)}, u32[]{:S(2)}) collective-permute-start(bf16[48,2048]{1,0:T(8,128)(2,1)S(1)} %get-tuple-element.60), channel_id=1, source_target_pairs={{0,8},{1,9},{2,10},{3,11},{4,12},{5,13},{6,14},{7,15},{8,0},{9,1},... | collective-permute-start | bytes 589832 | tf_op jit(solution)/shard_map/ppermute | solution.py:44
  82.2 1.7 %collective-permute-done.21.refs_2_ = bf16[80,2048]{1,0:T(8,128)(2,1)S(1)} collective-permute-done((bf16[80,2048]{1,0:T(8,128)(2,1)S(1)}, bf16[80,2048]{1,0:T(8,128)(2,1)S(1)}, u32[]{:S(2)}, u32[]{:S(2)}) %collective-permute-start.21) | collective-permute-done | bytes 327712 | tf_op jit(solution)/shard_map/ppermute | solution.py:44
  84.7 1.6 %collective-permute-start.27 = (bf16[32,2048]{1,0:T(8,128)(2,1)S(1)}, bf16[32,2048]{1,0:T(8,128)(2,1)S(1)}, u32[]{:S(2)}, u32[]{:S(2)}) collective-permute-start(bf16[32,2048]{1,0:T(8,128)(2,1)S(1)} %get-tuple-element.63), channel_id=1, source_target_pairs={{0,6},{1,7},{2,0},{3,1},{4,2},{5,3},{6,4},{7,5},{8,14},{9,15},{10,... | collective-permute-start | bytes 393224 | tf_op jit(solution)/shard_map/ppermute | solution.py:310
  86.3 1.9 %collective-permute-done.24.refs_2_ = bf16[48,2048]{1,0:T(8,128)(2,1)S(1)} collective-permute-done((bf16[48,2048]{1,0:T(8,128)(2,1)S(1)}, bf16[48,2048]{1,0:T(8,128)(2,1)S(1)}, u32[]{:S(2)}, u32[]{:S(2)}) %collective-permute-start.24) | collective-permute-done | bytes 196640 | tf_op jit(solution)/shard_map/ppermute | solution.py:44
  88.7 1.6 %collective-permute-start.28 = (bf16[32,2048]{1,0:T(8,128)(2,1)S(1)}, bf16[32,2048]{1,0:T(8,128)(2,1)S(1)}, u32[]{:S(2)}, u32[]{:S(2)}) collective-permute-start(bf16[32,2048]{1,0:T(8,128)(2,1)S(1)} %get-tuple-element.64), channel_id=1, source_target_pairs={{0,5},{1,6},{2,7},{3,0},{4,1},{5,2},{6,3},{7,4},{8,13},{9,14},{10,... | collective-permute-start | bytes 393224 | tf_op jit(solution)/shard_map/ppermute | solution.py:310
  90.3 2.7 %collective-permute-start.25 = (bf16[16,2048]{1,0:T(8,128)(2,1)S(1)}, bf16[16,2048]{1,0:T(8,128)(2,1)S(1)}, u32[]{:S(2)}, u32[]{:S(2)}) collective-permute-start(bf16[16,2048]{1,0:T(8,128)(2,1)S(1)} %get-tuple-element.61), channel_id=1, source_target_pairs={{0,4},{1,5},{2,6},{3,7},{4,0},{5,1},{6,2},{7,3},{8,12},{9,13},{10,... | collective-permute-start | bytes 196616 | tf_op jit(solution)/shard_map/ppermute | solution.py:44
  92.9 8.8 %collective-permute-done.25.refs_2_ = bf16[16,2048]{1,0:T(8,128)(2,1)S(1)} collective-permute-done((bf16[16,2048]{1,0:T(8,128)(2,1)S(1)}, bf16[16,2048]{1,0:T(8,128)(2,1)S(1)}, u32[]{:S(2)}, u32[]{:S(2)}) %collective-permute-start.25) | collective-permute-done | bytes 65568 | tf_op jit(solution)/shard_map/ppermute | solution.py:44
  102.5 1.2 %collective-permute-done.29.refs_3_ = bf16[16,2048]{1,0:T(8,128)(2,1)S(1)} collective-permute-done((bf16[16,2048]{1,0:T(8,128)(2,1)S(1)}, bf16[16,2048]{1,0:T(8,128)(2,1)S(1)}, u32[]{:S(2)}, u32[]{:S(2)}) %collective-permute-start.29) | collective-permute-done | bytes 65568 | tf_op jit(solution)/shard_map/ppermute | solution.py:40
  103.7 1.2 %shard_map.119 = bf16[16,2048]{1,0:T(8,128)(2,1)} custom-call(s32[4]{0:T(128)S(1)} %pad_add_fusion.refs_0_, bf16[32,2048]{1,0:T(8,128)(2,1)S(1)} %get-tuple-element.52.refs_1_, f32[16,2048]{1,0:T(8,128)S(1)} %get-tuple-element.65.refs_2_, bf16[16,2048]{1,0:T(8,128)(2,1)S(1)} %collective-permute-done.29.refs_3_), custom_call_target="tpu_custom_call" | custom-call | flops 98304 | bytes 327680 | tf_op jit(solution)/shard_map/pallas_call | solution.py:71
  (67 shorter events, 17.8 us)
Async XLA Ops:
  1.0 11.9 %collective-permute-start = (bf16[256,256]{1,0:T(8,128)(2,1)S(1)}, bf16[256,256]{1,0:T(8,128)(2,1)S(1)}, u32[]{:S(2)}, u32[]{:S(2)}) collective-permute-start(bf16[256,256]{1,0:T(8,128)(2,1)S(1)} %pad_maximum_fusion.2), channel_id=1, source_target_pairs={{0,128},{16,144},{32,160},{48,176},{64,192},{80,208},{96,224},{112... | collective-permute-start | bytes 393224 | tf_op jit(solution)/shard_map/ppermute | solution.py:40
  4.4 54.1 %copy-start.1 = (bf16[1,2048,768]{2,1,0:T(8,128)(2,1)S(1)}, bf16[1,2048,768]{2,1,0:T(8,128)(2,1)}, u32[]{:S(2)}) copy-start(bf16[1,2048,768]{2,1,0:T(8,128)(2,1)} %param.20) | copy-start | bytes 9437188
  4.4 54.1 %copy-start = (bf16[1,2048,768]{2,1,0:T(8,128)(2,1)S(1)}, bf16[1,2048,768]{2,1,0:T(8,128)(2,1)}, u32[]{:S(2)}) copy-start(bf16[1,2048,768]{2,1,0:T(8,128)(2,1)} %param.19) | copy-start | bytes 9437188
  4.4 17.4 %collective-permute-start.1 = (bf16[128,640]{1,0:T(8,128)(2,1)S(1)}, bf16[128,640]{1,0:T(8,128)(2,1)S(1)}, u32[]{:S(2)}, u32[]{:S(2)}) collective-permute-start(bf16[128,640]{1,0:T(8,128)(2,1)S(1)} %pad_maximum_fusion.1), channel_id=1, source_target_pairs={{0,4},{1,5},{2,6},{3,7},{4,0},{5,1},{6,2},{7,3},{8,12},{9,13},{10,... | collective-permute-start | bytes 491528 | tf_op jit(solution)/shard_map/ppermute | solution.py:44
  12.9 12.3 %collective-permute-start.4 = (bf16[512,256]{1,0:T(8,128)(2,1)S(1)}, bf16[512,256]{1,0:T(8,128)(2,1)S(1)}, u32[]{:S(2)}, u32[]{:S(2)}) collective-permute-start(bf16[512,256]{1,0:T(8,128)(2,1)S(1)} %pad_maximum_fusion.refs_3_), channel_id=1, source_target_pairs={{0,32},{16,48},{32,64},{48,80},{64,96},{80,112},{96,0},{112,16},{1... | collective-permute-start | bytes 786440 | tf_op jit(solution)/shard_map/ppermute | solution.py:40
  14.5 12.1 %collective-permute-start.5 = (bf16[512,256]{1,0:T(8,128)(2,1)S(1)}, bf16[512,256]{1,0:T(8,128)(2,1)S(1)}, u32[]{:S(2)}, u32[]{:S(2)}) collective-permute-start(bf16[512,256]{1,0:T(8,128)(2,1)S(1)} %pad_maximum_fusion.refs_3_), channel_id=1, source_target_pairs={{0,96},{16,112},{32,0},{48,16},{64,32},{80,48},{96,64},{112,80},{1... | collective-permute-start | bytes 786440 | tf_op jit(solution)/shard_map/ppermute | solution.py:40
  16.3 12.1 %collective-permute-start.6 = (bf16[512,256]{1,0:T(8,128)(2,1)S(1)}, bf16[512,256]{1,0:T(8,128)(2,1)S(1)}, u32[]{:S(2)}, u32[]{:S(2)}) collective-permute-start(bf16[512,256]{1,0:T(8,128)(2,1)S(1)} %pad_maximum_fusion.refs_3_), channel_id=1, source_target_pairs={{0,64},{16,80},{32,96},{48,112},{64,0},{80,16},{96,32},{112,48},{1... | collective-permute-start | bytes 786440 | tf_op jit(solution)/shard_map/ppermute | solution.py:40
  18.9 5.8 %collective-permute-start.2 = (bf16[16,2176]{1,0:T(8,128)(2,1)S(1)}, bf16[16,2176]{1,0:T(8,128)(2,1)S(1)}, u32[]{:S(2)}, u32[]{:S(2)}) collective-permute-start(bf16[16,2176]{1,0:T(8,128)(2,1)S(1)} %pad_maximum_fusion.3.refs_1_), channel_id=1, source_target_pairs={{0,8},{1,9},{2,10},{3,11},{4,12},{5,13},{6,14},{7,15},{8,0},{9,1},... | collective-permute-start | bytes 208904 | tf_op jit(solution)/shard_map/ppermute | solution.py:44
  21.8 3.4 %collective-permute-start.3 = (bf16[256,128]{1,0:T(8,128)(2,1)S(1)}, bf16[256,128]{1,0:T(8,128)(2,1)S(1)}, u32[]{:S(2)}, u32[]{:S(2)}) collective-permute-start(bf16[256,128]{1,0:T(8,128)(2,1)S(1)} %pad_maximum_fusion.4.refs_1_), channel_id=1, source_target_pairs={{0,16},{16,0},{32,48},{48,32},{64,80},{80,64},{96,112},{112,96},{1... | collective-permute-start | bytes 196616 | tf_op jit(solution)/shard_map/ppermute | solution.py:40
  24.7 6.8 %collective-permute-start.10 = (bf16[128,640]{1,0:T(8,128)(2,1)S(1)}, bf16[128,640]{1,0:T(8,128)(2,1)S(1)}, u32[]{:S(2)}, u32[]{:S(2)}) collective-permute-start(bf16[128,640]{1,0:T(8,128)(2,1)S(1)} %collective-permute-done.1.refs_3_), channel_id=1, source_target_pairs={{0,128},{16,144},{32,160},{48,176},{64,192},{80,208},{96,224},{112... | collective-permute-start | bytes 491528 | tf_op jit(solution)/shard_map/ppermute | solution.py:40
  31.0 2.4 %collective-permute-start.7 = (f32[256,256]{1,0:T(8,128)S(1)}, f32[256,256]{1,0:T(8,128)S(1)}, u32[]{:S(2)}, u32[]{:S(2)}) collective-permute-start(f32[256,256]{1,0:T(8,128)S(1)} %get-tuple-element.40), channel_id=1, source_target_pairs={{0,16},{16,0},{32,48},{48,32},{64,80},{80,64},{96,112},{112,96},{1... | collective-permute-start | bytes 786440 | tf_op jit(solution)/shard_map/ppermute | solution.py:40
  31.1 2.3 %collective-permute-start.11 = (bf16[128,640]{1,0:T(8,128)(2,1)S(1)}, bf16[128,640]{1,0:T(8,128)(2,1)S(1)}, u32[]{:S(2)}, u32[]{:S(2)}) collective-permute-start(bf16[128,640]{1,0:T(8,128)(2,1)S(1)} %collective-permute-done.1.refs_3_), channel_id=1, source_target_pairs={{0,16},{16,0},{32,48},{48,32},{64,80},{80,64},{96,112},{112,96},{1... | collective-permute-start | bytes 491528 | tf_op jit(solution)/shard_map/ppermute | solution.py:40
  31.6 1.8 %collective-permute-start.12 = (bf16[128,640]{1,0:T(8,128)(2,1)S(1)}, bf16[128,640]{1,0:T(8,128)(2,1)S(1)}, u32[]{:S(2)}, u32[]{:S(2)}) collective-permute-start(bf16[128,640]{1,0:T(8,128)(2,1)S(1)} %collective-permute-done.10.refs_4_), channel_id=1, source_target_pairs={{0,16},{16,0},{32,48},{48,32},{64,80},{80,64},{96,112},{112,96},{1... | collective-permute-start | bytes 491528 | tf_op jit(solution)/shard_map/ppermute | solution.py:40
  31.7 1.5 %collective-permute-start.8 = (bf16[16,2176]{1,0:T(8,128)(2,1)S(1)}, bf16[16,2176]{1,0:T(8,128)(2,1)S(1)}, u32[]{:S(2)}, u32[]{:S(2)}) collective-permute-start(bf16[16,2176]{1,0:T(8,128)(2,1)S(1)} %pad_maximum_fusion.3.refs_1_), channel_id=1, source_target_pairs={{0,16},{16,0},{32,48},{48,32},{64,80},{80,64},{96,112},{112,96},{1... | collective-permute-start | bytes 208904 | tf_op jit(solution)/shard_map/ppermute | solution.py:40
  32.1 1.3 %collective-permute-start.9 = (bf16[16,2176]{1,0:T(8,128)(2,1)S(1)}, bf16[16,2176]{1,0:T(8,128)(2,1)S(1)}, u32[]{:S(2)}, u32[]{:S(2)}) collective-permute-start(bf16[16,2176]{1,0:T(8,128)(2,1)S(1)} %collective-permute-done.2.refs_4_), channel_id=1, source_target_pairs={{0,16},{16,0},{32,48},{48,32},{64,80},{80,64},{96,112},{112,96},{1... | collective-permute-start | bytes 208904 | tf_op jit(solution)/shard_map/ppermute | solution.py:40
  34.7 7.6 %collective-permute-start.13 = (bf16[32,2048]{1,0:T(8,128)(2,1)S(1)}, bf16[32,2048]{1,0:T(8,128)(2,1)S(1)}, u32[]{:S(2)}, u32[]{:S(2)}) collective-permute-start(bf16[32,2048]{1,0:T(8,128)(2,1)S(1)} %get-tuple-element.44), channel_id=1, source_target_pairs={{0,7},{1,0},{2,1},{3,2},{4,3},{5,4},{6,5},{7,6},{8,15},{9,8},{10,9... | collective-permute-start | bytes 393224 | tf_op jit(solution)/shard_map/ppermute | solution.py:44
  35.7 6.5 %collective-permute-start.14 = (bf16[32,2048]{1,0:T(8,128)(2,1)S(1)}, bf16[32,2048]{1,0:T(8,128)(2,1)S(1)}, u32[]{:S(2)}, u32[]{:S(2)}) collective-permute-start(bf16[32,2048]{1,0:T(8,128)(2,1)S(1)} %get-tuple-element.45), channel_id=1, source_target_pairs={{0,1},{1,2},{2,3},{3,4},{4,5},{5,6},{6,7},{7,0},{8,9},{9,10},{10,1... | collective-permute-start | bytes 393224 | tf_op jit(solution)/shard_map/ppermute | solution.py:44
  36.8 8.5 %collective-permute-start.15 = (bf16[32,2048]{1,0:T(8,128)(2,1)S(1)}, bf16[32,2048]{1,0:T(8,128)(2,1)S(1)}, u32[]{:S(2)}, u32[]{:S(2)}) collective-permute-start(bf16[32,2048]{1,0:T(8,128)(2,1)S(1)} %get-tuple-element.46), channel_id=1, source_target_pairs={{0,2},{1,3},{2,4},{3,5},{4,6},{5,7},{6,0},{7,1},{8,10},{9,11},{10,... | collective-permute-start | bytes 393224 | tf_op jit(solution)/shard_map/ppermute | solution.py:310
  45.8 6.8 %collective-permute-start.16 = (bf16[32,2048]{1,0:T(8,128)(2,1)S(1)}, bf16[32,2048]{1,0:T(8,128)(2,1)S(1)}, u32[]{:S(2)}, u32[]{:S(2)}) collective-permute-start(bf16[32,2048]{1,0:T(8,128)(2,1)S(1)} %get-tuple-element.51), channel_id=1, source_target_pairs={{0,8},{1,9},{2,10},{3,11},{4,12},{5,13},{6,14},{7,15},{8,0},{9,1},... | collective-permute-start | bytes 393224 | tf_op jit(solution)/shard_map/ppermute | solution.py:44
  48.8 3.8 %collective-permute-start.17 = (bf16[32,2048]{1,0:T(8,128)(2,1)S(1)}, bf16[32,2048]{1,0:T(8,128)(2,1)S(1)}, u32[]{:S(2)}, u32[]{:S(2)}) collective-permute-start(bf16[32,2048]{1,0:T(8,128)(2,1)S(1)} %get-tuple-element.51), channel_id=1, source_target_pairs={{0,16},{16,0},{32,48},{48,32},{64,80},{80,64},{96,112},{112,96},{1... | collective-permute-start | bytes 393224 | tf_op jit(solution)/shard_map/ppermute | solution.py:40
  48.8 6.7 %collective-permute-start.18 = (bf16[32,2048]{1,0:T(8,128)(2,1)S(1)}, bf16[32,2048]{1,0:T(8,128)(2,1)S(1)}, u32[]{:S(2)}, u32[]{:S(2)}) collective-permute-start(bf16[32,2048]{1,0:T(8,128)(2,1)S(1)} %get-tuple-element.51), channel_id=1, source_target_pairs={{0,24},{1,25},{2,26},{3,27},{4,28},{5,29},{6,30},{7,31},{8,16},{9,... | collective-permute-start | bytes 393224 | tf_op jit(solution)/shard_map/ppermute | solution.py:310
  56.3 10.4 %collective-permute-start.20 = (bf16[64,2176]{1,0:T(8,128)(2,1)S(1)}, bf16[64,2176]{1,0:T(8,128)(2,1)S(1)}, u32[]{:S(2)}, u32[]{:S(2)}) collective-permute-start(bf16[64,2176]{1,0:T(8,128)(2,1)S(1)} %get-tuple-element.53.refs_1_), channel_id=1, source_target_pairs={{0,2},{1,3},{2,4},{3,5},{4,6},{5,7},{6,0},{7,1},{8,10},{9,11},{10,... | collective-permute-start | bytes 835592 | tf_op jit(solution)/shard_map/ppermute | solution.py:310
  57.4 13.0 %collective-permute-start.19 = (bf16[64,2176]{1,0:T(8,128)(2,1)S(1)}, bf16[64,2176]{1,0:T(8,128)(2,1)S(1)}, u32[]{:S(2)}, u32[]{:S(2)}) collective-permute-start(bf16[64,2176]{1,0:T(8,128)(2,1)S(1)} %get-tuple-element.53.refs_1_), channel_id=1, source_target_pairs={{0,1},{1,2},{2,3},{3,4},{4,5},{5,6},{6,7},{7,0},{8,9},{9,10},{10,1... | collective-permute-start | bytes 835592 | tf_op jit(solution)/shard_map/ppermute | solution.py:310
  66.7 11.9 %collective-permute-start.22 = (bf16[64,2176]{1,0:T(8,128)(2,1)S(1)}, bf16[64,2176]{1,0:T(8,128)(2,1)S(1)}, u32[]{:S(2)}, u32[]{:S(2)}) collective-permute-start(bf16[64,2176]{1,0:T(8,128)(2,1)S(1)} %collective-permute-done.20.refs_5_), channel_id=1, source_target_pairs={{0,1},{1,2},{2,3},{3,4},{4,5},{5,6},{6,7},{7,0},{8,9},{9,10},{10,1... | collective-permute-start | bytes 835592 | tf_op jit(solution)/shard_map/ppermute | solution.py:310
  66.7 11.9 %collective-permute-start.23 = (bf16[32,2176]{1,0:T(8,128)(2,1)S(1)}, bf16[32,2176]{1,0:T(8,128)(2,1)S(1)}, u32[]{:S(2)}, u32[]{:S(2)}) collective-permute-start(bf16[32,2176]{1,0:T(8,128)(2,1)S(1)} %slice.75), channel_id=1, source_target_pairs={{0,2},{1,3},{2,4},{3,5},{4,6},{5,7},{6,0},{7,1},{8,10},{9,11},{10,... | collective-permute-start | bytes 417800 | tf_op jit(solution)/shard_map/ppermute | solution.py:310
  72.7 11.2 %collective-permute-start.21 = (bf16[80,2048]{1,0:T(8,128)(2,1)S(1)}, bf16[80,2048]{1,0:T(8,128)(2,1)S(1)}, u32[]{:S(2)}, u32[]{:S(2)}) collective-permute-start(bf16[80,2048]{1,0:T(8,128)(2,1)S(1)} %get-tuple-element.57), channel_id=1, source_target_pairs={{0,8},{1,9},{2,10},{3,11},{4,12},{5,13},{6,14},{7,15},{8,0},{9,1},... | collective-permute-start | bytes 983048 | tf_op jit(solution)/shard_map/ppermute | solution.py:44
  80.9 7.3 %collective-permute-start.24 = (bf16[48,2048]{1,0:T(8,128)(2,1)S(1)}, bf16[48,2048]{1,0:T(8,128)(2,1)S(1)}, u32[]{:S(2)}, u32[]{:S(2)}) collective-permute-start(bf16[48,2048]{1,0:T(8,128)(2,1)S(1)} %get-tuple-element.60), channel_id=1, source_target_pairs={{0,8},{1,9},{2,10},{3,11},{4,12},{5,13},{6,14},{7,15},{8,0},{9,1},... | collective-permute-start | bytes 589832 | tf_op jit(solution)/shard_map/ppermute | solution.py:44
  84.6 8.4 %collective-permute-start.26 = (bf16[32,2048]{1,0:T(8,128)(2,1)S(1)}, bf16[32,2048]{1,0:T(8,128)(2,1)S(1)}, u32[]{:S(2)}, u32[]{:S(2)}) collective-permute-start(bf16[32,2048]{1,0:T(8,128)(2,1)S(1)} %get-tuple-element.62), channel_id=1, source_target_pairs={{0,7},{1,0},{2,1},{3,2},{4,3},{5,4},{6,5},{7,6},{8,15},{9,8},{10,9... | collective-permute-start | bytes 393224 | tf_op jit(solution)/shard_map/ppermute | solution.py:310
  84.7 8.3 %collective-permute-start.27 = (bf16[32,2048]{1,0:T(8,128)(2,1)S(1)}, bf16[32,2048]{1,0:T(8,128)(2,1)S(1)}, u32[]{:S(2)}, u32[]{:S(2)}) collective-permute-start(bf16[32,2048]{1,0:T(8,128)(2,1)S(1)} %get-tuple-element.63), channel_id=1, source_target_pairs={{0,6},{1,7},{2,0},{3,1},{4,2},{5,3},{6,4},{7,5},{8,14},{9,15},{10,... | collective-permute-start | bytes 393224 | tf_op jit(solution)/shard_map/ppermute | solution.py:310
  88.7 13.0 %collective-permute-start.28 = (bf16[32,2048]{1,0:T(8,128)(2,1)S(1)}, bf16[32,2048]{1,0:T(8,128)(2,1)S(1)}, u32[]{:S(2)}, u32[]{:S(2)}) collective-permute-start(bf16[32,2048]{1,0:T(8,128)(2,1)S(1)} %get-tuple-element.64), channel_id=1, source_target_pairs={{0,5},{1,6},{2,7},{3,0},{4,1},{5,2},{6,3},{7,4},{8,13},{9,14},{10,... | collective-permute-start | bytes 393224 | tf_op jit(solution)/shard_map/ppermute | solution.py:310
  90.3 11.5 %collective-permute-start.25 = (bf16[16,2048]{1,0:T(8,128)(2,1)S(1)}, bf16[16,2048]{1,0:T(8,128)(2,1)S(1)}, u32[]{:S(2)}, u32[]{:S(2)}) collective-permute-start(bf16[16,2048]{1,0:T(8,128)(2,1)S(1)} %get-tuple-element.61), channel_id=1, source_target_pairs={{0,4},{1,5},{2,6},{3,7},{4,0},{5,1},{6,2},{7,3},{8,12},{9,13},{10,... | collective-permute-start | bytes 196616 | tf_op jit(solution)/shard_map/ppermute | solution.py:44
  102.4 1.3 %collective-permute-start.29 = (bf16[16,2048]{1,0:T(8,128)(2,1)S(1)}, bf16[16,2048]{1,0:T(8,128)(2,1)S(1)}, u32[]{:S(2)}, u32[]{:S(2)}) collective-permute-start(bf16[16,2048]{1,0:T(8,128)(2,1)S(1)} %get-tuple-element.66), channel_id=1, source_target_pairs={{0,16},{16,0},{32,48},{48,32},{64,80},{80,64},{96,112},{112,96},{1... | collective-permute-start | bytes 196616 | tf_op jit(solution)/shard_map/ppermute | solution.py:40
  (4 other events, 93.8 us)

commit v8 on v7

--- a/solution.py
+++ b/solution.py
@@ -407,10 +407,12 @@
         [struct((32, D), F32), struct((32, D), BF16)],
         3 * 32 * D,
     )
+    sums_y = on_exp(send, Y_SWAP)
+    sums_others = [sums_y, on_ctx(send, CORE_SWAP), on_ctx(sums_y, CORE_SWAP)]
     hidden, round_0 = kernel_call(
         normalise,
         place,
-        [extended, sums, norm_gain.reshape(1, D), *extended_others, *to_three(send, send, send)],
+        [extended, sums, norm_gain.reshape(1, D), *extended_others, *sums_others],
         [],
         [struct((32, D), BF16), struct((64, D + 128), BF16)],
         16 * 32 * D,
@@ -418,8 +420,8 @@
 
     half = struct((32, D), BF16)
     w = [w_gate[0], w_up[0], w_down[0]]
+    round_2 = on_both(round_0, by_core(2))
     round_1 = on_both(round_0, by_core(1))
-    round_2 = on_both(round_0, by_core(2))
     (seen,) = kernel_call(
         early, place, [round_0], [], [struct((8, 128), BF16)], 8 * 128, idle=w
     )

time: 106 us -> 104 us (0.981)
  waiting for transfers between devices: 43.8 us -> 38.6 us
  starting transfers between devices: 39.7 us -> 43 us
    ppermute x9 -> x8, waiting for transfers between devices: 17.3 us -> 11.7 us  [on_both(): return lax.ppermute(block, ('ctx', 'exp'), route)]
    ppermute x8, starting transfers between devices: 18.5 us -> 23.2 us  [on_exp(): return lax.ppermute(block, 'exp', route)]
    ppermute x9 -> x8, starting transfers between devices: 12.6 us -> 11.2 us  [on_both(): return lax.ppermute(block, ('ctx', 'exp'), route)]
    ppermute x13 -> x14, waiting for transfers between devices: 5.47 us -> 6.79 us  [on_ctx(): return lax.ppermute(block, 'ctx', route)]
    ppermute x13 -> x14, starting transfers between devices: 8.63 us -> 8.63 us  [on_ctx(): return lax.ppermute(block, 'ctx', route)]
  transfers between devices with their start and end apart: 30 -> 30, of which waited for: 15 -> 14; matrix products, arithmetic and copies ran while one was open for 5% -> 5% of each run, Pallas kernels for 9% -> 9%
where the time goes in v8:
time: 104 us; the launch traced here: 103 us
  starting transfers between devices  43 us (41%)
  waiting for transfers between devices  38.6 us (37%)
  Pallas kernels  13.5 us (13%)
  local copies, waits for them, and re-layouts  5.76 us (6%)
  other arithmetic  1.92 us (2%)
    ppermute x8, starting transfers between devices, on_exp(): return lax.ppermute(block, 'exp', route)  23.2 us
    ppermute x8, waiting for transfers between devices, on_exp(): return lax.ppermute(block, 'exp', route)  20.1 us
    pallas_call x11, Pallas kernels, kernel_call(): pl.pallas_call(whole, out_shape=out_shapes, in_specs=[pl.BlockSpec(memory...  13.5 us
    ppermute x8, waiting for transfers between devices, on_both(): return lax.ppermute(block, ('ctx', 'exp'), route)  11.7 us
    ppermute x8, starting transfers between devices, on_both(): return lax.ppermute(block, ('ctx', 'exp'), route)  11.2 us
    ppermute x14, starting transfers between devices, on_ctx(): return lax.ppermute(block, 'ctx', route)  8.63 us
    ppermute x14, waiting for transfers between devices, on_ctx(): return lax.ppermute(block, 'ctx', route)  6.79 us
  transfers between devices with their start and end apart: 30, of which 14 were waited for; matrix products, arithmetic and copies ran while one was open for 5% of the time, Pallas kernels for 9%

profile of v8, /device:TPU:32, one launch (start us, length us, event | category | flops | bytes accessed | tf_op | source)
XLA Modules:
  0.0 103.0 jit_solution(4195931940231203314)
XLA Ops:
  1.0 1.7 %collective-permute-start = (bf16[256,256]{1,0:T(8,128)(2,1)S(1)}, bf16[256,256]{1,0:T(8,128)(2,1)S(1)}, u32[]{:S(2)}, u32[]{:S(2)}) collective-permute-start(bf16[256,256]{1,0:T(8,128)(2,1)S(1)} %pad_maximum_fusion.2), channel_id=1, source_target_pairs={{0,128},{16,144},{32,160},{48,176},{64,192},{80,208},{96,224},{112... | collective-permute-start | bytes 393224 | tf_op jit(solution)/shard_map/ppermute | solution.py:40
  4.4 6.4 %collective-permute-start.1 = (bf16[128,640]{1,0:T(8,128)(2,1)S(1)}, bf16[128,640]{1,0:T(8,128)(2,1)S(1)}, u32[]{:S(2)}, u32[]{:S(2)}) collective-permute-start(bf16[128,640]{1,0:T(8,128)(2,1)S(1)} %pad_maximum_fusion.1), channel_id=1, source_target_pairs={{0,4},{1,5},{2,6},{3,7},{4,0},{5,1},{6,2},{7,3},{8,12},{9,13},{10,... | collective-permute-start | bytes 491528 | tf_op jit(solution)/shard_map/ppermute | solution.py:44
  12.9 1.6 %collective-permute-start.4 = (bf16[512,256]{1,0:T(8,128)(2,1)S(1)}, bf16[512,256]{1,0:T(8,128)(2,1)S(1)}, u32[]{:S(2)}, u32[]{:S(2)}) collective-permute-start(bf16[512,256]{1,0:T(8,128)(2,1)S(1)} %pad_maximum_fusion.refs_3_), channel_id=1, source_target_pairs={{0,32},{16,48},{32,64},{48,80},{64,96},{80,112},{96,0},{112,16},{1... | collective-permute-start | bytes 786440 | tf_op jit(solution)/shard_map/ppermute | solution.py:40
  14.5 1.7 %collective-permute-start.5 = (bf16[512,256]{1,0:T(8,128)(2,1)S(1)}, bf16[512,256]{1,0:T(8,128)(2,1)S(1)}, u32[]{:S(2)}, u32[]{:S(2)}) collective-permute-start(bf16[512,256]{1,0:T(8,128)(2,1)S(1)} %pad_maximum_fusion.refs_3_), channel_id=1, source_target_pairs={{0,96},{16,112},{32,0},{48,16},{64,32},{80,48},{96,64},{112,80},{1... | collective-permute-start | bytes 786440 | tf_op jit(solution)/shard_map/ppermute | solution.py:40
  16.3 1.8 %collective-permute-start.6 = (bf16[512,256]{1,0:T(8,128)(2,1)S(1)}, bf16[512,256]{1,0:T(8,128)(2,1)S(1)}, u32[]{:S(2)}, u32[]{:S(2)}) collective-permute-start(bf16[512,256]{1,0:T(8,128)(2,1)S(1)} %pad_maximum_fusion.refs_3_), channel_id=1, source_target_pairs={{0,64},{16,80},{32,96},{48,112},{64,0},{80,16},{96,32},{112,48},{1... | collective-permute-start | bytes 786440 | tf_op jit(solution)/shard_map/ppermute | solution.py:40
  18.9 2.9 %collective-permute-start.2 = (bf16[16,2176]{1,0:T(8,128)(2,1)S(1)}, bf16[16,2176]{1,0:T(8,128)(2,1)S(1)}, u32[]{:S(2)}, u32[]{:S(2)}) collective-permute-start(bf16[16,2176]{1,0:T(8,128)(2,1)S(1)} %pad_maximum_fusion.3.refs_1_), channel_id=1, source_target_pairs={{0,8},{1,9},{2,10},{3,11},{4,12},{5,13},{6,14},{7,15},{8,0},{9,1},... | collective-permute-start | bytes 208904 | tf_op jit(solution)/shard_map/ppermute | solution.py:44
  21.9 2.8 %collective-permute-done.2.refs_4_ = bf16[16,2176]{1,0:T(8,128)(2,1)S(1)} collective-permute-done((bf16[16,2176]{1,0:T(8,128)(2,1)S(1)}, bf16[16,2176]{1,0:T(8,128)(2,1)S(1)}, u32[]{:S(2)}, u32[]{:S(2)}) %collective-permute-start.2) | collective-permute-done | bytes 69664 | tf_op jit(solution)/shard_map/ppermute | solution.py:44
  25.3 1.4 %collective-permute-done.5.refs_5_ = bf16[512,256]{1,0:T(8,128)(2,1)S(1)} collective-permute-done((bf16[512,256]{1,0:T(8,128)(2,1)S(1)}, bf16[512,256]{1,0:T(8,128)(2,1)S(1)}, u32[]{:S(2)}, u32[]{:S(2)}) %collective-permute-start.5) | collective-permute-done | bytes 262176 | tf_op jit(solution)/shard_map/ppermute | solution.py:40
  26.6 1.7 %collective-permute-done.6.refs_6_ = bf16[512,256]{1,0:T(8,128)(2,1)S(1)} collective-permute-done((bf16[512,256]{1,0:T(8,128)(2,1)S(1)}, bf16[512,256]{1,0:T(8,128)(2,1)S(1)}, u32[]{:S(2)}, u32[]{:S(2)}) %collective-permute-start.6) | collective-permute-done | bytes 262176 | tf_op jit(solution)/shard_map/ppermute | solution.py:40
  28.3 2.7 %shard_map.109 = (f32[256,256]{1,0:T(8,128)S(1)}, f32[256,256]{1,0:T(8,128)S(1)}) custom-call(s32[4]{0:T(128)S(1)} %pad_add_fusion.refs_0_, bf16[256,128]{1,0:T(8,128)(2,1)S(1)} %pad_maximum_fusion.4.refs_1_, bf16[256,128]{1,0:T(8,128)(2,1)S(1)} %collective-permute-done.3.refs_2_, bf16[512,256]{1,0:T(8,128)(2,1)S(1)} %pad_maximum_fusion.refs_3_, ...), custom_call_target="tpu_custom_call" | custom-call | flops 536870912 | bytes 1179648 | tf_op jit(solution)/shard_map/pallas_call | solution.py:71
  33.4 1.3 %shard_map.110 = (f32[32,2048]{1,0:T(8,128)S(1)}, bf16[32,2048]{1,0:T(8,128)(2,1)S(1)}, bf16[32,2048]{1,0:T(8,128)(2,1)S(1)}, bf16[32,2048]{1,0:T(8,128)(2,1)S(1)}) custom-call(s32[4]{0:T(128)S(1)} %pad_add_fusion.refs_0_, f32[256,256]{1,0:T(8,128)S(1)} %get-tuple-element.39.refs_1_, f32[256,256]{1,0:T(8,128)S(1)} %collective-permute-done.7.refs_2_, ...), custom_call_target="tpu_custom_call" | custom-call | flops 134217728 | bytes 1703936 | tf_op jit(solution)/shard_map/pallas_call | solution.py:71
  36.8 2.7 %collective-permute-start.15 = (bf16[32,2048]{1,0:T(8,128)(2,1)S(1)}, bf16[32,2048]{1,0:T(8,128)(2,1)S(1)}, u32[]{:S(2)}, u32[]{:S(2)}) collective-permute-start(bf16[32,2048]{1,0:T(8,128)(2,1)S(1)} %get-tuple-element.46), channel_id=1, source_target_pairs={{0,2},{1,3},{2,4},{3,5},{4,6},{5,7},{6,0},{7,1},{8,10},{9,11},{10,... | collective-permute-start | bytes 393224 | tf_op jit(solution)/shard_map/ppermute | solution.py:310
  39.5 2.8 %collective-permute-done.13.refs_2_ = bf16[32,2048]{1,0:T(8,128)(2,1)S(1)} collective-permute-done((bf16[32,2048]{1,0:T(8,128)(2,1)S(1)}, bf16[32,2048]{1,0:T(8,128)(2,1)S(1)}, u32[]{:S(2)}, u32[]{:S(2)}) %collective-permute-start.13) | collective-permute-done | bytes 131104 | tf_op jit(solution)/shard_map/ppermute | solution.py:44
  42.3 3.0 %collective-permute-done.15.refs_4_ = bf16[32,2048]{1,0:T(8,128)(2,1)S(1)} collective-permute-done((bf16[32,2048]{1,0:T(8,128)(2,1)S(1)}, bf16[32,2048]{1,0:T(8,128)(2,1)S(1)}, u32[]{:S(2)}, u32[]{:S(2)}) %collective-permute-start.15) | collective-permute-done | bytes 131104 | tf_op jit(solution)/shard_map/ppermute | solution.py:310
  45.8 3.0 %collective-permute-start.16 = (bf16[32,2048]{1,0:T(8,128)(2,1)S(1)}, bf16[32,2048]{1,0:T(8,128)(2,1)S(1)}, u32[]{:S(2)}, u32[]{:S(2)}) collective-permute-start(bf16[32,2048]{1,0:T(8,128)(2,1)S(1)} %get-tuple-element.51), channel_id=1, source_target_pairs={{0,8},{1,9},{2,10},{3,11},{4,12},{5,13},{6,14},{7,15},{8,0},{9,1},... | collective-permute-start | bytes 393224 | tf_op jit(solution)/shard_map/ppermute | solution.py:44
  48.8 3.6 %collective-permute-done.16.refs_7_ = bf16[32,2048]{1,0:T(8,128)(2,1)S(1)} collective-permute-done((bf16[32,2048]{1,0:T(8,128)(2,1)S(1)}, bf16[32,2048]{1,0:T(8,128)(2,1)S(1)}, u32[]{:S(2)}, u32[]{:S(2)}) %collective-permute-start.16) | collective-permute-done | bytes 131104 | tf_op jit(solution)/shard_map/ppermute | solution.py:44
  52.4 1.3 %collective-permute-done.18.refs_9_ = bf16[32,2048]{1,0:T(8,128)(2,1)S(1)} collective-permute-done((bf16[32,2048]{1,0:T(8,128)(2,1)S(1)}, bf16[32,2048]{1,0:T(8,128)(2,1)S(1)}, u32[]{:S(2)}, u32[]{:S(2)}) %collective-permute-start.18) | collective-permute-done | bytes 131104 | tf_op jit(solution)/shard_map/ppermute | solution.py:40
  56.8 1.9 %copy-done.2 = bf16[1,768,2048]{2,1,0:T(8,128)(2,1)S(1)} copy-done((bf16[1,768,2048]{2,1,0:T(8,128)(2,1)S(1)}, bf16[1,768,2048]{2,1,0:T(8,128)(2,1)}, u32[]{:S(2)}) %copy-start.2) | copy-done | bytes 3145752
  59.2 5.8 %collective-permute-done.20.refs_5_ = bf16[64,2176]{1,0:T(8,128)(2,1)S(1)} collective-permute-done((bf16[64,2176]{1,0:T(8,128)(2,1)S(1)}, bf16[64,2176]{1,0:T(8,128)(2,1)S(1)}, u32[]{:S(2)}, u32[]{:S(2)}) %collective-permute-start.20) | collective-permute-done | bytes 278560 | tf_op jit(solution)/shard_map/ppermute | solution.py:310
  65.1 3.6 %collective-permute-start.23 = (bf16[32,2176]{1,0:T(8,128)(2,1)S(1)}, bf16[32,2176]{1,0:T(8,128)(2,1)S(1)}, u32[]{:S(2)}, u32[]{:S(2)}) collective-permute-start(bf16[32,2176]{1,0:T(8,128)(2,1)S(1)} %slice.75), channel_id=1, source_target_pairs={{0,2},{1,3},{2,4},{3,5},{4,6},{5,7},{6,0},{7,1},{8,10},{9,11},{10,... | collective-permute-start | bytes 417800 | tf_op jit(solution)/shard_map/ppermute | solution.py:310
  68.7 2.3 %shard_map.114 = (f32[80,2048]{1,0:T(8,128)S(1)}, bf16[80,2048]{1,0:T(8,128)(2,1)S(1)}) custom-call(s32[4]{0:T(128)S(1)} %pad_add_fusion.refs_0_, bf16[2048,768]{1,0:T(8,128)(2,1)S(1)} %bitcast.43, bf16[2048,768]{1,0:T(8,128)(2,1)S(1)} %bitcast.46, bf16[768,2048]{1,0:T(8,128)(2,1)S(1)} %bitcast.49, bf16[64,2176]{1,0:T(8,128)(2,1)S(1)} %collective-permute-done.19.refs_4_, ...), custom_call_target="tpu_custom_call" | custom-call | flops 1509949440 | bytes 10133504 | tf_op jit(solution)/shard_map/pallas_call | solution.py:71
  71.0 3.0 %collective-permute-start.21 = (bf16[80,2048]{1,0:T(8,128)(2,1)S(1)}, bf16[80,2048]{1,0:T(8,128)(2,1)S(1)}, u32[]{:S(2)}, u32[]{:S(2)}) collective-permute-start(bf16[80,2048]{1,0:T(8,128)(2,1)S(1)} %get-tuple-element.57), channel_id=1, source_target_pairs={{0,8},{1,9},{2,10},{3,11},{4,12},{5,13},{6,14},{7,15},{8,0},{9,1},... | collective-permute-start | bytes 983048 | tf_op jit(solution)/shard_map/ppermute | solution.py:44
  74.0 2.9 %collective-permute-done.23.refs_5_ = bf16[32,2176]{1,0:T(8,128)(2,1)S(1)} collective-permute-done((bf16[32,2176]{1,0:T(8,128)(2,1)S(1)}, bf16[32,2176]{1,0:T(8,128)(2,1)S(1)}, u32[]{:S(2)}, u32[]{:S(2)}) %collective-permute-start.23) | collective-permute-done | bytes 139296 | tf_op jit(solution)/shard_map/ppermute | solution.py:310
  76.9 2.3 %shard_map.116 = (f32[48,2048]{1,0:T(8,128)S(1)}, bf16[48,2048]{1,0:T(8,128)(2,1)S(1)}) custom-call(s32[4]{0:T(128)S(1)} %pad_add_fusion.refs_0_, bf16[2048,768]{1,0:T(8,128)(2,1)S(1)} %bitcast.44, bf16[2048,768]{1,0:T(8,128)(2,1)S(1)} %bitcast.47, bf16[768,2048]{1,0:T(8,128)(2,1)S(1)} %bitcast.50, bf16[64,2176]{1,0:T(8,128)(2,1)S(1)} %collective-permute-done.22.refs_4_, ...), custom_call_target="tpu_custom_call" | custom-call | flops 905969664 | bytes 9854976 | tf_op jit(solution)/shard_map/pallas_call | solution.py:71
  79.1 3.0 %collective-permute-start.24 = (bf16[48,2048]{1,0:T(8,128)(2,1)S(1)}, bf16[48,2048]{1,0:T(8,128)(2,1)S(1)}, u32[]{:S(2)}, u32[]{:S(2)}) collective-permute-start(bf16[48,2048]{1,0:T(8,128)(2,1)S(1)} %get-tuple-element.60), channel_id=1, source_target_pairs={{0,8},{1,9},{2,10},{3,11},{4,12},{5,13},{6,14},{7,15},{8,0},{9,1},... | collective-permute-start | bytes 589832 | tf_op jit(solution)/shard_map/ppermute | solution.py:44
  82.8 1.4 %collective-permute-start.27 = (bf16[32,2048]{1,0:T(8,128)(2,1)S(1)}, bf16[32,2048]{1,0:T(8,128)(2,1)S(1)}, u32[]{:S(2)}, u32[]{:S(2)}) collective-permute-start(bf16[32,2048]{1,0:T(8,128)(2,1)S(1)} %get-tuple-element.63), channel_id=1, source_target_pairs={{0,6},{1,7},{2,0},{3,1},{4,2},{5,3},{6,4},{7,5},{8,14},{9,15},{10,... | collective-permute-start | bytes 393224 | tf_op jit(solution)/shard_map/ppermute | solution.py:310
  84.2 2.2 %collective-permute-done.24.refs_2_ = bf16[48,2048]{1,0:T(8,128)(2,1)S(1)} collective-permute-done((bf16[48,2048]{1,0:T(8,128)(2,1)S(1)}, bf16[48,2048]{1,0:T(8,128)(2,1)S(1)}, u32[]{:S(2)}, u32[]{:S(2)}) %collective-permute-start.24) | collective-permute-done | bytes 196640 | tf_op jit(solution)/shard_map/ppermute | solution.py:44
  87.0 1.2 %collective-permute-start.28 = (bf16[32,2048]{1,0:T(8,128)(2,1)S(1)}, bf16[32,2048]{1,0:T(8,128)(2,1)S(1)}, u32[]{:S(2)}, u32[]{:S(2)}) collective-permute-start(bf16[32,2048]{1,0:T(8,128)(2,1)S(1)} %get-tuple-element.64), channel_id=1, source_target_pairs={{0,5},{1,6},{2,7},{3,0},{4,1},{5,2},{6,3},{7,4},{8,13},{9,14},{10,... | collective-permute-start | bytes 393224 | tf_op jit(solution)/shard_map/ppermute | solution.py:310
  88.2 2.9 %collective-permute-start.25 = (bf16[16,2048]{1,0:T(8,128)(2,1)S(1)}, bf16[16,2048]{1,0:T(8,128)(2,1)S(1)}, u32[]{:S(2)}, u32[]{:S(2)}) collective-permute-start(bf16[16,2048]{1,0:T(8,128)(2,1)S(1)} %get-tuple-element.61), channel_id=1, source_target_pairs={{0,4},{1,5},{2,6},{3,7},{4,0},{5,1},{6,2},{7,3},{8,12},{9,13},{10,... | collective-permute-start | bytes 196616 | tf_op jit(solution)/shard_map/ppermute | solution.py:44
  91.1 8.7 %collective-permute-done.25.refs_2_ = bf16[16,2048]{1,0:T(8,128)(2,1)S(1)} collective-permute-done((bf16[16,2048]{1,0:T(8,128)(2,1)S(1)}, bf16[16,2048]{1,0:T(8,128)(2,1)S(1)}, u32[]{:S(2)}, u32[]{:S(2)}) %collective-permute-start.25) | collective-permute-done | bytes 65568 | tf_op jit(solution)/shard_map/ppermute | solution.py:44
  100.6 1.2 %collective-permute-done.29.refs_3_ = bf16[16,2048]{1,0:T(8,128)(2,1)S(1)} collective-permute-done((bf16[16,2048]{1,0:T(8,128)(2,1)S(1)}, bf16[16,2048]{1,0:T(8,128)(2,1)S(1)}, u32[]{:S(2)}, u32[]{:S(2)}) %collective-permute-start.29) | collective-permute-done | bytes 65568 | tf_op jit(solution)/shard_map/ppermute | solution.py:40
  101.8 1.2 %shard_map.119 = bf16[16,2048]{1,0:T(8,128)(2,1)} custom-call(s32[4]{0:T(128)S(1)} %pad_add_fusion.refs_0_, bf16[32,2048]{1,0:T(8,128)(2,1)S(1)} %get-tuple-element.52.refs_1_, f32[16,2048]{1,0:T(8,128)S(1)} %get-tuple-element.65.refs_2_, bf16[16,2048]{1,0:T(8,128)(2,1)S(1)} %collective-permute-done.29.refs_3_), custom_call_target="tpu_custom_call" | custom-call | flops 98304 | bytes 327680 | tf_op jit(solution)/shard_map/pallas_call | solution.py:71
  (67 shorter events, 17.0 us)
Async XLA Ops:
  1.0 11.9 %collective-permute-start = (bf16[256,256]{1,0:T(8,128)(2,1)S(1)}, bf16[256,256]{1,0:T(8,128)(2,1)S(1)}, u32[]{:S(2)}, u32[]{:S(2)}) collective-permute-start(bf16[256,256]{1,0:T(8,128)(2,1)S(1)} %pad_maximum_fusion.2), channel_id=1, source_target_pairs={{0,128},{16,144},{32,160},{48,176},{64,192},{80,208},{96,224},{112... | collective-permute-start | bytes 393224 | tf_op jit(solution)/shard_map/ppermute | solution.py:40
  4.4 52.4 %copy-start.1 = (bf16[1,2048,768]{2,1,0:T(8,128)(2,1)S(1)}, bf16[1,2048,768]{2,1,0:T(8,128)(2,1)}, u32[]{:S(2)}) copy-start(bf16[1,2048,768]{2,1,0:T(8,128)(2,1)} %param.20) | copy-start | bytes 9437188
  4.4 52.4 %copy-start = (bf16[1,2048,768]{2,1,0:T(8,128)(2,1)S(1)}, bf16[1,2048,768]{2,1,0:T(8,128)(2,1)}, u32[]{:S(2)}) copy-start(bf16[1,2048,768]{2,1,0:T(8,128)(2,1)} %param.19) | copy-start | bytes 9437188
  4.4 17.4 %collective-permute-start.1 = (bf16[128,640]{1,0:T(8,128)(2,1)S(1)}, bf16[128,640]{1,0:T(8,128)(2,1)S(1)}, u32[]{:S(2)}, u32[]{:S(2)}) collective-permute-start(bf16[128,640]{1,0:T(8,128)(2,1)S(1)} %pad_maximum_fusion.1), channel_id=1, source_target_pairs={{0,4},{1,5},{2,6},{3,7},{4,0},{5,1},{6,2},{7,3},{8,12},{9,13},{10,... | collective-permute-start | bytes 491528 | tf_op jit(solution)/shard_map/ppermute | solution.py:44
  12.9 12.3 %collective-permute-start.4 = (bf16[512,256]{1,0:T(8,128)(2,1)S(1)}, bf16[512,256]{1,0:T(8,128)(2,1)S(1)}, u32[]{:S(2)}, u32[]{:S(2)}) collective-permute-start(bf16[512,256]{1,0:T(8,128)(2,1)S(1)} %pad_maximum_fusion.refs_3_), channel_id=1, source_target_pairs={{0,32},{16,48},{32,64},{48,80},{64,96},{80,112},{96,0},{112,16},{1... | collective-permute-start | bytes 786440 | tf_op jit(solution)/shard_map/ppermute | solution.py:40
  14.5 12.1 %collective-permute-start.5 = (bf16[512,256]{1,0:T(8,128)(2,1)S(1)}, bf16[512,256]{1,0:T(8,128)(2,1)S(1)}, u32[]{:S(2)}, u32[]{:S(2)}) collective-permute-start(bf16[512,256]{1,0:T(8,128)(2,1)S(1)} %pad_maximum_fusion.refs_3_), channel_id=1, source_target_pairs={{0,96},{16,112},{32,0},{48,16},{64,32},{80,48},{96,64},{112,80},{1... | collective-permute-start | bytes 786440 | tf_op jit(solution)/shard_map/ppermute | solution.py:40
  16.3 12.1 %collective-permute-start.6 = (bf16[512,256]{1,0:T(8,128)(2,1)S(1)}, bf16[512,256]{1,0:T(8,128)(2,1)S(1)}, u32[]{:S(2)}, u32[]{:S(2)}) collective-permute-start(bf16[512,256]{1,0:T(8,128)(2,1)S(1)} %pad_maximum_fusion.refs_3_), channel_id=1, source_target_pairs={{0,64},{16,80},{32,96},{48,112},{64,0},{80,16},{96,32},{112,48},{1... | collective-permute-start | bytes 786440 | tf_op jit(solution)/shard_map/ppermute | solution.py:40
  18.9 5.8 %collective-permute-start.2 = (bf16[16,2176]{1,0:T(8,128)(2,1)S(1)}, bf16[16,2176]{1,0:T(8,128)(2,1)S(1)}, u32[]{:S(2)}, u32[]{:S(2)}) collective-permute-start(bf16[16,2176]{1,0:T(8,128)(2,1)S(1)} %pad_maximum_fusion.3.refs_1_), channel_id=1, source_target_pairs={{0,8},{1,9},{2,10},{3,11},{4,12},{5,13},{6,14},{7,15},{8,0},{9,1},... | collective-permute-start | bytes 208904 | tf_op jit(solution)/shard_map/ppermute | solution.py:44
  21.8 3.4 %collective-permute-start.3 = (bf16[256,128]{1,0:T(8,128)(2,1)S(1)}, bf16[256,128]{1,0:T(8,128)(2,1)S(1)}, u32[]{:S(2)}, u32[]{:S(2)}) collective-permute-start(bf16[256,128]{1,0:T(8,128)(2,1)S(1)} %pad_maximum_fusion.4.refs_1_), channel_id=1, source_target_pairs={{0,16},{16,0},{32,48},{48,32},{64,80},{80,64},{96,112},{112,96},{1... | collective-permute-start | bytes 196616 | tf_op jit(solution)/shard_map/ppermute | solution.py:40
  24.7 6.8 %collective-permute-start.10 = (bf16[128,640]{1,0:T(8,128)(2,1)S(1)}, bf16[128,640]{1,0:T(8,128)(2,1)S(1)}, u32[]{:S(2)}, u32[]{:S(2)}) collective-permute-start(bf16[128,640]{1,0:T(8,128)(2,1)S(1)} %collective-permute-done.1.refs_3_), channel_id=1, source_target_pairs={{0,128},{16,144},{32,160},{48,176},{64,192},{80,208},{96,224},{112... | collective-permute-start | bytes 491528 | tf_op jit(solution)/shard_map/ppermute | solution.py:40
  31.0 2.4 %collective-permute-start.7 = (f32[256,256]{1,0:T(8,128)S(1)}, f32[256,256]{1,0:T(8,128)S(1)}, u32[]{:S(2)}, u32[]{:S(2)}) collective-permute-start(f32[256,256]{1,0:T(8,128)S(1)} %get-tuple-element.40), channel_id=1, source_target_pairs={{0,16},{16,0},{32,48},{48,32},{64,80},{80,64},{96,112},{112,96},{1... | collective-permute-start | bytes 786440 | tf_op jit(solution)/shard_map/ppermute | solution.py:40
  31.1 2.3 %collective-permute-start.11 = (bf16[128,640]{1,0:T(8,128)(2,1)S(1)}, bf16[128,640]{1,0:T(8,128)(2,1)S(1)}, u32[]{:S(2)}, u32[]{:S(2)}) collective-permute-start(bf16[128,640]{1,0:T(8,128)(2,1)S(1)} %collective-permute-done.1.refs_3_), channel_id=1, source_target_pairs={{0,16},{16,0},{32,48},{48,32},{64,80},{80,64},{96,112},{112,96},{1... | collective-permute-start | bytes 491528 | tf_op jit(solution)/shard_map/ppermute | solution.py:40
  31.6 1.8 %collective-permute-start.12 = (bf16[128,640]{1,0:T(8,128)(2,1)S(1)}, bf16[128,640]{1,0:T(8,128)(2,1)S(1)}, u32[]{:S(2)}, u32[]{:S(2)}) collective-permute-start(bf16[128,640]{1,0:T(8,128)(2,1)S(1)} %collective-permute-done.10.refs_4_), channel_id=1, source_target_pairs={{0,16},{16,0},{32,48},{48,32},{64,80},{80,64},{96,112},{112,96},{1... | collective-permute-start | bytes 491528 | tf_op jit(solution)/shard_map/ppermute | solution.py:40
  31.7 1.5 %collective-permute-start.8 = (bf16[16,2176]{1,0:T(8,128)(2,1)S(1)}, bf16[16,2176]{1,0:T(8,128)(2,1)S(1)}, u32[]{:S(2)}, u32[]{:S(2)}) collective-permute-start(bf16[16,2176]{1,0:T(8,128)(2,1)S(1)} %pad_maximum_fusion.3.refs_1_), channel_id=1, source_target_pairs={{0,16},{16,0},{32,48},{48,32},{64,80},{80,64},{96,112},{112,96},{1... | collective-permute-start | bytes 208904 | tf_op jit(solution)/shard_map/ppermute | solution.py:40
  32.1 1.3 %collective-permute-start.9 = (bf16[16,2176]{1,0:T(8,128)(2,1)S(1)}, bf16[16,2176]{1,0:T(8,128)(2,1)S(1)}, u32[]{:S(2)}, u32[]{:S(2)}) collective-permute-start(bf16[16,2176]{1,0:T(8,128)(2,1)S(1)} %collective-permute-done.2.refs_4_), channel_id=1, source_target_pairs={{0,16},{16,0},{32,48},{48,32},{64,80},{80,64},{96,112},{112,96},{1... | collective-permute-start | bytes 208904 | tf_op jit(solution)/shard_map/ppermute | solution.py:40
  34.7 7.6 %collective-permute-start.13 = (bf16[32,2048]{1,0:T(8,128)(2,1)S(1)}, bf16[32,2048]{1,0:T(8,128)(2,1)S(1)}, u32[]{:S(2)}, u32[]{:S(2)}) collective-permute-start(bf16[32,2048]{1,0:T(8,128)(2,1)S(1)} %get-tuple-element.44), channel_id=1, source_target_pairs={{0,7},{1,0},{2,1},{3,2},{4,3},{5,4},{6,5},{7,6},{8,15},{9,8},{10,9... | collective-permute-start | bytes 393224 | tf_op jit(solution)/shard_map/ppermute | solution.py:44
  35.7 6.5 %collective-permute-start.14 = (bf16[32,2048]{1,0:T(8,128)(2,1)S(1)}, bf16[32,2048]{1,0:T(8,128)(2,1)S(1)}, u32[]{:S(2)}, u32[]{:S(2)}) collective-permute-start(bf16[32,2048]{1,0:T(8,128)(2,1)S(1)} %get-tuple-element.45), channel_id=1, source_target_pairs={{0,1},{1,2},{2,3},{3,4},{4,5},{5,6},{6,7},{7,0},{8,9},{9,10},{10,1... | collective-permute-start | bytes 393224 | tf_op jit(solution)/shard_map/ppermute | solution.py:44
  36.8 8.5 %collective-permute-start.15 = (bf16[32,2048]{1,0:T(8,128)(2,1)S(1)}, bf16[32,2048]{1,0:T(8,128)(2,1)S(1)}, u32[]{:S(2)}, u32[]{:S(2)}) collective-permute-start(bf16[32,2048]{1,0:T(8,128)(2,1)S(1)} %get-tuple-element.46), channel_id=1, source_target_pairs={{0,2},{1,3},{2,4},{3,5},{4,6},{5,7},{6,0},{7,1},{8,10},{9,11},{10,... | collective-permute-start | bytes 393224 | tf_op jit(solution)/shard_map/ppermute | solution.py:310
  45.8 6.6 %collective-permute-start.16 = (bf16[32,2048]{1,0:T(8,128)(2,1)S(1)}, bf16[32,2048]{1,0:T(8,128)(2,1)S(1)}, u32[]{:S(2)}, u32[]{:S(2)}) collective-permute-start(bf16[32,2048]{1,0:T(8,128)(2,1)S(1)} %get-tuple-element.51), channel_id=1, source_target_pairs={{0,8},{1,9},{2,10},{3,11},{4,12},{5,13},{6,14},{7,15},{8,0},{9,1},... | collective-permute-start | bytes 393224 | tf_op jit(solution)/shard_map/ppermute | solution.py:44
  48.8 3.6 %collective-permute-start.17 = (bf16[32,2048]{1,0:T(8,128)(2,1)S(1)}, bf16[32,2048]{1,0:T(8,128)(2,1)S(1)}, u32[]{:S(2)}, u32[]{:S(2)}) collective-permute-start(bf16[32,2048]{1,0:T(8,128)(2,1)S(1)} %get-tuple-element.51), channel_id=1, source_target_pairs={{0,16},{16,0},{32,48},{48,32},{64,80},{80,64},{96,112},{112,96},{1... | collective-permute-start | bytes 393224 | tf_op jit(solution)/shard_map/ppermute | solution.py:40
  52.4 1.3 %collective-permute-start.18 = (bf16[32,2048]{1,0:T(8,128)(2,1)S(1)}, bf16[32,2048]{1,0:T(8,128)(2,1)S(1)}, u32[]{:S(2)}, u32[]{:S(2)}) collective-permute-start(bf16[32,2048]{1,0:T(8,128)(2,1)S(1)} %collective-permute-done.16.refs_7_), channel_id=1, source_target_pairs={{0,16},{16,0},{32,48},{48,32},{64,80},{80,64},{96,112},{112,96},{1... | collective-permute-start | bytes 393224 | tf_op jit(solution)/shard_map/ppermute | solution.py:40
  54.6 10.5 %collective-permute-start.20 = (bf16[64,2176]{1,0:T(8,128)(2,1)S(1)}, bf16[64,2176]{1,0:T(8,128)(2,1)S(1)}, u32[]{:S(2)}, u32[]{:S(2)}) collective-permute-start(bf16[64,2176]{1,0:T(8,128)(2,1)S(1)} %get-tuple-element.53.refs_1_), channel_id=1, source_target_pairs={{0,2},{1,3},{2,4},{3,5},{4,6},{5,7},{6,0},{7,1},{8,10},{9,11},{10,... | collective-permute-start | bytes 835592 | tf_op jit(solution)/shard_map/ppermute | solution.py:310
  55.8 12.9 %collective-permute-start.19 = (bf16[64,2176]{1,0:T(8,128)(2,1)S(1)}, bf16[64,2176]{1,0:T(8,128)(2,1)S(1)}, u32[]{:S(2)}, u32[]{:S(2)}) collective-permute-start(bf16[64,2176]{1,0:T(8,128)(2,1)S(1)} %get-tuple-element.53.refs_1_), channel_id=1, source_target_pairs={{0,1},{1,2},{2,3},{3,4},{4,5},{5,6},{6,7},{7,0},{8,9},{9,10},{10,1... | collective-permute-start | bytes 835592 | tf_op jit(solution)/shard_map/ppermute | solution.py:310
  65.0 11.8 %collective-permute-start.22 = (bf16[64,2176]{1,0:T(8,128)(2,1)S(1)}, bf16[64,2176]{1,0:T(8,128)(2,1)S(1)}, u32[]{:S(2)}, u32[]{:S(2)}) collective-permute-start(bf16[64,2176]{1,0:T(8,128)(2,1)S(1)} %collective-permute-done.20.refs_5_), channel_id=1, source_target_pairs={{0,1},{1,2},{2,3},{3,4},{4,5},{5,6},{6,7},{7,0},{8,9},{9,10},{10,1... | collective-permute-start | bytes 835592 | tf_op jit(solution)/shard_map/ppermute | solution.py:310
  65.1 11.8 %collective-permute-start.23 = (bf16[32,2176]{1,0:T(8,128)(2,1)S(1)}, bf16[32,2176]{1,0:T(8,128)(2,1)S(1)}, u32[]{:S(2)}, u32[]{:S(2)}) collective-permute-start(bf16[32,2176]{1,0:T(8,128)(2,1)S(1)} %slice.75), channel_id=1, source_target_pairs={{0,2},{1,3},{2,4},{3,5},{4,6},{5,7},{6,0},{7,1},{8,10},{9,11},{10,... | collective-permute-start | bytes 417800 | tf_op jit(solution)/shard_map/ppermute | solution.py:310
  71.0 11.1 %collective-permute-start.21 = (bf16[80,2048]{1,0:T(8,128)(2,1)S(1)}, bf16[80,2048]{1,0:T(8,128)(2,1)S(1)}, u32[]{:S(2)}, u32[]{:S(2)}) collective-permute-start(bf16[80,2048]{1,0:T(8,128)(2,1)S(1)} %get-tuple-element.57), channel_id=1, source_target_pairs={{0,8},{1,9},{2,10},{3,11},{4,12},{5,13},{6,14},{7,15},{8,0},{9,1},... | collective-permute-start | bytes 983048 | tf_op jit(solution)/shard_map/ppermute | solution.py:44
  79.1 7.3 %collective-permute-start.24 = (bf16[48,2048]{1,0:T(8,128)(2,1)S(1)}, bf16[48,2048]{1,0:T(8,128)(2,1)S(1)}, u32[]{:S(2)}, u32[]{:S(2)}) collective-permute-start(bf16[48,2048]{1,0:T(8,128)(2,1)S(1)} %get-tuple-element.60), channel_id=1, source_target_pairs={{0,8},{1,9},{2,10},{3,11},{4,12},{5,13},{6,14},{7,15},{8,0},{9,1},... | collective-permute-start | bytes 589832 | tf_op jit(solution)/shard_map/ppermute | solution.py:44
  82.7 8.4 %collective-permute-start.26 = (bf16[32,2048]{1,0:T(8,128)(2,1)S(1)}, bf16[32,2048]{1,0:T(8,128)(2,1)S(1)}, u32[]{:S(2)}, u32[]{:S(2)}) collective-permute-start(bf16[32,2048]{1,0:T(8,128)(2,1)S(1)} %get-tuple-element.62), channel_id=1, source_target_pairs={{0,7},{1,0},{2,1},{3,2},{4,3},{5,4},{6,5},{7,6},{8,15},{9,8},{10,9... | collective-permute-start | bytes 393224 | tf_op jit(solution)/shard_map/ppermute | solution.py:310
  82.8 8.3 %collective-permute-start.27 = (bf16[32,2048]{1,0:T(8,128)(2,1)S(1)}, bf16[32,2048]{1,0:T(8,128)(2,1)S(1)}, u32[]{:S(2)}, u32[]{:S(2)}) collective-permute-start(bf16[32,2048]{1,0:T(8,128)(2,1)S(1)} %get-tuple-element.63), channel_id=1, source_target_pairs={{0,6},{1,7},{2,0},{3,1},{4,2},{5,3},{6,4},{7,5},{8,14},{9,15},{10,... | collective-permute-start | bytes 393224 | tf_op jit(solution)/shard_map/ppermute | solution.py:310
  87.0 12.9 %collective-permute-start.28 = (bf16[32,2048]{1,0:T(8,128)(2,1)S(1)}, bf16[32,2048]{1,0:T(8,128)(2,1)S(1)}, u32[]{:S(2)}, u32[]{:S(2)}) collective-permute-start(bf16[32,2048]{1,0:T(8,128)(2,1)S(1)} %get-tuple-element.64), channel_id=1, source_target_pairs={{0,5},{1,6},{2,7},{3,0},{4,1},{5,2},{6,3},{7,4},{8,13},{9,14},{10,... | collective-permute-start | bytes 393224 | tf_op jit(solution)/shard_map/ppermute | solution.py:310
  88.2 11.6 %collective-permute-start.25 = (bf16[16,2048]{1,0:T(8,128)(2,1)S(1)}, bf16[16,2048]{1,0:T(8,128)(2,1)S(1)}, u32[]{:S(2)}, u32[]{:S(2)}) collective-permute-start(bf16[16,2048]{1,0:T(8,128)(2,1)S(1)} %get-tuple-element.61), channel_id=1, source_target_pairs={{0,4},{1,5},{2,6},{3,7},{4,0},{5,1},{6,2},{7,3},{8,12},{9,13},{10,... | collective-permute-start | bytes 196616 | tf_op jit(solution)/shard_map/ppermute | solution.py:44
  100.5 1.3 %collective-permute-start.29 = (bf16[16,2048]{1,0:T(8,128)(2,1)S(1)}, bf16[16,2048]{1,0:T(8,128)(2,1)S(1)}, u32[]{:S(2)}, u32[]{:S(2)}) collective-permute-start(bf16[16,2048]{1,0:T(8,128)(2,1)S(1)} %get-tuple-element.66), channel_id=1, source_target_pairs={{0,16},{16,0},{32,48},{48,32},{64,80},{80,64},{96,112},{112,96},{1... | collective-permute-start | bytes 196616 | tf_op jit(solution)/shard_map/ppermute | solution.py:40
  (4 other events, 96.7 us)

commit v9 on v8

--- a/solution.py
+++ b/solution.py
@@ -216,7 +216,7 @@
 
 
 def early(place, resident, fetched, outs, wait):
-    outs[0][...] = resident[0][:8, :128]
+    outs[0][...] = resident[0][:16, :128]
 
 
 def expert(place, resident, fetched, outs, wait):
@@ -423,7 +423,7 @@
     round_2 = on_both(round_0, by_core(2))
     round_1 = on_both(round_0, by_core(1))
     (seen,) = kernel_call(
-        early, place, [round_0], [], [struct((8, 128), BF16)], 8 * 128, idle=w
+        early, place, [round_0], [], [struct((16, 128), BF16)], 16 * 128, idle=w
     )
     round_2, seen = after(round_2, seen)
     round_3 = on_both(round_2, by_core(1))

time: 104 us -> 104 us (level)
  no operation moved by 1% of the time
where the time goes in v9:
time: 104 us; the launch traced here: 103 us
  starting transfers between devices  43 us (41%)
  waiting for transfers between devices  38.6 us (37%)
  Pallas kernels  13.5 us (13%)
  local copies, waits for them, and re-layouts  5.76 us (6%)
  other arithmetic  1.92 us (2%)
    ppermute x8, starting transfers between devices, on_exp(): return lax.ppermute(block, 'exp', route)  23.2 us
    ppermute x8, waiting for transfers between devices, on_exp(): return lax.ppermute(block, 'exp', route)  20.1 us
    pallas_call x11, Pallas kernels, kernel_call(): pl.pallas_call(whole, out_shape=out_shapes, in_specs=[pl.BlockSpec(memory...  13.5 us
    ppermute x8, waiting for transfers between devices, on_both(): return lax.ppermute(block, ('ctx', 'exp'), route)  11.7 us
    ppermute x8, starting transfers between devices, on_both(): return lax.ppermute(block, ('ctx', 'exp'), route)  11.2 us
    ppermute x14, starting transfers between devices, on_ctx(): return lax.ppermute(block, 'ctx', route)  8.63 us
    ppermute x14, waiting for transfers between devices, on_ctx(): return lax.ppermute(block, 'ctx', route)  6.79 us
  transfers between devices with their start and end apart: 30, of which 14 were waited for; matrix products, arithmetic and copies ran while one was open for 5% of the time, Pallas kernels for 9%

profile of v9, /device:TPU:32, one launch (start us, length us, event | category | flops | bytes accessed | tf_op | source)
XLA Modules:
  0.0 103.0 jit_solution(8268337173833533567)
XLA Ops:
  1.0 1.7 %collective-permute-start = (bf16[256,256]{1,0:T(8,128)(2,1)S(1)}, bf16[256,256]{1,0:T(8,128)(2,1)S(1)}, u32[]{:S(2)}, u32[]{:S(2)}) collective-permute-start(bf16[256,256]{1,0:T(8,128)(2,1)S(1)} %pad_maximum_fusion.2), channel_id=1, source_target_pairs={{0,128},{16,144},{32,160},{48,176},{64,192},{80,208},{96,224},{112... | collective-permute-start | bytes 393224 | tf_op jit(solution)/shard_map/ppermute | solution.py:40
  4.4 6.4 %collective-permute-start.1 = (bf16[128,640]{1,0:T(8,128)(2,1)S(1)}, bf16[128,640]{1,0:T(8,128)(2,1)S(1)}, u32[]{:S(2)}, u32[]{:S(2)}) collective-permute-start(bf16[128,640]{1,0:T(8,128)(2,1)S(1)} %pad_maximum_fusion.1), channel_id=1, source_target_pairs={{0,4},{1,5},{2,6},{3,7},{4,0},{5,1},{6,2},{7,3},{8,12},{9,13},{10,... | collective-permute-start | bytes 491528 | tf_op jit(solution)/shard_map/ppermute | solution.py:44
  12.9 1.6 %collective-permute-start.4 = (bf16[512,256]{1,0:T(8,128)(2,1)S(1)}, bf16[512,256]{1,0:T(8,128)(2,1)S(1)}, u32[]{:S(2)}, u32[]{:S(2)}) collective-permute-start(bf16[512,256]{1,0:T(8,128)(2,1)S(1)} %pad_maximum_fusion.refs_3_), channel_id=1, source_target_pairs={{0,32},{16,48},{32,64},{48,80},{64,96},{80,112},{96,0},{112,16},{1... | collective-permute-start | bytes 786440 | tf_op jit(solution)/shard_map/ppermute | solution.py:40
  14.5 1.7 %collective-permute-start.5 = (bf16[512,256]{1,0:T(8,128)(2,1)S(1)}, bf16[512,256]{1,0:T(8,128)(2,1)S(1)}, u32[]{:S(2)}, u32[]{:S(2)}) collective-permute-start(bf16[512,256]{1,0:T(8,128)(2,1)S(1)} %pad_maximum_fusion.refs_3_), channel_id=1, source_target_pairs={{0,96},{16,112},{32,0},{48,16},{64,32},{80,48},{96,64},{112,80},{1... | collective-permute-start | bytes 786440 | tf_op jit(solution)/shard_map/ppermute | solution.py:40
  16.3 1.8 %collective-permute-start.6 = (bf16[512,256]{1,0:T(8,128)(2,1)S(1)}, bf16[512,256]{1,0:T(8,128)(2,1)S(1)}, u32[]{:S(2)}, u32[]{:S(2)}) collective-permute-start(bf16[512,256]{1,0:T(8,128)(2,1)S(1)} %pad_maximum_fusion.refs_3_), channel_id=1, source_target_pairs={{0,64},{16,80},{32,96},{48,112},{64,0},{80,16},{96,32},{112,48},{1... | collective-permute-start | bytes 786440 | tf_op jit(solution)/shard_map/ppermute | solution.py:40
  18.9 2.9 %collective-permute-start.2 = (bf16[16,2176]{1,0:T(8,128)(2,1)S(1)}, bf16[16,2176]{1,0:T(8,128)(2,1)S(1)}, u32[]{:S(2)}, u32[]{:S(2)}) collective-permute-start(bf16[16,2176]{1,0:T(8,128)(2,1)S(1)} %pad_maximum_fusion.3.refs_1_), channel_id=1, source_target_pairs={{0,8},{1,9},{2,10},{3,11},{4,12},{5,13},{6,14},{7,15},{8,0},{9,1},... | collective-permute-start | bytes 208904 | tf_op jit(solution)/shard_map/ppermute | solution.py:44
  21.9 2.8 %collective-permute-done.2.refs_4_ = bf16[16,2176]{1,0:T(8,128)(2,1)S(1)} collective-permute-done((bf16[16,2176]{1,0:T(8,128)(2,1)S(1)}, bf16[16,2176]{1,0:T(8,128)(2,1)S(1)}, u32[]{:S(2)}, u32[]{:S(2)}) %collective-permute-start.2) | collective-permute-done | bytes 69664 | tf_op jit(solution)/shard_map/ppermute | solution.py:44
  25.3 1.4 %collective-permute-done.5.refs_5_ = bf16[512,256]{1,0:T(8,128)(2,1)S(1)} collective-permute-done((bf16[512,256]{1,0:T(8,128)(2,1)S(1)}, bf16[512,256]{1,0:T(8,128)(2,1)S(1)}, u32[]{:S(2)}, u32[]{:S(2)}) %collective-permute-start.5) | collective-permute-done | bytes 262176 | tf_op jit(solution)/shard_map/ppermute | solution.py:40
  26.6 1.7 %collective-permute-done.6.refs_6_ = bf16[512,256]{1,0:T(8,128)(2,1)S(1)} collective-permute-done((bf16[512,256]{1,0:T(8,128)(2,1)S(1)}, bf16[512,256]{1,0:T(8,128)(2,1)S(1)}, u32[]{:S(2)}, u32[]{:S(2)}) %collective-permute-start.6) | collective-permute-done | bytes 262176 | tf_op jit(solution)/shard_map/ppermute | solution.py:40
  28.3 2.7 %shard_map.109 = (f32[256,256]{1,0:T(8,128)S(1)}, f32[256,256]{1,0:T(8,128)S(1)}) custom-call(s32[4]{0:T(128)S(1)} %pad_add_fusion.refs_0_, bf16[256,128]{1,0:T(8,128)(2,1)S(1)} %pad_maximum_fusion.4.refs_1_, bf16[256,128]{1,0:T(8,128)(2,1)S(1)} %collective-permute-done.3.refs_2_, bf16[512,256]{1,0:T(8,128)(2,1)S(1)} %pad_maximum_fusion.refs_3_, ...), custom_call_target="tpu_custom_call" | custom-call | flops 536870912 | bytes 1179648 | tf_op jit(solution)/shard_map/pallas_call | solution.py:71
  33.4 1.3 %shard_map.110 = (f32[32,2048]{1,0:T(8,128)S(1)}, bf16[32,2048]{1,0:T(8,128)(2,1)S(1)}, bf16[32,2048]{1,0:T(8,128)(2,1)S(1)}, bf16[32,2048]{1,0:T(8,128)(2,1)S(1)}) custom-call(s32[4]{0:T(128)S(1)} %pad_add_fusion.refs_0_, f32[256,256]{1,0:T(8,128)S(1)} %get-tuple-element.39.refs_1_, f32[256,256]{1,0:T(8,128)S(1)} %collective-permute-done.7.refs_2_, ...), custom_call_target="tpu_custom_call" | custom-call | flops 134217728 | bytes 1703936 | tf_op jit(solution)/shard_map/pallas_call | solution.py:71
  36.8 2.7 %collective-permute-start.15 = (bf16[32,2048]{1,0:T(8,128)(2,1)S(1)}, bf16[32,2048]{1,0:T(8,128)(2,1)S(1)}, u32[]{:S(2)}, u32[]{:S(2)}) collective-permute-start(bf16[32,2048]{1,0:T(8,128)(2,1)S(1)} %get-tuple-element.46), channel_id=1, source_target_pairs={{0,2},{1,3},{2,4},{3,5},{4,6},{5,7},{6,0},{7,1},{8,10},{9,11},{10,... | collective-permute-start | bytes 393224 | tf_op jit(solution)/shard_map/ppermute | solution.py:310
  39.5 2.8 %collective-permute-done.13.refs_2_ = bf16[32,2048]{1,0:T(8,128)(2,1)S(1)} collective-permute-done((bf16[32,2048]{1,0:T(8,128)(2,1)S(1)}, bf16[32,2048]{1,0:T(8,128)(2,1)S(1)}, u32[]{:S(2)}, u32[]{:S(2)}) %collective-permute-start.13) | collective-permute-done | bytes 131104 | tf_op jit(solution)/shard_map/ppermute | solution.py:44
  42.3 3.0 %collective-permute-done.15.refs_4_ = bf16[32,2048]{1,0:T(8,128)(2,1)S(1)} collective-permute-done((bf16[32,2048]{1,0:T(8,128)(2,1)S(1)}, bf16[32,2048]{1,0:T(8,128)(2,1)S(1)}, u32[]{:S(2)}, u32[]{:S(2)}) %collective-permute-start.15) | collective-permute-done | bytes 131104 | tf_op jit(solution)/shard_map/ppermute | solution.py:310
  45.8 3.0 %collective-permute-start.16 = (bf16[32,2048]{1,0:T(8,128)(2,1)S(1)}, bf16[32,2048]{1,0:T(8,128)(2,1)S(1)}, u32[]{:S(2)}, u32[]{:S(2)}) collective-permute-start(bf16[32,2048]{1,0:T(8,128)(2,1)S(1)} %get-tuple-element.51), channel_id=1, source_target_pairs={{0,8},{1,9},{2,10},{3,11},{4,12},{5,13},{6,14},{7,15},{8,0},{9,1},... | collective-permute-start | bytes 393224 | tf_op jit(solution)/shard_map/ppermute | solution.py:44
  48.8 3.6 %collective-permute-done.16.refs_7_ = bf16[32,2048]{1,0:T(8,128)(2,1)S(1)} collective-permute-done((bf16[32,2048]{1,0:T(8,128)(2,1)S(1)}, bf16[32,2048]{1,0:T(8,128)(2,1)S(1)}, u32[]{:S(2)}, u32[]{:S(2)}) %collective-permute-start.16) | collective-permute-done | bytes 131104 | tf_op jit(solution)/shard_map/ppermute | solution.py:44
  52.4 1.3 %collective-permute-done.18.refs_9_ = bf16[32,2048]{1,0:T(8,128)(2,1)S(1)} collective-permute-done((bf16[32,2048]{1,0:T(8,128)(2,1)S(1)}, bf16[32,2048]{1,0:T(8,128)(2,1)S(1)}, u32[]{:S(2)}, u32[]{:S(2)}) %collective-permute-start.18) | collective-permute-done | bytes 131104 | tf_op jit(solution)/shard_map/ppermute | solution.py:40
  56.8 1.9 %copy-done.2 = bf16[1,768,2048]{2,1,0:T(8,128)(2,1)S(1)} copy-done((bf16[1,768,2048]{2,1,0:T(8,128)(2,1)S(1)}, bf16[1,768,2048]{2,1,0:T(8,128)(2,1)}, u32[]{:S(2)}) %copy-start.2) | copy-done | bytes 3145752
  59.2 5.8 %collective-permute-done.20.refs_5_ = bf16[64,2176]{1,0:T(8,128)(2,1)S(1)} collective-permute-done((bf16[64,2176]{1,0:T(8,128)(2,1)S(1)}, bf16[64,2176]{1,0:T(8,128)(2,1)S(1)}, u32[]{:S(2)}, u32[]{:S(2)}) %collective-permute-start.20) | collective-permute-done | bytes 278560 | tf_op jit(solution)/shard_map/ppermute | solution.py:310
  65.1 3.6 %collective-permute-start.23 = (bf16[32,2176]{1,0:T(8,128)(2,1)S(1)}, bf16[32,2176]{1,0:T(8,128)(2,1)S(1)}, u32[]{:S(2)}, u32[]{:S(2)}) collective-permute-start(bf16[32,2176]{1,0:T(8,128)(2,1)S(1)} %slice.75), channel_id=1, source_target_pairs={{0,2},{1,3},{2,4},{3,5},{4,6},{5,7},{6,0},{7,1},{8,10},{9,11},{10,... | collective-permute-start | bytes 417800 | tf_op jit(solution)/shard_map/ppermute | solution.py:310
  68.7 2.3 %shard_map.114 = (f32[80,2048]{1,0:T(8,128)S(1)}, bf16[80,2048]{1,0:T(8,128)(2,1)S(1)}) custom-call(s32[4]{0:T(128)S(1)} %pad_add_fusion.refs_0_, bf16[2048,768]{1,0:T(8,128)(2,1)S(1)} %bitcast.43, bf16[2048,768]{1,0:T(8,128)(2,1)S(1)} %bitcast.46, bf16[768,2048]{1,0:T(8,128)(2,1)S(1)} %bitcast.49, bf16[64,2176]{1,0:T(8,128)(2,1)S(1)} %collective-permute-done.19.refs_4_, ...), custom_call_target="tpu_custom_call" | custom-call | flops 1509949440 | bytes 10133504 | tf_op jit(solution)/shard_map/pallas_call | solution.py:71
  71.0 3.0 %collective-permute-start.21 = (bf16[80,2048]{1,0:T(8,128)(2,1)S(1)}, bf16[80,2048]{1,0:T(8,128)(2,1)S(1)}, u32[]{:S(2)}, u32[]{:S(2)}) collective-permute-start(bf16[80,2048]{1,0:T(8,128)(2,1)S(1)} %get-tuple-element.57), channel_id=1, source_target_pairs={{0,8},{1,9},{2,10},{3,11},{4,12},{5,13},{6,14},{7,15},{8,0},{9,1},... | collective-permute-start | bytes 983048 | tf_op jit(solution)/shard_map/ppermute | solution.py:44
  74.0 2.9 %collective-permute-done.23.refs_5_ = bf16[32,2176]{1,0:T(8,128)(2,1)S(1)} collective-permute-done((bf16[32,2176]{1,0:T(8,128)(2,1)S(1)}, bf16[32,2176]{1,0:T(8,128)(2,1)S(1)}, u32[]{:S(2)}, u32[]{:S(2)}) %collective-permute-start.23) | collective-permute-done | bytes 139296 | tf_op jit(solution)/shard_map/ppermute | solution.py:310
  76.9 2.3 %shard_map.116 = (f32[48,2048]{1,0:T(8,128)S(1)}, bf16[48,2048]{1,0:T(8,128)(2,1)S(1)}) custom-call(s32[4]{0:T(128)S(1)} %pad_add_fusion.refs_0_, bf16[2048,768]{1,0:T(8,128)(2,1)S(1)} %bitcast.44, bf16[2048,768]{1,0:T(8,128)(2,1)S(1)} %bitcast.47, bf16[768,2048]{1,0:T(8,128)(2,1)S(1)} %bitcast.50, bf16[64,2176]{1,0:T(8,128)(2,1)S(1)} %collective-permute-done.22.refs_4_, ...), custom_call_target="tpu_custom_call" | custom-call | flops 905969664 | bytes 9854976 | tf_op jit(solution)/shard_map/pallas_call | solution.py:71
  79.1 3.0 %collective-permute-start.24 = (bf16[48,2048]{1,0:T(8,128)(2,1)S(1)}, bf16[48,2048]{1,0:T(8,128)(2,1)S(1)}, u32[]{:S(2)}, u32[]{:S(2)}) collective-permute-start(bf16[48,2048]{1,0:T(8,128)(2,1)S(1)} %get-tuple-element.60), channel_id=1, source_target_pairs={{0,8},{1,9},{2,10},{3,11},{4,12},{5,13},{6,14},{7,15},{8,0},{9,1},... | collective-permute-start | bytes 589832 | tf_op jit(solution)/shard_map/ppermute | solution.py:44
  82.8 1.4 %collective-permute-start.27 = (bf16[32,2048]{1,0:T(8,128)(2,1)S(1)}, bf16[32,2048]{1,0:T(8,128)(2,1)S(1)}, u32[]{:S(2)}, u32[]{:S(2)}) collective-permute-start(bf16[32,2048]{1,0:T(8,128)(2,1)S(1)} %get-tuple-element.63), channel_id=1, source_target_pairs={{0,6},{1,7},{2,0},{3,1},{4,2},{5,3},{6,4},{7,5},{8,14},{9,15},{10,... | collective-permute-start | bytes 393224 | tf_op jit(solution)/shard_map/ppermute | solution.py:310
  84.2 2.2 %collective-permute-done.24.refs_2_ = bf16[48,2048]{1,0:T(8,128)(2,1)S(1)} collective-permute-done((bf16[48,2048]{1,0:T(8,128)(2,1)S(1)}, bf16[48,2048]{1,0:T(8,128)(2,1)S(1)}, u32[]{:S(2)}, u32[]{:S(2)}) %collective-permute-start.24) | collective-permute-done | bytes 196640 | tf_op jit(solution)/shard_map/ppermute | solution.py:44
  87.0 1.2 %collective-permute-start.28 = (bf16[32,2048]{1,0:T(8,128)(2,1)S(1)}, bf16[32,2048]{1,0:T(8,128)(2,1)S(1)}, u32[]{:S(2)}, u32[]{:S(2)}) collective-permute-start(bf16[32,2048]{1,0:T(8,128)(2,1)S(1)} %get-tuple-element.64), channel_id=1, source_target_pairs={{0,5},{1,6},{2,7},{3,0},{4,1},{5,2},{6,3},{7,4},{8,13},{9,14},{10,... | collective-permute-start | bytes 393224 | tf_op jit(solution)/shard_map/ppermute | solution.py:310
  88.2 2.9 %collective-permute-start.25 = (bf16[16,2048]{1,0:T(8,128)(2,1)S(1)}, bf16[16,2048]{1,0:T(8,128)(2,1)S(1)}, u32[]{:S(2)}, u32[]{:S(2)}) collective-permute-start(bf16[16,2048]{1,0:T(8,128)(2,1)S(1)} %get-tuple-element.61), channel_id=1, source_target_pairs={{0,4},{1,5},{2,6},{3,7},{4,0},{5,1},{6,2},{7,3},{8,12},{9,13},{10,... | collective-permute-start | bytes 196616 | tf_op jit(solution)/shard_map/ppermute | solution.py:44
  91.1 8.7 %collective-permute-done.25.refs_2_ = bf16[16,2048]{1,0:T(8,128)(2,1)S(1)} collective-permute-done((bf16[16,2048]{1,0:T(8,128)(2,1)S(1)}, bf16[16,2048]{1,0:T(8,128)(2,1)S(1)}, u32[]{:S(2)}, u32[]{:S(2)}) %collective-permute-start.25) | collective-permute-done | bytes 65568 | tf_op jit(solution)/shard_map/ppermute | solution.py:44
  100.6 1.2 %collective-permute-done.29.refs_3_ = bf16[16,2048]{1,0:T(8,128)(2,1)S(1)} collective-permute-done((bf16[16,2048]{1,0:T(8,128)(2,1)S(1)}, bf16[16,2048]{1,0:T(8,128)(2,1)S(1)}, u32[]{:S(2)}, u32[]{:S(2)}) %collective-permute-start.29) | collective-permute-done | bytes 65568 | tf_op jit(solution)/shard_map/ppermute | solution.py:40
  101.8 1.2 %shard_map.119 = bf16[16,2048]{1,0:T(8,128)(2,1)} custom-call(s32[4]{0:T(128)S(1)} %pad_add_fusion.refs_0_, bf16[32,2048]{1,0:T(8,128)(2,1)S(1)} %get-tuple-element.52.refs_1_, f32[16,2048]{1,0:T(8,128)S(1)} %get-tuple-element.65.refs_2_, bf16[16,2048]{1,0:T(8,128)(2,1)S(1)} %collective-permute-done.29.refs_3_), custom_call_target="tpu_custom_call" | custom-call | flops 98304 | bytes 327680 | tf_op jit(solution)/shard_map/pallas_call | solution.py:71
  (67 shorter events, 17.0 us)
Async XLA Ops:
  1.0 11.9 %collective-permute-start = (bf16[256,256]{1,0:T(8,128)(2,1)S(1)}, bf16[256,256]{1,0:T(8,128)(2,1)S(1)}, u32[]{:S(2)}, u32[]{:S(2)}) collective-permute-start(bf16[256,256]{1,0:T(8,128)(2,1)S(1)} %pad_maximum_fusion.2), channel_id=1, source_target_pairs={{0,128},{16,144},{32,160},{48,176},{64,192},{80,208},{96,224},{112... | collective-permute-start | bytes 393224 | tf_op jit(solution)/shard_map/ppermute | solution.py:40
  4.4 52.4 %copy-start.1 = (bf16[1,2048,768]{2,1,0:T(8,128)(2,1)S(1)}, bf16[1,2048,768]{2,1,0:T(8,128)(2,1)}, u32[]{:S(2)}) copy-start(bf16[1,2048,768]{2,1,0:T(8,128)(2,1)} %param.20) | copy-start | bytes 9437188
  4.4 52.4 %copy-start = (bf16[1,2048,768]{2,1,0:T(8,128)(2,1)S(1)}, bf16[1,2048,768]{2,1,0:T(8,128)(2,1)}, u32[]{:S(2)}) copy-start(bf16[1,2048,768]{2,1,0:T(8,128)(2,1)} %param.19) | copy-start | bytes 9437188
  4.4 17.4 %collective-permute-start.1 = (bf16[128,640]{1,0:T(8,128)(2,1)S(1)}, bf16[128,640]{1,0:T(8,128)(2,1)S(1)}, u32[]{:S(2)}, u32[]{:S(2)}) collective-permute-start(bf16[128,640]{1,0:T(8,128)(2,1)S(1)} %pad_maximum_fusion.1), channel_id=1, source_target_pairs={{0,4},{1,5},{2,6},{3,7},{4,0},{5,1},{6,2},{7,3},{8,12},{9,13},{10,... | collective-permute-start | bytes 491528 | tf_op jit(solution)/shard_map/ppermute | solution.py:44
  12.9 12.3 %collective-permute-start.4 = (bf16[512,256]{1,0:T(8,128)(2,1)S(1)}, bf16[512,256]{1,0:T(8,128)(2,1)S(1)}, u32[]{:S(2)}, u32[]{:S(2)}) collective-permute-start(bf16[512,256]{1,0:T(8,128)(2,1)S(1)} %pad_maximum_fusion.refs_3_), channel_id=1, source_target_pairs={{0,32},{16,48},{32,64},{48,80},{64,96},{80,112},{96,0},{112,16},{1... | collective-permute-start | bytes 786440 | tf_op jit(solution)/shard_map/ppermute | solution.py:40
  14.5 12.1 %collective-permute-start.5 = (bf16[512,256]{1,0:T(8,128)(2,1)S(1)}, bf16[512,256]{1,0:T(8,128)(2,1)S(1)}, u32[]{:S(2)}, u32[]{:S(2)}) collective-permute-start(bf16[512,256]{1,0:T(8,128)(2,1)S(1)} %pad_maximum_fusion.refs_3_), channel_id=1, source_target_pairs={{0,96},{16,112},{32,0},{48,16},{64,32},{80,48},{96,64},{112,80},{1... | collective-permute-start | bytes 786440 | tf_op jit(solution)/shard_map/ppermute | solution.py:40
  16.3 12.1 %collective-permute-start.6 = (bf16[512,256]{1,0:T(8,128)(2,1)S(1)}, bf16[512,256]{1,0:T(8,128)(2,1)S(1)}, u32[]{:S(2)}, u32[]{:S(2)}) collective-permute-start(bf16[512,256]{1,0:T(8,128)(2,1)S(1)} %pad_maximum_fusion.refs_3_), channel_id=1, source_target_pairs={{0,64},{16,80},{32,96},{48,112},{64,0},{80,16},{96,32},{112,48},{1... | collective-permute-start | bytes 786440 | tf_op jit(solution)/shard_map/ppermute | solution.py:40
  18.9 5.8 %collective-permute-start.2 = (bf16[16,2176]{1,0:T(8,128)(2,1)S(1)}, bf16[16,2176]{1,0:T(8,128)(2,1)S(1)}, u32[]{:S(2)}, u32[]{:S(2)}) collective-permute-start(bf16[16,2176]{1,0:T(8,128)(2,1)S(1)} %pad_maximum_fusion.3.refs_1_), channel_id=1, source_target_pairs={{0,8},{1,9},{2,10},{3,11},{4,12},{5,13},{6,14},{7,15},{8,0},{9,1},... | collective-permute-start | bytes 208904 | tf_op jit(solution)/shard_map/ppermute | solution.py:44
  21.8 3.4 %collective-permute-start.3 = (bf16[256,128]{1,0:T(8,128)(2,1)S(1)}, bf16[256,128]{1,0:T(8,128)(2,1)S(1)}, u32[]{:S(2)}, u32[]{:S(2)}) collective-permute-start(bf16[256,128]{1,0:T(8,128)(2,1)S(1)} %pad_maximum_fusion.4.refs_1_), channel_id=1, source_target_pairs={{0,16},{16,0},{32,48},{48,32},{64,80},{80,64},{96,112},{112,96},{1... | collective-permute-start | bytes 196616 | tf_op jit(solution)/shard_map/ppermute | solution.py:40
  24.7 6.8 %collective-permute-start.10 = (bf16[128,640]{1,0:T(8,128)(2,1)S(1)}, bf16[128,640]{1,0:T(8,128)(2,1)S(1)}, u32[]{:S(2)}, u32[]{:S(2)}) collective-permute-start(bf16[128,640]{1,0:T(8,128)(2,1)S(1)} %collective-permute-done.1.refs_3_), channel_id=1, source_target_pairs={{0,128},{16,144},{32,160},{48,176},{64,192},{80,208},{96,224},{112... | collective-permute-start | bytes 491528 | tf_op jit(solution)/shard_map/ppermute | solution.py:40
  31.0 2.4 %collective-permute-start.7 = (f32[256,256]{1,0:T(8,128)S(1)}, f32[256,256]{1,0:T(8,128)S(1)}, u32[]{:S(2)}, u32[]{:S(2)}) collective-permute-start(f32[256,256]{1,0:T(8,128)S(1)} %get-tuple-element.40), channel_id=1, source_target_pairs={{0,16},{16,0},{32,48},{48,32},{64,80},{80,64},{96,112},{112,96},{1... | collective-permute-start | bytes 786440 | tf_op jit(solution)/shard_map/ppermute | solution.py:40
  31.1 2.3 %collective-permute-start.11 = (bf16[128,640]{1,0:T(8,128)(2,1)S(1)}, bf16[128,640]{1,0:T(8,128)(2,1)S(1)}, u32[]{:S(2)}, u32[]{:S(2)}) collective-permute-start(bf16[128,640]{1,0:T(8,128)(2,1)S(1)} %collective-permute-done.1.refs_3_), channel_id=1, source_target_pairs={{0,16},{16,0},{32,48},{48,32},{64,80},{80,64},{96,112},{112,96},{1... | collective-permute-start | bytes 491528 | tf_op jit(solution)/shard_map/ppermute | solution.py:40
  31.6 1.8 %collective-permute-start.12 = (bf16[128,640]{1,0:T(8,128)(2,1)S(1)}, bf16[128,640]{1,0:T(8,128)(2,1)S(1)}, u32[]{:S(2)}, u32[]{:S(2)}) collective-permute-start(bf16[128,640]{1,0:T(8,128)(2,1)S(1)} %collective-permute-done.10.refs_4_), channel_id=1, source_target_pairs={{0,16},{16,0},{32,48},{48,32},{64,80},{80,64},{96,112},{112,96},{1... | collective-permute-start | bytes 491528 | tf_op jit(solution)/shard_map/ppermute | solution.py:40
  31.7 1.5 %collective-permute-start.8 = (bf16[16,2176]{1,0:T(8,128)(2,1)S(1)}, bf16[16,2176]{1,0:T(8,128)(2,1)S(1)}, u32[]{:S(2)}, u32[]{:S(2)}) collective-permute-start(bf16[16,2176]{1,0:T(8,128)(2,1)S(1)} %pad_maximum_fusion.3.refs_1_), channel_id=1, source_target_pairs={{0,16},{16,0},{32,48},{48,32},{64,80},{80,64},{96,112},{112,96},{1... | collective-permute-start | bytes 208904 | tf_op jit(solution)/shard_map/ppermute | solution.py:40
  32.1 1.3 %collective-permute-start.9 = (bf16[16,2176]{1,0:T(8,128)(2,1)S(1)}, bf16[16,2176]{1,0:T(8,128)(2,1)S(1)}, u32[]{:S(2)}, u32[]{:S(2)}) collective-permute-start(bf16[16,2176]{1,0:T(8,128)(2,1)S(1)} %collective-permute-done.2.refs_4_), channel_id=1, source_target_pairs={{0,16},{16,0},{32,48},{48,32},{64,80},{80,64},{96,112},{112,96},{1... | collective-permute-start | bytes 208904 | tf_op jit(solution)/shard_map/ppermute | solution.py:40
  34.7 7.6 %collective-permute-start.13 = (bf16[32,2048]{1,0:T(8,128)(2,1)S(1)}, bf16[32,2048]{1,0:T(8,128)(2,1)S(1)}, u32[]{:S(2)}, u32[]{:S(2)}) collective-permute-start(bf16[32,2048]{1,0:T(8,128)(2,1)S(1)} %get-tuple-element.44), channel_id=1, source_target_pairs={{0,7},{1,0},{2,1},{3,2},{4,3},{5,4},{6,5},{7,6},{8,15},{9,8},{10,9... | collective-permute-start | bytes 393224 | tf_op jit(solution)/shard_map/ppermute | solution.py:44
  35.7 6.5 %collective-permute-start.14 = (bf16[32,2048]{1,0:T(8,128)(2,1)S(1)}, bf16[32,2048]{1,0:T(8,128)(2,1)S(1)}, u32[]{:S(2)}, u32[]{:S(2)}) collective-permute-start(bf16[32,2048]{1,0:T(8,128)(2,1)S(1)} %get-tuple-element.45), channel_id=1, source_target_pairs={{0,1},{1,2},{2,3},{3,4},{4,5},{5,6},{6,7},{7,0},{8,9},{9,10},{10,1... | collective-permute-start | bytes 393224 | tf_op jit(solution)/shard_map/ppermute | solution.py:44
  36.8 8.5 %collective-permute-start.15 = (bf16[32,2048]{1,0:T(8,128)(2,1)S(1)}, bf16[32,2048]{1,0:T(8,128)(2,1)S(1)}, u32[]{:S(2)}, u32[]{:S(2)}) collective-permute-start(bf16[32,2048]{1,0:T(8,128)(2,1)S(1)} %get-tuple-element.46), channel_id=1, source_target_pairs={{0,2},{1,3},{2,4},{3,5},{4,6},{5,7},{6,0},{7,1},{8,10},{9,11},{10,... | collective-permute-start | bytes 393224 | tf_op jit(solution)/shard_map/ppermute | solution.py:310
  45.8 6.6 %collective-permute-start.16 = (bf16[32,2048]{1,0:T(8,128)(2,1)S(1)}, bf16[32,2048]{1,0:T(8,128)(2,1)S(1)}, u32[]{:S(2)}, u32[]{:S(2)}) collective-permute-start(bf16[32,2048]{1,0:T(8,128)(2,1)S(1)} %get-tuple-element.51), channel_id=1, source_target_pairs={{0,8},{1,9},{2,10},{3,11},{4,12},{5,13},{6,14},{7,15},{8,0},{9,1},... | collective-permute-start | bytes 393224 | tf_op jit(solution)/shard_map/ppermute | solution.py:44
  48.8 3.6 %collective-permute-start.17 = (bf16[32,2048]{1,0:T(8,128)(2,1)S(1)}, bf16[32,2048]{1,0:T(8,128)(2,1)S(1)}, u32[]{:S(2)}, u32[]{:S(2)}) collective-permute-start(bf16[32,2048]{1,0:T(8,128)(2,1)S(1)} %get-tuple-element.51), channel_id=1, source_target_pairs={{0,16},{16,0},{32,48},{48,32},{64,80},{80,64},{96,112},{112,96},{1... | collective-permute-start | bytes 393224 | tf_op jit(solution)/shard_map/ppermute | solution.py:40
  52.4 1.3 %collective-permute-start.18 = (bf16[32,2048]{1,0:T(8,128)(2,1)S(1)}, bf16[32,2048]{1,0:T(8,128)(2,1)S(1)}, u32[]{:S(2)}, u32[]{:S(2)}) collective-permute-start(bf16[32,2048]{1,0:T(8,128)(2,1)S(1)} %collective-permute-done.16.refs_7_), channel_id=1, source_target_pairs={{0,16},{16,0},{32,48},{48,32},{64,80},{80,64},{96,112},{112,96},{1... | collective-permute-start | bytes 393224 | tf_op jit(solution)/shard_map/ppermute | solution.py:40
  54.6 10.5 %collective-permute-start.20 = (bf16[64,2176]{1,0:T(8,128)(2,1)S(1)}, bf16[64,2176]{1,0:T(8,128)(2,1)S(1)}, u32[]{:S(2)}, u32[]{:S(2)}) collective-permute-start(bf16[64,2176]{1,0:T(8,128)(2,1)S(1)} %get-tuple-element.53.refs_1_), channel_id=1, source_target_pairs={{0,2},{1,3},{2,4},{3,5},{4,6},{5,7},{6,0},{7,1},{8,10},{9,11},{10,... | collective-permute-start | bytes 835592 | tf_op jit(solution)/shard_map/ppermute | solution.py:310
  55.8 12.9 %collective-permute-start.19 = (bf16[64,2176]{1,0:T(8,128)(2,1)S(1)}, bf16[64,2176]{1,0:T(8,128)(2,1)S(1)}, u32[]{:S(2)}, u32[]{:S(2)}) collective-permute-start(bf16[64,2176]{1,0:T(8,128)(2,1)S(1)} %get-tuple-element.53.refs_1_), channel_id=1, source_target_pairs={{0,1},{1,2},{2,3},{3,4},{4,5},{5,6},{6,7},{7,0},{8,9},{9,10},{10,1... | collective-permute-start | bytes 835592 | tf_op jit(solution)/shard_map/ppermute | solution.py:310
  65.0 11.8 %collective-permute-start.22 = (bf16[64,2176]{1,0:T(8,128)(2,1)S(1)}, bf16[64,2176]{1,0:T(8,128)(2,1)S(1)}, u32[]{:S(2)}, u32[]{:S(2)}) collective-permute-start(bf16[64,2176]{1,0:T(8,128)(2,1)S(1)} %collective-permute-done.20.refs_5_), channel_id=1, source_target_pairs={{0,1},{1,2},{2,3},{3,4},{4,5},{5,6},{6,7},{7,0},{8,9},{9,10},{10,1... | collective-permute-start | bytes 835592 | tf_op jit(solution)/shard_map/ppermute | solution.py:310
  65.1 11.8 %collective-permute-start.23 = (bf16[32,2176]{1,0:T(8,128)(2,1)S(1)}, bf16[32,2176]{1,0:T(8,128)(2,1)S(1)}, u32[]{:S(2)}, u32[]{:S(2)}) collective-permute-start(bf16[32,2176]{1,0:T(8,128)(2,1)S(1)} %slice.75), channel_id=1, source_target_pairs={{0,2},{1,3},{2,4},{3,5},{4,6},{5,7},{6,0},{7,1},{8,10},{9,11},{10,... | collective-permute-start | bytes 417800 | tf_op jit(solution)/shard_map/ppermute | solution.py:310
  71.0 11.1 %collective-permute-start.21 = (bf16[80,2048]{1,0:T(8,128)(2,1)S(1)}, bf16[80,2048]{1,0:T(8,128)(2,1)S(1)}, u32[]{:S(2)}, u32[]{:S(2)}) collective-permute-start(bf16[80,2048]{1,0:T(8,128)(2,1)S(1)} %get-tuple-element.57), channel_id=1, source_target_pairs={{0,8},{1,9},{2,10},{3,11},{4,12},{5,13},{6,14},{7,15},{8,0},{9,1},... | collective-permute-start | bytes 983048 | tf_op jit(solution)/shard_map/ppermute | solution.py:44
  79.1 7.3 %collective-permute-start.24 = (bf16[48,2048]{1,0:T(8,128)(2,1)S(1)}, bf16[48,2048]{1,0:T(8,128)(2,1)S(1)}, u32[]{:S(2)}, u32[]{:S(2)}) collective-permute-start(bf16[48,2048]{1,0:T(8,128)(2,1)S(1)} %get-tuple-element.60), channel_id=1, source_target_pairs={{0,8},{1,9},{2,10},{3,11},{4,12},{5,13},{6,14},{7,15},{8,0},{9,1},... | collective-permute-start | bytes 589832 | tf_op jit(solution)/shard_map/ppermute | solution.py:44
  82.7 8.4 %collective-permute-start.26 = (bf16[32,2048]{1,0:T(8,128)(2,1)S(1)}, bf16[32,2048]{1,0:T(8,128)(2,1)S(1)}, u32[]{:S(2)}, u32[]{:S(2)}) collective-permute-start(bf16[32,2048]{1,0:T(8,128)(2,1)S(1)} %get-tuple-element.62), channel_id=1, source_target_pairs={{0,7},{1,0},{2,1},{3,2},{4,3},{5,4},{6,5},{7,6},{8,15},{9,8},{10,9... | collective-permute-start | bytes 393224 | tf_op jit(solution)/shard_map/ppermute | solution.py:310
  82.8 8.3 %collective-permute-start.27 = (bf16[32,2048]{1,0:T(8,128)(2,1)S(1)}, bf16[32,2048]{1,0:T(8,128)(2,1)S(1)}, u32[]{:S(2)}, u32[]{:S(2)}) collective-permute-start(bf16[32,2048]{1,0:T(8,128)(2,1)S(1)} %get-tuple-element.63), channel_id=1, source_target_pairs={{0,6},{1,7},{2,0},{3,1},{4,2},{5,3},{6,4},{7,5},{8,14},{9,15},{10,... | collective-permute-start | bytes 393224 | tf_op jit(solution)/shard_map/ppermute | solution.py:310
  87.0 12.9 %collective-permute-start.28 = (bf16[32,2048]{1,0:T(8,128)(2,1)S(1)}, bf16[32,2048]{1,0:T(8,128)(2,1)S(1)}, u32[]{:S(2)}, u32[]{:S(2)}) collective-permute-start(bf16[32,2048]{1,0:T(8,128)(2,1)S(1)} %get-tuple-element.64), channel_id=1, source_target_pairs={{0,5},{1,6},{2,7},{3,0},{4,1},{5,2},{6,3},{7,4},{8,13},{9,14},{10,... | collective-permute-start | bytes 393224 | tf_op jit(solution)/shard_map/ppermute | solution.py:310
  88.2 11.6 %collective-permute-start.25 = (bf16[16,2048]{1,0:T(8,128)(2,1)S(1)}, bf16[16,2048]{1,0:T(8,128)(2,1)S(1)}, u32[]{:S(2)}, u32[]{:S(2)}) collective-permute-start(bf16[16,2048]{1,0:T(8,128)(2,1)S(1)} %get-tuple-element.61), channel_id=1, source_target_pairs={{0,4},{1,5},{2,6},{3,7},{4,0},{5,1},{6,2},{7,3},{8,12},{9,13},{10,... | collective-permute-start | bytes 196616 | tf_op jit(solution)/shard_map/ppermute | solution.py:44
  100.5 1.3 %collective-permute-start.29 = (bf16[16,2048]{1,0:T(8,128)(2,1)S(1)}, bf16[16,2048]{1,0:T(8,128)(2,1)S(1)}, u32[]{:S(2)}, u32[]{:S(2)}) collective-permute-start(bf16[16,2048]{1,0:T(8,128)(2,1)S(1)} %get-tuple-element.66), channel_id=1, source_target_pairs={{0,16},{16,0},{32,48},{48,32},{64,80},{80,64},{96,112},{112,96},{1... | collective-permute-start | bytes 196616 | tf_op jit(solution)/shard_map/ppermute | solution.py:40
  (4 other events, 96.7 us)

commit v10 on v9

--- a/solution.py
+++ b/solution.py
@@ -269,23 +269,21 @@
     return kernel_call(join, place, [keep, got], [], outs, keep.size)
 
 
-def gather_up(place, resident, fetched, outs, wait):
-    own_ref, opposite_ref, *near_refs = resident
-    mine = own_ref[...] + opposite_ref[...].astype(F32)
+def gather_theirs(place, resident, fetched, outs, wait):
     theirs = 0.0
-    for ref in near_refs:
-        mine = mine + ref[:16, :].astype(F32)
+    for ref in resident:
         theirs = theirs + ref[16:, :].astype(F32)
-    outs[0][...] = mine
-    outs[1][...] = theirs.astype(BF16)
+    outs[0][...] = theirs.astype(BF16)
 
 
 def finish(place, resident, fetched, outs, wait):
-    hidden_ref, keep_ref, got_ref = resident
+    hidden_ref, own_ref, got_ref, opposite_ref, *near_refs = resident
     hidden = jnp.where(
         place[1] == 0, hidden_ref[:16, :].astype(F32), hidden_ref[16:, :].astype(F32)
     )
-    moe = keep_ref[...] + got_ref[...].astype(F32)
+    moe = own_ref[...] + got_ref[...].astype(F32) + opposite_ref[...].astype(F32)
+    for ref in near_refs:
+        moe = moe + ref[:16, :].astype(F32)
     outs[0][...] = (hidden + moe).astype(BF16)
 
 
@@ -436,21 +434,17 @@
     sum_3, sum_4 = run_join(place, keep_far, got_far, [half, struct((16, D), BF16)])
     back_3 = on_both(sum_3, by_core(-3))
     back_4 = on_exp(sum_4, z_shift(4))
-    keep, to_core = kernel_call(
-        gather_up,
-        place,
-        [own_sum, back_4, back_1, back_2, back_3],
-        [],
-        [struct((16, D), F32), struct((16, D), BF16)],
-        8 * 16 * D,
+    near = [back_1, back_2, back_3]
+    (theirs,) = kernel_call(
+        gather_theirs, place, near, [], [struct((16, D), BF16)], 3 * 16 * D
     )
     return kernel_call(
         finish,
         place,
-        [hidden, keep, on_ctx(to_core, CORE_SWAP)],
+        [hidden, own_sum, on_ctx(theirs, CORE_SWAP), back_4, *near],
         [],
         [struct((16, D), BF16)],
-        3 * 16 * D,
+        7 * 16 * D,
     )[0]
 
 

time: 104 us -> 103 us (level)
  the two profiles are of different devices: /device:TPU:32 before, /device:TPU:49 now
where the time goes in v10:
time: 103 us
  starting transfers between devices  49.7 us (48%)
  waiting for transfers between devices  31.9 us (31%)
  Pallas kernels  13.5 us (13%)
  local copies, waits for them, and re-layouts  5.76 us (6%)
  other arithmetic  1.93 us (2%)
    ppermute x14, starting transfers between devices, on_ctx(): return lax.ppermute(block, 'ctx', route)  26.2 us
    ppermute x8, waiting for transfers between devices, on_both(): return lax.ppermute(block, ('ctx', 'exp'), route)  17.2 us
    pallas_call x11, Pallas kernels, kernel_call(): pl.pallas_call(whole, out_shape=out_shapes, in_specs=[pl.BlockSpec(memory...  13.5 us
    ppermute x8, starting transfers between devices, on_both(): return lax.ppermute(block, ('ctx', 'exp'), route)  12.7 us
    ppermute x8, starting transfers between devices, on_exp(): return lax.ppermute(block, 'exp', route)  10.8 us
    ppermute x8, waiting for transfers between devices, on_exp(): return lax.ppermute(block, 'exp', route)  7.84 us
    ppermute x14, waiting for transfers between devices, on_ctx(): return lax.ppermute(block, 'ctx', route)  6.89 us
  transfers between devices with their start and end apart: 30, of which 15 were waited for; matrix products, arithmetic and copies ran while one was open for 5% of the time, Pallas kernels for 9%

profile of v10, /device:TPU:49, one launch (start us, length us, event | category | flops | bytes accessed | tf_op | source)
XLA Modules:
  0.0 103.1 jit_solution(15912611802578245496)
XLA Ops:
  1.0 1.1 %collective-permute-start = (bf16[256,256]{1,0:T(8,128)(2,1)S(1)}, bf16[256,256]{1,0:T(8,128)(2,1)S(1)}, u32[]{:S(2)}, u32[]{:S(2)}) collective-permute-start(bf16[256,256]{1,0:T(8,128)(2,1)S(1)} %pad_maximum_fusion.2), channel_id=1, source_target_pairs={{0,128},{16,144},{32,160},{48,176},{64,192},{80,208},{96,224},{112... | collective-permute-start | bytes 393224 | tf_op jit(solution)/shard_map/ppermute | solution.py:40
  3.9 6.1 %collective-permute-start.1 = (bf16[128,640]{1,0:T(8,128)(2,1)S(1)}, bf16[128,640]{1,0:T(8,128)(2,1)S(1)}, u32[]{:S(2)}, u32[]{:S(2)}) collective-permute-start(bf16[128,640]{1,0:T(8,128)(2,1)S(1)} %pad_maximum_fusion.1), channel_id=1, source_target_pairs={{0,4},{1,5},{2,6},{3,7},{4,0},{5,1},{6,2},{7,3},{8,12},{9,13},{10,... | collective-permute-start | bytes 491528 | tf_op jit(solution)/shard_map/ppermute | solution.py:44
  10.0 1.0 slice_bitcast_fusion.15
  12.1 1.3 %collective-permute-start.4 = (bf16[512,256]{1,0:T(8,128)(2,1)S(1)}, bf16[512,256]{1,0:T(8,128)(2,1)S(1)}, u32[]{:S(2)}, u32[]{:S(2)}) collective-permute-start(bf16[512,256]{1,0:T(8,128)(2,1)S(1)} %pad_maximum_fusion.refs_3_), channel_id=1, source_target_pairs={{0,32},{16,48},{32,64},{48,80},{64,96},{80,112},{96,0},{112,16},{1... | collective-permute-start | bytes 786440 | tf_op jit(solution)/shard_map/ppermute | solution.py:40
  13.4 1.5 %collective-permute-start.5 = (bf16[512,256]{1,0:T(8,128)(2,1)S(1)}, bf16[512,256]{1,0:T(8,128)(2,1)S(1)}, u32[]{:S(2)}, u32[]{:S(2)}) collective-permute-start(bf16[512,256]{1,0:T(8,128)(2,1)S(1)} %pad_maximum_fusion.refs_3_), channel_id=1, source_target_pairs={{0,96},{16,112},{32,0},{48,16},{64,32},{80,48},{96,64},{112,80},{1... | collective-permute-start | bytes 786440 | tf_op jit(solution)/shard_map/ppermute | solution.py:40
  14.8 1.5 %collective-permute-start.6 = (bf16[512,256]{1,0:T(8,128)(2,1)S(1)}, bf16[512,256]{1,0:T(8,128)(2,1)S(1)}, u32[]{:S(2)}, u32[]{:S(2)}) collective-permute-start(bf16[512,256]{1,0:T(8,128)(2,1)S(1)} %pad_maximum_fusion.refs_3_), channel_id=1, source_target_pairs={{0,64},{16,80},{32,96},{48,112},{64,0},{80,16},{96,32},{112,48},{1... | collective-permute-start | bytes 786440 | tf_op jit(solution)/shard_map/ppermute | solution.py:40
  17.6 2.5 %collective-permute-start.3 = (bf16[256,128]{1,0:T(8,128)(2,1)S(1)}, bf16[256,128]{1,0:T(8,128)(2,1)S(1)}, u32[]{:S(2)}, u32[]{:S(2)}) collective-permute-start(bf16[256,128]{1,0:T(8,128)(2,1)S(1)} %pad_maximum_fusion.4.refs_1_), channel_id=1, source_target_pairs={{0,16},{16,0},{32,48},{48,32},{64,80},{80,64},{96,112},{112,96},{1... | collective-permute-start | bytes 196616 | tf_op jit(solution)/shard_map/ppermute | solution.py:40
  20.0 2.1 %collective-permute-done.2.refs_4_ = bf16[16,2176]{1,0:T(8,128)(2,1)S(1)} collective-permute-done((bf16[16,2176]{1,0:T(8,128)(2,1)S(1)}, bf16[16,2176]{1,0:T(8,128)(2,1)S(1)}, u32[]{:S(2)}, u32[]{:S(2)}) %collective-permute-start.2) | collective-permute-done | bytes 69664 | tf_op jit(solution)/shard_map/ppermute | solution.py:44
  22.4 4.1 %collective-permute-done.6.refs_6_ = bf16[512,256]{1,0:T(8,128)(2,1)S(1)} collective-permute-done((bf16[512,256]{1,0:T(8,128)(2,1)S(1)}, bf16[512,256]{1,0:T(8,128)(2,1)S(1)}, u32[]{:S(2)}, u32[]{:S(2)}) %collective-permute-start.6) | collective-permute-done | bytes 262176 | tf_op jit(solution)/shard_map/ppermute | solution.py:40
  26.5 2.7 %shard_map.109 = (f32[256,256]{1,0:T(8,128)S(1)}, f32[256,256]{1,0:T(8,128)S(1)}) custom-call(s32[4]{0:T(128)S(1)} %pad_add_fusion.refs_0_, bf16[256,128]{1,0:T(8,128)(2,1)S(1)} %pad_maximum_fusion.4.refs_1_, bf16[256,128]{1,0:T(8,128)(2,1)S(1)} %collective-permute-done.3.refs_2_, bf16[512,256]{1,0:T(8,128)(2,1)S(1)} %pad_maximum_fusion.refs_3_, ...), custom_call_target="tpu_custom_call" | custom-call | flops 536870912 | bytes 1179648 | tf_op jit(solution)/shard_map/pallas_call | solution.py:71
  29.2 2.2 %collective-permute-start.7 = (f32[256,256]{1,0:T(8,128)S(1)}, f32[256,256]{1,0:T(8,128)S(1)}, u32[]{:S(2)}, u32[]{:S(2)}) collective-permute-start(f32[256,256]{1,0:T(8,128)S(1)} %get-tuple-element.38), channel_id=1, source_target_pairs={{0,16},{16,0},{32,48},{48,32},{64,80},{80,64},{96,112},{112,96},{1... | collective-permute-start | bytes 786440 | tf_op jit(solution)/shard_map/ppermute | solution.py:40
  33.4 1.3 %shard_map.110 = (f32[32,2048]{1,0:T(8,128)S(1)}, bf16[32,2048]{1,0:T(8,128)(2,1)S(1)}, bf16[32,2048]{1,0:T(8,128)(2,1)S(1)}, bf16[32,2048]{1,0:T(8,128)(2,1)S(1)}) custom-call(s32[4]{0:T(128)S(1)} %pad_add_fusion.refs_0_, f32[256,256]{1,0:T(8,128)S(1)} %get-tuple-element.37.refs_1_, f32[256,256]{1,0:T(8,128)S(1)} %collective-permute-done.7.refs_2_, ...), custom_call_target="tpu_custom_call" | custom-call | flops 134217728 | bytes 1703936 | tf_op jit(solution)/shard_map/pallas_call | solution.py:71
  36.2 1.9 %collective-permute-start.15 = (bf16[32,2048]{1,0:T(8,128)(2,1)S(1)}, bf16[32,2048]{1,0:T(8,128)(2,1)S(1)}, u32[]{:S(2)}, u32[]{:S(2)}) collective-permute-start(bf16[32,2048]{1,0:T(8,128)(2,1)S(1)} %get-tuple-element.44), channel_id=1, source_target_pairs={{0,2},{1,3},{2,4},{3,5},{4,6},{5,7},{6,0},{7,1},{8,10},{9,11},{10,... | collective-permute-start | bytes 393224 | tf_op jit(solution)/shard_map/ppermute | solution.py:308
  38.2 1.3 %collective-permute-done.13.refs_2_ = bf16[32,2048]{1,0:T(8,128)(2,1)S(1)} collective-permute-done((bf16[32,2048]{1,0:T(8,128)(2,1)S(1)}, bf16[32,2048]{1,0:T(8,128)(2,1)S(1)}, u32[]{:S(2)}, u32[]{:S(2)}) %collective-permute-start.13) | collective-permute-done | bytes 131104 | tf_op jit(solution)/shard_map/ppermute | solution.py:44
  39.9 2.7 %collective-permute-done.15.refs_4_ = bf16[32,2048]{1,0:T(8,128)(2,1)S(1)} collective-permute-done((bf16[32,2048]{1,0:T(8,128)(2,1)S(1)}, bf16[32,2048]{1,0:T(8,128)(2,1)S(1)}, u32[]{:S(2)}, u32[]{:S(2)}) %collective-permute-start.15) | collective-permute-done | bytes 131104 | tf_op jit(solution)/shard_map/ppermute | solution.py:308
  43.7 3.2 %collective-permute-start.17 = (bf16[32,2048]{1,0:T(8,128)(2,1)S(1)}, bf16[32,2048]{1,0:T(8,128)(2,1)S(1)}, u32[]{:S(2)}, u32[]{:S(2)}) collective-permute-start(bf16[32,2048]{1,0:T(8,128)(2,1)S(1)} %get-tuple-element.49), channel_id=1, source_target_pairs={{0,16},{16,0},{32,48},{48,32},{64,80},{80,64},{96,112},{112,96},{1... | collective-permute-start | bytes 393224 | tf_op jit(solution)/shard_map/ppermute | solution.py:40
  46.9 1.7 %collective-permute-done.16.refs_7_ = bf16[32,2048]{1,0:T(8,128)(2,1)S(1)} collective-permute-done((bf16[32,2048]{1,0:T(8,128)(2,1)S(1)}, bf16[32,2048]{1,0:T(8,128)(2,1)S(1)}, u32[]{:S(2)}, u32[]{:S(2)}) %collective-permute-start.16) | collective-permute-done | bytes 131104 | tf_op jit(solution)/shard_map/ppermute | solution.py:44
  48.7 4.1 %collective-permute-start.18 = (bf16[32,2048]{1,0:T(8,128)(2,1)S(1)}, bf16[32,2048]{1,0:T(8,128)(2,1)S(1)}, u32[]{:S(2)}, u32[]{:S(2)}) collective-permute-start(bf16[32,2048]{1,0:T(8,128)(2,1)S(1)} %collective-permute-done.16.refs_7_), channel_id=1, source_target_pairs={{0,16},{16,0},{32,48},{48,32},{64,80},{80,64},{96,112},{112,96},{1... | collective-permute-start | bytes 393224 | tf_op jit(solution)/shard_map/ppermute | solution.py:40
  55.4 1.9 %copy-done.2 = bf16[1,768,2048]{2,1,0:T(8,128)(2,1)S(1)} copy-done((bf16[1,768,2048]{2,1,0:T(8,128)(2,1)S(1)}, bf16[1,768,2048]{2,1,0:T(8,128)(2,1)}, u32[]{:S(2)}) %copy-start.2) | copy-done | bytes 3145752
  57.8 6.5 %collective-permute-done.20.refs_5_ = bf16[64,2176]{1,0:T(8,128)(2,1)S(1)} collective-permute-done((bf16[64,2176]{1,0:T(8,128)(2,1)S(1)}, bf16[64,2176]{1,0:T(8,128)(2,1)S(1)}, u32[]{:S(2)}, u32[]{:S(2)}) %collective-permute-start.20) | collective-permute-done | bytes 278560 | tf_op jit(solution)/shard_map/ppermute | solution.py:308
  64.3 1.8 %collective-permute-start.25 = (bf16[32,2176]{1,0:T(8,128)(2,1)S(1)}, bf16[32,2176]{1,0:T(8,128)(2,1)S(1)}, u32[]{:S(2)}, u32[]{:S(2)}) collective-permute-start(bf16[32,2176]{1,0:T(8,128)(2,1)S(1)} %slice.75), channel_id=1, source_target_pairs={{0,2},{1,3},{2,4},{3,5},{4,6},{5,7},{6,0},{7,1},{8,10},{9,11},{10,... | collective-permute-start | bytes 417800 | tf_op jit(solution)/shard_map/ppermute | solution.py:308
  66.1 2.3 %shard_map.114 = (f32[80,2048]{1,0:T(8,128)S(1)}, bf16[80,2048]{1,0:T(8,128)(2,1)S(1)}) custom-call(s32[4]{0:T(128)S(1)} %pad_add_fusion.refs_0_, bf16[2048,768]{1,0:T(8,128)(2,1)S(1)} %bitcast.43, bf16[2048,768]{1,0:T(8,128)(2,1)S(1)} %bitcast.46, bf16[768,2048]{1,0:T(8,128)(2,1)S(1)} %bitcast.49, bf16[64,2176]{1,0:T(8,128)(2,1)S(1)} %collective-permute-done.19.refs_4_, ...), custom_call_target="tpu_custom_call" | custom-call | flops 1509949440 | bytes 10133504 | tf_op jit(solution)/shard_map/pallas_call | solution.py:71
  68.9 2.7 %collective-permute-done.25.refs_5_ = bf16[32,2176]{1,0:T(8,128)(2,1)S(1)} collective-permute-done((bf16[32,2176]{1,0:T(8,128)(2,1)S(1)}, bf16[32,2176]{1,0:T(8,128)(2,1)S(1)}, u32[]{:S(2)}, u32[]{:S(2)}) %collective-permute-start.25) | collective-permute-done | bytes 139296 | tf_op jit(solution)/shard_map/ppermute | solution.py:308
  71.6 2.3 %shard_map.116 = (f32[48,2048]{1,0:T(8,128)S(1)}, bf16[48,2048]{1,0:T(8,128)(2,1)S(1)}) custom-call(s32[4]{0:T(128)S(1)} %pad_add_fusion.refs_0_, bf16[2048,768]{1,0:T(8,128)(2,1)S(1)} %bitcast.44, bf16[2048,768]{1,0:T(8,128)(2,1)S(1)} %bitcast.47, bf16[768,2048]{1,0:T(8,128)(2,1)S(1)} %bitcast.50, bf16[64,2176]{1,0:T(8,128)(2,1)S(1)} %collective-permute-done.24.refs_4_, ...), custom_call_target="tpu_custom_call" | custom-call | flops 905969664 | bytes 9854976 | tf_op jit(solution)/shard_map/pallas_call | solution.py:71
  74.3 2.0 %collective-permute-done.21.refs_2_ = bf16[80,2048]{1,0:T(8,128)(2,1)S(1)} collective-permute-done((bf16[80,2048]{1,0:T(8,128)(2,1)S(1)}, bf16[80,2048]{1,0:T(8,128)(2,1)S(1)}, u32[]{:S(2)}, u32[]{:S(2)}) %collective-permute-start.21) | collective-permute-done | bytes 327712 | tf_op jit(solution)/shard_map/ppermute | solution.py:44
  76.9 2.0 %collective-permute-start.22 = (bf16[32,2048]{1,0:T(8,128)(2,1)S(1)}, bf16[32,2048]{1,0:T(8,128)(2,1)S(1)}, u32[]{:S(2)}, u32[]{:S(2)}) collective-permute-start(bf16[32,2048]{1,0:T(8,128)(2,1)S(1)} %get-tuple-element.57), channel_id=1, source_target_pairs={{0,7},{1,0},{2,1},{3,2},{4,3},{5,4},{6,5},{7,6},{8,15},{9,8},{10,9... | collective-permute-start | bytes 393224 | tf_op jit(solution)/shard_map/ppermute | solution.py:308
  78.9 2.5 %collective-permute-start.23 = (bf16[32,2048]{1,0:T(8,128)(2,1)S(1)}, bf16[32,2048]{1,0:T(8,128)(2,1)S(1)}, u32[]{:S(2)}, u32[]{:S(2)}) collective-permute-start(bf16[32,2048]{1,0:T(8,128)(2,1)S(1)} %get-tuple-element.58), channel_id=1, source_target_pairs={{0,6},{1,7},{2,0},{3,1},{4,2},{5,3},{6,4},{7,5},{8,14},{9,15},{10,... | collective-permute-start | bytes 393224 | tf_op jit(solution)/shard_map/ppermute | solution.py:308
  82.2 3.7 %collective-permute-start.27 = (bf16[32,2048]{1,0:T(8,128)(2,1)S(1)}, bf16[32,2048]{1,0:T(8,128)(2,1)S(1)}, u32[]{:S(2)}, u32[]{:S(2)}) collective-permute-start(bf16[32,2048]{1,0:T(8,128)(2,1)S(1)} %get-tuple-element.61), channel_id=1, source_target_pairs={{0,5},{1,6},{2,7},{3,0},{4,1},{5,2},{6,3},{7,4},{8,13},{9,14},{10,... | collective-permute-start | bytes 393224 | tf_op jit(solution)/shard_map/ppermute | solution.py:308
  85.9 1.6 %collective-permute-start.29 = (bf16[16,2048]{1,0:T(8,128)(2,1)S(1)}, bf16[16,2048]{1,0:T(8,128)(2,1)S(1)}, u32[]{:S(2)}, u32[]{:S(2)}) collective-permute-start(bf16[16,2048]{1,0:T(8,128)(2,1)S(1)} %get-tuple-element.62), channel_id=1, source_target_pairs={{0,4},{1,5},{2,6},{3,7},{4,0},{5,1},{6,2},{7,3},{8,12},{9,13},{10,... | collective-permute-start | bytes 196616 | tf_op jit(solution)/shard_map/ppermute | solution.py:44
  87.4 5.3 %collective-permute-done.27.refs_3_.refs_7_ = bf16[32,2048]{1,0:T(8,128)(2,1)S(1)} collective-permute-done((bf16[32,2048]{1,0:T(8,128)(2,1)S(1)}, bf16[32,2048]{1,0:T(8,128)(2,1)S(1)}, u32[]{:S(2)}, u32[]{:S(2)}) %collective-permute-start.27) | collective-permute-done | bytes 131104 | tf_op jit(solution)/shard_map/ppermute | solution.py:308
  93.3 7.6 %collective-permute-start.28 = (bf16[16,2048]{1,0:T(8,128)(2,1)S(1)}, bf16[16,2048]{1,0:T(8,128)(2,1)S(1)}, u32[]{:S(2)}, u32[]{:S(2)}) collective-permute-start(bf16[16,2048]{1,0:T(8,128)(2,1)S(1)} %shard_map.118), channel_id=1, source_target_pairs={{0,16},{16,0},{32,48},{48,32},{64,80},{80,64},{96,112},{112,96},{1... | collective-permute-start | bytes 196616 | tf_op jit(solution)/shard_map/ppermute | solution.py:40
  101.9 1.2 %shard_map.119 = bf16[16,2048]{1,0:T(8,128)(2,1)} custom-call(s32[4]{0:T(128)S(1)} %pad_add_fusion.refs_0_, bf16[32,2048]{1,0:T(8,128)(2,1)S(1)} %get-tuple-element.50.refs_1_, f32[16,2048]{1,0:T(8,128)S(1)} %get-tuple-element.56.refs_2_, bf16[16,2048]{1,0:T(8,128)(2,1)S(1)} %collective-permute-done.28.refs_3_, ...), custom_call_target="tpu_custom_call" | custom-call | flops 229376 | bytes 786432 | tf_op jit(solution)/shard_map/pallas_call | solution.py:71
  (67 shorter events, 17.1 us)
Async XLA Ops:
  0.9 51.8 %copy-start.5 = (bf16[2048]{0:T(1024)(128)(2,1)S(1)}, bf16[2048]{0:T(1024)(128)(2,1)}, u32[]{:S(2)}) copy-start(bf16[2048]{0:T(1024)(128)(2,1)} %param.16) | copy-start | bytes 12292
  1.0 11.1 %collective-permute-start = (bf16[256,256]{1,0:T(8,128)(2,1)S(1)}, bf16[256,256]{1,0:T(8,128)(2,1)S(1)}, u32[]{:S(2)}, u32[]{:S(2)}) collective-permute-start(bf16[256,256]{1,0:T(8,128)(2,1)S(1)} %pad_maximum_fusion.2), channel_id=1, source_target_pairs={{0,128},{16,144},{32,160},{48,176},{64,192},{80,208},{96,224},{112... | collective-permute-start | bytes 393224 | tf_op jit(solution)/shard_map/ppermute | solution.py:40
  3.8 51.6 %copy-start.1 = (bf16[1,2048,768]{2,1,0:T(8,128)(2,1)S(1)}, bf16[1,2048,768]{2,1,0:T(8,128)(2,1)}, u32[]{:S(2)}) copy-start(bf16[1,2048,768]{2,1,0:T(8,128)(2,1)} %param.20) | copy-start | bytes 9437188
  3.9 13.7 %collective-permute-start.1 = (bf16[128,640]{1,0:T(8,128)(2,1)S(1)}, bf16[128,640]{1,0:T(8,128)(2,1)S(1)}, u32[]{:S(2)}, u32[]{:S(2)}) collective-permute-start(bf16[128,640]{1,0:T(8,128)(2,1)S(1)} %pad_maximum_fusion.1), channel_id=1, source_target_pairs={{0,4},{1,5},{2,6},{3,7},{4,0},{5,1},{6,2},{7,3},{8,12},{9,13},{10,... | collective-permute-start | bytes 491528 | tf_op jit(solution)/shard_map/ppermute | solution.py:44
  12.1 10.3 %collective-permute-start.4 = (bf16[512,256]{1,0:T(8,128)(2,1)S(1)}, bf16[512,256]{1,0:T(8,128)(2,1)S(1)}, u32[]{:S(2)}, u32[]{:S(2)}) collective-permute-start(bf16[512,256]{1,0:T(8,128)(2,1)S(1)} %pad_maximum_fusion.refs_3_), channel_id=1, source_target_pairs={{0,32},{16,48},{32,64},{48,80},{64,96},{80,112},{96,0},{112,16},{1... | collective-permute-start | bytes 786440 | tf_op jit(solution)/shard_map/ppermute | solution.py:40
  13.4 9.1 %collective-permute-start.5 = (bf16[512,256]{1,0:T(8,128)(2,1)S(1)}, bf16[512,256]{1,0:T(8,128)(2,1)S(1)}, u32[]{:S(2)}, u32[]{:S(2)}) collective-permute-start(bf16[512,256]{1,0:T(8,128)(2,1)S(1)} %pad_maximum_fusion.refs_3_), channel_id=1, source_target_pairs={{0,96},{16,112},{32,0},{48,16},{64,32},{80,48},{96,64},{112,80},{1... | collective-permute-start | bytes 786440 | tf_op jit(solution)/shard_map/ppermute | solution.py:40
  14.8 11.7 %collective-permute-start.6 = (bf16[512,256]{1,0:T(8,128)(2,1)S(1)}, bf16[512,256]{1,0:T(8,128)(2,1)S(1)}, u32[]{:S(2)}, u32[]{:S(2)}) collective-permute-start(bf16[512,256]{1,0:T(8,128)(2,1)S(1)} %pad_maximum_fusion.refs_3_), channel_id=1, source_target_pairs={{0,64},{16,80},{32,96},{48,112},{64,0},{80,16},{96,32},{112,48},{1... | collective-permute-start | bytes 786440 | tf_op jit(solution)/shard_map/ppermute | solution.py:40
  17.2 5.0 %collective-permute-start.2 = (bf16[16,2176]{1,0:T(8,128)(2,1)S(1)}, bf16[16,2176]{1,0:T(8,128)(2,1)S(1)}, u32[]{:S(2)}, u32[]{:S(2)}) collective-permute-start(bf16[16,2176]{1,0:T(8,128)(2,1)S(1)} %pad_maximum_fusion.3.refs_1_), channel_id=1, source_target_pairs={{0,8},{1,9},{2,10},{3,11},{4,12},{5,13},{6,14},{7,15},{8,0},{9,1},... | collective-permute-start | bytes 208904 | tf_op jit(solution)/shard_map/ppermute | solution.py:44
  17.6 4.8 %collective-permute-start.3 = (bf16[256,128]{1,0:T(8,128)(2,1)S(1)}, bf16[256,128]{1,0:T(8,128)(2,1)S(1)}, u32[]{:S(2)}, u32[]{:S(2)}) collective-permute-start(bf16[256,128]{1,0:T(8,128)(2,1)S(1)} %pad_maximum_fusion.4.refs_1_), channel_id=1, source_target_pairs={{0,16},{16,0},{32,48},{48,32},{64,80},{80,64},{96,112},{112,96},{1... | collective-permute-start | bytes 196616 | tf_op jit(solution)/shard_map/ppermute | solution.py:40
  22.2 9.4 %collective-permute-start.10 = (bf16[128,640]{1,0:T(8,128)(2,1)S(1)}, bf16[128,640]{1,0:T(8,128)(2,1)S(1)}, u32[]{:S(2)}, u32[]{:S(2)}) collective-permute-start(bf16[128,640]{1,0:T(8,128)(2,1)S(1)} %collective-permute-done.1.refs_3_), channel_id=1, source_target_pairs={{0,128},{16,144},{32,160},{48,176},{64,192},{80,208},{96,224},{112... | collective-permute-start | bytes 491528 | tf_op jit(solution)/shard_map/ppermute | solution.py:40
  29.2 4.2 %collective-permute-start.7 = (f32[256,256]{1,0:T(8,128)S(1)}, f32[256,256]{1,0:T(8,128)S(1)}, u32[]{:S(2)}, u32[]{:S(2)}) collective-permute-start(f32[256,256]{1,0:T(8,128)S(1)} %get-tuple-element.38), channel_id=1, source_target_pairs={{0,16},{16,0},{32,48},{48,32},{64,80},{80,64},{96,112},{112,96},{1... | collective-permute-start | bytes 786440 | tf_op jit(solution)/shard_map/ppermute | solution.py:40
  31.4 1.9 %collective-permute-start.11 = (bf16[128,640]{1,0:T(8,128)(2,1)S(1)}, bf16[128,640]{1,0:T(8,128)(2,1)S(1)}, u32[]{:S(2)}, u32[]{:S(2)}) collective-permute-start(bf16[128,640]{1,0:T(8,128)(2,1)S(1)} %collective-permute-done.1.refs_3_), channel_id=1, source_target_pairs={{0,16},{16,0},{32,48},{48,32},{64,80},{80,64},{96,112},{112,96},{1... | collective-permute-start | bytes 491528 | tf_op jit(solution)/shard_map/ppermute | solution.py:40
  31.5 1.8 %collective-permute-start.12 = (bf16[128,640]{1,0:T(8,128)(2,1)S(1)}, bf16[128,640]{1,0:T(8,128)(2,1)S(1)}, u32[]{:S(2)}, u32[]{:S(2)}) collective-permute-start(bf16[128,640]{1,0:T(8,128)(2,1)S(1)} %collective-permute-done.10.refs_4_), channel_id=1, source_target_pairs={{0,16},{16,0},{32,48},{48,32},{64,80},{80,64},{96,112},{112,96},{1... | collective-permute-start | bytes 491528 | tf_op jit(solution)/shard_map/ppermute | solution.py:40
  31.9 1.3 %collective-permute-start.8 = (bf16[16,2176]{1,0:T(8,128)(2,1)S(1)}, bf16[16,2176]{1,0:T(8,128)(2,1)S(1)}, u32[]{:S(2)}, u32[]{:S(2)}) collective-permute-start(bf16[16,2176]{1,0:T(8,128)(2,1)S(1)} %pad_maximum_fusion.3.refs_1_), channel_id=1, source_target_pairs={{0,16},{16,0},{32,48},{48,32},{64,80},{80,64},{96,112},{112,96},{1... | collective-permute-start | bytes 208904 | tf_op jit(solution)/shard_map/ppermute | solution.py:40
  32.0 1.3 %collective-permute-start.9 = (bf16[16,2176]{1,0:T(8,128)(2,1)S(1)}, bf16[16,2176]{1,0:T(8,128)(2,1)S(1)}, u32[]{:S(2)}, u32[]{:S(2)}) collective-permute-start(bf16[16,2176]{1,0:T(8,128)(2,1)S(1)} %collective-permute-done.2.refs_4_), channel_id=1, source_target_pairs={{0,16},{16,0},{32,48},{48,32},{64,80},{80,64},{96,112},{112,96},{1... | collective-permute-start | bytes 208904 | tf_op jit(solution)/shard_map/ppermute | solution.py:40
  34.7 4.8 %collective-permute-start.13 = (bf16[32,2048]{1,0:T(8,128)(2,1)S(1)}, bf16[32,2048]{1,0:T(8,128)(2,1)S(1)}, u32[]{:S(2)}, u32[]{:S(2)}) collective-permute-start(bf16[32,2048]{1,0:T(8,128)(2,1)S(1)} %get-tuple-element.42), channel_id=1, source_target_pairs={{0,7},{1,0},{2,1},{3,2},{4,3},{5,4},{6,5},{7,6},{8,15},{9,8},{10,9... | collective-permute-start | bytes 393224 | tf_op jit(solution)/shard_map/ppermute | solution.py:44
  35.5 4.4 %collective-permute-start.14 = (bf16[32,2048]{1,0:T(8,128)(2,1)S(1)}, bf16[32,2048]{1,0:T(8,128)(2,1)S(1)}, u32[]{:S(2)}, u32[]{:S(2)}) collective-permute-start(bf16[32,2048]{1,0:T(8,128)(2,1)S(1)} %get-tuple-element.43), channel_id=1, source_target_pairs={{0,1},{1,2},{2,3},{3,4},{4,5},{5,6},{6,7},{7,0},{8,9},{9,10},{10,1... | collective-permute-start | bytes 393224 | tf_op jit(solution)/shard_map/ppermute | solution.py:44
  36.2 6.4 %collective-permute-start.15 = (bf16[32,2048]{1,0:T(8,128)(2,1)S(1)}, bf16[32,2048]{1,0:T(8,128)(2,1)S(1)}, u32[]{:S(2)}, u32[]{:S(2)}) collective-permute-start(bf16[32,2048]{1,0:T(8,128)(2,1)S(1)} %get-tuple-element.44), channel_id=1, source_target_pairs={{0,2},{1,3},{2,4},{3,5},{4,6},{5,7},{6,0},{7,1},{8,10},{9,11},{10,... | collective-permute-start | bytes 393224 | tf_op jit(solution)/shard_map/ppermute | solution.py:308
  43.3 5.4 %collective-permute-start.16 = (bf16[32,2048]{1,0:T(8,128)(2,1)S(1)}, bf16[32,2048]{1,0:T(8,128)(2,1)S(1)}, u32[]{:S(2)}, u32[]{:S(2)}) collective-permute-start(bf16[32,2048]{1,0:T(8,128)(2,1)S(1)} %get-tuple-element.49), channel_id=1, source_target_pairs={{0,8},{1,9},{2,10},{3,11},{4,12},{5,13},{6,14},{7,15},{8,0},{9,1},... | collective-permute-start | bytes 393224 | tf_op jit(solution)/shard_map/ppermute | solution.py:44
  43.7 9.1 %collective-permute-start.17 = (bf16[32,2048]{1,0:T(8,128)(2,1)S(1)}, bf16[32,2048]{1,0:T(8,128)(2,1)S(1)}, u32[]{:S(2)}, u32[]{:S(2)}) collective-permute-start(bf16[32,2048]{1,0:T(8,128)(2,1)S(1)} %get-tuple-element.49), channel_id=1, source_target_pairs={{0,16},{16,0},{32,48},{48,32},{64,80},{80,64},{96,112},{112,96},{1... | collective-permute-start | bytes 393224 | tf_op jit(solution)/shard_map/ppermute | solution.py:40
  48.7 5.1 %collective-permute-start.18 = (bf16[32,2048]{1,0:T(8,128)(2,1)S(1)}, bf16[32,2048]{1,0:T(8,128)(2,1)S(1)}, u32[]{:S(2)}, u32[]{:S(2)}) collective-permute-start(bf16[32,2048]{1,0:T(8,128)(2,1)S(1)} %collective-permute-done.16.refs_7_), channel_id=1, source_target_pairs={{0,16},{16,0},{32,48},{48,32},{64,80},{80,64},{96,112},{112,96},{1... | collective-permute-start | bytes 393224 | tf_op jit(solution)/shard_map/ppermute | solution.py:40
  54.6 9.7 %collective-permute-start.20 = (bf16[64,2176]{1,0:T(8,128)(2,1)S(1)}, bf16[64,2176]{1,0:T(8,128)(2,1)S(1)}, u32[]{:S(2)}, u32[]{:S(2)}) collective-permute-start(bf16[64,2176]{1,0:T(8,128)(2,1)S(1)} %get-tuple-element.51.refs_1_), channel_id=1, source_target_pairs={{0,2},{1,3},{2,4},{3,5},{4,6},{5,7},{6,0},{7,1},{8,10},{9,11},{10,... | collective-permute-start | bytes 835592 | tf_op jit(solution)/shard_map/ppermute | solution.py:308
  55.4 10.7 %collective-permute-start.19 = (bf16[64,2176]{1,0:T(8,128)(2,1)S(1)}, bf16[64,2176]{1,0:T(8,128)(2,1)S(1)}, u32[]{:S(2)}, u32[]{:S(2)}) collective-permute-start(bf16[64,2176]{1,0:T(8,128)(2,1)S(1)} %get-tuple-element.51.refs_1_), channel_id=1, source_target_pairs={{0,1},{1,2},{2,3},{3,4},{4,5},{5,6},{6,7},{7,0},{8,9},{9,10},{10,1... | collective-permute-start | bytes 835592 | tf_op jit(solution)/shard_map/ppermute | solution.py:308
  64.3 7.3 %collective-permute-start.24 = (bf16[64,2176]{1,0:T(8,128)(2,1)S(1)}, bf16[64,2176]{1,0:T(8,128)(2,1)S(1)}, u32[]{:S(2)}, u32[]{:S(2)}) collective-permute-start(bf16[64,2176]{1,0:T(8,128)(2,1)S(1)} %collective-permute-done.20.refs_5_), channel_id=1, source_target_pairs={{0,1},{1,2},{2,3},{3,4},{4,5},{5,6},{6,7},{7,0},{8,9},{9,10},{10,1... | collective-permute-start | bytes 835592 | tf_op jit(solution)/shard_map/ppermute | solution.py:308
  64.3 7.2 %collective-permute-start.25 = (bf16[32,2176]{1,0:T(8,128)(2,1)S(1)}, bf16[32,2176]{1,0:T(8,128)(2,1)S(1)}, u32[]{:S(2)}, u32[]{:S(2)}) collective-permute-start(bf16[32,2176]{1,0:T(8,128)(2,1)S(1)} %slice.75), channel_id=1, source_target_pairs={{0,2},{1,3},{2,4},{3,5},{4,6},{5,7},{6,0},{7,1},{8,10},{9,11},{10,... | collective-permute-start | bytes 417800 | tf_op jit(solution)/shard_map/ppermute | solution.py:308
  68.4 7.9 %collective-permute-start.21 = (bf16[80,2048]{1,0:T(8,128)(2,1)S(1)}, bf16[80,2048]{1,0:T(8,128)(2,1)S(1)}, u32[]{:S(2)}, u32[]{:S(2)}) collective-permute-start(bf16[80,2048]{1,0:T(8,128)(2,1)S(1)} %get-tuple-element.55), channel_id=1, source_target_pairs={{0,8},{1,9},{2,10},{3,11},{4,12},{5,13},{6,14},{7,15},{8,0},{9,1},... | collective-permute-start | bytes 983048 | tf_op jit(solution)/shard_map/ppermute | solution.py:44
  73.8 7.7 %collective-permute-start.26 = (bf16[48,2048]{1,0:T(8,128)(2,1)S(1)}, bf16[48,2048]{1,0:T(8,128)(2,1)S(1)}, u32[]{:S(2)}, u32[]{:S(2)}) collective-permute-start(bf16[48,2048]{1,0:T(8,128)(2,1)S(1)} %get-tuple-element.60), channel_id=1, source_target_pairs={{0,8},{1,9},{2,10},{3,11},{4,12},{5,13},{6,14},{7,15},{8,0},{9,1},... | collective-permute-start | bytes 589832 | tf_op jit(solution)/shard_map/ppermute | solution.py:44
  76.9 10.5 %collective-permute-start.22 = (bf16[32,2048]{1,0:T(8,128)(2,1)S(1)}, bf16[32,2048]{1,0:T(8,128)(2,1)S(1)}, u32[]{:S(2)}, u32[]{:S(2)}) collective-permute-start(bf16[32,2048]{1,0:T(8,128)(2,1)S(1)} %get-tuple-element.57), channel_id=1, source_target_pairs={{0,7},{1,0},{2,1},{3,2},{4,3},{5,4},{6,5},{7,6},{8,15},{9,8},{10,9... | collective-permute-start | bytes 393224 | tf_op jit(solution)/shard_map/ppermute | solution.py:308
  78.9 8.5 %collective-permute-start.23 = (bf16[32,2048]{1,0:T(8,128)(2,1)S(1)}, bf16[32,2048]{1,0:T(8,128)(2,1)S(1)}, u32[]{:S(2)}, u32[]{:S(2)}) collective-permute-start(bf16[32,2048]{1,0:T(8,128)(2,1)S(1)} %get-tuple-element.58), channel_id=1, source_target_pairs={{0,6},{1,7},{2,0},{3,1},{4,2},{5,3},{6,4},{7,5},{8,14},{9,15},{10,... | collective-permute-start | bytes 393224 | tf_op jit(solution)/shard_map/ppermute | solution.py:308
  82.2 10.6 %collective-permute-start.27 = (bf16[32,2048]{1,0:T(8,128)(2,1)S(1)}, bf16[32,2048]{1,0:T(8,128)(2,1)S(1)}, u32[]{:S(2)}, u32[]{:S(2)}) collective-permute-start(bf16[32,2048]{1,0:T(8,128)(2,1)S(1)} %get-tuple-element.61), channel_id=1, source_target_pairs={{0,5},{1,6},{2,7},{3,0},{4,1},{5,2},{6,3},{7,4},{8,13},{9,14},{10,... | collective-permute-start | bytes 393224 | tf_op jit(solution)/shard_map/ppermute | solution.py:308
  85.9 15.1 %collective-permute-start.29 = (bf16[16,2048]{1,0:T(8,128)(2,1)S(1)}, bf16[16,2048]{1,0:T(8,128)(2,1)S(1)}, u32[]{:S(2)}, u32[]{:S(2)}) collective-permute-start(bf16[16,2048]{1,0:T(8,128)(2,1)S(1)} %get-tuple-element.62), channel_id=1, source_target_pairs={{0,4},{1,5},{2,6},{3,7},{4,0},{5,1},{6,2},{7,3},{8,12},{9,13},{10,... | collective-permute-start | bytes 196616 | tf_op jit(solution)/shard_map/ppermute | solution.py:44
  93.3 8.5 %collective-permute-start.28 = (bf16[16,2048]{1,0:T(8,128)(2,1)S(1)}, bf16[16,2048]{1,0:T(8,128)(2,1)S(1)}, u32[]{:S(2)}, u32[]{:S(2)}) collective-permute-start(bf16[16,2048]{1,0:T(8,128)(2,1)S(1)} %shard_map.118), channel_id=1, source_target_pairs={{0,16},{16,0},{32,48},{48,32},{64,80},{80,64},{96,112},{112,96},{1... | collective-permute-start | bytes 196616 | tf_op jit(solution)/shard_map/ppermute | solution.py:40
  (4 other events, 95.6 us)

commit v11 on v10

--- a/solution.py
+++ b/solution.py
@@ -382,7 +382,6 @@
         512 * 2048,
     )
     joined = on_ctx(swap, CORE_SWAP)
-    joined, *extended_others = after(joined, *extended_others)
     keep, *sends = kernel_call(
         project,
         place,

time: 103 us -> 104 us (level)
  transfers between devices with their start and end apart: 30 -> 30, of which waited for: 15 -> 16; matrix products, arithmetic and copies ran while one was open for 5% -> 5% of each run, Pallas kernels for 9% -> 9%
where the time goes in v11:
time: 104 us; the launch traced here: 103 us
  starting transfers between devices  49.5 us (48%)
  waiting for transfers between devices  32.3 us (31%)
  Pallas kernels  13.5 us (13%)
  local copies, waits for them, and re-layouts  5.76 us (6%)
  other arithmetic  1.93 us (2%)
    ppermute x14, starting transfers between devices, on_ctx(): return lax.ppermute(block, 'ctx', route)  25.9 us
    ppermute x8, waiting for transfers between devices, on_both(): return lax.ppermute(block, ('ctx', 'exp'), route)  17.4 us
    pallas_call x11, Pallas kernels, kernel_call(): pl.pallas_call(whole, out_shape=out_shapes, in_specs=[pl.BlockSpec(memory...  13.5 us
    ppermute x8, starting transfers between devices, on_both(): return lax.ppermute(block, ('ctx', 'exp'), route)  12.7 us
    ppermute x8, starting transfers between devices, on_exp(): return lax.ppermute(block, 'exp', route)  10.9 us
    ppermute x8, waiting for transfers between devices, on_exp(): return lax.ppermute(block, 'exp', route)  7.88 us
    ppermute x14, waiting for transfers between devices, on_ctx(): return lax.ppermute(block, 'ctx', route)  7.02 us
  transfers between devices with their start and end apart: 30, of which 16 were waited for; matrix products, arithmetic and copies ran while one was open for 5% of the time, Pallas kernels for 9%

profile of v11, /device:TPU:49, one launch (start us, length us, event | category | flops | bytes accessed | tf_op | source)
XLA Modules:
  0.0 103.2 jit_solution(14950987604268478423)
XLA Ops:
  1.0 1.1 %collective-permute-start = (bf16[256,256]{1,0:T(8,128)(2,1)S(1)}, bf16[256,256]{1,0:T(8,128)(2,1)S(1)}, u32[]{:S(2)}, u32[]{:S(2)}) collective-permute-start(bf16[256,256]{1,0:T(8,128)(2,1)S(1)} %pad_maximum_fusion.2), channel_id=1, source_target_pairs={{0,128},{16,144},{32,160},{48,176},{64,192},{80,208},{96,224},{112... | collective-permute-start | bytes 393224 | tf_op jit(solution)/shard_map/ppermute | solution.py:40
  3.9 6.1 %collective-permute-start.1 = (bf16[128,640]{1,0:T(8,128)(2,1)S(1)}, bf16[128,640]{1,0:T(8,128)(2,1)S(1)}, u32[]{:S(2)}, u32[]{:S(2)}) collective-permute-start(bf16[128,640]{1,0:T(8,128)(2,1)S(1)} %pad_maximum_fusion.1), channel_id=1, source_target_pairs={{0,4},{1,5},{2,6},{3,7},{4,0},{5,1},{6,2},{7,3},{8,12},{9,13},{10,... | collective-permute-start | bytes 491528 | tf_op jit(solution)/shard_map/ppermute | solution.py:44
  10.0 1.0 slice_bitcast_fusion.15
  12.1 1.3 %collective-permute-start.4 = (bf16[512,256]{1,0:T(8,128)(2,1)S(1)}, bf16[512,256]{1,0:T(8,128)(2,1)S(1)}, u32[]{:S(2)}, u32[]{:S(2)}) collective-permute-start(bf16[512,256]{1,0:T(8,128)(2,1)S(1)} %pad_maximum_fusion.refs_3_), channel_id=1, source_target_pairs={{0,32},{16,48},{32,64},{48,80},{64,96},{80,112},{96,0},{112,16},{1... | collective-permute-start | bytes 786440 | tf_op jit(solution)/shard_map/ppermute | solution.py:40
  13.4 1.5 %collective-permute-start.5 = (bf16[512,256]{1,0:T(8,128)(2,1)S(1)}, bf16[512,256]{1,0:T(8,128)(2,1)S(1)}, u32[]{:S(2)}, u32[]{:S(2)}) collective-permute-start(bf16[512,256]{1,0:T(8,128)(2,1)S(1)} %pad_maximum_fusion.refs_3_), channel_id=1, source_target_pairs={{0,96},{16,112},{32,0},{48,16},{64,32},{80,48},{96,64},{112,80},{1... | collective-permute-start | bytes 786440 | tf_op jit(solution)/shard_map/ppermute | solution.py:40
  14.8 1.5 %collective-permute-start.6 = (bf16[512,256]{1,0:T(8,128)(2,1)S(1)}, bf16[512,256]{1,0:T(8,128)(2,1)S(1)}, u32[]{:S(2)}, u32[]{:S(2)}) collective-permute-start(bf16[512,256]{1,0:T(8,128)(2,1)S(1)} %pad_maximum_fusion.refs_3_), channel_id=1, source_target_pairs={{0,64},{16,80},{32,96},{48,112},{64,0},{80,16},{96,32},{112,48},{1... | collective-permute-start | bytes 786440 | tf_op jit(solution)/shard_map/ppermute | solution.py:40
  17.6 2.5 %collective-permute-start.3 = (bf16[256,128]{1,0:T(8,128)(2,1)S(1)}, bf16[256,128]{1,0:T(8,128)(2,1)S(1)}, u32[]{:S(2)}, u32[]{:S(2)}) collective-permute-start(bf16[256,128]{1,0:T(8,128)(2,1)S(1)} %pad_maximum_fusion.4.refs_1_), channel_id=1, source_target_pairs={{0,16},{16,0},{32,48},{48,32},{64,80},{80,64},{96,112},{112,96},{1... | collective-permute-start | bytes 196616 | tf_op jit(solution)/shard_map/ppermute | solution.py:40
  20.0 2.1 %collective-permute-done.2.refs_4_ = bf16[16,2176]{1,0:T(8,128)(2,1)S(1)} collective-permute-done((bf16[16,2176]{1,0:T(8,128)(2,1)S(1)}, bf16[16,2176]{1,0:T(8,128)(2,1)S(1)}, u32[]{:S(2)}, u32[]{:S(2)}) %collective-permute-start.2) | collective-permute-done | bytes 69664 | tf_op jit(solution)/shard_map/ppermute | solution.py:44
  22.4 4.1 %collective-permute-done.6.refs_6_ = bf16[512,256]{1,0:T(8,128)(2,1)S(1)} collective-permute-done((bf16[512,256]{1,0:T(8,128)(2,1)S(1)}, bf16[512,256]{1,0:T(8,128)(2,1)S(1)}, u32[]{:S(2)}, u32[]{:S(2)}) %collective-permute-start.6) | collective-permute-done | bytes 262176 | tf_op jit(solution)/shard_map/ppermute | solution.py:40
  26.5 2.7 %shard_map.109 = (f32[256,256]{1,0:T(8,128)S(1)}, f32[256,256]{1,0:T(8,128)S(1)}) custom-call(s32[4]{0:T(128)S(1)} %pad_add_fusion.refs_0_, bf16[256,128]{1,0:T(8,128)(2,1)S(1)} %pad_maximum_fusion.4.refs_1_, bf16[256,128]{1,0:T(8,128)(2,1)S(1)} %collective-permute-done.3.refs_2_, bf16[512,256]{1,0:T(8,128)(2,1)S(1)} %pad_maximum_fusion.refs_3_, ...), custom_call_target="tpu_custom_call" | custom-call | flops 536870912 | bytes 1179648 | tf_op jit(solution)/shard_map/pallas_call | solution.py:71
  29.2 2.3 %collective-permute-start.7 = (f32[256,256]{1,0:T(8,128)S(1)}, f32[256,256]{1,0:T(8,128)S(1)}, u32[]{:S(2)}, u32[]{:S(2)}) collective-permute-start(f32[256,256]{1,0:T(8,128)S(1)} %get-tuple-element.34), channel_id=1, source_target_pairs={{0,16},{16,0},{32,48},{48,32},{64,80},{80,64},{96,112},{112,96},{1... | collective-permute-start | bytes 786440 | tf_op jit(solution)/shard_map/ppermute | solution.py:40
  33.1 1.3 %shard_map.110 = (f32[32,2048]{1,0:T(8,128)S(1)}, bf16[32,2048]{1,0:T(8,128)(2,1)S(1)}, bf16[32,2048]{1,0:T(8,128)(2,1)S(1)}, bf16[32,2048]{1,0:T(8,128)(2,1)S(1)}) custom-call(s32[4]{0:T(128)S(1)} %pad_add_fusion.refs_0_, f32[256,256]{1,0:T(8,128)S(1)} %get-tuple-element.33.refs_1_, f32[256,256]{1,0:T(8,128)S(1)} %collective-permute-done.7.refs_2_, ...), custom_call_target="tpu_custom_call" | custom-call | flops 134217728 | bytes 1703936 | tf_op jit(solution)/shard_map/pallas_call | solution.py:71
  35.9 1.9 %collective-permute-start.13 = (bf16[32,2048]{1,0:T(8,128)(2,1)S(1)}, bf16[32,2048]{1,0:T(8,128)(2,1)S(1)}, u32[]{:S(2)}, u32[]{:S(2)}) collective-permute-start(bf16[32,2048]{1,0:T(8,128)(2,1)S(1)} %get-tuple-element.38), channel_id=1, source_target_pairs={{0,2},{1,3},{2,4},{3,5},{4,6},{5,7},{6,0},{7,1},{8,10},{9,11},{10,... | collective-permute-start | bytes 393224 | tf_op jit(solution)/shard_map/ppermute | solution.py:308
  37.8 1.4 %collective-permute-done.11.refs_2_ = bf16[32,2048]{1,0:T(8,128)(2,1)S(1)} collective-permute-done((bf16[32,2048]{1,0:T(8,128)(2,1)S(1)}, bf16[32,2048]{1,0:T(8,128)(2,1)S(1)}, u32[]{:S(2)}, u32[]{:S(2)}) %collective-permute-start.11) | collective-permute-done | bytes 131104 | tf_op jit(solution)/shard_map/ppermute | solution.py:44
  39.6 2.8 %collective-permute-done.13.refs_4_ = bf16[32,2048]{1,0:T(8,128)(2,1)S(1)} collective-permute-done((bf16[32,2048]{1,0:T(8,128)(2,1)S(1)}, bf16[32,2048]{1,0:T(8,128)(2,1)S(1)}, u32[]{:S(2)}, u32[]{:S(2)}) %collective-permute-start.13) | collective-permute-done | bytes 131104 | tf_op jit(solution)/shard_map/ppermute | solution.py:308
  43.6 3.3 %collective-permute-start.17 = (bf16[32,2048]{1,0:T(8,128)(2,1)S(1)}, bf16[32,2048]{1,0:T(8,128)(2,1)S(1)}, u32[]{:S(2)}, u32[]{:S(2)}) collective-permute-start(bf16[32,2048]{1,0:T(8,128)(2,1)S(1)} %get-tuple-element.41), channel_id=1, source_target_pairs={{0,16},{16,0},{32,48},{48,32},{64,80},{80,64},{96,112},{112,96},{1... | collective-permute-start | bytes 393224 | tf_op jit(solution)/shard_map/ppermute | solution.py:40
  46.8 1.7 %collective-permute-done.16.refs_7_ = bf16[32,2048]{1,0:T(8,128)(2,1)S(1)} collective-permute-done((bf16[32,2048]{1,0:T(8,128)(2,1)S(1)}, bf16[32,2048]{1,0:T(8,128)(2,1)S(1)}, u32[]{:S(2)}, u32[]{:S(2)}) %collective-permute-start.16) | collective-permute-done | bytes 131104 | tf_op jit(solution)/shard_map/ppermute | solution.py:44
  48.6 4.1 %collective-permute-start.18 = (bf16[32,2048]{1,0:T(8,128)(2,1)S(1)}, bf16[32,2048]{1,0:T(8,128)(2,1)S(1)}, u32[]{:S(2)}, u32[]{:S(2)}) collective-permute-start(bf16[32,2048]{1,0:T(8,128)(2,1)S(1)} %collective-permute-done.16.refs_7_), channel_id=1, source_target_pairs={{0,16},{16,0},{32,48},{48,32},{64,80},{80,64},{96,112},{112,96},{1... | collective-permute-start | bytes 393224 | tf_op jit(solution)/shard_map/ppermute | solution.py:40
  55.7 1.9 %copy-done.2 = bf16[1,768,2048]{2,1,0:T(8,128)(2,1)S(1)} copy-done((bf16[1,768,2048]{2,1,0:T(8,128)(2,1)S(1)}, bf16[1,768,2048]{2,1,0:T(8,128)(2,1)}, u32[]{:S(2)}) %copy-start.2) | copy-done | bytes 3145752
  58.2 6.5 %collective-permute-done.20.refs_5_ = bf16[64,2176]{1,0:T(8,128)(2,1)S(1)} collective-permute-done((bf16[64,2176]{1,0:T(8,128)(2,1)S(1)}, bf16[64,2176]{1,0:T(8,128)(2,1)S(1)}, u32[]{:S(2)}, u32[]{:S(2)}) %collective-permute-start.20) | collective-permute-done | bytes 278560 | tf_op jit(solution)/shard_map/ppermute | solution.py:308
  64.7 1.8 %collective-permute-start.25 = (bf16[32,2176]{1,0:T(8,128)(2,1)S(1)}, bf16[32,2176]{1,0:T(8,128)(2,1)S(1)}, u32[]{:S(2)}, u32[]{:S(2)}) collective-permute-start(bf16[32,2176]{1,0:T(8,128)(2,1)S(1)} %slice.75), channel_id=1, source_target_pairs={{0,2},{1,3},{2,4},{3,5},{4,6},{5,7},{6,0},{7,1},{8,10},{9,11},{10,... | collective-permute-start | bytes 417800 | tf_op jit(solution)/shard_map/ppermute | solution.py:308
  66.4 2.3 %shard_map.114 = (f32[80,2048]{1,0:T(8,128)S(1)}, bf16[80,2048]{1,0:T(8,128)(2,1)S(1)}) custom-call(s32[4]{0:T(128)S(1)} %pad_add_fusion.refs_0_, bf16[2048,768]{1,0:T(8,128)(2,1)S(1)} %bitcast.43, bf16[2048,768]{1,0:T(8,128)(2,1)S(1)} %bitcast.46, bf16[768,2048]{1,0:T(8,128)(2,1)S(1)} %bitcast.49, bf16[64,2176]{1,0:T(8,128)(2,1)S(1)} %collective-permute-done.19.refs_4_, ...), custom_call_target="tpu_custom_call" | custom-call | flops 1509949440 | bytes 10133504 | tf_op jit(solution)/shard_map/pallas_call | solution.py:71
  69.2 2.7 %collective-permute-done.25.refs_5_ = bf16[32,2176]{1,0:T(8,128)(2,1)S(1)} collective-permute-done((bf16[32,2176]{1,0:T(8,128)(2,1)S(1)}, bf16[32,2176]{1,0:T(8,128)(2,1)S(1)}, u32[]{:S(2)}, u32[]{:S(2)}) %collective-permute-start.25) | collective-permute-done | bytes 139296 | tf_op jit(solution)/shard_map/ppermute | solution.py:308
  71.9 2.3 %shard_map.116 = (f32[48,2048]{1,0:T(8,128)S(1)}, bf16[48,2048]{1,0:T(8,128)(2,1)S(1)}) custom-call(s32[4]{0:T(128)S(1)} %pad_add_fusion.refs_0_, bf16[2048,768]{1,0:T(8,128)(2,1)S(1)} %bitcast.44, bf16[2048,768]{1,0:T(8,128)(2,1)S(1)} %bitcast.47, bf16[768,2048]{1,0:T(8,128)(2,1)S(1)} %bitcast.50, bf16[64,2176]{1,0:T(8,128)(2,1)S(1)} %collective-permute-done.24.refs_4_, ...), custom_call_target="tpu_custom_call" | custom-call | flops 905969664 | bytes 9854976 | tf_op jit(solution)/shard_map/pallas_call | solution.py:71
  74.6 2.1 %collective-permute-done.21.refs_2_ = bf16[80,2048]{1,0:T(8,128)(2,1)S(1)} collective-permute-done((bf16[80,2048]{1,0:T(8,128)(2,1)S(1)}, bf16[80,2048]{1,0:T(8,128)(2,1)S(1)}, u32[]{:S(2)}, u32[]{:S(2)}) %collective-permute-start.21) | collective-permute-done | bytes 327712 | tf_op jit(solution)/shard_map/ppermute | solution.py:44
  77.3 2.0 %collective-permute-start.22 = (bf16[32,2048]{1,0:T(8,128)(2,1)S(1)}, bf16[32,2048]{1,0:T(8,128)(2,1)S(1)}, u32[]{:S(2)}, u32[]{:S(2)}) collective-permute-start(bf16[32,2048]{1,0:T(8,128)(2,1)S(1)} %get-tuple-element.49), channel_id=1, source_target_pairs={{0,7},{1,0},{2,1},{3,2},{4,3},{5,4},{6,5},{7,6},{8,15},{9,8},{10,9... | collective-permute-start | bytes 393224 | tf_op jit(solution)/shard_map/ppermute | solution.py:308
  79.3 2.5 %collective-permute-start.23 = (bf16[32,2048]{1,0:T(8,128)(2,1)S(1)}, bf16[32,2048]{1,0:T(8,128)(2,1)S(1)}, u32[]{:S(2)}, u32[]{:S(2)}) collective-permute-start(bf16[32,2048]{1,0:T(8,128)(2,1)S(1)} %get-tuple-element.50), channel_id=1, source_target_pairs={{0,6},{1,7},{2,0},{3,1},{4,2},{5,3},{6,4},{7,5},{8,14},{9,15},{10,... | collective-permute-start | bytes 393224 | tf_op jit(solution)/shard_map/ppermute | solution.py:308
  82.5 3.8 %collective-permute-start.27 = (bf16[32,2048]{1,0:T(8,128)(2,1)S(1)}, bf16[32,2048]{1,0:T(8,128)(2,1)S(1)}, u32[]{:S(2)}, u32[]{:S(2)}) collective-permute-start(bf16[32,2048]{1,0:T(8,128)(2,1)S(1)} %get-tuple-element.53), channel_id=1, source_target_pairs={{0,5},{1,6},{2,7},{3,0},{4,1},{5,2},{6,3},{7,4},{8,13},{9,14},{10,... | collective-permute-start | bytes 393224 | tf_op jit(solution)/shard_map/ppermute | solution.py:308
  86.3 1.4 %collective-permute-start.29 = (bf16[16,2048]{1,0:T(8,128)(2,1)S(1)}, bf16[16,2048]{1,0:T(8,128)(2,1)S(1)}, u32[]{:S(2)}, u32[]{:S(2)}) collective-permute-start(bf16[16,2048]{1,0:T(8,128)(2,1)S(1)} %get-tuple-element.54), channel_id=1, source_target_pairs={{0,4},{1,5},{2,6},{3,7},{4,0},{5,1},{6,2},{7,3},{8,12},{9,13},{10,... | collective-permute-start | bytes 196616 | tf_op jit(solution)/shard_map/ppermute | solution.py:44
  87.8 5.4 %collective-permute-done.27.refs_3_.refs_7_ = bf16[32,2048]{1,0:T(8,128)(2,1)S(1)} collective-permute-done((bf16[32,2048]{1,0:T(8,128)(2,1)S(1)}, bf16[32,2048]{1,0:T(8,128)(2,1)S(1)}, u32[]{:S(2)}, u32[]{:S(2)}) %collective-permute-start.27) | collective-permute-done | bytes 131104 | tf_op jit(solution)/shard_map/ppermute | solution.py:308
  93.8 7.3 %collective-permute-start.28 = (bf16[16,2048]{1,0:T(8,128)(2,1)S(1)}, bf16[16,2048]{1,0:T(8,128)(2,1)S(1)}, u32[]{:S(2)}, u32[]{:S(2)}) collective-permute-start(bf16[16,2048]{1,0:T(8,128)(2,1)S(1)} %shard_map.118), channel_id=1, source_target_pairs={{0,16},{16,0},{32,48},{48,32},{64,80},{80,64},{96,112},{112,96},{1... | collective-permute-start | bytes 196616 | tf_op jit(solution)/shard_map/ppermute | solution.py:40
  102.0 1.2 %shard_map.119 = bf16[16,2048]{1,0:T(8,128)(2,1)} custom-call(s32[4]{0:T(128)S(1)} %pad_add_fusion.refs_0_, bf16[32,2048]{1,0:T(8,128)(2,1)S(1)} %get-tuple-element.42.refs_1_, f32[16,2048]{1,0:T(8,128)S(1)} %get-tuple-element.48.refs_2_, bf16[16,2048]{1,0:T(8,128)(2,1)S(1)} %collective-permute-done.28.refs_3_, ...), custom_call_target="tpu_custom_call" | custom-call | flops 229376 | bytes 786432 | tf_op jit(solution)/shard_map/pallas_call | solution.py:71
  (67 shorter events, 17.4 us)
Async XLA Ops:
  0.9 52.3 %copy-start.5 = (bf16[2048]{0:T(1024)(128)(2,1)S(1)}, bf16[2048]{0:T(1024)(128)(2,1)}, u32[]{:S(2)}) copy-start(bf16[2048]{0:T(1024)(128)(2,1)} %param.16) | copy-start | bytes 12292
  1.0 11.1 %collective-permute-start = (bf16[256,256]{1,0:T(8,128)(2,1)S(1)}, bf16[256,256]{1,0:T(8,128)(2,1)S(1)}, u32[]{:S(2)}, u32[]{:S(2)}) collective-permute-start(bf16[256,256]{1,0:T(8,128)(2,1)S(1)} %pad_maximum_fusion.2), channel_id=1, source_target_pairs={{0,128},{16,144},{32,160},{48,176},{64,192},{80,208},{96,224},{112... | collective-permute-start | bytes 393224 | tf_op jit(solution)/shard_map/ppermute | solution.py:40
  3.8 51.9 %copy-start.1 = (bf16[1,2048,768]{2,1,0:T(8,128)(2,1)S(1)}, bf16[1,2048,768]{2,1,0:T(8,128)(2,1)}, u32[]{:S(2)}) copy-start(bf16[1,2048,768]{2,1,0:T(8,128)(2,1)} %param.20) | copy-start | bytes 9437188
  3.9 13.7 %collective-permute-start.1 = (bf16[128,640]{1,0:T(8,128)(2,1)S(1)}, bf16[128,640]{1,0:T(8,128)(2,1)S(1)}, u32[]{:S(2)}, u32[]{:S(2)}) collective-permute-start(bf16[128,640]{1,0:T(8,128)(2,1)S(1)} %pad_maximum_fusion.1), channel_id=1, source_target_pairs={{0,4},{1,5},{2,6},{3,7},{4,0},{5,1},{6,2},{7,3},{8,12},{9,13},{10,... | collective-permute-start | bytes 491528 | tf_op jit(solution)/shard_map/ppermute | solution.py:44
  12.1 10.3 %collective-permute-start.4 = (bf16[512,256]{1,0:T(8,128)(2,1)S(1)}, bf16[512,256]{1,0:T(8,128)(2,1)S(1)}, u32[]{:S(2)}, u32[]{:S(2)}) collective-permute-start(bf16[512,256]{1,0:T(8,128)(2,1)S(1)} %pad_maximum_fusion.refs_3_), channel_id=1, source_target_pairs={{0,32},{16,48},{32,64},{48,80},{64,96},{80,112},{96,0},{112,16},{1... | collective-permute-start | bytes 786440 | tf_op jit(solution)/shard_map/ppermute | solution.py:40
  13.4 9.1 %collective-permute-start.5 = (bf16[512,256]{1,0:T(8,128)(2,1)S(1)}, bf16[512,256]{1,0:T(8,128)(2,1)S(1)}, u32[]{:S(2)}, u32[]{:S(2)}) collective-permute-start(bf16[512,256]{1,0:T(8,128)(2,1)S(1)} %pad_maximum_fusion.refs_3_), channel_id=1, source_target_pairs={{0,96},{16,112},{32,0},{48,16},{64,32},{80,48},{96,64},{112,80},{1... | collective-permute-start | bytes 786440 | tf_op jit(solution)/shard_map/ppermute | solution.py:40
  14.8 11.7 %collective-permute-start.6 = (bf16[512,256]{1,0:T(8,128)(2,1)S(1)}, bf16[512,256]{1,0:T(8,128)(2,1)S(1)}, u32[]{:S(2)}, u32[]{:S(2)}) collective-permute-start(bf16[512,256]{1,0:T(8,128)(2,1)S(1)} %pad_maximum_fusion.refs_3_), channel_id=1, source_target_pairs={{0,64},{16,80},{32,96},{48,112},{64,0},{80,16},{96,32},{112,48},{1... | collective-permute-start | bytes 786440 | tf_op jit(solution)/shard_map/ppermute | solution.py:40
  17.2 5.0 %collective-permute-start.2 = (bf16[16,2176]{1,0:T(8,128)(2,1)S(1)}, bf16[16,2176]{1,0:T(8,128)(2,1)S(1)}, u32[]{:S(2)}, u32[]{:S(2)}) collective-permute-start(bf16[16,2176]{1,0:T(8,128)(2,1)S(1)} %pad_maximum_fusion.3.refs_1_), channel_id=1, source_target_pairs={{0,8},{1,9},{2,10},{3,11},{4,12},{5,13},{6,14},{7,15},{8,0},{9,1},... | collective-permute-start | bytes 208904 | tf_op jit(solution)/shard_map/ppermute | solution.py:44
  17.6 4.8 %collective-permute-start.3 = (bf16[256,128]{1,0:T(8,128)(2,1)S(1)}, bf16[256,128]{1,0:T(8,128)(2,1)S(1)}, u32[]{:S(2)}, u32[]{:S(2)}) collective-permute-start(bf16[256,128]{1,0:T(8,128)(2,1)S(1)} %pad_maximum_fusion.4.refs_1_), channel_id=1, source_target_pairs={{0,16},{16,0},{32,48},{48,32},{64,80},{80,64},{96,112},{112,96},{1... | collective-permute-start | bytes 196616 | tf_op jit(solution)/shard_map/ppermute | solution.py:40
  22.2 9.4 %collective-permute-start.8 = (bf16[128,640]{1,0:T(8,128)(2,1)S(1)}, bf16[128,640]{1,0:T(8,128)(2,1)S(1)}, u32[]{:S(2)}, u32[]{:S(2)}) collective-permute-start(bf16[128,640]{1,0:T(8,128)(2,1)S(1)} %collective-permute-done.1.refs_3_), channel_id=1, source_target_pairs={{0,128},{16,144},{32,160},{48,176},{64,192},{80,208},{96,224},{112... | collective-permute-start | bytes 491528 | tf_op jit(solution)/shard_map/ppermute | solution.py:40
  29.2 3.9 %collective-permute-start.7 = (f32[256,256]{1,0:T(8,128)S(1)}, f32[256,256]{1,0:T(8,128)S(1)}, u32[]{:S(2)}, u32[]{:S(2)}) collective-permute-start(f32[256,256]{1,0:T(8,128)S(1)} %get-tuple-element.34), channel_id=1, source_target_pairs={{0,16},{16,0},{32,48},{48,32},{64,80},{80,64},{96,112},{112,96},{1... | collective-permute-start | bytes 786440 | tf_op jit(solution)/shard_map/ppermute | solution.py:40
  31.4 1.4 %collective-permute-start.9 = (bf16[128,640]{1,0:T(8,128)(2,1)S(1)}, bf16[128,640]{1,0:T(8,128)(2,1)S(1)}, u32[]{:S(2)}, u32[]{:S(2)}) collective-permute-start(bf16[128,640]{1,0:T(8,128)(2,1)S(1)} %collective-permute-done.1.refs_3_), channel_id=1, source_target_pairs={{0,16},{16,0},{32,48},{48,32},{64,80},{80,64},{96,112},{112,96},{1... | collective-permute-start | bytes 491528 | tf_op jit(solution)/shard_map/ppermute | solution.py:40
  31.5 1.5 %collective-permute-start.10 = (bf16[128,640]{1,0:T(8,128)(2,1)S(1)}, bf16[128,640]{1,0:T(8,128)(2,1)S(1)}, u32[]{:S(2)}, u32[]{:S(2)}) collective-permute-start(bf16[128,640]{1,0:T(8,128)(2,1)S(1)} %collective-permute-done.8.refs_4_), channel_id=1, source_target_pairs={{0,16},{16,0},{32,48},{48,32},{64,80},{80,64},{96,112},{112,96},{1... | collective-permute-start | bytes 491528 | tf_op jit(solution)/shard_map/ppermute | solution.py:40
  34.4 4.8 %collective-permute-start.11 = (bf16[32,2048]{1,0:T(8,128)(2,1)S(1)}, bf16[32,2048]{1,0:T(8,128)(2,1)S(1)}, u32[]{:S(2)}, u32[]{:S(2)}) collective-permute-start(bf16[32,2048]{1,0:T(8,128)(2,1)S(1)} %get-tuple-element.36), channel_id=1, source_target_pairs={{0,7},{1,0},{2,1},{3,2},{4,3},{5,4},{6,5},{7,6},{8,15},{9,8},{10,9... | collective-permute-start | bytes 393224 | tf_op jit(solution)/shard_map/ppermute | solution.py:44
  35.2 4.4 %collective-permute-start.12 = (bf16[32,2048]{1,0:T(8,128)(2,1)S(1)}, bf16[32,2048]{1,0:T(8,128)(2,1)S(1)}, u32[]{:S(2)}, u32[]{:S(2)}) collective-permute-start(bf16[32,2048]{1,0:T(8,128)(2,1)S(1)} %get-tuple-element.37), channel_id=1, source_target_pairs={{0,1},{1,2},{2,3},{3,4},{4,5},{5,6},{6,7},{7,0},{8,9},{9,10},{10,1... | collective-permute-start | bytes 393224 | tf_op jit(solution)/shard_map/ppermute | solution.py:44
  35.9 6.5 %collective-permute-start.13 = (bf16[32,2048]{1,0:T(8,128)(2,1)S(1)}, bf16[32,2048]{1,0:T(8,128)(2,1)S(1)}, u32[]{:S(2)}, u32[]{:S(2)}) collective-permute-start(bf16[32,2048]{1,0:T(8,128)(2,1)S(1)} %get-tuple-element.38), channel_id=1, source_target_pairs={{0,2},{1,3},{2,4},{3,5},{4,6},{5,7},{6,0},{7,1},{8,10},{9,11},{10,... | collective-permute-start | bytes 393224 | tf_op jit(solution)/shard_map/ppermute | solution.py:308
  43.0 5.6 %collective-permute-start.16 = (bf16[32,2048]{1,0:T(8,128)(2,1)S(1)}, bf16[32,2048]{1,0:T(8,128)(2,1)S(1)}, u32[]{:S(2)}, u32[]{:S(2)}) collective-permute-start(bf16[32,2048]{1,0:T(8,128)(2,1)S(1)} %get-tuple-element.41), channel_id=1, source_target_pairs={{0,8},{1,9},{2,10},{3,11},{4,12},{5,13},{6,14},{7,15},{8,0},{9,1},... | collective-permute-start | bytes 393224 | tf_op jit(solution)/shard_map/ppermute | solution.py:44
  43.6 10.5 %collective-permute-start.17 = (bf16[32,2048]{1,0:T(8,128)(2,1)S(1)}, bf16[32,2048]{1,0:T(8,128)(2,1)S(1)}, u32[]{:S(2)}, u32[]{:S(2)}) collective-permute-start(bf16[32,2048]{1,0:T(8,128)(2,1)S(1)} %get-tuple-element.41), channel_id=1, source_target_pairs={{0,16},{16,0},{32,48},{48,32},{64,80},{80,64},{96,112},{112,96},{1... | collective-permute-start | bytes 393224 | tf_op jit(solution)/shard_map/ppermute | solution.py:40
  48.6 5.5 %collective-permute-start.18 = (bf16[32,2048]{1,0:T(8,128)(2,1)S(1)}, bf16[32,2048]{1,0:T(8,128)(2,1)S(1)}, u32[]{:S(2)}, u32[]{:S(2)}) collective-permute-start(bf16[32,2048]{1,0:T(8,128)(2,1)S(1)} %collective-permute-done.16.refs_7_), channel_id=1, source_target_pairs={{0,16},{16,0},{32,48},{48,32},{64,80},{80,64},{96,112},{112,96},{1... | collective-permute-start | bytes 393224 | tf_op jit(solution)/shard_map/ppermute | solution.py:40
  52.7 1.3 %collective-permute-start.14 = (bf16[16,2176]{1,0:T(8,128)(2,1)S(1)}, bf16[16,2176]{1,0:T(8,128)(2,1)S(1)}, u32[]{:S(2)}, u32[]{:S(2)}) collective-permute-start(bf16[16,2176]{1,0:T(8,128)(2,1)S(1)} %pad_maximum_fusion.3.refs_1_), channel_id=1, source_target_pairs={{0,16},{16,0},{32,48},{48,32},{64,80},{80,64},{96,112},{112,96},{1... | collective-permute-start | bytes 208904 | tf_op jit(solution)/shard_map/ppermute | solution.py:40
  52.7 1.4 %collective-permute-start.15 = (bf16[16,2176]{1,0:T(8,128)(2,1)S(1)}, bf16[16,2176]{1,0:T(8,128)(2,1)S(1)}, u32[]{:S(2)}, u32[]{:S(2)}) collective-permute-start(bf16[16,2176]{1,0:T(8,128)(2,1)S(1)} %collective-permute-done.2.refs_4_), channel_id=1, source_target_pairs={{0,16},{16,0},{32,48},{48,32},{64,80},{80,64},{96,112},{112,96},{1... | collective-permute-start | bytes 208904 | tf_op jit(solution)/shard_map/ppermute | solution.py:40
  54.9 9.7 %collective-permute-start.20 = (bf16[64,2176]{1,0:T(8,128)(2,1)S(1)}, bf16[64,2176]{1,0:T(8,128)(2,1)S(1)}, u32[]{:S(2)}, u32[]{:S(2)}) collective-permute-start(bf16[64,2176]{1,0:T(8,128)(2,1)S(1)} %get-tuple-element.43.refs_1_), channel_id=1, source_target_pairs={{0,2},{1,3},{2,4},{3,5},{4,6},{5,7},{6,0},{7,1},{8,10},{9,11},{10,... | collective-permute-start | bytes 835592 | tf_op jit(solution)/shard_map/ppermute | solution.py:308
  55.7 10.7 %collective-permute-start.19 = (bf16[64,2176]{1,0:T(8,128)(2,1)S(1)}, bf16[64,2176]{1,0:T(8,128)(2,1)S(1)}, u32[]{:S(2)}, u32[]{:S(2)}) collective-permute-start(bf16[64,2176]{1,0:T(8,128)(2,1)S(1)} %get-tuple-element.43.refs_1_), channel_id=1, source_target_pairs={{0,1},{1,2},{2,3},{3,4},{4,5},{5,6},{6,7},{7,0},{8,9},{9,10},{10,1... | collective-permute-start | bytes 835592 | tf_op jit(solution)/shard_map/ppermute | solution.py:308
  64.6 7.3 %collective-permute-start.24 = (bf16[64,2176]{1,0:T(8,128)(2,1)S(1)}, bf16[64,2176]{1,0:T(8,128)(2,1)S(1)}, u32[]{:S(2)}, u32[]{:S(2)}) collective-permute-start(bf16[64,2176]{1,0:T(8,128)(2,1)S(1)} %collective-permute-done.20.refs_5_), channel_id=1, source_target_pairs={{0,1},{1,2},{2,3},{3,4},{4,5},{5,6},{6,7},{7,0},{8,9},{9,10},{10,1... | collective-permute-start | bytes 835592 | tf_op jit(solution)/shard_map/ppermute | solution.py:308
  64.7 7.2 %collective-permute-start.25 = (bf16[32,2176]{1,0:T(8,128)(2,1)S(1)}, bf16[32,2176]{1,0:T(8,128)(2,1)S(1)}, u32[]{:S(2)}, u32[]{:S(2)}) collective-permute-start(bf16[32,2176]{1,0:T(8,128)(2,1)S(1)} %slice.75), channel_id=1, source_target_pairs={{0,2},{1,3},{2,4},{3,5},{4,6},{5,7},{6,0},{7,1},{8,10},{9,11},{10,... | collective-permute-start | bytes 417800 | tf_op jit(solution)/shard_map/ppermute | solution.py:308
  68.8 7.9 %collective-permute-start.21 = (bf16[80,2048]{1,0:T(8,128)(2,1)S(1)}, bf16[80,2048]{1,0:T(8,128)(2,1)S(1)}, u32[]{:S(2)}, u32[]{:S(2)}) collective-permute-start(bf16[80,2048]{1,0:T(8,128)(2,1)S(1)} %get-tuple-element.47), channel_id=1, source_target_pairs={{0,8},{1,9},{2,10},{3,11},{4,12},{5,13},{6,14},{7,15},{8,0},{9,1},... | collective-permute-start | bytes 983048 | tf_op jit(solution)/shard_map/ppermute | solution.py:44
  74.2 7.7 %collective-permute-start.26 = (bf16[48,2048]{1,0:T(8,128)(2,1)S(1)}, bf16[48,2048]{1,0:T(8,128)(2,1)S(1)}, u32[]{:S(2)}, u32[]{:S(2)}) collective-permute-start(bf16[48,2048]{1,0:T(8,128)(2,1)S(1)} %get-tuple-element.52), channel_id=1, source_target_pairs={{0,8},{1,9},{2,10},{3,11},{4,12},{5,13},{6,14},{7,15},{8,0},{9,1},... | collective-permute-start | bytes 589832 | tf_op jit(solution)/shard_map/ppermute | solution.py:44
  77.3 10.5 %collective-permute-start.22 = (bf16[32,2048]{1,0:T(8,128)(2,1)S(1)}, bf16[32,2048]{1,0:T(8,128)(2,1)S(1)}, u32[]{:S(2)}, u32[]{:S(2)}) collective-permute-start(bf16[32,2048]{1,0:T(8,128)(2,1)S(1)} %get-tuple-element.49), channel_id=1, source_target_pairs={{0,7},{1,0},{2,1},{3,2},{4,3},{5,4},{6,5},{7,6},{8,15},{9,8},{10,9... | collective-permute-start | bytes 393224 | tf_op jit(solution)/shard_map/ppermute | solution.py:308
  79.3 8.4 %collective-permute-start.23 = (bf16[32,2048]{1,0:T(8,128)(2,1)S(1)}, bf16[32,2048]{1,0:T(8,128)(2,1)S(1)}, u32[]{:S(2)}, u32[]{:S(2)}) collective-permute-start(bf16[32,2048]{1,0:T(8,128)(2,1)S(1)} %get-tuple-element.50), channel_id=1, source_target_pairs={{0,6},{1,7},{2,0},{3,1},{4,2},{5,3},{6,4},{7,5},{8,14},{9,15},{10,... | collective-permute-start | bytes 393224 | tf_op jit(solution)/shard_map/ppermute | solution.py:308
  82.5 10.7 %collective-permute-start.27 = (bf16[32,2048]{1,0:T(8,128)(2,1)S(1)}, bf16[32,2048]{1,0:T(8,128)(2,1)S(1)}, u32[]{:S(2)}, u32[]{:S(2)}) collective-permute-start(bf16[32,2048]{1,0:T(8,128)(2,1)S(1)} %get-tuple-element.53), channel_id=1, source_target_pairs={{0,5},{1,6},{2,7},{3,0},{4,1},{5,2},{6,3},{7,4},{8,13},{9,14},{10,... | collective-permute-start | bytes 393224 | tf_op jit(solution)/shard_map/ppermute | solution.py:308
  86.3 14.7 %collective-permute-start.29 = (bf16[16,2048]{1,0:T(8,128)(2,1)S(1)}, bf16[16,2048]{1,0:T(8,128)(2,1)S(1)}, u32[]{:S(2)}, u32[]{:S(2)}) collective-permute-start(bf16[16,2048]{1,0:T(8,128)(2,1)S(1)} %get-tuple-element.54), channel_id=1, source_target_pairs={{0,4},{1,5},{2,6},{3,7},{4,0},{5,1},{6,2},{7,3},{8,12},{9,13},{10,... | collective-permute-start | bytes 196616 | tf_op jit(solution)/shard_map/ppermute | solution.py:44
  93.8 8.2 %collective-permute-start.28 = (bf16[16,2048]{1,0:T(8,128)(2,1)S(1)}, bf16[16,2048]{1,0:T(8,128)(2,1)S(1)}, u32[]{:S(2)}, u32[]{:S(2)}) collective-permute-start(bf16[16,2048]{1,0:T(8,128)(2,1)S(1)} %shard_map.118), channel_id=1, source_target_pairs={{0,16},{16,0},{32,48},{48,32},{64,80},{80,64},{96,112},{112,96},{1... | collective-permute-start | bytes 196616 | tf_op jit(solution)/shard_map/ppermute | solution.py:40
  (4 other events, 95.6 us)
